TPU v7x, 32 devices: a whole 2x2x4 slice. The times are simulated.
32 devices in a mesh: seq: 8 (over z, core), chan: 4 (over y, x).
Axes of the slice: x: 2, y: 2, z: 4, core: 2. Of those that a mesh axis runs over, the one named last changes fastest.
Arguments:
- values: bfloat16 [2048, 4096], P('seq', 'chan'), may hold values from -6 to 6
- gate_in: bfloat16 [2048, 4096], P('seq', 'chan'), may hold values from -6 to 6
- gate_out: bfloat16 [2048, 4096], P('seq', 'chan'), may hold values from -6 to 6
- spectrum: float32 [2, 2, 1024, 4096], P(None, None, 'seq', 'chan'), may hold values from -6 to 6
- out_weight: bfloat16 [4096, 8192], P('chan'), may hold values from -0.125 to 0.125
Outputs:
- mixed: bfloat16 [2048, 8192], P('seq', 'chan')
All inputs are finite; a program needn't handle non-finite values.
Results may differ from a plain program's by a relative error of at most 0.024.
Values may be sent and summed in bfloat16 or wider, within the bound.
No kernel may reach another device: no remote copies, remote signals or barrier semaphores. Data moves between devices by JAX's collectives and lax.ppermute only.
A program may use at most 64 MiB of HBM per device.

v0:
```python
import math

import jax
import jax.numpy as jnp
from jax import lax
from jax.sharding import PartitionSpec as P

BLOCK = 1024


def angle_table(first, second, period):
    product = first[:, None] * second[None, :] % period
    return product.astype(jnp.float32) * (2.0 * math.pi / period)


def to_columns(data):
    return lax.all_to_all(data, "seq", split_axis=2, concat_axis=1, tiled=True)


def to_rows(data):
    return lax.all_to_all(data, "seq", split_axis=1, concat_axis=2, tiled=True)


def shards(values, gate_in, gate_out, spectrum, out_weight):
    seq_count = lax.axis_size("seq")
    seq_index = lax.axis_index("seq")
    tok_rows, chan_width = values.shape
    block_len = BLOCK
    block_rows = block_len // seq_count
    span = tok_rows // block_rows
    tokens_all = block_len * span
    col_share = span * chan_width // seq_count
    full_block = jnp.arange(block_len, dtype=jnp.int32)
    full_span = jnp.arange(span, dtype=jnp.int32)
    block_angle = angle_table(full_block, full_block, block_len)
    block_cos = jnp.cos(block_angle).astype(jnp.bfloat16)
    block_sin = jnp.sin(block_angle).astype(jnp.bfloat16)
    span_angle = angle_table(full_span, full_span, span)
    span_cos = jnp.cos(span_angle).astype(jnp.bfloat16)
    span_sin = jnp.sin(span_angle).astype(jnp.bfloat16)
    source = (values.astype(jnp.float32) * gate_in.astype(jnp.float32)).astype(jnp.bfloat16)
    spread = to_columns(source.reshape(1, block_rows, seq_count, col_share))
    columns = spread.reshape(block_len, col_share)
    cos_part = jnp.dot(jnp.transpose(block_cos), columns, preferred_element_type=jnp.float32)
    sin_part = jnp.dot(jnp.transpose(block_sin), columns, preferred_element_type=jnp.float32)
    col_pos = (seq_index * col_share + jnp.arange(col_share, dtype=jnp.int32)) // chan_width
    turn = angle_table(full_block, col_pos, tokens_all)
    turn_cos = jnp.cos(turn)
    turn_sin = jnp.sin(turn)
    twist_re = cos_part * turn_cos - sin_part * turn_sin
    twist_im = -sin_part * turn_cos - cos_part * turn_sin
    twisted = jnp.stack([twist_re, twist_im]).astype(jnp.bfloat16)
    arranged = to_rows(twisted).reshape(2, block_rows, span, chan_width)
    with_cos = jnp.einsum("bd,kcbh->kdch", span_cos, arranged, preferred_element_type=jnp.float32)
    with_sin = jnp.einsum("bd,kcbh->kdch", span_sin, arranged, preferred_element_type=jnp.float32)
    freq_re = with_cos[0] + with_sin[1]
    freq_im = with_cos[1] - with_sin[0]
    prod_re = freq_re * spectrum[0] - freq_im * spectrum[1]
    prod_im = freq_re * spectrum[1] + freq_im * spectrum[0]
    product = jnp.stack([prod_re, prod_im]).astype(jnp.bfloat16)
    back_cos = jnp.einsum("db,kdch->kcbh", span_cos, product, preferred_element_type=jnp.float32)
    back_sin = jnp.einsum("db,kdch->kcbh", span_sin, product, preferred_element_type=jnp.float32)
    back_re = (back_cos[0] - back_sin[1]) / span
    back_im = (back_cos[1] + back_sin[0]) / span
    local_freq = seq_index * block_rows + jnp.arange(block_rows, dtype=jnp.int32)
    turn_back = angle_table(local_freq, full_span, tokens_all)
    back_tc = jnp.cos(turn_back)[:, :, None]
    back_ts = jnp.sin(turn_back)[:, :, None]
    rotated = jnp.stack(
        [back_re * back_tc - back_im * back_ts, back_im * back_tc + back_re * back_ts]
    ).astype(jnp.bfloat16)
    gathered = to_columns(rotated.reshape(2, block_rows, seq_count, col_share)).reshape(
        2, block_len, col_share
    )
    summed = jnp.dot(block_cos, gathered[0], preferred_element_type=jnp.float32)
    summed = summed - jnp.dot(block_sin, gathered[1], preferred_element_type=jnp.float32)
    ordered = (summed / block_len).astype(jnp.bfloat16).reshape(1, block_len, col_share)
    conv = to_rows(ordered).reshape(tok_rows, chan_width)
    gated = (conv.astype(jnp.float32) * gate_out.astype(jnp.float32)).astype(jnp.bfloat16)
    partial_sum = jnp.dot(gated, out_weight, preferred_element_type=jnp.float32)
    mixed = lax.psum_scatter(
        partial_sum.astype(jnp.bfloat16), "chan", scatter_dimension=1, tiled=True
    )
    return mixed


def solution(mesh):
    placed = (
        P("seq", "chan"),
        P("seq", "chan"),
        P("seq", "chan"),
        P(None, None, "seq", "chan"),
        P("chan", None),
    )
    return jax.shard_map(
        shards, mesh=mesh, in_specs=placed, out_specs=P("seq", "chan"), check_vma=False
    )
```

profile of v0, /device:TPU:0, one launch (start us, length us, event | category | flops | bytes accessed | tf_op | source)
XLA Modules:
  0.0 278.6 jit_solution(7113191784648816883)
XLA Ops:
  6.5 1.4 multiply_convert_fusion.1
  7.9 0.3 reshape.107
  8.3 0.9 copy.33
  9.2 6.3 %all-to-all-start = ((bf16[1,128,8,256]{3,1,0,2:T(8,128)(2,1)}), bf16[1,128,8,256]{3,1,0,2:T(8,128)(2,1)S(1)}, u32[]{:S(2)}, u32[]{:S(2)}) async-start(bf16[1,128,8,256]{3,1,0,2:T(8,128)(2,1)} %copy.33), calls=%async_computation | async-start | bytes 1048576 | tf_op jit(solution)/shard_map/all_to_all | solution.py:17
  15.5 15.3 %all-to-all-done = bf16[1,128,8,256]{3,1,0,2:T(8,128)(2,1)S(1)} async-done(((bf16[1,128,8,256]{3,1,0,2:T(8,128)(2,1)}), bf16[1,128,8,256]{3,1,0,2:T(8,128)(2,1)S(1)}, u32[]{:S(2)}, u32[]{:S(2)}) %all-to-all-start) | async-done | bytes 524320 | tf_op jit(solution)/shard_map/all_to_all | solution.py:17
  30.8 17.0 %fusion.7 = f32[1024,256]{1,0:T(8,128)S(1)} fusion(bf16[1024,256]{1,0:T(8,128)(2,1)S(1)} %bitcast.66), kind=kOutput, calls=%fused_computation.13 | convolution fusion | flops 552599552 | bytes 1572864 | tf_op jit(solution)/shard_map/dot_general | solution.py:44
  47.8 20.6 %fusion.20 = (bf16[1,1024,256]{2,1,0:T(8,128)(2,1)S(1)}, bf16[1,1024,256]{2,1,0:T(8,128)(2,1)S(1)}) fusion(f32[1024,256]{1,0:T(8,128)S(1)} %fusion.7, s32[256]{0:T(256)S(1)} %and_select_fusion.2, bf16[1024,256]{1,0:T(8,128)(2,1)S(1)} %bitcast.67), kind=kOutput, calls=%fused_computation.51 | convolution fusion | flops 558628864 | bytes 2622464 | tf_op jit(solution)/shard_map/dot_general | solution.py:45
  68.4 0.1 pad_maximum_fusion
  68.5 2.0 copy.34
  70.6 3.6 %all-to-all-start.1 = ((bf16[2,1024,256]{2,0,1:T(2,128)(2,1)}), bf16[2,1024,256]{2,0,1:T(2,128)(2,1)S(1)}, u32[]{:S(2)}, u32[]{:S(2)}) async-start(bf16[2,1024,256]{2,0,1:T(2,128)(2,1)} %copy.34), calls=%async_computation.1 | async-start | bytes 2097152 | tf_op jit(solution)/shard_map/all_to_all | solution.py:21
  74.1 0.2 reduce-scatter.2.cloned.1.call-start
  74.4 0.1 cosine_multiply_fusion
  74.4 0.1 copy.38
  74.6 0.1 copy.39
  74.7 1.7 fusion.68
  76.4 24.3 %all-to-all-done.1 = bf16[2,1024,256]{2,0,1:T(2,128)(2,1)S(1)} async-done(((bf16[2,1024,256]{2,0,1:T(2,128)(2,1)}), bf16[2,1024,256]{2,0,1:T(2,128)(2,1)S(1)}, u32[]{:S(2)}, u32[]{:S(2)}) %all-to-all-start.1) | async-done | bytes 1048608 | tf_op jit(solution)/shard_map/all_to_all | solution.py:21
  100.7 1.6 copy.57
  102.2 1.5 reshape.109
  103.7 1.3 convolution_bitcast_fusion.2
  105.0 1.3 convolution_bitcast_fusion.3
  106.3 3.9 %subtract_convert_fusion.1 = (bf16[1,2,128,1024]{3,1,2,0:T(2,128)(2,1)S(1)}, bf16[1,2,128,1024]{3,1,2,0:T(2,128)(2,1)S(1)}) fusion(f32[1,2,128,1024]{3,2,1,0:T(8,128)S(1)} %get-tuple-element.12, f32[1,2,128,1024]{3,2,1,0:T(8,128)S(1)} %get-tuple-element.11, f32[2,2,128,1024]{3,1,2,0:T(2,128)S(1)} %convolution_bitcast_fusion.2, ...), kind=kLoop, calls=%fused_computation.44 | loop fusion | flops 2621440 | bytes 7340032 | tf_op jit(solution)/shard_map/convert.7
  110.2 1.3 convolution_bitcast_fusion.1
  111.5 1.3 convolution_bitcast_fusion
  112.8 1.7 subtract_convert_fusion
  114.4 0.2 stack.31
  114.6 0.1 copy.40
  114.7 0.2 stack.32
  115.0 0.1 copy.41
  115.1 0.1 pad_maximum_fusion.2
  115.2 29.0 %all_to_all.54 = bf16[2,128,8,256]{3,1,0,2:T(8,128)(2,1)S(1)} all-to-all(bf16[2,128,8,256]{3,1,0,2:T(8,128)(2,1)S(1)} %pad_maximum_fusion.2), channel_id=1, replica_groups=mesh['seq'=8,'chan'=4] {'seq'}, dimensions={2} | all-to-all | bytes 2097152 | tf_op jit(solution)/shard_map/all_to_all | solution.py:17
  144.2 0.1 copy.56
  144.3 0.1 fusion.69
  144.4 20.2 %fusion.6 = f32[1024,256]{1,0:T(8,128)S(1)} fusion(bf16[1024,256]{1,0:T(8,128)(2,1)S(1)} %bitcast.69), kind=kOutput, calls=%fused_computation.12 | convolution fusion | flops 552599552 | bytes 1572864 | tf_op jit(solution)/shard_map/dot_general | solution.py:75
  164.6 17.9 %fusion.13 = bf16[1,1024,256]{2,1,0:T(8,128)(2,1)S(1)} fusion(f32[1024,256]{1,0:T(8,128)S(1)} %fusion.6, bf16[1024,256]{1,0:T(8,128)(2,1)S(1)} %bitcast.68), kind=kOutput, calls=%fused_computation.26 | convolution fusion | flops 553385984 | bytes 2097152 | tf_op jit(solution)/shard_map/dot_general | solution.py:76
  182.5 0.8 copy.58
  183.3 0.5 broadcast.210
  183.9 3.8 %reduce = bf16[1024,256]{1,0:T(8,128)(2,1)S(1)} reduce(bf16[1024,1,256]{2,1,0:T(2,128)(2,1)S(1)} %bitcast.63, bf16[]{:T(256)} %broadcast.210), dimensions={1}, to_apply=%bitcast.60.reduce_sub_computation | reduce | bytes 1048578
  187.7 0.1 reshape.115
  187.8 17.8 %all_to_all.55 = bf16[8,2,16384]{2,1,0:T(2,128)(2,1)S(1)} all-to-all(bf16[8,2,16384]{2,1,0:T(2,128)(2,1)S(1)} %reshape.115), channel_id=1, replica_groups=mesh['seq'=8,'chan'=4] {'seq'}, dimensions={0} | all-to-all | bytes 1048576 | tf_op jit(solution)/shard_map/all_to_all | solution.py:21
  205.6 0.0 copy-start
  205.6 0.5 reshape.116
  206.1 1.1 convert_bitcast_fusion
  207.2 0.6 copy.44
  207.8 0.3 reshape.111
  208.1 0.0 copy-done
  208.1 11.8 %convolution_convert_fusion = bf16[256,8192]{1,0:T(8,128)(2,1)} fusion(bf16[1024,8192]{1,0:T(8,128)(2,1)} %param.9, f32[256,1024]{1,0:T(8,128)S(1)} %reshape.111, bf16[256,1024]{1,0:T(8,128)(2,1)S(1)} %copy-done), kind=kOutput, calls=%fused_computation | convolution fusion | flops 4297850880 | bytes 22544384 | tf_op jit(solution)/shard_map/dot_general | solution.py:80
  220.0 0.0 reduce-scatter.2.cloned.1.call-update
  220.0 51.7 %reduce-scatter.2.cloned.1.call-done = bf16[256,2048]{1,0:T(8,128)(2,1)} async-done(((bf16[256,8192]{1,0:T(8,128)(2,1)}), bf16[256,2048]{1,0:T(8,128)(2,1)}) %reduce-scatter.2.cloned.1.call-update) | async-done | bytes 1048592 | tf_op jit(solution)/shard_map/reduce_scatter | solution.py:81
  (2 shorter events, 0.0 us)
Async XLA Ops:
  9.2 21.7 %all-to-all-start = ((bf16[1,128,8,256]{3,1,0,2:T(8,128)(2,1)}), bf16[1,128,8,256]{3,1,0,2:T(8,128)(2,1)S(1)}, u32[]{:S(2)}, u32[]{:S(2)}) async-start(bf16[1,128,8,256]{3,1,0,2:T(8,128)(2,1)} %copy.33), calls=%async_computation | async-start | bytes 1048576 | tf_op jit(solution)/shard_map/all_to_all | solution.py:17
  70.6 30.1 %all-to-all-start.1 = ((bf16[2,1024,256]{2,0,1:T(2,128)(2,1)}), bf16[2,1024,256]{2,0,1:T(2,128)(2,1)S(1)}, u32[]{:S(2)}, u32[]{:S(2)}) async-start(bf16[2,1024,256]{2,0,1:T(2,128)(2,1)} %copy.34), calls=%async_computation.1 | async-start | bytes 2097152 | tf_op jit(solution)/shard_map/all_to_all | solution.py:21
  74.1 197.6 %reduce-scatter.2.cloned.1.call-start = ((), (), s32[]{:S(2)}) async-start(), calls=%async_computation.5 | async-start | bytes 5242880 | tf_op jit(solution)/shard_map/reduce_scatter | solution.py:81
  205.6 2.5 copy-start
Sparse Core Ops, SparseCore 0:
  220.1 51.5 reduce-scatter.1
where the time goes:
time: 279 us
  matrix products  92.6 us (33%)
  waiting for transfers between devices  91.4 us (33%)
  blocking collectives  46.8 us (17%)
  between operations  13.6 us (5%)
  other arithmetic  12.1 us (4%)
  local copies, waits for them, and re-layouts  11.9 us (4%)
  starting transfers between devices  10.1 us (4%)
    reduce_scatter x1, waiting for transfers between devices, shards(): lax.psum_scatter(partial_sum.astype(jnp.bfloat16), 'chan', scatter_dimens...  51.7 us
    all_to_all x1, blocking collectives, to_columns(): return lax.all_to_all(data, 'seq', split_axis=2, concat_axis=1, tiled=True)  29 us
    all_to_all x1, waiting for transfers between devices, to_rows(): return lax.all_to_all(data, 'seq', split_axis=1, concat_axis=2, tiled=True)  24.3 us
    dot_general x1, matrix products, shards(): jnp.dot(jnp.transpose(block_sin), columns, preferred_element_type=jnp.flo...  20.6 us
    dot_general x1, matrix products, shards(): summed = jnp.dot(block_cos, gathered[0], preferred_element_type=jnp.float32)  20.2 us
    dot_general x1, matrix products, shards(): jnp.dot(block_sin, gathered[1], preferred_element_type=jnp.float32)  17.9 us
    all_to_all x1, blocking collectives, to_rows(): return lax.all_to_all(data, 'seq', split_axis=1, concat_axis=2, tiled=True)  17.8 us
    dot_general x1, matrix products, shards(): jnp.dot(jnp.transpose(block_cos), columns, preferred_element_type=jnp.flo...  17 us
  transfers between devices with their start and end apart: 3, of which 3 were waited for; matrix products, arithmetic and copies ran while one was open for 1% of the time, Pallas kernels for 0%

commit v1 on v0

v1 whole, which is shorter than its diff:
```python
import functools
import math

import jax
import jax.numpy as jnp
import ml_dtypes
import numpy as np
from jax import lax
from jax.experimental import pallas as pl
from jax.experimental.pallas import tpu as pltpu
from jax.sharding import PartitionSpec as P

BLOCK = 1024
LANES = 128


def angles(first, second, period):
    return (np.arange(first)[:, None] * np.arange(second)[None, :] % period) * (2.0 * math.pi / period)


def rounded(table):
    return jnp.asarray(table.astype(np.float32).astype(ml_dtypes.bfloat16))


def split_rows(rows, span):
    out = lax.broadcasted_iota(jnp.int32, (rows, rows), 0)
    token = lax.broadcasted_iota(jnp.int32, (rows, rows), 1)
    block_rows = rows // span
    return jnp.where(token == (out % block_rows) * span + out // block_rows, 1.0, 0.0).astype(jnp.bfloat16)


def join_rows(rows, span):
    token = lax.broadcasted_iota(jnp.int32, (rows, rows), 0)
    held = lax.broadcasted_iota(jnp.int32, (rows, rows), 1)
    block_rows = rows // span
    return jnp.where(token == (held % block_rows) * span + held // block_rows, 1.0, 0.0).astype(jnp.bfloat16)


def pack_kernel(span, values_ref, gate_ref, spectrum_ref, out_ref):
    rows = values_ref.shape[0]
    block_rows = rows // span
    source = (values_ref[...].astype(jnp.float32) * gate_ref[...].astype(jnp.float32)).astype(jnp.bfloat16)
    source = jnp.dot(split_rows(rows, span), source, preferred_element_type=jnp.float32).astype(jnp.bfloat16)
    for dest in range(out_ref.shape[0]):
        lanes = slice(dest * LANES, (dest + 1) * LANES)
        for part in range(2):
            for d in range(span):
                out_ref[dest, part * span + d] = spectrum_ref[part, d, :, lanes].astype(jnp.bfloat16)
        for b in range(span):
            out_ref[dest, 2 * span + b] = source[b * block_rows:(b + 1) * block_rows, lanes]


def pack(values, gate_in, spectrum, seq_count):
    rows, width = values.shape
    _, span, block_rows, _ = spectrum.shape
    per_step = 2
    cols = per_step * LANES
    return pl.pallas_call(
        functools.partial(pack_kernel, span),
        grid=(seq_count // per_step,),
        in_specs=[
            pl.BlockSpec((rows, cols), lambda i: (0, i)),
            pl.BlockSpec((rows, cols), lambda i: (0, i)),
            pl.BlockSpec((2, span, block_rows, cols), lambda i: (0, 0, 0, i)),
        ],
        out_specs=pl.BlockSpec((per_step, 3 * span, block_rows, LANES), lambda i: (i, 0, 0, 0)),
        out_shape=jax.ShapeDtypeStruct((seq_count, 3 * span, block_rows, LANES), jnp.bfloat16),
        compiler_params=pltpu.CompilerParams(vmem_limit_bytes=16 << 20),
        name="pack",
    )(values, gate_in, spectrum)


def conv_kernel(parts, data_ref, cos_ref, sin_ref, turn_cos_ref, turn_sin_ref, *refs):
    outs, (cols_ref, re_ref, im_ref) = refs[:parts], refs[parts:]
    shares, _, rows, _ = data_ref.shape
    for s in range(shares):
        for b in range(2):
            cols_ref[s * rows:(s + 1) * rows, b * LANES:(b + 1) * LANES] = data_ref[s, 4 + b]
    step = 2 * rows
    for i in range(shares * rows // step):
        at = slice(i * step, (i + 1) * step)
        cols = cols_ref[...]
        first_re = jnp.dot(cos_ref[at, :], cols, preferred_element_type=jnp.float32)
        first_sin = jnp.dot(sin_ref[at, :], cols, preferred_element_type=jnp.float32)
        tc, ts = turn_cos_ref[at, :], turn_sin_ref[at, :]
        re0, im0 = first_re[:, :LANES], -first_sin[:, :LANES]
        re1, im1 = first_re[:, LANES:], -first_sin[:, LANES:]
        re1, im1 = re1 * tc + im1 * ts, im1 * tc - re1 * ts

        def filt(part):
            return jnp.concatenate([data_ref[2 * i, part], data_ref[2 * i + 1, part]], axis=0).astype(jnp.float32)

        f0r, f0i, f1r, f1i = re0 + re1, im0 + im1, re0 - re1, im0 - im1
        s0r, s1r, s0i, s1i = filt(0), filt(1), filt(2), filt(3)
        p0r, p0i = f0r * s0r - f0i * s0i, f0r * s0i + f0i * s0r
        p1r, p1i = f1r * s1r - f1i * s1i, f1r * s1i + f1i * s1r
        b0r, b0i = 0.5 * (p0r + p1r), 0.5 * (p0i + p1i)
        b1r, b1i = 0.5 * (p0r - p1r), 0.5 * (p0i - p1i)
        b1r, b1i = b1r * tc - b1i * ts, b1i * tc + b1r * ts
        re_ref[at, :] = jnp.concatenate([b0r, b1r], axis=1).astype(jnp.bfloat16)
        im_ref[at, :] = jnp.concatenate([b0i, b1i], axis=1).astype(jnp.bfloat16)
    scale = 1.0 / (shares * rows)
    part_rows = rows // parts
    for i in range(shares * rows // step):
        at = slice(i * step, (i + 1) * step)
        conv = jnp.dot(cos_ref[at, :], re_ref[...], preferred_element_type=jnp.float32)
        conv = conv - jnp.dot(sin_ref[at, :], im_ref[...], preferred_element_type=jnp.float32)
        conv = (conv * scale).astype(jnp.bfloat16)
        for s in range(2):
            for p in range(parts):
                begin = s * rows + p * part_rows
                for b in range(2):
                    outs[p][2 * i + s, b] = conv[begin:begin + part_rows, b * LANES:(b + 1) * LANES]


def convolve(data, parts):
    shares, _, rows, _ = data.shape
    block = shares * rows
    angle = angles(block, block, block)
    turn = np.broadcast_to(angles(block, 2, 2 * block)[:, 1:], (block, LANES))
    vmem = pl.BlockSpec(memory_space=pltpu.VMEM)
    return pl.pallas_call(
        functools.partial(conv_kernel, parts),
        in_specs=[vmem] * 5,
        out_specs=[vmem] * parts,
        out_shape=[jax.ShapeDtypeStruct((shares, 2, rows // parts, LANES), jnp.bfloat16)] * parts,
        scratch_shapes=[pltpu.VMEM((block, 2 * LANES), jnp.bfloat16)] * 3,
        compiler_params=pltpu.CompilerParams(vmem_limit_bytes=32 << 20),
        name="convolve",
    )(
        data, rounded(np.cos(angle)), rounded(np.sin(angle)),
        jnp.asarray(np.cos(turn).astype(np.float32)), jnp.asarray(np.sin(turn).astype(np.float32)),
    )


def project_kernel(me_ref, conv_ref, gate_ref, weight_ref, first_ref, second_ref, gated_ref):
    step = pl.program_id(0)

    @pl.when(step == 0)
    def _():
        shares, span, part_rows, _ = conv_ref.shape
        join = join_rows(span * part_rows, span)
        for s in range(shares):
            lanes = slice(s * LANES, (s + 1) * LANES)
            held = conv_ref[s].reshape(span * part_rows, LANES)
            conv = jnp.dot(join, held, preferred_element_type=jnp.float32)
            gated_ref[:, lanes] = (conv * gate_ref[:, lanes].astype(jnp.float32)).astype(jnp.bfloat16)

    partial_sum = jnp.dot(gated_ref[...], weight_ref[...], preferred_element_type=jnp.float32).astype(jnp.bfloat16)

    @pl.when(step < 2)
    def _():
        first_ref[0] = partial_sum

    @pl.when(step >= 2)
    def _():
        second_ref[0] = partial_sum


def project(me, conv, gate, weight, part, blocks):
    shares, span, part_rows, _ = conv.shape
    depth, width = weight.shape
    rows = span * part_rows
    cols = width // 8
    (f0, h0), (f1, h1), (f2, h2), (f3, h3) = blocks

    def column(i, me_ref):
        flip = jnp.where(i == 0, f0, jnp.where(i == 1, f1, jnp.where(i == 2, f2, f3)))
        half = jnp.where(i == 0, h0, jnp.where(i == 1, h1, jnp.where(i == 2, h2, h3)))
        return 0, (me_ref[0] ^ flip) * 2 + half

    shape = jax.ShapeDtypeStruct((2, rows, cols), jnp.bfloat16)
    return pl.pallas_call(
        project_kernel,
        grid_spec=pltpu.PrefetchScalarGridSpec(
            num_scalar_prefetch=1,
            grid=(4,),
            in_specs=[
                pl.BlockSpec((shares, span, part_rows, LANES), lambda i, m: (0, 0, 0, 0)),
                pl.BlockSpec((rows, depth), lambda i, m: (part, 0)),
                pl.BlockSpec((depth, cols), column),
            ],
            out_specs=[
                pl.BlockSpec((1, rows, cols), lambda i, m: (jnp.minimum(i, 1), 0, 0)),
                pl.BlockSpec((1, rows, cols), lambda i, m: (jnp.maximum(i - 2, 0), 0, 0)),
            ],
            scratch_shapes=[pltpu.VMEM((rows, depth), jnp.bfloat16)],
        ),
        out_shape=[shape, shape],
        compiler_params=pltpu.CompilerParams(vmem_limit_bytes=24 << 20),
        cost_estimate=pl.CostEstimate(
            flops=2 * rows * depth * cols * 4, bytes_accessed=2 * depth * cols * 4, transcendentals=0
        ),
        name="project",
    )(me, conv, gate, weight)


def swap(data, axis, flip):
    return lax.ppermute(data, axis, [(i, i ^ flip) for i in range(lax.axis_size(axis))])


def add(first, second):
    return (first.astype(jnp.float32) + second.astype(jnp.float32)).astype(jnp.bfloat16)


def by_channels(values, gate_in, gate_out, spectrum, out_weight):
    seq_count = lax.axis_size("seq")
    me = lax.axis_index("chan").astype(jnp.int32).reshape(1)
    parts = 2
    data = pack(values, gate_in, spectrum, seq_count)
    data = lax.all_to_all(data, "seq", split_axis=0, concat_axis=0, tiled=True)
    convs = convolve(data, parts)
    outs = []
    for part, conv in enumerate(convs):
        conv = lax.all_to_all(conv, "seq", split_axis=0, concat_axis=0, tiled=True)
        send_a, send_b = project(me, conv, gate_out, out_weight, part, ((1, 0), (3, 0), (2, 1), (3, 1)))
        keep_a, keep_b = project(me, conv, gate_out, out_weight, part, ((0, 0), (2, 0), (0, 1), (1, 1)))
        sum_a = add(keep_a, swap(send_a, "chan", 1))
        sum_b = add(keep_b, swap(send_b, "chan", 2))
        out_a = add(sum_a[0], swap(sum_a[1], "chan", 2))
        out_b = add(sum_b[0], swap(sum_b[1], "chan", 1))
        outs.append(jnp.concatenate([out_a, out_b], axis=1))
    return jnp.concatenate(outs, axis=0)


def to_columns(data):
    return lax.all_to_all(data, "seq", split_axis=2, concat_axis=1, tiled=True)


def to_rows(data):
    return lax.all_to_all(data, "seq", split_axis=1, concat_axis=2, tiled=True)


def by_frequencies(values, gate_in, gate_out, spectrum, out_weight):
    seq_count = lax.axis_size("seq")
    seq_index = lax.axis_index("seq")
    tok_rows, chan_width = values.shape
    block_rows = BLOCK // seq_count
    span = tok_rows // block_rows
    tokens_all = BLOCK * span
    col_share = span * chan_width // seq_count
    block_cos = rounded(np.cos(angles(BLOCK, BLOCK, BLOCK)))
    block_sin = rounded(np.sin(angles(BLOCK, BLOCK, BLOCK)))
    span_cos = rounded(np.cos(angles(span, span, span)))
    span_sin = rounded(np.sin(angles(span, span, span)))
    turn_all = angles(BLOCK, span, tokens_all)
    turn_cos_all = jnp.asarray(np.cos(turn_all).astype(np.float32))
    turn_sin_all = jnp.asarray(np.sin(turn_all).astype(np.float32))
    source = (values.astype(jnp.float32) * gate_in.astype(jnp.float32)).astype(jnp.bfloat16)
    spread = to_columns(source.reshape(1, block_rows, seq_count, col_share))
    columns = spread.reshape(BLOCK, col_share)
    cos_part = jnp.dot(jnp.transpose(block_cos), columns, preferred_element_type=jnp.float32)
    sin_part = jnp.dot(jnp.transpose(block_sin), columns, preferred_element_type=jnp.float32)
    col_pos = (seq_index * col_share + jnp.arange(col_share, dtype=jnp.int32)) // chan_width
    turn_cos = jnp.take(turn_cos_all, col_pos, axis=1)
    turn_sin = jnp.take(turn_sin_all, col_pos, axis=1)
    twist_re = cos_part * turn_cos - sin_part * turn_sin
    twist_im = -sin_part * turn_cos - cos_part * turn_sin
    twisted = jnp.stack([twist_re, twist_im]).astype(jnp.bfloat16)
    arranged = to_rows(twisted).reshape(2, block_rows, span, chan_width)
    with_cos = jnp.einsum("bd,kcbh->kdch", span_cos, arranged, preferred_element_type=jnp.float32)
    with_sin = jnp.einsum("bd,kcbh->kdch", span_sin, arranged, preferred_element_type=jnp.float32)
    freq_re = with_cos[0] + with_sin[1]
    freq_im = with_cos[1] - with_sin[0]
    prod_re = freq_re * spectrum[0] - freq_im * spectrum[1]
    prod_im = freq_re * spectrum[1] + freq_im * spectrum[0]
    product = jnp.stack([prod_re, prod_im]).astype(jnp.bfloat16)
    back_cos = jnp.einsum("db,kdch->kcbh", span_cos, product, preferred_element_type=jnp.float32)
    back_sin = jnp.einsum("db,kdch->kcbh", span_sin, product, preferred_element_type=jnp.float32)
    back_re = (back_cos[0] - back_sin[1]) / span
    back_im = (back_cos[1] + back_sin[0]) / span
    back_tc = lax.dynamic_slice_in_dim(turn_cos_all, seq_index * block_rows, block_rows)[:, :, None]
    back_ts = lax.dynamic_slice_in_dim(turn_sin_all, seq_index * block_rows, block_rows)[:, :, None]
    rotated = jnp.stack(
        [back_re * back_tc - back_im * back_ts, back_im * back_tc + back_re * back_ts]
    ).astype(jnp.bfloat16)
    gathered = to_columns(rotated.reshape(2, block_rows, seq_count, col_share)).reshape(2, BLOCK, col_share)
    summed = jnp.dot(block_cos, gathered[0], preferred_element_type=jnp.float32)
    summed = summed - jnp.dot(block_sin, gathered[1], preferred_element_type=jnp.float32)
    ordered = (summed / BLOCK).astype(jnp.bfloat16).reshape(1, BLOCK, col_share)
    conv = to_rows(ordered).reshape(tok_rows, chan_width)
    gated = (conv.astype(jnp.float32) * gate_out.astype(jnp.float32)).astype(jnp.bfloat16)
    partial_sum = jnp.dot(gated, out_weight, preferred_element_type=jnp.float32)
    return lax.psum_scatter(partial_sum.astype(jnp.bfloat16), "chan", scatter_dimension=1, tiled=True)


def shards(values, gate_in, gate_out, spectrum, out_weight):
    seq_count, chan_count = lax.axis_size("seq"), lax.axis_size("chan")
    _, span, block_rows, width = spectrum.shape
    one_lane_block = width == seq_count * LANES and seq_count % 2 == 0 and block_rows % 32 == 0
    if span == 2 and chan_count == 4 and one_lane_block:
        return by_channels(values, gate_in, gate_out, spectrum, out_weight)
    return by_frequencies(values, gate_in, gate_out, spectrum, out_weight)


def solution(mesh):
    placed = (
        P("seq", "chan"),
        P("seq", "chan"),
        P("seq", "chan"),
        P(None, None, "seq", "chan"),
        P("chan", None),
    )
    return jax.shard_map(
        shards, mesh=mesh, in_specs=placed, out_specs=P("seq", "chan"), check_vma=False
    )
```

time: 279 us -> 116 us (0.42)
  matrix products: 92.6 us -> 0 us
  waiting for transfers between devices: 91.4 us -> 13.2 us
  Pallas kernels: 0 us -> 15.8 us
  between operations: 13.6 us -> 0.24 us
  other arithmetic: 12.1 us -> 2.09 us
  blocking collectives: 46.8 us -> 56.4 us
  local copies, waits for them, and re-layouts: 11.9 us -> 17.2 us
    dot_general x9 -> x0, matrix products: 92.6 us -> none  [the longest x1 20.6 us: shards(): jnp.dot(jnp.transpose(block_sin), columns, preferred_element_type=jnp.flo...]
    reduce_scatter x1 -> x0, waiting for transfers between devices: 51.7 us -> none  [shards(): lax.psum_scatter(partial_sum.astype(jnp.bfloat16), 'chan', scatter_dimens...]
    all_to_all x2 -> x1, waiting for transfers between devices: 39.7 us -> 0.01 us  [by_channels(): conv = lax.all_to_all(conv, 'seq', split_axis=0, concat_axis=0, tiled=True)]
    unnamed x5 -> x22, local copies, waits for them, and re-layouts: 1.16 us -> 17.1 us
    pallas_call x0 -> x6, Pallas kernels: none -> 15.8 us  [the longest x4 11.3 us: project(): pl.pallas_call(project_kernel, grid_spec=pltpu.PrefetchScalarGridSpec(num...]
    ppermute x0 -> x8, waiting for transfers between devices: none -> 13.2 us  [swap(): lax.ppermute(data, axis, [(i, i ^ flip) for i in range(lax.axis_size(axis...]
    all_to_all x2, blocking collectives: 46.8 us -> 56.4 us  [the longest x1 44.2 us: by_channels(): data = lax.all_to_all(data, 'seq', split_axis=0, concat_axis=0, tiled=True)]
    ppermute x0 -> x8, starting transfers between devices: none -> 7.61 us  [swap(): lax.ppermute(data, axis, [(i, i ^ flip) for i in range(lax.axis_size(axis...]
  transfers between devices with their start and end apart: 3 -> 9, of which waited for: 3 -> 4; matrix products, arithmetic and copies ran while one was open for 1% -> 1% of each run, Pallas kernels for 0% -> 10%
where the time goes in v1:
time: 116 us
  blocking collectives  56.4 us (49%)
  local copies, waits for them, and re-layouts  17.2 us (15%)
  Pallas kernels  15.8 us (14%)
  waiting for transfers between devices  13.2 us (11%)
  starting transfers between devices  11 us (9%)
  other arithmetic  2.09 us (2%)
    all_to_all x1, blocking collectives, by_channels(): data = lax.all_to_all(data, 'seq', split_axis=0, concat_axis=0, tiled=True)  44.2 us
    unnamed x22, local copies, waits for them, and re-layouts  17.1 us
    ppermute x8, waiting for transfers between devices, swap(): lax.ppermute(data, axis, [(i, i ^ flip) for i in range(lax.axis_size(axis...  13.2 us
    all_to_all x1, blocking collectives, by_channels(): conv = lax.all_to_all(conv, 'seq', split_axis=0, concat_axis=0, tiled=True)  12.1 us
    pallas_call x4, Pallas kernels, project(): pl.pallas_call(project_kernel, grid_spec=pltpu.PrefetchScalarGridSpec(num...  11.3 us
    ppermute x8, starting transfers between devices, swap(): lax.ppermute(data, axis, [(i, i ^ flip) for i in range(lax.axis_size(axis...  7.61 us
    all_to_all x1, starting transfers between devices, by_channels(): conv = lax.all_to_all(conv, 'seq', split_axis=0, concat_axis=0, tiled=True)  3.41 us
    pallas_call x1, Pallas kernels, convolve(): pl.pallas_call(functools.partial(conv_kernel, parts), in_specs=[vmem] * 5...  3.22 us
  transfers between devices with their start and end apart: 9, of which 4 were waited for; matrix products, arithmetic and copies ran while one was open for 1% of the time, Pallas kernels for 10%

profile of v1, /device:TPU:0, one launch (start us, length us, event | category | flops | bytes accessed | tf_op | source)
XLA Modules:
  0.0 115.8 jit_solution(16726103773675844641)
XLA Ops:
  0.0 0.0 copy-start.4
  0.0 1.6 %copy-done.4 = f32[2,2,128,1024]{3,2,1,0:T(8,128)S(1)} copy-done((f32[2,2,128,1024]{3,2,1,0:T(8,128)S(1)}, f32[2,2,128,1024]{3,2,1,0:T(8,128)}, u32[]{:S(2)}) %copy-start.4) | copy-done | bytes 2097176
  1.6 0.0 copy-start.7
  1.6 1.0 copy-done.7
  2.6 0.0 copy-start.8
  2.6 1.0 copy-done.8
  3.7 0.0 copy-start.6
  3.7 1.3 %pack.1 = bf16[8,6,128,128]{3,2,1,0:T(8,128)(2,1)S(1)} custom-call(bf16[256,1024]{1,0:T(8,128)(2,1)S(1)} %copy-done.7, bf16[256,1024]{1,0:T(8,128)(2,1)S(1)} %copy-done.8, f32[2,2,128,1024]{3,2,1,0:T(8,128)S(1)} %copy-done.4), custom_call_target="tpu_custom_call" | custom-call | tf_op jit(solution)/shard_map/pack/pallas_call | solution.py:58
  4.9 0.0 copy-start.5
  5.0 0.0 copy-start.9
  5.0 0.0 copy-start.10
  5.0 44.2 %all_to_all.15.data_ref = bf16[8,6,128,128]{3,2,1,0:T(8,128)(2,1)S(1)} all-to-all(bf16[8,6,128,128]{3,2,1,0:T(8,128)(2,1)S(1)} %pack.1), channel_id=1, replica_groups=mesh['seq'=8,'chan'=4] {'seq'}, dimensions={0} | all-to-all | bytes 3145728 | tf_op jit(solution)/shard_map/all_to_all | solution.py:211
  49.2 0.0 copy-done.6
  49.2 0.0 copy-done.5
  49.2 0.0 copy-done.9
  49.2 0.0 copy-done.10
  49.2 0.0 copy-start.3
  49.2 3.2 %convolve.1 = (bf16[8,2,64,128]{3,2,1,0:T(8,128)(2,1)}, bf16[8,2,64,128]{3,2,1,0:T(8,128)(2,1)S(1)}) custom-call(bf16[8,6,128,128]{3,2,1,0:T(8,128)(2,1)S(1)} %all_to_all.15.data_ref, bf16[1024,1024]{1,0:T(8,128)(2,1)S(1)} %copy-done.6, bf16[1024,1024]{1,0:T(8,128)(2,1)S(1)} %copy-done.5, f32[1024,128]{1,0:T(8,128)S(1)} %copy-done.10, f32[1024,128]{1,0:T(8,128)S(1)} %copy-done.9), custom_call_target="tpu_custom_call" | custom-call | tf_op jit(solution)/shard_map/convolve/pallas_call | solution.py:122
  52.5 12.1 %all_to_all.16.conv_ref = bf16[8,2,64,128]{3,2,1,0:T(8,128)(2,1)S(1)} all-to-all(bf16[8,2,64,128]{3,2,1,0:T(8,128)(2,1)S(1)} %get-tuple-element.20), channel_id=1, replica_groups=mesh['seq'=8,'chan'=4] {'seq'}, dimensions={0} | all-to-all | bytes 524288 | tf_op jit(solution)/shard_map/all_to_all | solution.py:215
  64.6 3.4 %all-to-all-start.1 = ((bf16[8,2,64,128]{3,2,1,0:T(8,128)(2,1)}), bf16[8,2,64,128]{3,2,1,0:T(8,128)(2,1)S(1)}, u32[]{:S(2)}, u32[]{:S(2)}) async-start(bf16[8,2,64,128]{3,2,1,0:T(8,128)(2,1)} %get-tuple-element.15), calls=%async_computation.1 | async-start | bytes 524288 | tf_op jit(solution)/shard_map/all_to_all | solution.py:215
  68.0 0.0 copy-done.3
  68.0 0.0 copy-start
  68.0 5.8 %copy-done = bf16[1024,8192]{1,0:T(8,128)(2,1)S(1)} copy-done((bf16[1024,8192]{1,0:T(8,128)(2,1)S(1)}, bf16[1024,8192]{1,0:T(8,128)(2,1)}, u32[]{:S(2)}) %copy-start) | copy-done | bytes 16777240
  73.8 2.8 %project.7 = (bf16[2,128,1024]{2,1,0:T(8,128)(2,1)S(1)}, bf16[2,128,1024]{2,1,0:T(8,128)(2,1)S(1)}) custom-call(s32[1]{0:T(128)} %bitcast.me_ref, bf16[8,2,64,128]{3,2,1,0:T(8,128)(2,1)S(1)} %all_to_all.16.conv_ref, bf16[256,1024]{1,0:T(8,128)(2,1)S(1)} %copy-done.3, bf16[1024,8192]{1,0:T(8,128)(2,1)S(1)} %copy-done), custom_call_target="tpu_custom_call" | custom-call | flops 1073741824 | bytes 8388608 | tf_op jit(solution)/shard_map/project/pallas_call | solution.py:173
  76.6 1.6 %collective-permute-start.4 = (bf16[2,128,1024]{2,1,0:T(8,128)(2,1)S(1)}, bf16[2,128,1024]{2,1,0:T(8,128)(2,1)S(1)}, u32[]{:S(2)}, u32[]{:S(2)}) collective-permute-start(bf16[2,128,1024]{2,1,0:T(8,128)(2,1)S(1)} %get-tuple-element.22), channel_id=1, source_target_pairs={{0,1},{1,0},{2,3},{3,2},{4,5},{5,4},{6,7},{7,6},{8,9},{9,8},{10,11... | collective-permute-start | bytes 1572872 | tf_op jit(solution)/shard_map/ppermute | solution.py:199
  78.2 1.5 %collective-permute-start.6 = (bf16[2,128,1024]{2,1,0:T(8,128)(2,1)S(1)}, bf16[2,128,1024]{2,1,0:T(8,128)(2,1)S(1)}, u32[]{:S(2)}, u32[]{:S(2)}) collective-permute-start(bf16[2,128,1024]{2,1,0:T(8,128)(2,1)S(1)} %get-tuple-element.24), channel_id=1, source_target_pairs={{0,2},{1,3},{2,0},{3,1},{4,6},{5,7},{6,4},{7,5},{8,10},{9,11},{10,... | collective-permute-start | bytes 1572872 | tf_op jit(solution)/shard_map/ppermute | solution.py:199
  79.7 0.0 all-to-all-done.1.conv_ref
  79.7 0.0 copy-start.1
  79.7 5.8 %copy-done.1 = bf16[1024,8192]{1,0:T(8,128)(2,1)S(1)} copy-done((bf16[1024,8192]{1,0:T(8,128)(2,1)S(1)}, bf16[1024,8192]{1,0:T(8,128)(2,1)}, u32[]{:S(2)}) %copy-start.1) | copy-done | bytes 16777240
  85.5 0.0 copy-start.2
  85.5 2.8 %project.5 = (bf16[2,128,1024]{2,1,0:T(8,128)(2,1)S(1)}, bf16[2,128,1024]{2,1,0:T(8,128)(2,1)S(1)}) custom-call(s32[1]{0:T(128)} %bitcast.me_ref, bf16[8,2,64,128]{3,2,1,0:T(8,128)(2,1)S(1)} %all-to-all-done.1.conv_ref, bf16[256,1024]{1,0:T(8,128)(2,1)S(1)} %copy-done.3, bf16[1024,8192]{1,0:T(8,128)(2,1)S(1)} %copy-done.1), custom_call_target="tpu_custom_call" | custom-call | flops 1073741824 | bytes 8388608 | tf_op jit(solution)/shard_map/project/pallas_call | solution.py:173
  88.3 0.6 collective-permute-start
  88.9 0.5 collective-permute-start.2
  89.4 1.8 %copy-done.2 = bf16[1024,8192]{1,0:T(8,128)(2,1)S(1)} copy-done((bf16[1024,8192]{1,0:T(8,128)(2,1)S(1)}, bf16[1024,8192]{1,0:T(8,128)(2,1)}, u32[]{:S(2)}) %copy-start.2) | copy-done | bytes 16777240
  91.3 2.8 %project.6 = (bf16[2,128,1024]{2,1,0:T(8,128)(2,1)S(1)}, bf16[2,128,1024]{2,1,0:T(8,128)(2,1)S(1)}) custom-call(s32[1]{0:T(128)} %bitcast.me_ref, bf16[8,2,64,128]{3,2,1,0:T(8,128)(2,1)S(1)} %all_to_all.16.conv_ref, bf16[256,1024]{1,0:T(8,128)(2,1)S(1)} %copy-done.3, bf16[1024,8192]{1,0:T(8,128)(2,1)S(1)} %copy-done.2), custom_call_target="tpu_custom_call" | custom-call | flops 1073741824 | bytes 8388608 | tf_op jit(solution)/shard_map/project/pallas_call | solution.py:173
  94.1 2.8 %project.4 = (bf16[2,128,1024]{2,1,0:T(8,128)(2,1)S(1)}, bf16[2,128,1024]{2,1,0:T(8,128)(2,1)S(1)}) custom-call(s32[1]{0:T(128)} %bitcast.me_ref, bf16[8,2,64,128]{3,2,1,0:T(8,128)(2,1)S(1)} %all-to-all-done.1.conv_ref, bf16[256,1024]{1,0:T(8,128)(2,1)S(1)} %copy-done.3, bf16[1024,8192]{1,0:T(8,128)(2,1)S(1)} %copy-done.2), custom_call_target="tpu_custom_call" | custom-call | flops 1073741824 | bytes 8388608 | tf_op jit(solution)/shard_map/project/pallas_call | solution.py:173
  97.0 0.0 collective-permute-done.4
  97.0 0.2 add_convert_fusion.1
  97.2 0.6 collective-permute-start.5
  97.8 0.0 collective-permute-done.6
  97.8 0.2 add_convert_fusion
  98.0 0.7 collective-permute-start.7
  98.7 4.5 %collective-permute-done = bf16[2,128,1024]{2,1,0:T(8,128)(2,1)S(1)} collective-permute-done((bf16[2,128,1024]{2,1,0:T(8,128)(2,1)S(1)}, bf16[2,128,1024]{2,1,0:T(8,128)(2,1)S(1)}, u32[]{:S(2)}, u32[]{:S(2)}) %collective-permute-start) | collective-permute-done | bytes 524320 | tf_op jit(solution)/shard_map/ppermute | solution.py:199
  103.2 0.2 add_convert_fusion.3
  103.4 0.8 collective-permute-done.2
  104.2 0.2 add_convert_fusion.2
  104.5 1.6 %collective-permute-start.1 = (bf16[128,1024]{1,0:T(8,128)(2,1)S(1)}, bf16[128,1024]{1,0:T(8,128)(2,1)S(1)}, u32[]{:S(2)}, u32[]{:S(2)}) collective-permute-start(bf16[128,1024]{1,0:T(8,128)(2,1)S(1)} %slice_bitcast_fusion.6), channel_id=1, source_target_pairs={{0,2},{1,3},{2,0},{3,1},{4,6},{5,7},{6,4},{7,5},{8,10},{9,11},{10,... | collective-permute-start | bytes 786440 | tf_op jit(solution)/shard_map/ppermute | solution.py:199
  106.1 0.5 collective-permute-start.3
  106.6 3.2 %collective-permute-done.5 = bf16[128,1024]{1,0:T(8,128)(2,1)S(1)} collective-permute-done((bf16[128,1024]{1,0:T(8,128)(2,1)S(1)}, bf16[128,1024]{1,0:T(8,128)(2,1)S(1)}, u32[]{:S(2)}, u32[]{:S(2)}) %collective-permute-start.5) | collective-permute-done | bytes 262176 | tf_op jit(solution)/shard_map/ppermute | solution.py:199
  109.8 0.1 fusion.1
  109.9 0.0 collective-permute-done.7
  109.9 0.1 fusion
  110.0 4.6 %collective-permute-done.1 = bf16[128,1024]{1,0:T(8,128)(2,1)S(1)} collective-permute-done((bf16[128,1024]{1,0:T(8,128)(2,1)S(1)}, bf16[128,1024]{1,0:T(8,128)(2,1)S(1)}, u32[]{:S(2)}, u32[]{:S(2)}) %collective-permute-start.1) | collective-permute-done | bytes 262176 | tf_op jit(solution)/shard_map/ppermute | solution.py:199
  114.6 0.1 fusion.3
  114.6 0.0 collective-permute-done.3
  114.7 0.1 fusion.2
  114.7 1.1 maximum_maximum_fusion
  (4 shorter events, 0.1 us)
Async XLA Ops:
  0.0 1.6 %copy-start.4 = (f32[2,2,128,1024]{3,2,1,0:T(8,128)S(1)}, f32[2,2,128,1024]{3,2,1,0:T(8,128)}, u32[]{:S(2)}) copy-start(f32[2,2,128,1024]{3,2,1,0:T(8,128)} %spectrum_ref.1) | copy-start | bytes 6291460
  1.6 1.0 copy-start.7
  2.6 1.0 copy-start.8
  3.7 45.5 %copy-start.6 = (bf16[1024,1024]{1,0:T(8,128)(2,1)S(1)}, bf16[1024,1024]{1,0:T(8,128)(2,1)}, u32[]{:S(2)}) copy-start(bf16[1024,1024]{1,0:T(8,128)(2,1)} %constant.12.clone.cos_ref) | copy-start | bytes 6291460
  4.9 44.3 %copy-start.5 = (bf16[1024,1024]{1,0:T(8,128)(2,1)S(1)}, bf16[1024,1024]{1,0:T(8,128)(2,1)}, u32[]{:S(2)}) copy-start(bf16[1024,1024]{1,0:T(8,128)(2,1)} %constant.13.clone.sin_ref) | copy-start | bytes 6291460
  5.0 44.2 %copy-start.9 = (f32[1024,128]{1,0:T(8,128)S(1)}, f32[1024,128]{1,0:T(8,128)}, u32[]{:S(2)}) copy-start(f32[1024,128]{1,0:T(8,128)} %constant.15.clone.turn_sin_ref) | copy-start | bytes 1572868
  5.0 44.2 %copy-start.10 = (f32[1024,128]{1,0:T(8,128)S(1)}, f32[1024,128]{1,0:T(8,128)}, u32[]{:S(2)}) copy-start(f32[1024,128]{1,0:T(8,128)} %constant.14.clone.turn_cos_ref) | copy-start | bytes 1572868
  49.2 18.8 %copy-start.3 = (bf16[256,1024]{1,0:T(8,128)(2,1)S(1)}, bf16[256,1024]{1,0:T(8,128)(2,1)}, u32[]{:S(2)}) copy-start(bf16[256,1024]{1,0:T(8,128)(2,1)} %gate_ref.9) | copy-start | bytes 1572868
  64.6 15.1 %all-to-all-start.1 = ((bf16[8,2,64,128]{3,2,1,0:T(8,128)(2,1)}), bf16[8,2,64,128]{3,2,1,0:T(8,128)(2,1)S(1)}, u32[]{:S(2)}, u32[]{:S(2)}) async-start(bf16[8,2,64,128]{3,2,1,0:T(8,128)(2,1)} %get-tuple-element.15), calls=%async_computation.1 | async-start | bytes 524288 | tf_op jit(solution)/shard_map/all_to_all | solution.py:215
  68.0 5.8 %copy-start = (bf16[1024,8192]{1,0:T(8,128)(2,1)S(1)}, bf16[1024,8192]{1,0:T(8,128)(2,1)}, u32[]{:S(2)}) copy-start(bf16[1024,8192]{1,0:T(8,128)(2,1)} %weight_ref.7) | copy-start | bytes 50331652
  76.6 20.3 %collective-permute-start.4 = (bf16[2,128,1024]{2,1,0:T(8,128)(2,1)S(1)}, bf16[2,128,1024]{2,1,0:T(8,128)(2,1)S(1)}, u32[]{:S(2)}, u32[]{:S(2)}) collective-permute-start(bf16[2,128,1024]{2,1,0:T(8,128)(2,1)S(1)} %get-tuple-element.22), channel_id=1, source_target_pairs={{0,1},{1,0},{2,3},{3,2},{4,5},{5,4},{6,7},{7,6},{8,9},{9,8},{10,11... | collective-permute-start | bytes 1572872 | tf_op jit(solution)/shard_map/ppermute | solution.py:199
  78.2 19.6 %collective-permute-start.6 = (bf16[2,128,1024]{2,1,0:T(8,128)(2,1)S(1)}, bf16[2,128,1024]{2,1,0:T(8,128)(2,1)S(1)}, u32[]{:S(2)}, u32[]{:S(2)}) collective-permute-start(bf16[2,128,1024]{2,1,0:T(8,128)(2,1)S(1)} %get-tuple-element.24), channel_id=1, source_target_pairs={{0,2},{1,3},{2,0},{3,1},{4,6},{5,7},{6,4},{7,5},{8,10},{9,11},{10,... | collective-permute-start | bytes 1572872 | tf_op jit(solution)/shard_map/ppermute | solution.py:199
  79.7 5.8 %copy-start.1 = (bf16[1024,8192]{1,0:T(8,128)(2,1)S(1)}, bf16[1024,8192]{1,0:T(8,128)(2,1)}, u32[]{:S(2)}) copy-start(bf16[1024,8192]{1,0:T(8,128)(2,1)} %weight_ref.7) | copy-start | bytes 50331652
  85.5 5.8 %copy-start.2 = (bf16[1024,8192]{1,0:T(8,128)(2,1)S(1)}, bf16[1024,8192]{1,0:T(8,128)(2,1)}, u32[]{:S(2)}) copy-start(bf16[1024,8192]{1,0:T(8,128)(2,1)} %weight_ref.7) | copy-start | bytes 50331652
  88.3 14.9 %collective-permute-start = (bf16[2,128,1024]{2,1,0:T(8,128)(2,1)S(1)}, bf16[2,128,1024]{2,1,0:T(8,128)(2,1)S(1)}, u32[]{:S(2)}, u32[]{:S(2)}) collective-permute-start(bf16[2,128,1024]{2,1,0:T(8,128)(2,1)S(1)} %get-tuple-element.17), channel_id=1, source_target_pairs={{0,1},{1,0},{2,3},{3,2},{4,5},{5,4},{6,7},{7,6},{8,9},{9,8},{10,11... | collective-permute-start | bytes 1572872 | tf_op jit(solution)/shard_map/ppermute | solution.py:199
  88.9 15.3 %collective-permute-start.2 = (bf16[2,128,1024]{2,1,0:T(8,128)(2,1)S(1)}, bf16[2,128,1024]{2,1,0:T(8,128)(2,1)S(1)}, u32[]{:S(2)}, u32[]{:S(2)}) collective-permute-start(bf16[2,128,1024]{2,1,0:T(8,128)(2,1)S(1)} %get-tuple-element.19), channel_id=1, source_target_pairs={{0,2},{1,3},{2,0},{3,1},{4,6},{5,7},{6,4},{7,5},{8,10},{9,11},{10,... | collective-permute-start | bytes 1572872 | tf_op jit(solution)/shard_map/ppermute | solution.py:199
  97.2 12.6 %collective-permute-start.5 = (bf16[128,1024]{1,0:T(8,128)(2,1)S(1)}, bf16[128,1024]{1,0:T(8,128)(2,1)S(1)}, u32[]{:S(2)}, u32[]{:S(2)}) collective-permute-start(bf16[128,1024]{1,0:T(8,128)(2,1)S(1)} %slice_bitcast_fusion.2), channel_id=1, source_target_pairs={{0,2},{1,3},{2,0},{3,1},{4,6},{5,7},{6,4},{7,5},{8,10},{9,11},{10,... | collective-permute-start | bytes 786440 | tf_op jit(solution)/shard_map/ppermute | solution.py:199
  98.0 11.9 %collective-permute-start.7 = (bf16[128,1024]{1,0:T(8,128)(2,1)S(1)}, bf16[128,1024]{1,0:T(8,128)(2,1)S(1)}, u32[]{:S(2)}, u32[]{:S(2)}) collective-permute-start(bf16[128,1024]{1,0:T(8,128)(2,1)S(1)} %slice_bitcast_fusion), channel_id=1, source_target_pairs={{0,1},{1,0},{2,3},{3,2},{4,5},{5,4},{6,7},{7,6},{8,9},{9,8},{10,11... | collective-permute-start | bytes 786440 | tf_op jit(solution)/shard_map/ppermute | solution.py:199
  104.5 10.1 %collective-permute-start.1 = (bf16[128,1024]{1,0:T(8,128)(2,1)S(1)}, bf16[128,1024]{1,0:T(8,128)(2,1)S(1)}, u32[]{:S(2)}, u32[]{:S(2)}) collective-permute-start(bf16[128,1024]{1,0:T(8,128)(2,1)S(1)} %slice_bitcast_fusion.6), channel_id=1, source_target_pairs={{0,2},{1,3},{2,0},{3,1},{4,6},{5,7},{6,4},{7,5},{8,10},{9,11},{10,... | collective-permute-start | bytes 786440 | tf_op jit(solution)/shard_map/ppermute | solution.py:199
  106.1 8.6 %collective-permute-start.3 = (bf16[128,1024]{1,0:T(8,128)(2,1)S(1)}, bf16[128,1024]{1,0:T(8,128)(2,1)S(1)}, u32[]{:S(2)}, u32[]{:S(2)}) collective-permute-start(bf16[128,1024]{1,0:T(8,128)(2,1)S(1)} %slice_bitcast_fusion.4), channel_id=1, source_target_pairs={{0,1},{1,0},{2,3},{3,2},{4,5},{5,4},{6,7},{7,6},{8,9},{9,8},{10,11... | collective-permute-start | bytes 786440 | tf_op jit(solution)/shard_map/ppermute | solution.py:199

commit v2 on v1

--- a/solution.py
+++ b/solution.py
@@ -36,62 +36,87 @@
     return jnp.where(token == (held % block_rows) * span + held // block_rows, 1.0, 0.0).astype(jnp.bfloat16)
 
 
-def pack_kernel(span, values_ref, gate_ref, spectrum_ref, out_ref):
+def pack_kernel(span, order, me_ref, values_ref, gate_ref, spectrum_ref, *outs):
+    step = pl.program_id(0)
     rows = values_ref.shape[0]
     block_rows = rows // span
     source = (values_ref[...].astype(jnp.float32) * gate_ref[...].astype(jnp.float32)).astype(jnp.bfloat16)
     source = jnp.dot(split_rows(rows, span), source, preferred_element_type=jnp.float32).astype(jnp.bfloat16)
-    for dest in range(out_ref.shape[0]):
-        lanes = slice(dest * LANES, (dest + 1) * LANES)
+    odd = me_ref[0] % 2 == 1
+
+    def fill(out_ref, lanes):
         for part in range(2):
             for d in range(span):
-                out_ref[dest, part * span + d] = spectrum_ref[part, d, :, lanes].astype(jnp.bfloat16)
+                out_ref[part * span + d] = spectrum_ref[part, d, :, lanes].astype(jnp.bfloat16)
         for b in range(span):
-            out_ref[dest, 2 * span + b] = source[b * block_rows:(b + 1) * block_rows, lanes]
-
-
-def pack(values, gate_in, spectrum, seq_count):
-    rows, width = values.shape
+            out_ref[2 * span + b] = source[b * block_rows:(b + 1) * block_rows, lanes]
+
+    for place in range(len(order)):
+
+        @pl.when(step == place)
+        def _():
+            for core in range(2):
+                lanes = slice(core * LANES, (core + 1) * LANES)
+
+                @pl.when(odd)
+                def _():
+                    fill(outs[2 * place + 1 - core], lanes)
+
+                @pl.when(jnp.logical_not(odd))
+                def _():
+                    fill(outs[2 * place + core], lanes)
+
+
+def pack(me, values, gate_in, spectrum, order):
+    rows, _ = values.shape
     _, span, block_rows, _ = spectrum.shape
-    per_step = 2
-    cols = per_step * LANES
+    cols = 2 * LANES
+
+    def column(i, me_ref):
+        flip = sum((jnp.where(i == place, chip, 0) for place, chip in enumerate(order)), 0)
+        return (me_ref[0] // 2) ^ flip
+
+    shape = (3 * span, block_rows, LANES)
     return pl.pallas_call(
-        functools.partial(pack_kernel, span),
-        grid=(seq_count // per_step,),
-        in_specs=[
-            pl.BlockSpec((rows, cols), lambda i: (0, i)),
-            pl.BlockSpec((rows, cols), lambda i: (0, i)),
-            pl.BlockSpec((2, span, block_rows, cols), lambda i: (0, 0, 0, i)),
-        ],
-        out_specs=pl.BlockSpec((per_step, 3 * span, block_rows, LANES), lambda i: (i, 0, 0, 0)),
-        out_shape=jax.ShapeDtypeStruct((seq_count, 3 * span, block_rows, LANES), jnp.bfloat16),
-        compiler_params=pltpu.CompilerParams(vmem_limit_bytes=16 << 20),
+        functools.partial(pack_kernel, span, order),
+        grid_spec=pltpu.PrefetchScalarGridSpec(
+            num_scalar_prefetch=1,
+            grid=(len(order),),
+            in_specs=[
+                pl.BlockSpec((rows, cols), lambda i, m: (0, column(i, m))),
+                pl.BlockSpec((rows, cols), lambda i, m: (0, column(i, m))),
+                pl.BlockSpec((2, span, block_rows, cols), lambda i, m: (0, 0, 0, column(i, m))),
+            ],
+            out_specs=[pl.BlockSpec(shape, lambda i, m: (0, 0, 0))] * (2 * len(order)),
+        ),
+        out_shape=[jax.ShapeDtypeStruct(shape, jnp.bfloat16)] * (2 * len(order)),
+        compiler_params=pltpu.CompilerParams(vmem_limit_bytes=48 << 20),
         name="pack",
-    )(values, gate_in, spectrum)
-
-
-def conv_kernel(parts, data_ref, cos_ref, sin_ref, turn_cos_ref, turn_sin_ref, *refs):
-    outs, (cols_ref, re_ref, im_ref) = refs[:parts], refs[parts:]
-    shares, _, rows, _ = data_ref.shape
-    for s in range(shares):
+    )(me, values, gate_in, spectrum)
+
+
+def conv_kernel(parts, shares, me_ref, *refs):
+    data, (cos_ref, sin_ref, turn_cos_ref, turn_sin_ref) = refs[:shares], refs[shares:shares + 4]
+    outs, (cols_ref, fre_ref, fim_ref, re_ref, im_ref) = refs[shares + 4:shares + 4 + parts], refs[shares + 4 + parts:]
+    me = me_ref[0]
+    rows = data[0].shape[1]
+    for m in range(shares):
+        at = pl.ds(pl.multiple_of((me ^ m) * rows, rows), rows)
         for b in range(2):
-            cols_ref[s * rows:(s + 1) * rows, b * LANES:(b + 1) * LANES] = data_ref[s, 4 + b]
+            cols_ref[at, b * LANES:(b + 1) * LANES] = data[m][4 + b]
     step = 2 * rows
     for i in range(shares * rows // step):
         at = slice(i * step, (i + 1) * step)
-        cols = cols_ref[...]
-        first_re = jnp.dot(cos_ref[at, :], cols, preferred_element_type=jnp.float32)
-        first_sin = jnp.dot(sin_ref[at, :], cols, preferred_element_type=jnp.float32)
+        fre_ref[at, :] = jnp.dot(cos_ref[at, :], cols_ref[...], preferred_element_type=jnp.float32)
+        fim_ref[at, :] = jnp.dot(sin_ref[at, :], cols_ref[...], preferred_element_type=jnp.float32)
+    for m in range(shares):
+        at = pl.ds(pl.multiple_of((me ^ m) * rows, rows), rows)
         tc, ts = turn_cos_ref[at, :], turn_sin_ref[at, :]
-        re0, im0 = first_re[:, :LANES], -first_sin[:, :LANES]
-        re1, im1 = first_re[:, LANES:], -first_sin[:, LANES:]
+        re0, im0 = fre_ref[at, :LANES], -fim_ref[at, :LANES]
+        re1, im1 = fre_ref[at, LANES:], -fim_ref[at, LANES:]
         re1, im1 = re1 * tc + im1 * ts, im1 * tc - re1 * ts
-
-        def filt(part):
-            return jnp.concatenate([data_ref[2 * i, part], data_ref[2 * i + 1, part]], axis=0).astype(jnp.float32)
-
         f0r, f0i, f1r, f1i = re0 + re1, im0 + im1, re0 - re1, im0 - im1
-        s0r, s1r, s0i, s1i = filt(0), filt(1), filt(2), filt(3)
+        s0r, s1r, s0i, s1i = (data[m][part].astype(jnp.float32) for part in range(4))
         p0r, p0i = f0r * s0r - f0i * s0i, f0r * s0i + f0i * s0r
         p1r, p1i = f1r * s1r - f1i * s1i, f1r * s1i + f1i * s1r
         b0r, b0i = 0.5 * (p0r + p1r), 0.5 * (p0i + p1i)
@@ -113,22 +138,24 @@
                     outs[p][2 * i + s, b] = conv[begin:begin + part_rows, b * LANES:(b + 1) * LANES]
 
 
-def convolve(data, parts):
-    shares, _, rows, _ = data.shape
+def convolve(me, data, parts):
+    shares = len(data)
+    rows = data[0].shape[1]
     block = shares * rows
     angle = angles(block, block, block)
     turn = np.broadcast_to(angles(block, 2, 2 * block)[:, 1:], (block, LANES))
     vmem = pl.BlockSpec(memory_space=pltpu.VMEM)
     return pl.pallas_call(
-        functools.partial(conv_kernel, parts),
-        in_specs=[vmem] * 5,
+        functools.partial(conv_kernel, parts, shares),
+        in_specs=[pl.BlockSpec(memory_space=pltpu.SMEM)] + [vmem] * (shares + 4),
         out_specs=[vmem] * parts,
         out_shape=[jax.ShapeDtypeStruct((shares, 2, rows // parts, LANES), jnp.bfloat16)] * parts,
-        scratch_shapes=[pltpu.VMEM((block, 2 * LANES), jnp.bfloat16)] * 3,
+        scratch_shapes=[pltpu.VMEM((block, 2 * LANES), dtype) for dtype in
+                        (jnp.bfloat16, jnp.float32, jnp.float32, jnp.bfloat16, jnp.bfloat16)],
         compiler_params=pltpu.CompilerParams(vmem_limit_bytes=32 << 20),
         name="convolve",
     )(
-        data, rounded(np.cos(angle)), rounded(np.sin(angle)),
+        me, *data, rounded(np.cos(angle)), rounded(np.sin(angle)),
         jnp.asarray(np.cos(turn).astype(np.float32)), jnp.asarray(np.sin(turn).astype(np.float32)),
     )
 
@@ -187,7 +214,7 @@
             scratch_shapes=[pltpu.VMEM((rows, depth), jnp.bfloat16)],
         ),
         out_shape=[shape, shape],
-        compiler_params=pltpu.CompilerParams(vmem_limit_bytes=24 << 20),
+        compiler_params=pltpu.CompilerParams(vmem_limit_bytes=52 << 20),
         cost_estimate=pl.CostEstimate(
             flops=2 * rows * depth * cols * 4, bytes_accessed=2 * depth * cols * 4, transcendentals=0
         ),
@@ -205,11 +232,17 @@
 
 def by_channels(values, gate_in, gate_out, spectrum, out_weight):
     seq_count = lax.axis_size("seq")
+    here = lax.axis_index("seq").astype(jnp.int32).reshape(1)
     me = lax.axis_index("chan").astype(jnp.int32).reshape(1)
     parts = 2
-    data = pack(values, gate_in, spectrum, seq_count)
-    data = lax.all_to_all(data, "seq", split_axis=0, concat_axis=0, tiled=True)
-    convs = convolve(data, parts)
+    order = tuple(reversed(range(seq_count // 2)))
+    packed = pack(here, values, gate_in, spectrum, order)
+    data = [None] * seq_count
+    for place, flip in enumerate(order):
+        for core in range(2):
+            mine = packed[2 * place + core]
+            data[2 * flip + core] = swap(mine, "seq", 2 * flip + core) if flip or core else mine
+    convs = convolve(here, data, parts)
     outs = []
     for part, conv in enumerate(convs):
         conv = lax.all_to_all(conv, "seq", split_axis=0, concat_axis=0, tiled=True)
@@ -287,8 +320,8 @@
 def shards(values, gate_in, gate_out, spectrum, out_weight):
     seq_count, chan_count = lax.axis_size("seq"), lax.axis_size("chan")
     _, span, block_rows, width = spectrum.shape
-    one_lane_block = width == seq_count * LANES and seq_count % 2 == 0 and block_rows % 32 == 0
-    if span == 2 and chan_count == 4 and one_lane_block:
+    one_lane_block = width == seq_count * LANES and block_rows % 32 == 0
+    if span == 2 and chan_count == 4 and seq_count & (seq_count - 1) == 0 and one_lane_block:
         return by_channels(values, gate_in, gate_out, spectrum, out_weight)
     return by_frequencies(values, gate_in, gate_out, spectrum, out_weight)
 

time: 116 us -> 114 us (0.983)
  blocking collectives: 56.4 us -> 22.4 us
  waiting for transfers between devices: 13.2 us -> 33.4 us
  starting transfers between devices: 11 us -> 22.9 us
  local copies, waits for them, and re-layouts: 17.2 us -> 5.35 us
  Pallas kernels: 15.8 us -> 26.7 us
    all_to_all x1 -> x0, blocking collectives: 44.2 us -> none  [by_channels(): data = lax.all_to_all(data, 'seq', split_axis=0, concat_axis=0, tiled=True)]
    ppermute x8 -> x15, waiting for transfers between devices: 13.2 us -> 32 us  [swap(): lax.ppermute(data, axis, [(i, i ^ flip) for i in range(lax.axis_size(axis...]
    ppermute x8 -> x15, starting transfers between devices: 7.61 us -> 19.5 us  [swap(): lax.ppermute(data, axis, [(i, i ^ flip) for i in range(lax.axis_size(axis...]
    unnamed x22 -> x16, local copies, waits for them, and re-layouts: 17.1 us -> 5.27 us
    all_to_all x1, blocking collectives: 12.1 us -> 22.4 us  [by_channels(): conv = lax.all_to_all(conv, 'seq', split_axis=0, concat_axis=0, tiled=True)]
    pallas_call x4, Pallas kernels: 11.3 us -> 20.7 us  [project(): pl.pallas_call(project_kernel, grid_spec=pltpu.PrefetchScalarGridSpec(num...]
    pallas_call x2, Pallas kernels: 4.48 us -> 6.05 us  [the longest x1 4.49 us: convolve(): pl.pallas_call(functools.partial(conv_kernel, parts, shares), in_specs=[p...]
    all_to_all x1, waiting for transfers between devices: 0.01 us -> 1.35 us  [by_channels(): conv = lax.all_to_all(conv, 'seq', split_axis=0, concat_axis=0, tiled=True)]
  transfers between devices with their start and end apart: 9 -> 16, of which waited for: 4 -> 10; matrix products, arithmetic and copies ran while one was open for 1% -> 1% of each run, Pallas kernels for 10% -> 18%
where the time goes in v2:
time: 114 us; the launch traced here: 113 us
  waiting for transfers between devices  33.4 us (29%)
  Pallas kernels  26.7 us (23%)
  starting transfers between devices  22.9 us (20%)
  blocking collectives  22.4 us (20%)
  local copies, waits for them, and re-layouts  5.35 us (5%)
  other arithmetic  2.09 us (2%)
    ppermute x15, waiting for transfers between devices, swap(): lax.ppermute(data, axis, [(i, i ^ flip) for i in range(lax.axis_size(axis...  32 us
    all_to_all x1, blocking collectives, by_channels(): conv = lax.all_to_all(conv, 'seq', split_axis=0, concat_axis=0, tiled=True)  22.4 us
    pallas_call x4, Pallas kernels, project(): pl.pallas_call(project_kernel, grid_spec=pltpu.PrefetchScalarGridSpec(num...  20.7 us
    ppermute x15, starting transfers between devices, swap(): lax.ppermute(data, axis, [(i, i ^ flip) for i in range(lax.axis_size(axis...  19.5 us
    unnamed x16, local copies, waits for them, and re-layouts  5.27 us
    pallas_call x1, Pallas kernels, convolve(): pl.pallas_call(functools.partial(conv_kernel, parts, shares), in_specs=[p...  4.49 us
    all_to_all x1, starting transfers between devices, by_channels(): conv = lax.all_to_all(conv, 'seq', split_axis=0, concat_axis=0, tiled=True)  3.41 us
  transfers between devices with their start and end apart: 16, of which 10 were waited for; matrix products, arithmetic and copies ran while one was open for 1% of the time, Pallas kernels for 18%

profile of v2, /device:TPU:0, one launch (start us, length us, event | category | flops | bytes accessed | tf_op | source)
XLA Modules:
  0.0 113.1 jit_solution(12635894044808740548)
XLA Ops:
  0.0 0.0 copy-start.1
  0.0 1.6 %copy-done.1 = f32[2,2,128,1024]{3,2,1,0:T(8,128)S(1)} copy-done((f32[2,2,128,1024]{3,2,1,0:T(8,128)S(1)}, f32[2,2,128,1024]{3,2,1,0:T(8,128)}, u32[]{:S(2)}) %copy-start.1) | copy-done | bytes 2097176
  1.6 0.0 copy-start.4
  1.6 1.0 copy-done.4
  2.6 0.0 copy-start.5
  2.6 1.0 copy-done.5
  3.7 0.0 copy-start.2
  3.7 0.0 copy-start.6
  3.7 0.0 copy-start.7
  3.7 1.6 %pack.1 = (bf16[6,128,128]{2,1,0:T(8,128)(2,1)S(1)}, bf16[6,128,128]{2,1,0:T(8,128)(2,1)S(1)}, bf16[6,128,128]{2,1,0:T(8,128)(2,1)S(1)}, bf16[6,128,128]{2,1,0:T...) custom-call(s32[1]{0:T(128)} %bitcast.1.me_ref, ...), custom_call_target="tpu_custom_call" | custom-call | tf_op jit(solution)/shard_map/pack/pallas_call | solution.py:80
  5.3 0.5 collective-permute-start
  5.8 2.6 %collective-permute-start.1 = (bf16[6,128,128]{2,1,0:T(8,128)(2,1)S(1)}, bf16[6,128,128]{2,1,0:T(8,128)(2,1)S(1)}, u32[]{:S(2)}, u32[]{:S(2)}) collective-permute-start(bf16[6,128,128]{2,1,0:T(8,128)(2,1)S(1)} %get-tuple-element.25), channel_id=1, source_target_pairs={{0,8},{4,12},{8,0},{12,4},{16,24},{20,28},{24,16},{28,20},{1,9},{5... | collective-permute-start | bytes 589832 | tf_op jit(solution)/shard_map/ppermute | solution.py:226
  8.4 0.1 collective-permute-start.2
  8.5 2.8 %collective-permute-start.3 = (bf16[6,128,128]{2,1,0:T(8,128)(2,1)S(1)}, bf16[6,128,128]{2,1,0:T(8,128)(2,1)S(1)}, u32[]{:S(2)}, u32[]{:S(2)}) collective-permute-start(bf16[6,128,128]{2,1,0:T(8,128)(2,1)S(1)} %get-tuple-element.27), channel_id=1, source_target_pairs={{0,16},{4,20},{8,24},{12,28},{16,0},{20,4},{24,8},{28,12},{1,17},{... | collective-permute-start | bytes 589832 | tf_op jit(solution)/shard_map/ppermute | solution.py:226
  11.2 0.0 collective-permute-start.4
  11.2 0.0 collective-permute-done.refs_1_
  11.3 3.6 %collective-permute-start.5 = (bf16[6,128,128]{2,1,0:T(8,128)(2,1)S(1)}, bf16[6,128,128]{2,1,0:T(8,128)(2,1)S(1)}, u32[]{:S(2)}, u32[]{:S(2)}) collective-permute-start(bf16[6,128,128]{2,1,0:T(8,128)(2,1)S(1)} %get-tuple-element.29), channel_id=1, source_target_pairs={{0,24},{4,28},{8,16},{12,20},{16,8},{20,12},{24,0},{28,4},{1,25},{... | collective-permute-start | bytes 589832 | tf_op jit(solution)/shard_map/ppermute | solution.py:226
  14.8 7.3 %collective-permute-done.1.refs_2_ = bf16[6,128,128]{2,1,0:T(8,128)(2,1)S(1)} collective-permute-done((bf16[6,128,128]{2,1,0:T(8,128)(2,1)S(1)}, bf16[6,128,128]{2,1,0:T(8,128)(2,1)S(1)}, u32[]{:S(2)}, u32[]{:S(2)}) %collective-permute-start.1) | collective-permute-done | bytes 196640 | tf_op jit(solution)/shard_map/ppermute | solution.py:226
  22.1 0.5 collective-permute-start.6
  22.6 3.2 %collective-permute-done.2.refs_3_ = bf16[6,128,128]{2,1,0:T(8,128)(2,1)S(1)} collective-permute-done((bf16[6,128,128]{2,1,0:T(8,128)(2,1)S(1)}, bf16[6,128,128]{2,1,0:T(8,128)(2,1)S(1)}, u32[]{:S(2)}, u32[]{:S(2)}) %collective-permute-start.2) | collective-permute-done | bytes 196640 | tf_op jit(solution)/shard_map/ppermute | solution.py:226
  25.8 0.0 collective-permute-done.3.refs_4_
  25.8 0.5 collective-permute-done.4.refs_5_
  26.3 7.2 %collective-permute-done.5.refs_6_ = bf16[6,128,128]{2,1,0:T(8,128)(2,1)S(1)} collective-permute-done((bf16[6,128,128]{2,1,0:T(8,128)(2,1)S(1)}, bf16[6,128,128]{2,1,0:T(8,128)(2,1)S(1)}, u32[]{:S(2)}, u32[]{:S(2)}) %collective-permute-start.5) | collective-permute-done | bytes 196640 | tf_op jit(solution)/shard_map/ppermute | solution.py:226
  33.5 3.3 %collective-permute-done.6.refs_7_ = bf16[6,128,128]{2,1,0:T(8,128)(2,1)S(1)} collective-permute-done((bf16[6,128,128]{2,1,0:T(8,128)(2,1)S(1)}, bf16[6,128,128]{2,1,0:T(8,128)(2,1)S(1)}, u32[]{:S(2)}, u32[]{:S(2)}) %collective-permute-start.6) | collective-permute-done | bytes 196640 | tf_op jit(solution)/shard_map/ppermute | solution.py:226
  36.8 0.0 copy-done.2
  36.8 0.0 copy-done.6
  36.8 0.0 copy-done.7
  36.8 0.0 copy-start.3
  36.9 1.6 %copy-done.3 = bf16[1024,1024]{1,0:T(8,128)(2,1)S(1)} copy-done((bf16[1024,1024]{1,0:T(8,128)(2,1)S(1)}, bf16[1024,1024]{1,0:T(8,128)(2,1)}, u32[]{:S(2)}) %copy-start.3) | copy-done | bytes 2097176
  38.4 0.0 copy-start
  38.4 4.5 %convolve.1 = (bf16[8,2,64,128]{3,2,1,0:T(8,128)(2,1)}, bf16[8,2,64,128]{3,2,1,0:T(8,128)(2,1)S(1)}) custom-call(s32[1]{0:T(128)} %bitcast.1.me_ref, bf16[6,128,128]{2,1,0:T(8,128)(2,1)S(1)} %get-tuple-element.23.refs_0_, bf16[6,128,128]{2,1,0:T(8,128)(2,1)S(1)} %collective-permute-done.refs_1_, bf16[6,128,128]{2,1,0:T(8,128)(2,1)S(1)} %collective-permute-done.1.refs_2_, ...), custom_call_target="tpu_custom_call" | custom-call | tf_op jit(solution)/shard_map/convolve/pallas_call | solution.py:148
  42.9 22.4 %all_to_all.10.conv_ref = bf16[8,2,64,128]{3,2,1,0:T(8,128)(2,1)S(1)} all-to-all(bf16[8,2,64,128]{3,2,1,0:T(8,128)(2,1)S(1)} %get-tuple-element.36), channel_id=1, replica_groups=mesh['seq'=8,'chan'=4] {'seq'}, dimensions={0} | all-to-all | bytes 524288 | tf_op jit(solution)/shard_map/all_to_all | solution.py:248
  65.3 3.4 %all-to-all-start = ((bf16[8,2,64,128]{3,2,1,0:T(8,128)(2,1)}), bf16[8,2,64,128]{3,2,1,0:T(8,128)(2,1)S(1)}, u32[]{:S(2)}, u32[]{:S(2)}) async-start(bf16[8,2,64,128]{3,2,1,0:T(8,128)(2,1)} %get-tuple-element.31), calls=%async_computation | async-start | bytes 524288 | tf_op jit(solution)/shard_map/all_to_all | solution.py:248
  68.7 0.0 copy-done
  68.7 5.2 %project.7 = (bf16[2,128,1024]{2,1,0:T(8,128)(2,1)S(1)}, bf16[2,128,1024]{2,1,0:T(8,128)(2,1)S(1)}) custom-call(s32[1]{0:T(128)} %bitcast.me_ref, bf16[8,2,64,128]{3,2,1,0:T(8,128)(2,1)S(1)} %all_to_all.10.conv_ref, bf16[256,1024]{1,0:T(8,128)(2,1)S(1)} %copy-done, bf16[1024,8192]{1,0:T(8,128)(2,1)} %weight_ref.7), custom_call_target="tpu_custom_call" | custom-call | flops 1073741824 | bytes 8388608 | tf_op jit(solution)/shard_map/project/pallas_call | solution.py:200
  73.9 1.6 %collective-permute-start.11 = (bf16[2,128,1024]{2,1,0:T(8,128)(2,1)S(1)}, bf16[2,128,1024]{2,1,0:T(8,128)(2,1)S(1)}, u32[]{:S(2)}, u32[]{:S(2)}) collective-permute-start(bf16[2,128,1024]{2,1,0:T(8,128)(2,1)S(1)} %get-tuple-element.38), channel_id=1, source_target_pairs={{0,1},{1,0},{2,3},{3,2},{4,5},{5,4},{6,7},{7,6},{8,9},{9,8},{10,11... | collective-permute-start | bytes 1572872 | tf_op jit(solution)/shard_map/ppermute | solution.py:226
  75.5 1.5 %collective-permute-start.13 = (bf16[2,128,1024]{2,1,0:T(8,128)(2,1)S(1)}, bf16[2,128,1024]{2,1,0:T(8,128)(2,1)S(1)}, u32[]{:S(2)}, u32[]{:S(2)}) collective-permute-start(bf16[2,128,1024]{2,1,0:T(8,128)(2,1)S(1)} %get-tuple-element.40), channel_id=1, source_target_pairs={{0,2},{1,3},{2,0},{3,1},{4,6},{5,7},{6,4},{7,5},{8,10},{9,11},{10,... | collective-permute-start | bytes 1572872 | tf_op jit(solution)/shard_map/ppermute | solution.py:226
  77.0 1.4 %all-to-all-done.conv_ref = bf16[8,2,64,128]{3,2,1,0:T(8,128)(2,1)S(1)} async-done(((bf16[8,2,64,128]{3,2,1,0:T(8,128)(2,1)}), bf16[8,2,64,128]{3,2,1,0:T(8,128)(2,1)S(1)}, u32[]{:S(2)}, u32[]{:S(2)}) %all-to-all-start) | async-done | bytes 262176 | tf_op jit(solution)/shard_map/all_to_all | solution.py:248
  78.4 5.2 %project.5 = (bf16[2,128,1024]{2,1,0:T(8,128)(2,1)S(1)}, bf16[2,128,1024]{2,1,0:T(8,128)(2,1)S(1)}) custom-call(s32[1]{0:T(128)} %bitcast.me_ref, bf16[8,2,64,128]{3,2,1,0:T(8,128)(2,1)S(1)} %all-to-all-done.conv_ref, bf16[256,1024]{1,0:T(8,128)(2,1)S(1)} %copy-done, bf16[1024,8192]{1,0:T(8,128)(2,1)} %weight_ref.7), custom_call_target="tpu_custom_call" | custom-call | flops 1073741824 | bytes 8388608 | tf_op jit(solution)/shard_map/project/pallas_call | solution.py:200
  83.6 1.5 %collective-permute-start.7 = (bf16[2,128,1024]{2,1,0:T(8,128)(2,1)S(1)}, bf16[2,128,1024]{2,1,0:T(8,128)(2,1)S(1)}, u32[]{:S(2)}, u32[]{:S(2)}) collective-permute-start(bf16[2,128,1024]{2,1,0:T(8,128)(2,1)S(1)} %get-tuple-element.33), channel_id=1, source_target_pairs={{0,1},{1,0},{2,3},{3,2},{4,5},{5,4},{6,7},{7,6},{8,9},{9,8},{10,11... | collective-permute-start | bytes 1572872 | tf_op jit(solution)/shard_map/ppermute | solution.py:226
  85.1 1.5 %collective-permute-start.9 = (bf16[2,128,1024]{2,1,0:T(8,128)(2,1)S(1)}, bf16[2,128,1024]{2,1,0:T(8,128)(2,1)S(1)}, u32[]{:S(2)}, u32[]{:S(2)}) collective-permute-start(bf16[2,128,1024]{2,1,0:T(8,128)(2,1)S(1)} %get-tuple-element.35), channel_id=1, source_target_pairs={{0,2},{1,3},{2,0},{3,1},{4,6},{5,7},{6,4},{7,5},{8,10},{9,11},{10,... | collective-permute-start | bytes 1572872 | tf_op jit(solution)/shard_map/ppermute | solution.py:226
  86.6 5.2 %project.6 = (bf16[2,128,1024]{2,1,0:T(8,128)(2,1)S(1)}, bf16[2,128,1024]{2,1,0:T(8,128)(2,1)S(1)}) custom-call(s32[1]{0:T(128)} %bitcast.me_ref, bf16[8,2,64,128]{3,2,1,0:T(8,128)(2,1)S(1)} %all_to_all.10.conv_ref, bf16[256,1024]{1,0:T(8,128)(2,1)S(1)} %copy-done, bf16[1024,8192]{1,0:T(8,128)(2,1)} %weight_ref.7), custom_call_target="tpu_custom_call" | custom-call | flops 1073741824 | bytes 8388608 | tf_op jit(solution)/shard_map/project/pallas_call | solution.py:200
  91.8 5.2 %project.4 = (bf16[2,128,1024]{2,1,0:T(8,128)(2,1)S(1)}, bf16[2,128,1024]{2,1,0:T(8,128)(2,1)S(1)}) custom-call(s32[1]{0:T(128)} %bitcast.me_ref, bf16[8,2,64,128]{3,2,1,0:T(8,128)(2,1)S(1)} %all-to-all-done.conv_ref, bf16[256,1024]{1,0:T(8,128)(2,1)S(1)} %copy-done, bf16[1024,8192]{1,0:T(8,128)(2,1)} %weight_ref.7), custom_call_target="tpu_custom_call" | custom-call | flops 1073741824 | bytes 8388608 | tf_op jit(solution)/shard_map/project/pallas_call | solution.py:200
  97.0 0.0 collective-permute-done.11
  97.0 0.2 add_convert_fusion.1
  97.2 0.6 collective-permute-start.12
  97.8 0.0 collective-permute-done.13
  97.8 0.2 add_convert_fusion
  98.0 0.6 collective-permute-start.14
  98.6 0.8 collective-permute-done.7
  99.5 0.2 add_convert_fusion.3
  99.7 1.8 %collective-permute-done.9 = bf16[2,128,1024]{2,1,0:T(8,128)(2,1)S(1)} collective-permute-done((bf16[2,128,1024]{2,1,0:T(8,128)(2,1)S(1)}, bf16[2,128,1024]{2,1,0:T(8,128)(2,1)S(1)}, u32[]{:S(2)}, u32[]{:S(2)}) %collective-permute-start.9) | collective-permute-done | bytes 524320 | tf_op jit(solution)/shard_map/ppermute | solution.py:226
  101.5 0.2 add_convert_fusion.2
  101.8 1.6 %collective-permute-start.8 = (bf16[128,1024]{1,0:T(8,128)(2,1)S(1)}, bf16[128,1024]{1,0:T(8,128)(2,1)S(1)}, u32[]{:S(2)}, u32[]{:S(2)}) collective-permute-start(bf16[128,1024]{1,0:T(8,128)(2,1)S(1)} %slice_bitcast_fusion.6), channel_id=1, source_target_pairs={{0,2},{1,3},{2,0},{3,1},{4,6},{5,7},{6,4},{7,5},{8,10},{9,11},{10,... | collective-permute-start | bytes 786440 | tf_op jit(solution)/shard_map/ppermute | solution.py:226
  103.4 0.5 collective-permute-start.10
  103.9 3.2 %collective-permute-done.12 = bf16[128,1024]{1,0:T(8,128)(2,1)S(1)} collective-permute-done((bf16[128,1024]{1,0:T(8,128)(2,1)S(1)}, bf16[128,1024]{1,0:T(8,128)(2,1)S(1)}, u32[]{:S(2)}, u32[]{:S(2)}) %collective-permute-start.12) | collective-permute-done | bytes 262176 | tf_op jit(solution)/shard_map/ppermute | solution.py:226
  107.1 0.1 fusion.1
  107.2 0.0 collective-permute-done.14
  107.2 0.1 fusion
  107.3 4.6 %collective-permute-done.8 = bf16[128,1024]{1,0:T(8,128)(2,1)S(1)} collective-permute-done((bf16[128,1024]{1,0:T(8,128)(2,1)S(1)}, bf16[128,1024]{1,0:T(8,128)(2,1)S(1)}, u32[]{:S(2)}, u32[]{:S(2)}) %collective-permute-start.8) | collective-permute-done | bytes 262176 | tf_op jit(solution)/shard_map/ppermute | solution.py:226
  111.9 0.1 fusion.3
  111.9 0.0 collective-permute-done.10
  111.9 0.1 fusion.2
  112.0 1.1 maximum_maximum_fusion
  (4 shorter events, 0.1 us)
Async XLA Ops:
  0.0 1.6 %copy-start.1 = (f32[2,2,128,1024]{3,2,1,0:T(8,128)S(1)}, f32[2,2,128,1024]{3,2,1,0:T(8,128)}, u32[]{:S(2)}) copy-start(f32[2,2,128,1024]{3,2,1,0:T(8,128)} %spectrum_ref.1) | copy-start | bytes 6291460
  1.6 1.0 copy-start.4
  2.6 1.0 copy-start.5
  3.7 33.2 %copy-start.2 = (bf16[1024,1024]{1,0:T(8,128)(2,1)S(1)}, bf16[1024,1024]{1,0:T(8,128)(2,1)}, u32[]{:S(2)}) copy-start(bf16[1024,1024]{1,0:T(8,128)(2,1)} %constant.18.clone.refs_9_) | copy-start | bytes 6291460
  3.7 33.2 %copy-start.6 = (f32[1024,128]{1,0:T(8,128)S(1)}, f32[1024,128]{1,0:T(8,128)}, u32[]{:S(2)}) copy-start(f32[1024,128]{1,0:T(8,128)} %constant.20.clone.refs_11_) | copy-start | bytes 1572868
  3.7 33.2 %copy-start.7 = (f32[1024,128]{1,0:T(8,128)S(1)}, f32[1024,128]{1,0:T(8,128)}, u32[]{:S(2)}) copy-start(f32[1024,128]{1,0:T(8,128)} %constant.19.clone.refs_10_) | copy-start | bytes 1572868
  5.3 6.0 %collective-permute-start = (bf16[6,128,128]{2,1,0:T(8,128)(2,1)S(1)}, bf16[6,128,128]{2,1,0:T(8,128)(2,1)S(1)}, u32[]{:S(2)}, u32[]{:S(2)}) collective-permute-start(bf16[6,128,128]{2,1,0:T(8,128)(2,1)S(1)} %get-tuple-element.24), channel_id=1, source_target_pairs={{0,4},{4,0},{8,12},{12,8},{16,20},{20,16},{24,28},{28,24},{1,5},{5... | collective-permute-start | bytes 589832 | tf_op jit(solution)/shard_map/ppermute | solution.py:226
  5.8 16.4 %collective-permute-start.1 = (bf16[6,128,128]{2,1,0:T(8,128)(2,1)S(1)}, bf16[6,128,128]{2,1,0:T(8,128)(2,1)S(1)}, u32[]{:S(2)}, u32[]{:S(2)}) collective-permute-start(bf16[6,128,128]{2,1,0:T(8,128)(2,1)S(1)} %get-tuple-element.25), channel_id=1, source_target_pairs={{0,8},{4,12},{8,0},{12,4},{16,24},{20,28},{24,16},{28,20},{1,9},{5... | collective-permute-start | bytes 589832 | tf_op jit(solution)/shard_map/ppermute | solution.py:226
  8.4 17.4 %collective-permute-start.2 = (bf16[6,128,128]{2,1,0:T(8,128)(2,1)S(1)}, bf16[6,128,128]{2,1,0:T(8,128)(2,1)S(1)}, u32[]{:S(2)}, u32[]{:S(2)}) collective-permute-start(bf16[6,128,128]{2,1,0:T(8,128)(2,1)S(1)} %get-tuple-element.26), channel_id=1, source_target_pairs={{0,12},{4,8},{8,4},{12,0},{16,28},{20,24},{24,20},{28,16},{1,13},{... | collective-permute-start | bytes 589832 | tf_op jit(solution)/shard_map/ppermute | solution.py:226
  8.5 17.3 %collective-permute-start.3 = (bf16[6,128,128]{2,1,0:T(8,128)(2,1)S(1)}, bf16[6,128,128]{2,1,0:T(8,128)(2,1)S(1)}, u32[]{:S(2)}, u32[]{:S(2)}) collective-permute-start(bf16[6,128,128]{2,1,0:T(8,128)(2,1)S(1)} %get-tuple-element.27), channel_id=1, source_target_pairs={{0,16},{4,20},{8,24},{12,28},{16,0},{20,4},{24,8},{28,12},{1,17},{... | collective-permute-start | bytes 589832 | tf_op jit(solution)/shard_map/ppermute | solution.py:226
  11.2 15.1 %collective-permute-start.4 = (bf16[6,128,128]{2,1,0:T(8,128)(2,1)S(1)}, bf16[6,128,128]{2,1,0:T(8,128)(2,1)S(1)}, u32[]{:S(2)}, u32[]{:S(2)}) collective-permute-start(bf16[6,128,128]{2,1,0:T(8,128)(2,1)S(1)} %get-tuple-element.28), channel_id=1, source_target_pairs={{0,20},{4,16},{8,28},{12,24},{16,4},{20,0},{24,12},{28,8},{1,21},{... | collective-permute-start | bytes 589832 | tf_op jit(solution)/shard_map/ppermute | solution.py:226
  11.3 22.3 %collective-permute-start.5 = (bf16[6,128,128]{2,1,0:T(8,128)(2,1)S(1)}, bf16[6,128,128]{2,1,0:T(8,128)(2,1)S(1)}, u32[]{:S(2)}, u32[]{:S(2)}) collective-permute-start(bf16[6,128,128]{2,1,0:T(8,128)(2,1)S(1)} %get-tuple-element.29), channel_id=1, source_target_pairs={{0,24},{4,28},{8,16},{12,20},{16,8},{20,12},{24,0},{28,4},{1,25},{... | collective-permute-start | bytes 589832 | tf_op jit(solution)/shard_map/ppermute | solution.py:226
  22.1 14.7 %collective-permute-start.6 = (bf16[6,128,128]{2,1,0:T(8,128)(2,1)S(1)}, bf16[6,128,128]{2,1,0:T(8,128)(2,1)S(1)}, u32[]{:S(2)}, u32[]{:S(2)}) collective-permute-start(bf16[6,128,128]{2,1,0:T(8,128)(2,1)S(1)} %get-tuple-element.30), channel_id=1, source_target_pairs={{0,28},{4,24},{8,20},{12,16},{16,12},{20,8},{24,4},{28,0},{1,29},{... | collective-permute-start | bytes 589832 | tf_op jit(solution)/shard_map/ppermute | solution.py:226
  36.8 1.6 %copy-start.3 = (bf16[1024,1024]{1,0:T(8,128)(2,1)S(1)}, bf16[1024,1024]{1,0:T(8,128)(2,1)}, u32[]{:S(2)}) copy-start(bf16[1024,1024]{1,0:T(8,128)(2,1)} %constant.17.clone.refs_8_) | copy-start | bytes 6291460
  38.4 30.3 %copy-start = (bf16[256,1024]{1,0:T(8,128)(2,1)S(1)}, bf16[256,1024]{1,0:T(8,128)(2,1)}, u32[]{:S(2)}) copy-start(bf16[256,1024]{1,0:T(8,128)(2,1)} %gate_ref.9) | copy-start | bytes 1572868
  65.3 13.1 %all-to-all-start = ((bf16[8,2,64,128]{3,2,1,0:T(8,128)(2,1)}), bf16[8,2,64,128]{3,2,1,0:T(8,128)(2,1)S(1)}, u32[]{:S(2)}, u32[]{:S(2)}) async-start(bf16[8,2,64,128]{3,2,1,0:T(8,128)(2,1)} %get-tuple-element.31), calls=%async_computation | async-start | bytes 524288 | tf_op jit(solution)/shard_map/all_to_all | solution.py:248
  73.9 23.1 %collective-permute-start.11 = (bf16[2,128,1024]{2,1,0:T(8,128)(2,1)S(1)}, bf16[2,128,1024]{2,1,0:T(8,128)(2,1)S(1)}, u32[]{:S(2)}, u32[]{:S(2)}) collective-permute-start(bf16[2,128,1024]{2,1,0:T(8,128)(2,1)S(1)} %get-tuple-element.38), channel_id=1, source_target_pairs={{0,1},{1,0},{2,3},{3,2},{4,5},{5,4},{6,7},{7,6},{8,9},{9,8},{10,11... | collective-permute-start | bytes 1572872 | tf_op jit(solution)/shard_map/ppermute | solution.py:226
  75.5 22.3 %collective-permute-start.13 = (bf16[2,128,1024]{2,1,0:T(8,128)(2,1)S(1)}, bf16[2,128,1024]{2,1,0:T(8,128)(2,1)S(1)}, u32[]{:S(2)}, u32[]{:S(2)}) collective-permute-start(bf16[2,128,1024]{2,1,0:T(8,128)(2,1)S(1)} %get-tuple-element.40), channel_id=1, source_target_pairs={{0,2},{1,3},{2,0},{3,1},{4,6},{5,7},{6,4},{7,5},{8,10},{9,11},{10,... | collective-permute-start | bytes 1572872 | tf_op jit(solution)/shard_map/ppermute | solution.py:226
  83.6 15.9 %collective-permute-start.7 = (bf16[2,128,1024]{2,1,0:T(8,128)(2,1)S(1)}, bf16[2,128,1024]{2,1,0:T(8,128)(2,1)S(1)}, u32[]{:S(2)}, u32[]{:S(2)}) collective-permute-start(bf16[2,128,1024]{2,1,0:T(8,128)(2,1)S(1)} %get-tuple-element.33), channel_id=1, source_target_pairs={{0,1},{1,0},{2,3},{3,2},{4,5},{5,4},{6,7},{7,6},{8,9},{9,8},{10,11... | collective-permute-start | bytes 1572872 | tf_op jit(solution)/shard_map/ppermute | solution.py:226
  85.1 16.4 %collective-permute-start.9 = (bf16[2,128,1024]{2,1,0:T(8,128)(2,1)S(1)}, bf16[2,128,1024]{2,1,0:T(8,128)(2,1)S(1)}, u32[]{:S(2)}, u32[]{:S(2)}) collective-permute-start(bf16[2,128,1024]{2,1,0:T(8,128)(2,1)S(1)} %get-tuple-element.35), channel_id=1, source_target_pairs={{0,2},{1,3},{2,0},{3,1},{4,6},{5,7},{6,4},{7,5},{8,10},{9,11},{10,... | collective-permute-start | bytes 1572872 | tf_op jit(solution)/shard_map/ppermute | solution.py:226
  97.2 9.9 %collective-permute-start.12 = (bf16[128,1024]{1,0:T(8,128)(2,1)S(1)}, bf16[128,1024]{1,0:T(8,128)(2,1)S(1)}, u32[]{:S(2)}, u32[]{:S(2)}) collective-permute-start(bf16[128,1024]{1,0:T(8,128)(2,1)S(1)} %slice_bitcast_fusion.2), channel_id=1, source_target_pairs={{0,2},{1,3},{2,0},{3,1},{4,6},{5,7},{6,4},{7,5},{8,10},{9,11},{10,... | collective-permute-start | bytes 786440 | tf_op jit(solution)/shard_map/ppermute | solution.py:226
  98.0 9.2 %collective-permute-start.14 = (bf16[128,1024]{1,0:T(8,128)(2,1)S(1)}, bf16[128,1024]{1,0:T(8,128)(2,1)S(1)}, u32[]{:S(2)}, u32[]{:S(2)}) collective-permute-start(bf16[128,1024]{1,0:T(8,128)(2,1)S(1)} %slice_bitcast_fusion), channel_id=1, source_target_pairs={{0,1},{1,0},{2,3},{3,2},{4,5},{5,4},{6,7},{7,6},{8,9},{9,8},{10,11... | collective-permute-start | bytes 786440 | tf_op jit(solution)/shard_map/ppermute | solution.py:226
  101.8 10.1 %collective-permute-start.8 = (bf16[128,1024]{1,0:T(8,128)(2,1)S(1)}, bf16[128,1024]{1,0:T(8,128)(2,1)S(1)}, u32[]{:S(2)}, u32[]{:S(2)}) collective-permute-start(bf16[128,1024]{1,0:T(8,128)(2,1)S(1)} %slice_bitcast_fusion.6), channel_id=1, source_target_pairs={{0,2},{1,3},{2,0},{3,1},{4,6},{5,7},{6,4},{7,5},{8,10},{9,11},{10,... | collective-permute-start | bytes 786440 | tf_op jit(solution)/shard_map/ppermute | solution.py:226
  103.4 8.6 %collective-permute-start.10 = (bf16[128,1024]{1,0:T(8,128)(2,1)S(1)}, bf16[128,1024]{1,0:T(8,128)(2,1)S(1)}, u32[]{:S(2)}, u32[]{:S(2)}) collective-permute-start(bf16[128,1024]{1,0:T(8,128)(2,1)S(1)} %slice_bitcast_fusion.4), channel_id=1, source_target_pairs={{0,1},{1,0},{2,3},{3,2},{4,5},{5,4},{6,7},{7,6},{8,9},{9,8},{10,11... | collective-permute-start | bytes 786440 | tf_op jit(solution)/shard_map/ppermute | solution.py:226

commit v3 on v1

v3 whole, which is shorter than its diff:
```python
import functools
import math

import jax
import jax.numpy as jnp
import ml_dtypes
import numpy as np
from jax import lax
from jax.experimental import pallas as pl
from jax.experimental.pallas import tpu as pltpu
from jax.sharding import PartitionSpec as P

BLOCK = 1024
LANES = 128


def angles(first, second, period):
    return (np.arange(first)[:, None] * np.arange(second)[None, :] % period) * (2.0 * math.pi / period)


def rounded(table):
    return jnp.asarray(table.astype(np.float32).astype(ml_dtypes.bfloat16))


def split_rows(rows, span):
    out = lax.broadcasted_iota(jnp.int32, (rows, rows), 0)
    token = lax.broadcasted_iota(jnp.int32, (rows, rows), 1)
    block_rows = rows // span
    return jnp.where(token == (out % block_rows) * span + out // block_rows, 1.0, 0.0).astype(jnp.bfloat16)


def join_rows(rows, span):
    token = lax.broadcasted_iota(jnp.int32, (rows, rows), 0)
    held = lax.broadcasted_iota(jnp.int32, (rows, rows), 1)
    block_rows = rows // span
    return jnp.where(token == (held % block_rows) * span + held // block_rows, 1.0, 0.0).astype(jnp.bfloat16)


def pack_kernel(span, me_ref, values_hbm, gate_hbm, spectrum_hbm, *refs):
    outs, (values_ref, gate_ref, spectrum_ref, sems) = refs[:-4], refs[-4:]
    copies = [
        pltpu.make_async_copy(values_hbm, values_ref, sems.at[0]),
        pltpu.make_async_copy(gate_hbm, gate_ref, sems.at[1]),
    ]
    for part in range(2):
        for d in range(span):
            copies.append(pltpu.make_async_copy(
                spectrum_hbm.at[part, d], spectrum_ref.at[part * span + d], sems.at[2 + part * span + d]
            ))
    for copy in copies:
        copy.start()
    me = me_ref[0]
    rows = values_ref.shape[0]
    block_rows = rows // span
    copies[0].wait()
    copies[1].wait()
    source = (values_ref[...].astype(jnp.float32) * gate_ref[...].astype(jnp.float32)).astype(jnp.bfloat16)
    values_ref[...] = jnp.dot(
        split_rows(rows, span), source, preferred_element_type=jnp.float32
    ).astype(jnp.bfloat16)

    def lanes_of(m):
        return pl.ds(pl.multiple_of((me ^ m) * LANES, LANES), LANES)

    for m, out_ref in enumerate(outs):
        for b in range(span):
            out_ref[2 * span + b] = values_ref[b * block_rows:(b + 1) * block_rows, lanes_of(m)]
    for part in range(2 * span):
        copies[2 + part].wait()
        for m, out_ref in enumerate(outs):
            out_ref[part] = spectrum_ref[part, :, lanes_of(m)].astype(jnp.bfloat16)


def pack(me, values, gate_in, spectrum, shares):
    rows, width = values.shape
    _, span, block_rows, _ = spectrum.shape
    shape = (3 * span, block_rows, LANES)
    vmem, hbm = pl.BlockSpec(memory_space=pltpu.VMEM), pl.BlockSpec(memory_space=pltpu.HBM)
    return pl.pallas_call(
        functools.partial(pack_kernel, span),
        in_specs=[pl.BlockSpec(memory_space=pltpu.SMEM), hbm, hbm, hbm],
        out_specs=[vmem] * shares,
        out_shape=[jax.ShapeDtypeStruct(shape, jnp.bfloat16)] * shares,
        scratch_shapes=[
            pltpu.VMEM((rows, width), jnp.bfloat16),
            pltpu.VMEM((rows, width), jnp.bfloat16),
            pltpu.VMEM((2 * span, block_rows, width), jnp.float32),
            pltpu.SemaphoreType.DMA((2 + 2 * span,)),
        ],
        compiler_params=pltpu.CompilerParams(vmem_limit_bytes=60 << 20),
        name="pack",
    )(me, values, gate_in, spectrum)


def take_kernel(places_ref, weight_hbm, *refs):
    outs, sems = refs[:-1], refs[-1]
    slabs = sems.shape[1]
    depth, cols = outs[0].shape[0] // slabs, outs[0].shape[1]
    copies = [
        pltpu.make_async_copy(
            weight_hbm.at[i * depth:(i + 1) * depth, pl.ds(pl.multiple_of(places_ref[k] * cols, cols), cols)],
            out_ref.at[i * depth:(i + 1) * depth],
            sems.at[k, i],
        )
        for k, out_ref in enumerate(outs)
        for i in range(slabs)
    ]
    for copy in copies:
        copy.start()
    for copy in copies:
        copy.wait()


def take_blocks(places, weight):
    depth, cols = weight.shape[0], weight.shape[1] // 8
    count, slabs = places.shape[0], 4
    return pl.pallas_call(
        take_kernel,
        in_specs=[pl.BlockSpec(memory_space=pltpu.SMEM), pl.BlockSpec(memory_space=pltpu.HBM)],
        out_specs=[pl.BlockSpec(memory_space=pltpu.VMEM)] * count,
        out_shape=[jax.ShapeDtypeStruct((depth, cols), weight.dtype)] * count,
        scratch_shapes=[pltpu.SemaphoreType.DMA((count, slabs))],
        compiler_params=pltpu.CompilerParams(vmem_limit_bytes=48 << 20),
        cost_estimate=pl.CostEstimate(flops=0, bytes_accessed=128 * depth * cols, transcendentals=0),
        name="take_blocks",
    )(places, weight)


def conv_kernel(parts, order, me_ref, *refs):
    shares = len(order)
    data, (cos_ref, sin_ref, turn_cos_ref, turn_sin_ref) = refs[:shares], refs[shares:shares + 4]
    outs, (cols_ref, filt_ref, re_ref, im_ref) = refs[shares + 4:shares + 4 + parts], refs[shares + 4 + parts:]
    me = me_ref[0]
    rows = data[0].shape[1]
    for m, ref in zip(order, data):
        at = pl.ds(pl.multiple_of((me ^ m) * rows, rows), rows)
        for b in range(2):
            cols_ref[at, b * LANES:(b + 1) * LANES] = ref[4 + b]
        for part in range(4):
            filt_ref[part, at, :] = ref[part]
    step = 2 * rows
    for i in range(shares * rows // step):
        at = slice(i * step, (i + 1) * step)
        first_re = jnp.dot(cos_ref[at, :], cols_ref[...], preferred_element_type=jnp.float32)
        first_sin = jnp.dot(sin_ref[at, :], cols_ref[...], preferred_element_type=jnp.float32)
        tc, ts = turn_cos_ref[at, :], turn_sin_ref[at, :]
        re0, im0 = first_re[:, :LANES], -first_sin[:, :LANES]
        re1, im1 = first_re[:, LANES:], -first_sin[:, LANES:]
        re1, im1 = re1 * tc + im1 * ts, im1 * tc - re1 * ts
        f0r, f0i, f1r, f1i = re0 + re1, im0 + im1, re0 - re1, im0 - im1
        s0r, s1r, s0i, s1i = (filt_ref[part, at, :].astype(jnp.float32) for part in range(4))
        p0r, p0i = f0r * s0r - f0i * s0i, f0r * s0i + f0i * s0r
        p1r, p1i = f1r * s1r - f1i * s1i, f1r * s1i + f1i * s1r
        b0r, b0i = 0.5 * (p0r + p1r), 0.5 * (p0i + p1i)
        b1r, b1i = 0.5 * (p0r - p1r), 0.5 * (p0i - p1i)
        b1r, b1i = b1r * tc - b1i * ts, b1i * tc + b1r * ts
        re_ref[at, :] = jnp.concatenate([b0r, b1r], axis=1).astype(jnp.bfloat16)
        im_ref[at, :] = jnp.concatenate([b0i, b1i], axis=1).astype(jnp.bfloat16)
    scale = 1.0 / (shares * rows)
    part_rows = rows // parts
    for i in range(shares * rows // step):
        at = slice(i * step, (i + 1) * step)
        conv = jnp.dot(cos_ref[at, :], re_ref[...], preferred_element_type=jnp.float32)
        conv = conv - jnp.dot(sin_ref[at, :], im_ref[...], preferred_element_type=jnp.float32)
        conv = (conv * scale).astype(jnp.bfloat16)
        for s in range(2):
            for p in range(parts):
                begin = s * rows + p * part_rows
                for b in range(2):
                    outs[p][2 * i + s, b] = conv[begin:begin + part_rows, b * LANES:(b + 1) * LANES]


def convolve(me, data, order, parts):
    shares = len(data)
    rows = data[0].shape[1]
    block = shares * rows
    angle = angles(block, block, block)
    turn = np.broadcast_to(angles(block, 2, 2 * block)[:, 1:], (block, LANES))
    vmem = pl.BlockSpec(memory_space=pltpu.VMEM)
    columns = pltpu.VMEM((block, 2 * LANES), jnp.bfloat16)
    return pl.pallas_call(
        functools.partial(conv_kernel, parts, order),
        in_specs=[pl.BlockSpec(memory_space=pltpu.SMEM)] + [vmem] * (shares + 4),
        out_specs=[vmem] * parts,
        out_shape=[jax.ShapeDtypeStruct((shares, 2, rows // parts, LANES), jnp.bfloat16)] * parts,
        scratch_shapes=[columns, pltpu.VMEM((4, block, LANES), jnp.bfloat16), columns, columns],
        compiler_params=pltpu.CompilerParams(vmem_limit_bytes=24 << 20),
        cost_estimate=pl.CostEstimate(flops=64 * block * block * LANES, bytes_accessed=8 * block * block, transcendentals=0),
        name="convolve",
    )(
        me, *data, rounded(np.cos(angle)), rounded(np.sin(angle)),
        jnp.asarray(np.cos(turn).astype(np.float32)), jnp.asarray(np.sin(turn).astype(np.float32)),
    )


def gate_kernel(conv_ref, gate_ref, *refs):
    outs, held_ref = refs[:-1], refs[-1]
    shares, span, block_rows, _ = conv_ref.shape
    rows = span * block_rows
    for s in range(shares):
        held_ref[:, s * LANES:(s + 1) * LANES] = conv_ref[s].reshape(rows, LANES)
    conv = jnp.dot(join_rows(rows, span), held_ref[...], preferred_element_type=jnp.float32)
    gated = (conv * gate_ref[...].astype(jnp.float32)).astype(jnp.bfloat16)
    part = rows // len(outs)
    for p, out_ref in enumerate(outs):
        out_ref[...] = gated[p * part:(p + 1) * part]


def gate(conv, gate_out, parts):
    rows, width = gate_out.shape
    vmem = pl.BlockSpec(memory_space=pltpu.VMEM)
    return pl.pallas_call(
        gate_kernel,
        in_specs=[vmem, vmem],
        out_specs=[vmem] * parts,
        out_shape=[jax.ShapeDtypeStruct((rows // parts, width), jnp.bfloat16)] * parts,
        scratch_shapes=[pltpu.VMEM((rows, width), jnp.bfloat16)],
        compiler_params=pltpu.CompilerParams(vmem_limit_bytes=16 << 20),
        name="gate",
    )(conv, gate_out)


def own_kernel(me_ref, *refs):
    parts = (len(refs) - 1) // 2
    gated, slabs, out_ref = refs[:parts], refs[parts:-1], refs[-1]
    rows, depth = gated[0].shape[0], slabs[0].shape[0]
    for p, gated_ref in enumerate(gated):
        out_ref[0, p * rows:(p + 1) * rows] = sum(
            jnp.dot(gated_ref[:, i * depth:(i + 1) * depth], slab[...], preferred_element_type=jnp.float32)
            for i, slab in enumerate(slabs)
        )


def own_part(me, gated, weight, blocks):
    parts = len(gated)
    part_rows, depth = gated[0].shape
    cols = weight.shape[1] // 8

    def column(slab, i, me_ref):
        flip = sum((jnp.where(i == place, f, 0) for place, (f, _) in enumerate(blocks)), 0)
        half = sum((jnp.where(i == place, h, 0) for place, (_, h) in enumerate(blocks)), 0)
        return slab, (me_ref[0] ^ flip) * 2 + half

    return pl.pallas_call(
        own_kernel,
        grid_spec=pltpu.PrefetchScalarGridSpec(
            num_scalar_prefetch=1,
            grid=(len(blocks),),
            in_specs=[pl.BlockSpec((part_rows, depth), lambda i, m: (0, 0))] * parts
            + [pl.BlockSpec((depth // parts, cols), functools.partial(column, slab)) for slab in range(parts)],
            out_specs=pl.BlockSpec((1, parts * part_rows, cols), lambda i, m: (i, 0, 0)),
        ),
        out_shape=jax.ShapeDtypeStruct((len(blocks), parts * part_rows, cols), jnp.float32),
        compiler_params=pltpu.CompilerParams(vmem_limit_bytes=40 << 20),
        cost_estimate=pl.CostEstimate(
            flops=2 * parts * part_rows * depth * cols * len(blocks),
            bytes_accessed=2 * depth * cols * len(blocks), transcendentals=0,
        ),
        name="own_part",
    )(me, *gated, *[weight] * parts)


def add_kernel(parts, kept, core_ref, own_ref, *refs):
    moved, refs = refs[:2 * parts], refs[2 * parts:]
    weights, (a_ref, b_ref, held_ref, sems) = refs[:4], refs[4:]
    slabs = sems.shape[1]
    depth = held_ref.shape[1] // slabs

    def copies(side, take_mine):
        source = weights[2 * side] if take_mine else weights[2 * side + 1]
        return [
            pltpu.make_async_copy(
                source.at[i * depth:(i + 1) * depth], held_ref.at[side, i * depth:(i + 1) * depth], sems.at[side, i]
            )
            for i in range(slabs)
        ]

    mine_core = 0 if kept else 1
    for side in range(2):

        @pl.when(core_ref[0] == mine_core)
        def _():
            for copy in copies(side, True):
                copy.start()

        @pl.when(core_ref[0] != mine_core)
        def _():
            for copy in copies(side, False):
                copy.start()

    rows = moved[0].shape[0]
    for side, out_ref in enumerate((a_ref, b_ref)):
        for i, copy in enumerate(copies(side, True)):
            copy.wait()
        for p in range(parts):
            at = slice(p * rows, (p + 1) * rows)
            total = own_ref[side, at] + jnp.dot(
                moved[side * parts + p][...], held_ref[side], preferred_element_type=jnp.float32
            )
            out_ref[at] = total.astype(out_ref.dtype)


def add_moved(core, own, moved_x, moved_y, weights, first, kept, dtype):
    parts = len(moved_x)
    rows, depth = moved_x[0].shape
    cols = own.shape[2]
    whole = pl.BlockSpec((rows, depth), lambda i: (0, 0))
    shape = jax.ShapeDtypeStruct((parts * rows, cols), dtype)
    out = pl.BlockSpec((parts * rows, cols), lambda i: (0, 0))
    return pl.pallas_call(
        functools.partial(add_kernel, parts, kept),
        grid=(1,),
        in_specs=[
            pl.BlockSpec(memory_space=pltpu.SMEM),
            pl.BlockSpec((2, parts * rows, cols), lambda i: (0, first, 0)),
        ]
        + [whole] * (2 * parts)
        + [pl.BlockSpec(memory_space=pl.ANY)] * 4,
        out_specs=[out, out],
        out_shape=[shape, shape],
        scratch_shapes=[pltpu.VMEM((2, depth, cols), jnp.bfloat16), pltpu.SemaphoreType.DMA((2, 4))],
        compiler_params=pltpu.CompilerParams(vmem_limit_bytes=40 << 20),
        cost_estimate=pl.CostEstimate(
            flops=4 * parts * rows * depth * cols, bytes_accessed=4 * depth * cols, transcendentals=0
        ),
        name="add_kept" if kept else "add_sent",
    )(core, own, *moved_x, *moved_y, *weights)


def swap(data, axis, flip):
    return lax.ppermute(data, axis, [(i, i ^ flip) for i in range(lax.axis_size(axis))])


def by_channels(values, gate_in, gate_out, spectrum, out_weight):
    seq_count = lax.axis_size("seq")
    here = lax.axis_index("seq").astype(jnp.int32)
    me = lax.axis_index("chan").astype(jnp.int32)
    core = here % 2
    parts = 2

    order = tuple(sorted(range(seq_count), key=lambda m: (m == 0, m == 1, m % 2, -m)))
    packed = list(pack(here.reshape(1), values, gate_in, spectrum, seq_count))
    places = jnp.stack([(me ^ (1 + 2 * core)) * 2, (me ^ (2 + core)) * 2 + 1])
    _, places = lax.optimization_barrier((packed, places))
    block_x, block_y = take_blocks(places, out_weight)
    weight_x, weight_y = swap(block_x, "chan", 1), swap(block_y, "chan", 2)
    late = [m for m in order if m % 2]
    held, _ = lax.optimization_barrier(([packed[m] for m in late], block_y))
    for m, mine in zip(late, held):
        packed[m] = mine
    data = [swap(packed[m], "seq", m) if m else packed[m] for m in order]
    (conv,) = convolve(here.reshape(1), data, order, 1)
    conv = lax.all_to_all(conv, "seq", split_axis=0, concat_axis=0, tiled=True)
    gated = gate(conv, gate_out, parts)
    weight_x, weight_y, _ = lax.optimization_barrier((weight_x, weight_y, gated))
    weights = [weight_x, swap(weight_x, "seq", 1), weight_y, swap(weight_y, "seq", 1)]
    own = own_part(me.reshape(1), gated, out_weight, ((2, 0), (1, 1)))
    core = core.reshape(1)
    moved_x, moved_y = [], []
    for p in range(parts):
        mine = gated[p]
        if p:
            mine, _ = lax.optimization_barrier((mine, own))
        moved_x.append(swap(mine, "chan", 1))
        moved_y.append(swap(mine, "chan", 2))
    sums_a, sums_b = [], []
    for p in range(parts):
        sent = add_moved(core, own, moved_x[p:p + 1], moved_y[p:p + 1], weights, p, False, jnp.bfloat16)
        sums_a.append(swap(sent[0], "chan", 2))
        sums_b.append(swap(sent[1], "chan", 1))
    gated, _ = lax.optimization_barrier((gated, sent))
    own = own_part(me.reshape(1), gated, out_weight, ((0, 0), (0, 1)))
    kept_a, kept_b = add_moved(core, own, moved_x, moved_y, weights, 0, True, jnp.float32)
    sums = jnp.concatenate([jnp.concatenate(sums_a, axis=0), jnp.concatenate(sums_b, axis=0)], axis=1)
    return (jnp.concatenate([kept_a, kept_b], axis=1) + sums.astype(jnp.float32)).astype(jnp.bfloat16)


def to_columns(data):
    return lax.all_to_all(data, "seq", split_axis=2, concat_axis=1, tiled=True)


def to_rows(data):
    return lax.all_to_all(data, "seq", split_axis=1, concat_axis=2, tiled=True)


def by_frequencies(values, gate_in, gate_out, spectrum, out_weight):
    seq_count = lax.axis_size("seq")
    seq_index = lax.axis_index("seq")
    tok_rows, chan_width = values.shape
    block_rows = BLOCK // seq_count
    span = tok_rows // block_rows
    tokens_all = BLOCK * span
    col_share = span * chan_width // seq_count
    block_cos = rounded(np.cos(angles(BLOCK, BLOCK, BLOCK)))
    block_sin = rounded(np.sin(angles(BLOCK, BLOCK, BLOCK)))
    span_cos = rounded(np.cos(angles(span, span, span)))
    span_sin = rounded(np.sin(angles(span, span, span)))
    turn_all = angles(BLOCK, span, tokens_all)
    turn_cos_all = jnp.asarray(np.cos(turn_all).astype(np.float32))
    turn_sin_all = jnp.asarray(np.sin(turn_all).astype(np.float32))
    source = (values.astype(jnp.float32) * gate_in.astype(jnp.float32)).astype(jnp.bfloat16)
    spread = to_columns(source.reshape(1, block_rows, seq_count, col_share))
    columns = spread.reshape(BLOCK, col_share)
    cos_part = jnp.dot(jnp.transpose(block_cos), columns, preferred_element_type=jnp.float32)
    sin_part = jnp.dot(jnp.transpose(block_sin), columns, preferred_element_type=jnp.float32)
    col_pos = (seq_index * col_share + jnp.arange(col_share, dtype=jnp.int32)) // chan_width
    turn_cos = jnp.take(turn_cos_all, col_pos, axis=1)
    turn_sin = jnp.take(turn_sin_all, col_pos, axis=1)
    twist_re = cos_part * turn_cos - sin_part * turn_sin
    twist_im = -sin_part * turn_cos - cos_part * turn_sin
    twisted = jnp.stack([twist_re, twist_im]).astype(jnp.bfloat16)
    arranged = to_rows(twisted).reshape(2, block_rows, span, chan_width)
    with_cos = jnp.einsum("bd,kcbh->kdch", span_cos, arranged, preferred_element_type=jnp.float32)
    with_sin = jnp.einsum("bd,kcbh->kdch", span_sin, arranged, preferred_element_type=jnp.float32)
    freq_re = with_cos[0] + with_sin[1]
    freq_im = with_cos[1] - with_sin[0]
    prod_re = freq_re * spectrum[0] - freq_im * spectrum[1]
    prod_im = freq_re * spectrum[1] + freq_im * spectrum[0]
    product = jnp.stack([prod_re, prod_im]).astype(jnp.bfloat16)
    back_cos = jnp.einsum("db,kdch->kcbh", span_cos, product, preferred_element_type=jnp.float32)
    back_sin = jnp.einsum("db,kdch->kcbh", span_sin, product, preferred_element_type=jnp.float32)
    back_re = (back_cos[0] - back_sin[1]) / span
    back_im = (back_cos[1] + back_sin[0]) / span
    back_tc = lax.dynamic_slice_in_dim(turn_cos_all, seq_index * block_rows, block_rows)[:, :, None]
    back_ts = lax.dynamic_slice_in_dim(turn_sin_all, seq_index * block_rows, block_rows)[:, :, None]
    rotated = jnp.stack(
        [back_re * back_tc - back_im * back_ts, back_im * back_tc + back_re * back_ts]
    ).astype(jnp.bfloat16)
    gathered = to_columns(rotated.reshape(2, block_rows, seq_count, col_share)).reshape(2, BLOCK, col_share)
    summed = jnp.dot(block_cos, gathered[0], preferred_element_type=jnp.float32)
    summed = summed - jnp.dot(block_sin, gathered[1], preferred_element_type=jnp.float32)
    ordered = (summed / BLOCK).astype(jnp.bfloat16).reshape(1, BLOCK, col_share)
    conv = to_rows(ordered).reshape(tok_rows, chan_width)
    gated = (conv.astype(jnp.float32) * gate_out.astype(jnp.float32)).astype(jnp.bfloat16)
    partial_sum = jnp.dot(gated, out_weight, preferred_element_type=jnp.float32)
    return lax.psum_scatter(partial_sum.astype(jnp.bfloat16), "chan", scatter_dimension=1, tiled=True)


def shards(values, gate_in, gate_out, spectrum, out_weight):
    seq_count, chan_count = lax.axis_size("seq"), lax.axis_size("chan")
    _, span, block_rows, width = spectrum.shape
    one_lane_block = width == seq_count * LANES and block_rows % 32 == 0
    if span == 2 and chan_count == 4 and seq_count & (seq_count - 1) == 0 and one_lane_block:
        return by_channels(values, gate_in, gate_out, spectrum, out_weight)
    return by_frequencies(values, gate_in, gate_out, spectrum, out_weight)


def solution(mesh):
    placed = (
        P("seq", "chan"),
        P("seq", "chan"),
        P("seq", "chan"),
        P(None, None, "seq", "chan"),
        P("chan", None),
    )
    return jax.shard_map(
        shards, mesh=mesh, in_specs=placed, out_specs=P("seq", "chan"), check_vma=False
    )
```

time: 116 us -> 95.1 us (0.82)
  blocking collectives: 56.4 us -> 18.3 us
  waiting for transfers between devices: 13.2 us -> 30.9 us
  local copies, waits for them, and re-layouts: 17.2 us -> 0.05 us
  starting transfers between devices: 11 us -> 22.8 us
  Pallas kernels: 15.8 us -> 20.2 us
    all_to_all x1 -> x0, blocking collectives: 44.2 us -> none  [by_channels(): data = lax.all_to_all(data, 'seq', split_axis=0, concat_axis=0, tiled=True)]
    ppermute x8 -> x19, waiting for transfers between devices: 13.2 us -> 30.9 us  [swap(): lax.ppermute(data, axis, [(i, i ^ flip) for i in range(lax.axis_size(axis...]
    unnamed x22 -> x20, local copies, waits for them, and re-layouts: 17.1 us -> 0.05 us
    ppermute x8 -> x19, starting transfers between devices: 7.61 us -> 22.8 us  [swap(): lax.ppermute(data, axis, [(i, i ^ flip) for i in range(lax.axis_size(axis...]
    all_to_all x1, blocking collectives: 12.1 us -> 18.3 us  [by_channels(): conv = lax.all_to_all(conv, 'seq', split_axis=0, concat_axis=0, tiled=True)]
    pallas_call x6 -> x9, Pallas kernels: 15.8 us -> 20.2 us  [the longest x2 6.09 us: own_part(): pl.pallas_call(own_kernel, grid_spec=pltpu.PrefetchScalarGridSpec(num_sca...]
    all_to_all x1 -> x0, starting transfers between devices: 3.41 us -> none  [by_channels(): conv = lax.all_to_all(conv, 'seq', split_axis=0, concat_axis=0, tiled=True)]
  transfers between devices with their start and end apart: 9 -> 19, of which waited for: 4 -> 8; matrix products, arithmetic and copies ran while one was open for 1% -> 0% of each run, Pallas kernels for 10% -> 18%
where the time goes in v3:
time: 95.1 us; the launch traced here: 93.9 us
  waiting for transfers between devices  30.9 us (32%)
  starting transfers between devices  22.8 us (24%)
  Pallas kernels  20.2 us (21%)
  blocking collectives  18.3 us (19%)
  other arithmetic  1.35 us (1%)
    ppermute x19, waiting for transfers between devices, swap(): lax.ppermute(data, axis, [(i, i ^ flip) for i in range(lax.axis_size(axis...  30.9 us
    ppermute x19, starting transfers between devices, swap(): lax.ppermute(data, axis, [(i, i ^ flip) for i in range(lax.axis_size(axis...  22.8 us
    all_to_all x1, blocking collectives, by_channels(): conv = lax.all_to_all(conv, 'seq', split_axis=0, concat_axis=0, tiled=True)  18.3 us
    pallas_call x2, Pallas kernels, own_part(): pl.pallas_call(own_kernel, grid_spec=pltpu.PrefetchScalarGridSpec(num_sca...  6.09 us
    pallas_call x3, Pallas kernels, add_moved(): pl.pallas_call(functools.partial(add_kernel, parts, kept), grid=(1,), in_...  4.68 us
    pallas_call x1, Pallas kernels, take_blocks(): pl.pallas_call(take_kernel, in_specs=[pl.BlockSpec(memory_space=pltpu.SME...  3.18 us
    pallas_call x1, Pallas kernels, pack(): pl.pallas_call(functools.partial(pack_kernel, span), in_specs=[pl.BlockSp...  3.17 us
    pallas_call x1, Pallas kernels, convolve(): pl.pallas_call(functools.partial(conv_kernel, parts, order), in_specs=[pl...  2.71 us
  transfers between devices with their start and end apart: 19, of which 8 were waited for; matrix products, arithmetic and copies ran while one was open for 0% of the time, Pallas kernels for 18%

profile of v3, /device:TPU:0, one launch (start us, length us, event | category | flops | bytes accessed | tf_op | source)
XLA Modules:
  0.0 93.9 jit_solution(16350686300520823963)
XLA Ops:
  0.0 3.2 %pack.1 = (bf16[6,128,128]{2,1,0:T(8,128)(2,1)}, bf16[6,128,128]{2,1,0:T(8,128)(2,1)}, bf16[6,128,128]{2,1,0:T(8,128)(2,1)}, bf16[6,128,128]{2,1,0:T(8,128)(2,1)...) custom-call(s32[1]{0:T(128)} %bitcast.2.me_ref, ...), custom_call_target="tpu_custom_call" | custom-call | tf_op jit(solution)/shard_map/pack/pallas_call | solution.py:79
  3.2 5.1 %collective-permute-start = (bf16[6,128,128]{2,1,0:T(8,128)(2,1)}, bf16[6,128,128]{2,1,0:T(8,128)(2,1)S(1)}, u32[]{:S(2)}, u32[]{:S(2)}) collective-permute-start(bf16[6,128,128]{2,1,0:T(8,128)(2,1)} %get-tuple-element.33), channel_id=1, source_target_pairs={{0,24},{4,28},{8,16},{12,20},{16,8},{20,12},{24,0},{28,4},{1,25},{... | collective-permute-start | bytes 589832 | tf_op jit(solution)/shard_map/ppermute | solution.py:331
  8.3 0.0 collective-permute-start.1
  8.3 0.6 collective-permute-start.2
  8.9 0.1 pad_add_fusion.places_ref
  9.0 0.0 copy-start.1
  9.0 0.0 copy-start.2
  9.1 0.0 copy-start.3
  9.1 0.0 copy-start.4
  9.1 0.0 copy-start.5
  9.1 3.2 %take_blocks.1 = (bf16[1024,1024]{1,0:T(8,128)(2,1)S(1)}, bf16[1024,1024]{1,0:T(8,128)(2,1)S(1)}) custom-call(s32[2]{0:T(128)S(1)} %pad_add_fusion.places_ref, bf16[1024,8192]{1,0:T(8,128)(2,1)} %refs_3_.3), custom_call_target="tpu_custom_call" | custom-call | bytes 134217728 | tf_op jit(solution)/shard_map/take_blocks/pallas_call | solution.py:117
  12.3 0.0 copy-done.9
  12.3 2.4 %collective-permute-start.3 = (bf16[6,128,128]{2,1,0:T(8,128)(2,1)S(1)}, bf16[6,128,128]{2,1,0:T(8,128)(2,1)S(1)}, u32[]{:S(2)}, u32[]{:S(2)}) collective-permute-start(bf16[6,128,128]{2,1,0:T(8,128)(2,1)S(1)} %copy-done.9), channel_id=1, source_target_pairs={{0,28},{4,24},{8,20},{12,16},{16,12},{20,8},{24,4},{28,0},{1,29},{... | collective-permute-start | bytes 589832 | tf_op jit(solution)/shard_map/ppermute | solution.py:331
  14.7 1.5 %collective-permute-start.9 = (bf16[1024,1024]{1,0:T(8,128)(2,1)S(1)}, bf16[1024,1024]{1,0:T(8,128)(2,1)S(1)}, u32[]{:S(2)}, u32[]{:S(2)}) collective-permute-start(bf16[1024,1024]{1,0:T(8,128)(2,1)S(1)} %get-tuple-element.50), channel_id=1, source_target_pairs={{0,1},{1,0},{2,3},{3,2},{4,5},{5,4},{6,7},{7,6},{8,9},{9,8},{10,11... | collective-permute-start | bytes 6291464 | tf_op jit(solution)/shard_map/ppermute | solution.py:331
  16.2 0.0 collective-permute-done.refs_0_
  16.2 1.5 %collective-permute-start.10 = (bf16[1024,1024]{1,0:T(8,128)(2,1)S(1)}, bf16[1024,1024]{1,0:T(8,128)(2,1)S(1)}, u32[]{:S(2)}, u32[]{:S(2)}) collective-permute-start(bf16[1024,1024]{1,0:T(8,128)(2,1)S(1)} %get-tuple-element.42), channel_id=1, source_target_pairs={{0,2},{1,3},{2,0},{3,1},{4,6},{5,7},{6,4},{7,5},{8,10},{9,11},{10,... | collective-permute-start | bytes 6291464 | tf_op jit(solution)/shard_map/ppermute | solution.py:331
  17.7 12.7 %collective-permute-done.1.refs_1_ = bf16[6,128,128]{2,1,0:T(8,128)(2,1)S(1)} collective-permute-done((bf16[6,128,128]{2,1,0:T(8,128)(2,1)}, bf16[6,128,128]{2,1,0:T(8,128)(2,1)S(1)}, u32[]{:S(2)}, u32[]{:S(2)}) %collective-permute-start.1) | collective-permute-done | bytes 196640 | tf_op jit(solution)/shard_map/ppermute | solution.py:331
  30.4 0.0 copy-done.8
  30.4 0.0 collective-permute-start.4
  30.4 0.0 collective-permute-done.2.refs_2_
  30.4 0.0 copy-done.7
  30.4 2.9 %collective-permute-start.5 = (bf16[6,128,128]{2,1,0:T(8,128)(2,1)S(1)}, bf16[6,128,128]{2,1,0:T(8,128)(2,1)S(1)}, u32[]{:S(2)}, u32[]{:S(2)}) collective-permute-start(bf16[6,128,128]{2,1,0:T(8,128)(2,1)S(1)} %copy-done.7), channel_id=1, source_target_pairs={{0,12},{4,8},{8,4},{12,0},{16,28},{20,24},{24,20},{28,16},{1,13},{... | collective-permute-start | bytes 589832 | tf_op jit(solution)/shard_map/ppermute | solution.py:331
  33.3 0.0 collective-permute-done.3.refs_3_
  33.3 0.0 copy-done.6
  33.3 0.0 collective-permute-start.6
  33.3 8.7 %collective-permute-done.4.refs_4_ = bf16[6,128,128]{2,1,0:T(8,128)(2,1)S(1)} collective-permute-done((bf16[6,128,128]{2,1,0:T(8,128)(2,1)S(1)}, bf16[6,128,128]{2,1,0:T(8,128)(2,1)S(1)}, u32[]{:S(2)}, u32[]{:S(2)}) %collective-permute-start.4) | collective-permute-done | bytes 196640 | tf_op jit(solution)/shard_map/ppermute | solution.py:331
  42.1 0.0 collective-permute-done.5.refs_5_
  42.1 0.0 collective-permute-done.6.refs_6_
  42.1 0.0 copy-done.1
  42.1 0.0 copy-done.2
  42.1 0.0 copy-done.3
  42.1 0.0 copy-done.4
  42.1 0.0 copy-done.5
  42.1 2.7 %convolve.1 = bf16[8,2,128,128]{3,2,1,0:T(8,128)(2,1)S(1)} custom-call(s32[1]{0:T(128)} %bitcast.2.me_ref, bf16[6,128,128]{2,1,0:T(8,128)(2,1)S(1)} %collective-permute-done.refs_0_, bf16[6,128,128]{2,1,0:T(8,128)(2,1)S(1)} %collective-permute-done.1.refs_1_, bf16[6,128,128]{2,1,0:T(8,128)(2,1)S(1)} %collective-permute-done.2.refs_2_, ...), custom_call_target="tpu_custom_call" | custom-call | flops 8589934592 | bytes 8388608 | tf_op jit(solution)/shard_map/convolve/pallas_call | solution.py:181
  44.8 18.3 %all_to_all.5.conv_ref = bf16[8,2,128,128]{3,2,1,0:T(8,128)(2,1)S(1)} all-to-all(bf16[8,2,128,128]{3,2,1,0:T(8,128)(2,1)S(1)} %convolve.1), channel_id=1, replica_groups=mesh['seq'=8,'chan'=4] {'seq'}, dimensions={0} | all-to-all | bytes 1048576 | tf_op jit(solution)/shard_map/all_to_all | solution.py:353
  63.2 0.4 gate.1
  63.5 0.0 collective-permute-done.9.refs_2_.refs_4_
  63.5 0.9 collective-permute-done.10.refs_4_.refs_6_
  64.4 0.1 collective-permute-start.11
  64.6 0.4 collective-permute-start.12
  64.9 1.5 %collective-permute-start.14 = (bf16[128,1024]{1,0:T(8,128)(2,1)S(1)}, bf16[128,1024]{1,0:T(8,128)(2,1)S(1)}, u32[]{:S(2)}, u32[]{:S(2)}) collective-permute-start(bf16[128,1024]{1,0:T(8,128)(2,1)S(1)} %get-tuple-element.55.refs_0_), channel_id=1, source_target_pairs={{0,2},{1,3},{2,0},{3,1},{4,6},{5,7},{6,4},{7,5},{8,10},{9,11},{10,... | collective-permute-start | bytes 786440 | tf_op jit(solution)/shard_map/ppermute | solution.py:331
  66.4 0.7 collective-permute-start.13
  67.1 3.1 %own_part.2.own_ref = f32[2,256,1024]{2,1,0:T(8,128)S(1)} custom-call(s32[1]{0:T(128)} %bitcast.1.me_ref, bf16[128,1024]{1,0:T(8,128)(2,1)S(1)} %get-tuple-element.55.refs_0_, bf16[128,1024]{1,0:T(8,128)(2,1)S(1)} %get-tuple-element.56.refs_1_, bf16[1024,8192]{1,0:T(8,128)(2,1)} %refs_3_.3, bf16[1024,8192]{1,0:T(8,128)(2,1)} %refs_3_.3), custom_call_target="tpu_custom_call" | custom-call | flops 1073741824 | bytes 4194304 | tf_op jit(solution)/shard_map/own_part/pallas_call | solution.py:244
  70.2 0.6 collective-permute-start.8
  70.8 3.3 %collective-permute-done.14.refs_2_.refs_1_ = bf16[128,1024]{1,0:T(8,128)(2,1)S(1)} collective-permute-done((bf16[128,1024]{1,0:T(8,128)(2,1)S(1)}, bf16[128,1024]{1,0:T(8,128)(2,1)S(1)}, u32[]{:S(2)}, u32[]{:S(2)}) %collective-permute-start.14) | collective-permute-done | bytes 262176 | tf_op jit(solution)/shard_map/ppermute | solution.py:331
  74.1 0.0 collective-permute-start.7
  74.1 0.4 collective-permute-done.13.refs_0_
  74.5 0.0 collective-permute-done.11.refs_3_.refs_5_
  74.5 0.0 collective-permute-done.12.refs_5_.refs_7_
  74.5 1.4 %add_sent.3 = (bf16[128,1024]{1,0:T(8,128)(2,1)S(1)}, bf16[128,1024]{1,0:T(8,128)(2,1)S(1)}) custom-call(s32[1]{0:T(128)} %bitcast.core_ref, f32[2,256,1024]{2,1,0:T(8,128)S(1)} %own_part.2.own_ref, bf16[128,1024]{1,0:T(8,128)(2,1)S(1)} %collective-permute-done.13.refs_0_, bf16[128,1024]{1,0:T(8,128)(2,1)S(1)} %collective-permute-done.14.refs_2_.refs_1_, ...), custom_call_target="tpu_custom_call" | custom-call | flops 536870912 | bytes 4194304 | tf_op jit(solution)/shard_map/add_sent/pallas_call | solution.py:310
  75.9 1.9 %collective-permute-start.15 = (bf16[128,1024]{1,0:T(8,128)(2,1)S(1)}, bf16[128,1024]{1,0:T(8,128)(2,1)S(1)}, u32[]{:S(2)}, u32[]{:S(2)}) collective-permute-start(bf16[128,1024]{1,0:T(8,128)(2,1)S(1)} %get-tuple-element.59), channel_id=1, source_target_pairs={{0,2},{1,3},{2,0},{3,1},{4,6},{5,7},{6,4},{7,5},{8,10},{9,11},{10,... | collective-permute-start | bytes 786440 | tf_op jit(solution)/shard_map/ppermute | solution.py:331
  77.8 1.3 %collective-permute-start.17 = (bf16[128,1024]{1,0:T(8,128)(2,1)S(1)}, bf16[128,1024]{1,0:T(8,128)(2,1)S(1)}, u32[]{:S(2)}, u32[]{:S(2)}) collective-permute-start(bf16[128,1024]{1,0:T(8,128)(2,1)S(1)} %get-tuple-element.60), channel_id=1, source_target_pairs={{0,1},{1,0},{2,3},{3,2},{4,5},{5,4},{6,7},{7,6},{8,9},{9,8},{10,11... | collective-permute-start | bytes 786440 | tf_op jit(solution)/shard_map/ppermute | solution.py:331
  79.1 0.6 collective-permute-done.8.refs_1_.refs_3_
  79.7 3.6 %collective-permute-done.7.refs_0_.refs_1_ = bf16[128,1024]{1,0:T(8,128)(2,1)S(1)} collective-permute-done((bf16[128,1024]{1,0:T(8,128)(2,1)S(1)}, bf16[128,1024]{1,0:T(8,128)(2,1)S(1)}, u32[]{:S(2)}, u32[]{:S(2)}) %collective-permute-start.7) | collective-permute-done | bytes 262176 | tf_op jit(solution)/shard_map/ppermute | solution.py:331
  83.3 1.4 %add_sent.2 = (bf16[128,1024]{1,0:T(8,128)(2,1)S(1)}, bf16[128,1024]{1,0:T(8,128)(2,1)S(1)}) custom-call(s32[1]{0:T(128)} %bitcast.core_ref, f32[2,256,1024]{2,1,0:T(8,128)S(1)} %own_part.2.own_ref, bf16[128,1024]{1,0:T(8,128)(2,1)S(1)} %collective-permute-done.7.refs_0_.refs_1_, bf16[128,1024]{1,0:T(8,128)(2,1)S(1)} %collective-permute-done.8.refs_1_.refs_3_, ...), custom_call_target="tpu_custom_call" | custom-call | flops 536870912 | bytes 4194304 | tf_op jit(solution)/shard_map/add_sent/pallas_call | solution.py:310
  84.7 1.6 %collective-permute-start.16 = (bf16[128,1024]{1,0:T(8,128)(2,1)S(1)}, bf16[128,1024]{1,0:T(8,128)(2,1)S(1)}, u32[]{:S(2)}, u32[]{:S(2)}) collective-permute-start(bf16[128,1024]{1,0:T(8,128)(2,1)S(1)} %get-tuple-element.53), channel_id=1, source_target_pairs={{0,2},{1,3},{2,0},{3,1},{4,6},{5,7},{6,4},{7,5},{8,10},{9,11},{10,... | collective-permute-start | bytes 786440 | tf_op jit(solution)/shard_map/ppermute | solution.py:331
  86.3 0.7 collective-permute-start.18
  87.0 3.0 %own_part.3.own_ref = f32[2,256,1024]{2,1,0:T(8,128)S(1)} custom-call(s32[1]{0:T(128)} %bitcast.1.me_ref, bf16[128,1024]{1,0:T(8,128)(2,1)S(1)} %get-tuple-element.55.refs_0_, bf16[128,1024]{1,0:T(8,128)(2,1)S(1)} %get-tuple-element.56.refs_1_, bf16[1024,8192]{1,0:T(8,128)(2,1)} %refs_3_.3, bf16[1024,8192]{1,0:T(8,128)(2,1)} %refs_3_.3), custom_call_target="tpu_custom_call" | custom-call | flops 1073741824 | bytes 4194304 | tf_op jit(solution)/shard_map/own_part/pallas_call | solution.py:244
  90.0 1.9 %add_kept.1 = (f32[256,1024]{1,0:T(8,128)S(1)}, f32[256,1024]{1,0:T(8,128)S(1)}) custom-call(s32[1]{0:T(128)} %bitcast.core_ref, f32[2,256,1024]{2,1,0:T(8,128)S(1)} %own_part.3.own_ref, bf16[128,1024]{1,0:T(8,128)(2,1)S(1)} %collective-permute-done.13.refs_0_, bf16[128,1024]{1,0:T(8,128)(2,1)S(1)} %collective-permute-done.7.refs_0_.refs_1_, ...), custom_call_target="tpu_custom_call" | custom-call | flops 1073741824 | bytes 4194304 | tf_op jit(solution)/shard_map/add_kept/pallas_call | solution.py:310
  92.0 0.0 collective-permute-done.15
  92.0 0.0 collective-permute-done.17
  92.0 0.0 collective-permute-done.16
  92.0 0.7 collective-permute-done.18
  92.7 1.3 %fusion = bf16[256,2048]{1,0:T(8,128)(2,1)} fusion(f32[256,1024]{1,0:T(8,128)S(1)} %get-tuple-element.58, f32[256,1024]{1,0:T(8,128)S(1)} %get-tuple-element.57, bf16[128,1024]{1,0:T(8,128)(2,1)S(1)} %collective-permute-done.18, bf16[128,1024]{1,0:T(8,128)(2,1)S(1)} %collective-permute-done.17, bf16[128,1024]{1,0:T(8,128)(2,1)S(1)} %collective-permute-done.16, ...), kind=kLoop, calls=%fused_computation.1 | loop fusion | flops 5767168 | bytes 4194304 | tf_op jit(solution)/shard_map/convert_element_type | solution.py:375
  (6 shorter events, 0.0 us)
Async XLA Ops:
  3.2 13.0 %collective-permute-start = (bf16[6,128,128]{2,1,0:T(8,128)(2,1)}, bf16[6,128,128]{2,1,0:T(8,128)(2,1)S(1)}, u32[]{:S(2)}, u32[]{:S(2)}) collective-permute-start(bf16[6,128,128]{2,1,0:T(8,128)(2,1)} %get-tuple-element.33), channel_id=1, source_target_pairs={{0,24},{4,28},{8,16},{12,20},{16,8},{20,12},{24,0},{28,4},{1,25},{... | collective-permute-start | bytes 589832 | tf_op jit(solution)/shard_map/ppermute | solution.py:331
  8.3 22.1 %collective-permute-start.1 = (bf16[6,128,128]{2,1,0:T(8,128)(2,1)}, bf16[6,128,128]{2,1,0:T(8,128)(2,1)S(1)}, u32[]{:S(2)}, u32[]{:S(2)}) collective-permute-start(bf16[6,128,128]{2,1,0:T(8,128)(2,1)} %get-tuple-element.34), channel_id=1, source_target_pairs={{0,16},{4,20},{8,24},{12,28},{16,0},{20,4},{24,8},{28,12},{1,17},{... | collective-permute-start | bytes 589832 | tf_op jit(solution)/shard_map/ppermute | solution.py:331
  8.3 22.1 %collective-permute-start.2 = (bf16[6,128,128]{2,1,0:T(8,128)(2,1)}, bf16[6,128,128]{2,1,0:T(8,128)(2,1)S(1)}, u32[]{:S(2)}, u32[]{:S(2)}) collective-permute-start(bf16[6,128,128]{2,1,0:T(8,128)(2,1)} %get-tuple-element.35), channel_id=1, source_target_pairs={{0,8},{4,12},{8,0},{12,4},{16,24},{20,28},{24,16},{28,20},{1,9},{5... | collective-permute-start | bytes 589832 | tf_op jit(solution)/shard_map/ppermute | solution.py:331
  9.0 3.3 %copy-start.9 = (bf16[6,128,128]{2,1,0:T(8,128)(2,1)S(1)}, bf16[6,128,128]{2,1,0:T(8,128)(2,1)}, u32[]{:S(2)}) copy-start(bf16[6,128,128]{2,1,0:T(8,128)(2,1)} %get-tuple-element.43) | copy-start | bytes 589828
  9.0 21.4 %copy-start.8 = (bf16[6,128,128]{2,1,0:T(8,128)(2,1)S(1)}, bf16[6,128,128]{2,1,0:T(8,128)(2,1)}, u32[]{:S(2)}) copy-start(bf16[6,128,128]{2,1,0:T(8,128)(2,1)} %get-tuple-element.44) | copy-start | bytes 589828
  9.0 21.4 %copy-start.7 = (bf16[6,128,128]{2,1,0:T(8,128)(2,1)S(1)}, bf16[6,128,128]{2,1,0:T(8,128)(2,1)}, u32[]{:S(2)}) copy-start(bf16[6,128,128]{2,1,0:T(8,128)(2,1)} %get-tuple-element.45) | copy-start | bytes 589828
  9.0 24.3 %copy-start.6 = (bf16[6,128,128]{2,1,0:T(8,128)(2,1)S(1)}, bf16[6,128,128]{2,1,0:T(8,128)(2,1)}, u32[]{:S(2)}) copy-start(bf16[6,128,128]{2,1,0:T(8,128)(2,1)} %get-tuple-element.46) | copy-start | bytes 589828
  9.0 33.0 %copy-start.1 = (bf16[6,128,128]{2,1,0:T(8,128)(2,1)S(1)}, bf16[6,128,128]{2,1,0:T(8,128)(2,1)}, u32[]{:S(2)}) copy-start(bf16[6,128,128]{2,1,0:T(8,128)(2,1)} %get-tuple-element.40.refs_7_) | copy-start | bytes 589828
  9.0 33.0 %copy-start.2 = (bf16[1024,1024]{1,0:T(8,128)(2,1)S(1)}, bf16[1024,1024]{1,0:T(8,128)(2,1)}, u32[]{:S(2)}) copy-start(bf16[1024,1024]{1,0:T(8,128)(2,1)} %constant.32.clone.refs_9_) | copy-start | bytes 6291460
  9.1 33.0 %copy-start.3 = (bf16[1024,1024]{1,0:T(8,128)(2,1)S(1)}, bf16[1024,1024]{1,0:T(8,128)(2,1)}, u32[]{:S(2)}) copy-start(bf16[1024,1024]{1,0:T(8,128)(2,1)} %constant.31.clone.refs_8_) | copy-start | bytes 6291460
  9.1 33.0 %copy-start.4 = (f32[1024,128]{1,0:T(8,128)S(1)}, f32[1024,128]{1,0:T(8,128)}, u32[]{:S(2)}) copy-start(f32[1024,128]{1,0:T(8,128)} %constant.34.clone.refs_11_) | copy-start | bytes 1572868
  9.1 33.0 %copy-start.5 = (f32[1024,128]{1,0:T(8,128)S(1)}, f32[1024,128]{1,0:T(8,128)}, u32[]{:S(2)}) copy-start(f32[1024,128]{1,0:T(8,128)} %constant.33.clone.refs_10_) | copy-start | bytes 1572868
  12.3 21.0 %collective-permute-start.3 = (bf16[6,128,128]{2,1,0:T(8,128)(2,1)S(1)}, bf16[6,128,128]{2,1,0:T(8,128)(2,1)S(1)}, u32[]{:S(2)}, u32[]{:S(2)}) collective-permute-start(bf16[6,128,128]{2,1,0:T(8,128)(2,1)S(1)} %copy-done.9), channel_id=1, source_target_pairs={{0,28},{4,24},{8,20},{12,16},{16,12},{20,8},{24,4},{28,0},{1,29},{... | collective-permute-start | bytes 589832 | tf_op jit(solution)/shard_map/ppermute | solution.py:331
  14.7 48.5 %copy-start = (bf16[256,1024]{1,0:T(8,128)(2,1)S(1)}, bf16[256,1024]{1,0:T(8,128)(2,1)}, u32[]{:S(2)}) copy-start(bf16[256,1024]{1,0:T(8,128)(2,1)} %gate_ref.1) | copy-start | bytes 1572868
  14.7 48.8 %collective-permute-start.9 = (bf16[1024,1024]{1,0:T(8,128)(2,1)S(1)}, bf16[1024,1024]{1,0:T(8,128)(2,1)S(1)}, u32[]{:S(2)}, u32[]{:S(2)}) collective-permute-start(bf16[1024,1024]{1,0:T(8,128)(2,1)S(1)} %get-tuple-element.50), channel_id=1, source_target_pairs={{0,1},{1,0},{2,3},{3,2},{4,5},{5,4},{6,7},{7,6},{8,9},{9,8},{10,11... | collective-permute-start | bytes 6291464 | tf_op jit(solution)/shard_map/ppermute | solution.py:331
  16.2 48.2 %collective-permute-start.10 = (bf16[1024,1024]{1,0:T(8,128)(2,1)S(1)}, bf16[1024,1024]{1,0:T(8,128)(2,1)S(1)}, u32[]{:S(2)}, u32[]{:S(2)}) collective-permute-start(bf16[1024,1024]{1,0:T(8,128)(2,1)S(1)} %get-tuple-element.42), channel_id=1, source_target_pairs={{0,2},{1,3},{2,0},{3,1},{4,6},{5,7},{6,4},{7,5},{8,10},{9,11},{10,... | collective-permute-start | bytes 6291464 | tf_op jit(solution)/shard_map/ppermute | solution.py:331
  30.4 11.7 %collective-permute-start.4 = (bf16[6,128,128]{2,1,0:T(8,128)(2,1)S(1)}, bf16[6,128,128]{2,1,0:T(8,128)(2,1)S(1)}, u32[]{:S(2)}, u32[]{:S(2)}) collective-permute-start(bf16[6,128,128]{2,1,0:T(8,128)(2,1)S(1)} %copy-done.8), channel_id=1, source_target_pairs={{0,20},{4,16},{8,28},{12,24},{16,4},{20,0},{24,12},{28,8},{1,21},{... | collective-permute-start | bytes 589832 | tf_op jit(solution)/shard_map/ppermute | solution.py:331
  30.4 11.7 %collective-permute-start.5 = (bf16[6,128,128]{2,1,0:T(8,128)(2,1)S(1)}, bf16[6,128,128]{2,1,0:T(8,128)(2,1)S(1)}, u32[]{:S(2)}, u32[]{:S(2)}) collective-permute-start(bf16[6,128,128]{2,1,0:T(8,128)(2,1)S(1)} %copy-done.7), channel_id=1, source_target_pairs={{0,12},{4,8},{8,4},{12,0},{16,28},{20,24},{24,20},{28,16},{1,13},{... | collective-permute-start | bytes 589832 | tf_op jit(solution)/shard_map/ppermute | solution.py:331
  33.3 8.7 %collective-permute-start.6 = (bf16[6,128,128]{2,1,0:T(8,128)(2,1)S(1)}, bf16[6,128,128]{2,1,0:T(8,128)(2,1)S(1)}, u32[]{:S(2)}, u32[]{:S(2)}) collective-permute-start(bf16[6,128,128]{2,1,0:T(8,128)(2,1)S(1)} %copy-done.6), channel_id=1, source_target_pairs={{0,4},{4,0},{8,12},{12,8},{16,20},{20,16},{24,28},{28,24},{1,5},{5... | collective-permute-start | bytes 589832 | tf_op jit(solution)/shard_map/ppermute | solution.py:331
  64.4 10.1 %collective-permute-start.11 = (bf16[1024,1024]{1,0:T(8,128)(2,1)S(1)}, bf16[1024,1024]{1,0:T(8,128)(2,1)S(1)}, u32[]{:S(2)}, u32[]{:S(2)}) collective-permute-start(bf16[1024,1024]{1,0:T(8,128)(2,1)S(1)} %collective-permute-done.9.refs_2_.refs_4_), channel_id=1, source_target_pairs={{0,4},{4,0},{8,12},{12,8},{16,20},{20,16},{24,28},{28,24},{1,5},{5... | collective-permute-start | bytes 6291464 | tf_op jit(solution)/shard_map/ppermute | solution.py:331
  64.6 9.9 %collective-permute-start.12 = (bf16[1024,1024]{1,0:T(8,128)(2,1)S(1)}, bf16[1024,1024]{1,0:T(8,128)(2,1)S(1)}, u32[]{:S(2)}, u32[]{:S(2)}) collective-permute-start(bf16[1024,1024]{1,0:T(8,128)(2,1)S(1)} %collective-permute-done.10.refs_4_.refs_6_), channel_id=1, source_target_pairs={{0,4},{4,0},{8,12},{12,8},{16,20},{20,16},{24,28},{28,24},{1,5},{5... | collective-permute-start | bytes 6291464 | tf_op jit(solution)/shard_map/ppermute | solution.py:331
  64.9 9.2 %collective-permute-start.14 = (bf16[128,1024]{1,0:T(8,128)(2,1)S(1)}, bf16[128,1024]{1,0:T(8,128)(2,1)S(1)}, u32[]{:S(2)}, u32[]{:S(2)}) collective-permute-start(bf16[128,1024]{1,0:T(8,128)(2,1)S(1)} %get-tuple-element.55.refs_0_), channel_id=1, source_target_pairs={{0,2},{1,3},{2,0},{3,1},{4,6},{5,7},{6,4},{7,5},{8,10},{9,11},{10,... | collective-permute-start | bytes 786440 | tf_op jit(solution)/shard_map/ppermute | solution.py:331
  66.4 8.0 %collective-permute-start.13 = (bf16[128,1024]{1,0:T(8,128)(2,1)S(1)}, bf16[128,1024]{1,0:T(8,128)(2,1)S(1)}, u32[]{:S(2)}, u32[]{:S(2)}) collective-permute-start(bf16[128,1024]{1,0:T(8,128)(2,1)S(1)} %get-tuple-element.55.refs_0_), channel_id=1, source_target_pairs={{0,1},{1,0},{2,3},{3,2},{4,5},{5,4},{6,7},{7,6},{8,9},{9,8},{10,11... | collective-permute-start | bytes 786440 | tf_op jit(solution)/shard_map/ppermute | solution.py:331
  70.2 9.5 %collective-permute-start.8 = (bf16[128,1024]{1,0:T(8,128)(2,1)S(1)}, bf16[128,1024]{1,0:T(8,128)(2,1)S(1)}, u32[]{:S(2)}, u32[]{:S(2)}) collective-permute-start(bf16[128,1024]{1,0:T(8,128)(2,1)S(1)} %get-tuple-element.56.refs_1_), channel_id=1, source_target_pairs={{0,2},{1,3},{2,0},{3,1},{4,6},{5,7},{6,4},{7,5},{8,10},{9,11},{10,... | collective-permute-start | bytes 786440 | tf_op jit(solution)/shard_map/ppermute | solution.py:331
  74.1 9.2 %collective-permute-start.7 = (bf16[128,1024]{1,0:T(8,128)(2,1)S(1)}, bf16[128,1024]{1,0:T(8,128)(2,1)S(1)}, u32[]{:S(2)}, u32[]{:S(2)}) collective-permute-start(bf16[128,1024]{1,0:T(8,128)(2,1)S(1)} %get-tuple-element.56.refs_1_), channel_id=1, source_target_pairs={{0,1},{1,0},{2,3},{3,2},{4,5},{5,4},{6,7},{7,6},{8,9},{9,8},{10,11... | collective-permute-start | bytes 786440 | tf_op jit(solution)/shard_map/ppermute | solution.py:331
  75.9 16.1 %collective-permute-start.15 = (bf16[128,1024]{1,0:T(8,128)(2,1)S(1)}, bf16[128,1024]{1,0:T(8,128)(2,1)S(1)}, u32[]{:S(2)}, u32[]{:S(2)}) collective-permute-start(bf16[128,1024]{1,0:T(8,128)(2,1)S(1)} %get-tuple-element.59), channel_id=1, source_target_pairs={{0,2},{1,3},{2,0},{3,1},{4,6},{5,7},{6,4},{7,5},{8,10},{9,11},{10,... | collective-permute-start | bytes 786440 | tf_op jit(solution)/shard_map/ppermute | solution.py:331
  77.8 14.2 %collective-permute-start.17 = (bf16[128,1024]{1,0:T(8,128)(2,1)S(1)}, bf16[128,1024]{1,0:T(8,128)(2,1)S(1)}, u32[]{:S(2)}, u32[]{:S(2)}) collective-permute-start(bf16[128,1024]{1,0:T(8,128)(2,1)S(1)} %get-tuple-element.60), channel_id=1, source_target_pairs={{0,1},{1,0},{2,3},{3,2},{4,5},{5,4},{6,7},{7,6},{8,9},{9,8},{10,11... | collective-permute-start | bytes 786440 | tf_op jit(solution)/shard_map/ppermute | solution.py:331
  84.7 7.3 %collective-permute-start.16 = (bf16[128,1024]{1,0:T(8,128)(2,1)S(1)}, bf16[128,1024]{1,0:T(8,128)(2,1)S(1)}, u32[]{:S(2)}, u32[]{:S(2)}) collective-permute-start(bf16[128,1024]{1,0:T(8,128)(2,1)S(1)} %get-tuple-element.53), channel_id=1, source_target_pairs={{0,2},{1,3},{2,0},{3,1},{4,6},{5,7},{6,4},{7,5},{8,10},{9,11},{10,... | collective-permute-start | bytes 786440 | tf_op jit(solution)/shard_map/ppermute | solution.py:331
  86.3 6.4 %collective-permute-start.18 = (bf16[128,1024]{1,0:T(8,128)(2,1)S(1)}, bf16[128,1024]{1,0:T(8,128)(2,1)S(1)}, u32[]{:S(2)}, u32[]{:S(2)}) collective-permute-start(bf16[128,1024]{1,0:T(8,128)(2,1)S(1)} %get-tuple-element.54), channel_id=1, source_target_pairs={{0,1},{1,0},{2,3},{3,2},{4,5},{5,4},{6,7},{7,6},{8,9},{9,8},{10,11... | collective-permute-start | bytes 786440 | tf_op jit(solution)/shard_map/ppermute | solution.py:331

commit v4 on v3

--- a/solution.py
+++ b/solution.py
@@ -185,7 +185,7 @@
         out_shape=[jax.ShapeDtypeStruct((shares, 2, rows // parts, LANES), jnp.bfloat16)] * parts,
         scratch_shapes=[columns, pltpu.VMEM((4, block, LANES), jnp.bfloat16), columns, columns],
         compiler_params=pltpu.CompilerParams(vmem_limit_bytes=24 << 20),
-        cost_estimate=pl.CostEstimate(flops=64 * block * block * LANES, bytes_accessed=8 * block * block, transcendentals=0),
+        cost_estimate=pl.CostEstimate(flops=50 * block * block * LANES, bytes_accessed=8 * block * block, transcendentals=0),
         name="convolve",
     )(
         me, *data, rounded(np.cos(angle)), rounded(np.sin(angle)),
@@ -343,9 +343,9 @@
     places = jnp.stack([(me ^ (1 + 2 * core)) * 2, (me ^ (2 + core)) * 2 + 1])
     _, places = lax.optimization_barrier((packed, places))
     block_x, block_y = take_blocks(places, out_weight)
+    late = [m for m in order if m % 2]
+    held, block_x, block_y = lax.optimization_barrier(([packed[m] for m in late], block_x, block_y))
     weight_x, weight_y = swap(block_x, "chan", 1), swap(block_y, "chan", 2)
-    late = [m for m in order if m % 2]
-    held, _ = lax.optimization_barrier(([packed[m] for m in late], block_y))
     for m, mine in zip(late, held):
         packed[m] = mine
     data = [swap(packed[m], "seq", m) if m else packed[m] for m in order]

time: 95.1 us -> 93.5 us (0.983); the launches traced: 93.9 us -> 93.3 us
  waiting for transfers between devices: 30.9 us -> 26.2 us
  starting transfers between devices: 22.8 us -> 26.9 us
    ppermute x19, waiting for transfers between devices: 30.9 us -> 26.2 us  [swap(): lax.ppermute(data, axis, [(i, i ^ flip) for i in range(lax.axis_size(axis...]
    ppermute x19, starting transfers between devices: 22.8 us -> 26.9 us  [swap(): lax.ppermute(data, axis, [(i, i ^ flip) for i in range(lax.axis_size(axis...]
  transfers between devices with their start and end apart: 19 -> 19, of which waited for: 8 -> 5; matrix products, arithmetic and copies ran while one was open for 0% -> 0% of each run, Pallas kernels for 18% -> 18%
where the time goes in v4:
time: 93.5 us; the launch traced here: 93.3 us
  starting transfers between devices  26.9 us (29%)
  waiting for transfers between devices  26.2 us (28%)
  Pallas kernels  20.2 us (22%)
  blocking collectives  18.3 us (20%)
  other arithmetic  1.35 us (1%)
    ppermute x19, starting transfers between devices, swap(): lax.ppermute(data, axis, [(i, i ^ flip) for i in range(lax.axis_size(axis...  26.9 us
    ppermute x19, waiting for transfers between devices, swap(): lax.ppermute(data, axis, [(i, i ^ flip) for i in range(lax.axis_size(axis...  26.2 us
    all_to_all x1, blocking collectives, by_channels(): conv = lax.all_to_all(conv, 'seq', split_axis=0, concat_axis=0, tiled=True)  18.3 us
    pallas_call x2, Pallas kernels, own_part(): pl.pallas_call(own_kernel, grid_spec=pltpu.PrefetchScalarGridSpec(num_sca...  6.09 us
    pallas_call x3, Pallas kernels, add_moved(): pl.pallas_call(functools.partial(add_kernel, parts, kept), grid=(1,), in_...  4.66 us
    pallas_call x1, Pallas kernels, take_blocks(): pl.pallas_call(take_kernel, in_specs=[pl.BlockSpec(memory_space=pltpu.SME...  3.19 us
    pallas_call x1, Pallas kernels, pack(): pl.pallas_call(functools.partial(pack_kernel, span), in_specs=[pl.BlockSp...  3.18 us
    pallas_call x1, Pallas kernels, convolve(): pl.pallas_call(functools.partial(conv_kernel, parts, order), in_specs=[pl...  2.71 us
  transfers between devices with their start and end apart: 19, of which 5 were waited for; matrix products, arithmetic and copies ran while one was open for 0% of the time, Pallas kernels for 18%

profile of v4, /device:TPU:0, one launch (start us, length us, event | category | flops | bytes accessed | tf_op | source)
XLA Modules:
  0.0 93.3 jit_solution(3193674767916835553)
XLA Ops:
  0.0 3.2 %pack.1 = (bf16[6,128,128]{2,1,0:T(8,128)(2,1)}, bf16[6,128,128]{2,1,0:T(8,128)(2,1)}, bf16[6,128,128]{2,1,0:T(8,128)(2,1)}, bf16[6,128,128]{2,1,0:T(8,128)(2,1)...) custom-call(s32[1]{0:T(128)} %bitcast.2.me_ref, ...), custom_call_target="tpu_custom_call" | custom-call | tf_op jit(solution)/shard_map/pack/pallas_call | solution.py:79
  3.2 5.1 %collective-permute-start = (bf16[6,128,128]{2,1,0:T(8,128)(2,1)}, bf16[6,128,128]{2,1,0:T(8,128)(2,1)S(1)}, u32[]{:S(2)}, u32[]{:S(2)}) collective-permute-start(bf16[6,128,128]{2,1,0:T(8,128)(2,1)} %get-tuple-element.35), channel_id=1, source_target_pairs={{0,24},{4,28},{8,16},{12,20},{16,8},{20,12},{24,0},{28,4},{1,25},{... | collective-permute-start | bytes 589832 | tf_op jit(solution)/shard_map/ppermute | solution.py:331
  8.3 0.1 pad_add_fusion.places_ref
  8.4 0.0 copy-start.7
  8.4 0.0 copy-start.6
  8.4 0.0 copy-start.1
  8.4 0.0 copy-start.2
  8.4 0.0 copy-start.3
  8.5 0.0 copy-start.4
  8.5 0.0 copy-start.5
  8.5 3.2 %take_blocks.1 = (bf16[1024,1024]{1,0:T(8,128)(2,1)S(1)}, bf16[1024,1024]{1,0:T(8,128)(2,1)S(1)}) custom-call(s32[2]{0:T(128)S(1)} %pad_add_fusion.places_ref, bf16[1024,8192]{1,0:T(8,128)(2,1)} %refs_3_.3), custom_call_target="tpu_custom_call" | custom-call | bytes 134217728 | tf_op jit(solution)/shard_map/take_blocks/pallas_call | solution.py:117
  11.7 0.0 copy-start
  11.7 1.6 %collective-permute-start.9 = (bf16[1024,1024]{1,0:T(8,128)(2,1)S(1)}, bf16[1024,1024]{1,0:T(8,128)(2,1)S(1)}, u32[]{:S(2)}, u32[]{:S(2)}) collective-permute-start(bf16[1024,1024]{1,0:T(8,128)(2,1)S(1)} %get-tuple-element.53), channel_id=1, source_target_pairs={{0,1},{1,0},{2,3},{3,2},{4,5},{5,4},{6,7},{7,6},{8,9},{9,8},{10,11... | collective-permute-start | bytes 6291464 | tf_op jit(solution)/shard_map/ppermute | solution.py:331
  13.2 1.5 %collective-permute-start.10 = (bf16[1024,1024]{1,0:T(8,128)(2,1)S(1)}, bf16[1024,1024]{1,0:T(8,128)(2,1)S(1)}, u32[]{:S(2)}, u32[]{:S(2)}) collective-permute-start(bf16[1024,1024]{1,0:T(8,128)(2,1)S(1)} %get-tuple-element.54), channel_id=1, source_target_pairs={{0,2},{1,3},{2,0},{3,1},{4,6},{5,7},{6,4},{7,5},{8,10},{9,11},{10,... | collective-permute-start | bytes 6291464 | tf_op jit(solution)/shard_map/ppermute | solution.py:331
  14.8 0.0 copy-done.11
  14.8 0.0 collective-permute-start.1
  14.8 0.0 copy-done.10
  14.8 0.8 collective-permute-start.2
  15.5 0.0 collective-permute-done.refs_0_
  15.6 0.0 copy-done.9
  15.6 1.6 %collective-permute-start.3 = (bf16[6,128,128]{2,1,0:T(8,128)(2,1)S(1)}, bf16[6,128,128]{2,1,0:T(8,128)(2,1)S(1)}, u32[]{:S(2)}, u32[]{:S(2)}) collective-permute-start(bf16[6,128,128]{2,1,0:T(8,128)(2,1)S(1)} %copy-done.9), channel_id=1, source_target_pairs={{0,28},{4,24},{8,20},{12,16},{16,12},{20,8},{24,4},{28,0},{1,29},{... | collective-permute-start | bytes 589832 | tf_op jit(solution)/shard_map/ppermute | solution.py:331
  17.2 12.6 %collective-permute-done.1.refs_1_ = bf16[6,128,128]{2,1,0:T(8,128)(2,1)S(1)} collective-permute-done((bf16[6,128,128]{2,1,0:T(8,128)(2,1)S(1)}, bf16[6,128,128]{2,1,0:T(8,128)(2,1)S(1)}, u32[]{:S(2)}, u32[]{:S(2)}) %collective-permute-start.1) | collective-permute-done | bytes 196640 | tf_op jit(solution)/shard_map/ppermute | solution.py:331
  29.8 0.0 copy-done.8
  29.8 0.0 collective-permute-start.4
  29.8 0.0 collective-permute-done.2.refs_2_
  29.8 3.5 %collective-permute-start.5 = (bf16[6,128,128]{2,1,0:T(8,128)(2,1)S(1)}, bf16[6,128,128]{2,1,0:T(8,128)(2,1)S(1)}, u32[]{:S(2)}, u32[]{:S(2)}) collective-permute-start(bf16[6,128,128]{2,1,0:T(8,128)(2,1)S(1)} %copy-done.7), channel_id=1, source_target_pairs={{0,12},{4,8},{8,4},{12,0},{16,28},{20,24},{24,20},{28,16},{1,13},{... | collective-permute-start | bytes 589832 | tf_op jit(solution)/shard_map/ppermute | solution.py:331
  33.3 0.0 collective-permute-done.3.refs_3_
  33.3 0.0 copy-done.6
  33.3 0.0 collective-permute-start.6
  33.3 8.7 %collective-permute-done.4.refs_4_ = bf16[6,128,128]{2,1,0:T(8,128)(2,1)S(1)} collective-permute-done((bf16[6,128,128]{2,1,0:T(8,128)(2,1)S(1)}, bf16[6,128,128]{2,1,0:T(8,128)(2,1)S(1)}, u32[]{:S(2)}, u32[]{:S(2)}) %collective-permute-start.4) | collective-permute-done | bytes 196640 | tf_op jit(solution)/shard_map/ppermute | solution.py:331
  42.1 0.0 collective-permute-done.5.refs_5_
  42.1 0.0 collective-permute-done.6.refs_6_
  42.1 2.7 %convolve.1 = bf16[8,2,128,128]{3,2,1,0:T(8,128)(2,1)S(1)} custom-call(s32[1]{0:T(128)} %bitcast.2.me_ref, bf16[6,128,128]{2,1,0:T(8,128)(2,1)S(1)} %collective-permute-done.refs_0_, bf16[6,128,128]{2,1,0:T(8,128)(2,1)S(1)} %collective-permute-done.1.refs_1_, bf16[6,128,128]{2,1,0:T(8,128)(2,1)S(1)} %collective-permute-done.2.refs_2_, ...), custom_call_target="tpu_custom_call" | custom-call | flops 6710886400 | bytes 8388608 | tf_op jit(solution)/shard_map/convolve/pallas_call | solution.py:181
  44.8 18.3 %all_to_all.5.conv_ref = bf16[8,2,128,128]{3,2,1,0:T(8,128)(2,1)S(1)} all-to-all(bf16[8,2,128,128]{3,2,1,0:T(8,128)(2,1)S(1)} %convolve.1), channel_id=1, replica_groups=mesh['seq'=8,'chan'=4] {'seq'}, dimensions={0} | all-to-all | bytes 1048576 | tf_op jit(solution)/shard_map/all_to_all | solution.py:353
  63.2 0.0 copy-done
  63.2 0.4 gate.1
  63.5 0.0 collective-permute-done.9.refs_2_.refs_4_
  63.5 0.0 collective-permute-done.10.refs_4_.refs_6_
  63.6 0.1 collective-permute-start.11
  63.6 0.5 collective-permute-start.12
  64.1 1.5 %collective-permute-start.14 = (bf16[128,1024]{1,0:T(8,128)(2,1)S(1)}, bf16[128,1024]{1,0:T(8,128)(2,1)S(1)}, u32[]{:S(2)}, u32[]{:S(2)}) collective-permute-start(bf16[128,1024]{1,0:T(8,128)(2,1)S(1)} %get-tuple-element.59.refs_0_), channel_id=1, source_target_pairs={{0,2},{1,3},{2,0},{3,1},{4,6},{5,7},{6,4},{7,5},{8,10},{9,11},{10,... | collective-permute-start | bytes 786440 | tf_op jit(solution)/shard_map/ppermute | solution.py:331
  65.7 1.5 %collective-permute-start.13 = (bf16[128,1024]{1,0:T(8,128)(2,1)S(1)}, bf16[128,1024]{1,0:T(8,128)(2,1)S(1)}, u32[]{:S(2)}, u32[]{:S(2)}) collective-permute-start(bf16[128,1024]{1,0:T(8,128)(2,1)S(1)} %get-tuple-element.59.refs_0_), channel_id=1, source_target_pairs={{0,1},{1,0},{2,3},{3,2},{4,5},{5,4},{6,7},{7,6},{8,9},{9,8},{10,11... | collective-permute-start | bytes 786440 | tf_op jit(solution)/shard_map/ppermute | solution.py:331
  67.2 3.0 %own_part.2.own_ref = f32[2,256,1024]{2,1,0:T(8,128)S(1)} custom-call(s32[1]{0:T(128)} %bitcast.1.me_ref, bf16[128,1024]{1,0:T(8,128)(2,1)S(1)} %get-tuple-element.59.refs_0_, bf16[128,1024]{1,0:T(8,128)(2,1)S(1)} %get-tuple-element.60.refs_1_, bf16[1024,8192]{1,0:T(8,128)(2,1)} %refs_3_.3, bf16[1024,8192]{1,0:T(8,128)(2,1)} %refs_3_.3), custom_call_target="tpu_custom_call" | custom-call | flops 1073741824 | bytes 4194304 | tf_op jit(solution)/shard_map/own_part/pallas_call | solution.py:244
  70.2 0.6 collective-permute-start.8
  70.8 1.6 %collective-permute-done.14.refs_2_.refs_1_ = bf16[128,1024]{1,0:T(8,128)(2,1)S(1)} collective-permute-done((bf16[128,1024]{1,0:T(8,128)(2,1)S(1)}, bf16[128,1024]{1,0:T(8,128)(2,1)S(1)}, u32[]{:S(2)}, u32[]{:S(2)}) %collective-permute-start.14) | collective-permute-done | bytes 262176 | tf_op jit(solution)/shard_map/ppermute | solution.py:331
  72.4 2.4 %collective-permute-start.7 = (bf16[128,1024]{1,0:T(8,128)(2,1)S(1)}, bf16[128,1024]{1,0:T(8,128)(2,1)S(1)}, u32[]{:S(2)}, u32[]{:S(2)}) collective-permute-start(bf16[128,1024]{1,0:T(8,128)(2,1)S(1)} %get-tuple-element.60.refs_1_), channel_id=1, source_target_pairs={{0,1},{1,0},{2,3},{3,2},{4,5},{5,4},{6,7},{7,6},{8,9},{9,8},{10,11... | collective-permute-start | bytes 786440 | tf_op jit(solution)/shard_map/ppermute | solution.py:331
  74.8 0.0 collective-permute-done.13.refs_0_
  74.8 0.0 collective-permute-done.11.refs_3_.refs_5_
  74.8 0.0 collective-permute-done.12.refs_5_.refs_7_
  74.8 1.4 %add_sent.3 = (bf16[128,1024]{1,0:T(8,128)(2,1)S(1)}, bf16[128,1024]{1,0:T(8,128)(2,1)S(1)}) custom-call(s32[1]{0:T(128)} %bitcast.core_ref, f32[2,256,1024]{2,1,0:T(8,128)S(1)} %own_part.2.own_ref, bf16[128,1024]{1,0:T(8,128)(2,1)S(1)} %collective-permute-done.13.refs_0_, bf16[128,1024]{1,0:T(8,128)(2,1)S(1)} %collective-permute-done.14.refs_2_.refs_1_, ...), custom_call_target="tpu_custom_call" | custom-call | flops 536870912 | bytes 4194304 | tf_op jit(solution)/shard_map/add_sent/pallas_call | solution.py:310
  76.2 1.6 %collective-permute-start.15 = (bf16[128,1024]{1,0:T(8,128)(2,1)S(1)}, bf16[128,1024]{1,0:T(8,128)(2,1)S(1)}, u32[]{:S(2)}, u32[]{:S(2)}) collective-permute-start(bf16[128,1024]{1,0:T(8,128)(2,1)S(1)} %get-tuple-element.63), channel_id=1, source_target_pairs={{0,2},{1,3},{2,0},{3,1},{4,6},{5,7},{6,4},{7,5},{8,10},{9,11},{10,... | collective-permute-start | bytes 786440 | tf_op jit(solution)/shard_map/ppermute | solution.py:331
  77.8 0.5 collective-permute-start.17
  78.3 0.8 collective-permute-done.8.refs_1_.refs_3_
  79.1 2.5 %collective-permute-done.7.refs_0_.refs_1_ = bf16[128,1024]{1,0:T(8,128)(2,1)S(1)} collective-permute-done((bf16[128,1024]{1,0:T(8,128)(2,1)S(1)}, bf16[128,1024]{1,0:T(8,128)(2,1)S(1)}, u32[]{:S(2)}, u32[]{:S(2)}) %collective-permute-start.7) | collective-permute-done | bytes 262176 | tf_op jit(solution)/shard_map/ppermute | solution.py:331
  81.5 1.4 %add_sent.2 = (bf16[128,1024]{1,0:T(8,128)(2,1)S(1)}, bf16[128,1024]{1,0:T(8,128)(2,1)S(1)}) custom-call(s32[1]{0:T(128)} %bitcast.core_ref, f32[2,256,1024]{2,1,0:T(8,128)S(1)} %own_part.2.own_ref, bf16[128,1024]{1,0:T(8,128)(2,1)S(1)} %collective-permute-done.7.refs_0_.refs_1_, bf16[128,1024]{1,0:T(8,128)(2,1)S(1)} %collective-permute-done.8.refs_1_.refs_3_, ...), custom_call_target="tpu_custom_call" | custom-call | flops 536870912 | bytes 4194304 | tf_op jit(solution)/shard_map/add_sent/pallas_call | solution.py:310
  82.9 2.6 %collective-permute-start.16 = (bf16[128,1024]{1,0:T(8,128)(2,1)S(1)}, bf16[128,1024]{1,0:T(8,128)(2,1)S(1)}, u32[]{:S(2)}, u32[]{:S(2)}) collective-permute-start(bf16[128,1024]{1,0:T(8,128)(2,1)S(1)} %get-tuple-element.57), channel_id=1, source_target_pairs={{0,2},{1,3},{2,0},{3,1},{4,6},{5,7},{6,4},{7,5},{8,10},{9,11},{10,... | collective-permute-start | bytes 786440 | tf_op jit(solution)/shard_map/ppermute | solution.py:331
  85.5 1.5 %collective-permute-start.18 = (bf16[128,1024]{1,0:T(8,128)(2,1)S(1)}, bf16[128,1024]{1,0:T(8,128)(2,1)S(1)}, u32[]{:S(2)}, u32[]{:S(2)}) collective-permute-start(bf16[128,1024]{1,0:T(8,128)(2,1)S(1)} %get-tuple-element.58), channel_id=1, source_target_pairs={{0,1},{1,0},{2,3},{3,2},{4,5},{5,4},{6,7},{7,6},{8,9},{9,8},{10,11... | collective-permute-start | bytes 786440 | tf_op jit(solution)/shard_map/ppermute | solution.py:331
  87.0 3.0 %own_part.3.own_ref = f32[2,256,1024]{2,1,0:T(8,128)S(1)} custom-call(s32[1]{0:T(128)} %bitcast.1.me_ref, bf16[128,1024]{1,0:T(8,128)(2,1)S(1)} %get-tuple-element.59.refs_0_, bf16[128,1024]{1,0:T(8,128)(2,1)S(1)} %get-tuple-element.60.refs_1_, bf16[1024,8192]{1,0:T(8,128)(2,1)} %refs_3_.3, bf16[1024,8192]{1,0:T(8,128)(2,1)} %refs_3_.3), custom_call_target="tpu_custom_call" | custom-call | flops 1073741824 | bytes 4194304 | tf_op jit(solution)/shard_map/own_part/pallas_call | solution.py:244
  90.1 1.9 %add_kept.1 = (f32[256,1024]{1,0:T(8,128)S(1)}, f32[256,1024]{1,0:T(8,128)S(1)}) custom-call(s32[1]{0:T(128)} %bitcast.core_ref, f32[2,256,1024]{2,1,0:T(8,128)S(1)} %own_part.3.own_ref, bf16[128,1024]{1,0:T(8,128)(2,1)S(1)} %collective-permute-done.13.refs_0_, bf16[128,1024]{1,0:T(8,128)(2,1)S(1)} %collective-permute-done.7.refs_0_.refs_1_, ...), custom_call_target="tpu_custom_call" | custom-call | flops 1073741824 | bytes 4194304 | tf_op jit(solution)/shard_map/add_kept/pallas_call | solution.py:310
  92.0 0.0 collective-permute-done.15
  92.0 0.0 collective-permute-done.17
  92.0 0.0 collective-permute-done.16
  92.0 0.0 collective-permute-done.18
  92.0 1.3 %fusion = bf16[256,2048]{1,0:T(8,128)(2,1)} fusion(f32[256,1024]{1,0:T(8,128)S(1)} %get-tuple-element.62, f32[256,1024]{1,0:T(8,128)S(1)} %get-tuple-element.61, bf16[128,1024]{1,0:T(8,128)(2,1)S(1)} %collective-permute-done.18, bf16[128,1024]{1,0:T(8,128)(2,1)S(1)} %collective-permute-done.17, bf16[128,1024]{1,0:T(8,128)(2,1)S(1)} %collective-permute-done.16, ...), kind=kLoop, calls=%fused_computation.1 | loop fusion | flops 5767168 | bytes 4194304 | tf_op jit(solution)/shard_map/convert_element_type | solution.py:375
  (10 shorter events, 0.0 us)
Async XLA Ops:
  3.2 12.4 %collective-permute-start = (bf16[6,128,128]{2,1,0:T(8,128)(2,1)}, bf16[6,128,128]{2,1,0:T(8,128)(2,1)S(1)}, u32[]{:S(2)}, u32[]{:S(2)}) collective-permute-start(bf16[6,128,128]{2,1,0:T(8,128)(2,1)} %get-tuple-element.35), channel_id=1, source_target_pairs={{0,24},{4,28},{8,16},{12,20},{16,8},{20,12},{24,0},{28,4},{1,25},{... | collective-permute-start | bytes 589832 | tf_op jit(solution)/shard_map/ppermute | solution.py:331
  8.4 6.4 %copy-start.11 = (bf16[6,128,128]{2,1,0:T(8,128)(2,1)S(1)}, bf16[6,128,128]{2,1,0:T(8,128)(2,1)}, u32[]{:S(2)}) copy-start(bf16[6,128,128]{2,1,0:T(8,128)(2,1)} %get-tuple-element.36) | copy-start | bytes 589828
  8.4 6.4 %copy-start.10 = (bf16[6,128,128]{2,1,0:T(8,128)(2,1)S(1)}, bf16[6,128,128]{2,1,0:T(8,128)(2,1)}, u32[]{:S(2)}) copy-start(bf16[6,128,128]{2,1,0:T(8,128)(2,1)} %get-tuple-element.37) | copy-start | bytes 589828
  8.4 7.2 %copy-start.9 = (bf16[6,128,128]{2,1,0:T(8,128)(2,1)S(1)}, bf16[6,128,128]{2,1,0:T(8,128)(2,1)}, u32[]{:S(2)}) copy-start(bf16[6,128,128]{2,1,0:T(8,128)(2,1)} %get-tuple-element.46) | copy-start | bytes 589828
  8.4 21.4 %copy-start.8 = (bf16[6,128,128]{2,1,0:T(8,128)(2,1)S(1)}, bf16[6,128,128]{2,1,0:T(8,128)(2,1)}, u32[]{:S(2)}) copy-start(bf16[6,128,128]{2,1,0:T(8,128)(2,1)} %get-tuple-element.47) | copy-start | bytes 589828
  8.4 21.4 %copy-start.7 = (bf16[6,128,128]{2,1,0:T(8,128)(2,1)S(1)}, bf16[6,128,128]{2,1,0:T(8,128)(2,1)}, u32[]{:S(2)}) copy-start(bf16[6,128,128]{2,1,0:T(8,128)(2,1)} %get-tuple-element.48) | copy-start | bytes 589828
  8.4 24.9 %copy-start.6 = (bf16[6,128,128]{2,1,0:T(8,128)(2,1)S(1)}, bf16[6,128,128]{2,1,0:T(8,128)(2,1)}, u32[]{:S(2)}) copy-start(bf16[6,128,128]{2,1,0:T(8,128)(2,1)} %get-tuple-element.49) | copy-start | bytes 589828
  8.4 33.7 %copy-start.1 = (bf16[6,128,128]{2,1,0:T(8,128)(2,1)S(1)}, bf16[6,128,128]{2,1,0:T(8,128)(2,1)}, u32[]{:S(2)}) copy-start(bf16[6,128,128]{2,1,0:T(8,128)(2,1)} %get-tuple-element.42.refs_7_) | copy-start | bytes 589828
  8.4 33.7 %copy-start.2 = (bf16[1024,1024]{1,0:T(8,128)(2,1)S(1)}, bf16[1024,1024]{1,0:T(8,128)(2,1)}, u32[]{:S(2)}) copy-start(bf16[1024,1024]{1,0:T(8,128)(2,1)} %constant.32.clone.refs_9_) | copy-start | bytes 6291460
  8.4 33.6 %copy-start.3 = (bf16[1024,1024]{1,0:T(8,128)(2,1)S(1)}, bf16[1024,1024]{1,0:T(8,128)(2,1)}, u32[]{:S(2)}) copy-start(bf16[1024,1024]{1,0:T(8,128)(2,1)} %constant.31.clone.refs_8_) | copy-start | bytes 6291460
  8.5 33.6 %copy-start.4 = (f32[1024,128]{1,0:T(8,128)S(1)}, f32[1024,128]{1,0:T(8,128)}, u32[]{:S(2)}) copy-start(f32[1024,128]{1,0:T(8,128)} %constant.34.clone.refs_11_) | copy-start | bytes 1572868
  8.5 33.6 %copy-start.5 = (f32[1024,128]{1,0:T(8,128)S(1)}, f32[1024,128]{1,0:T(8,128)}, u32[]{:S(2)}) copy-start(f32[1024,128]{1,0:T(8,128)} %constant.33.clone.refs_10_) | copy-start | bytes 1572868
  11.7 51.5 %copy-start = (bf16[256,1024]{1,0:T(8,128)(2,1)S(1)}, bf16[256,1024]{1,0:T(8,128)(2,1)}, u32[]{:S(2)}) copy-start(bf16[256,1024]{1,0:T(8,128)(2,1)} %gate_ref.1) | copy-start | bytes 1572868
  11.7 51.9 %collective-permute-start.9 = (bf16[1024,1024]{1,0:T(8,128)(2,1)S(1)}, bf16[1024,1024]{1,0:T(8,128)(2,1)S(1)}, u32[]{:S(2)}, u32[]{:S(2)}) collective-permute-start(bf16[1024,1024]{1,0:T(8,128)(2,1)S(1)} %get-tuple-element.53), channel_id=1, source_target_pairs={{0,1},{1,0},{2,3},{3,2},{4,5},{5,4},{6,7},{7,6},{8,9},{9,8},{10,11... | collective-permute-start | bytes 6291464 | tf_op jit(solution)/shard_map/ppermute | solution.py:331
  13.2 50.3 %collective-permute-start.10 = (bf16[1024,1024]{1,0:T(8,128)(2,1)S(1)}, bf16[1024,1024]{1,0:T(8,128)(2,1)S(1)}, u32[]{:S(2)}, u32[]{:S(2)}) collective-permute-start(bf16[1024,1024]{1,0:T(8,128)(2,1)S(1)} %get-tuple-element.54), channel_id=1, source_target_pairs={{0,2},{1,3},{2,0},{3,1},{4,6},{5,7},{6,4},{7,5},{8,10},{9,11},{10,... | collective-permute-start | bytes 6291464 | tf_op jit(solution)/shard_map/ppermute | solution.py:331
  14.8 15.0 %collective-permute-start.1 = (bf16[6,128,128]{2,1,0:T(8,128)(2,1)S(1)}, bf16[6,128,128]{2,1,0:T(8,128)(2,1)S(1)}, u32[]{:S(2)}, u32[]{:S(2)}) collective-permute-start(bf16[6,128,128]{2,1,0:T(8,128)(2,1)S(1)} %copy-done.11), channel_id=1, source_target_pairs={{0,16},{4,20},{8,24},{12,28},{16,0},{20,4},{24,8},{28,12},{1,17},{... | collective-permute-start | bytes 589832 | tf_op jit(solution)/shard_map/ppermute | solution.py:331
  14.8 15.0 %collective-permute-start.2 = (bf16[6,128,128]{2,1,0:T(8,128)(2,1)S(1)}, bf16[6,128,128]{2,1,0:T(8,128)(2,1)S(1)}, u32[]{:S(2)}, u32[]{:S(2)}) collective-permute-start(bf16[6,128,128]{2,1,0:T(8,128)(2,1)S(1)} %copy-done.10), channel_id=1, source_target_pairs={{0,8},{4,12},{8,0},{12,4},{16,24},{20,28},{24,16},{28,20},{1,9},{5... | collective-permute-start | bytes 589832 | tf_op jit(solution)/shard_map/ppermute | solution.py:331
  15.6 17.8 %collective-permute-start.3 = (bf16[6,128,128]{2,1,0:T(8,128)(2,1)S(1)}, bf16[6,128,128]{2,1,0:T(8,128)(2,1)S(1)}, u32[]{:S(2)}, u32[]{:S(2)}) collective-permute-start(bf16[6,128,128]{2,1,0:T(8,128)(2,1)S(1)} %copy-done.9), channel_id=1, source_target_pairs={{0,28},{4,24},{8,20},{12,16},{16,12},{20,8},{24,4},{28,0},{1,29},{... | collective-permute-start | bytes 589832 | tf_op jit(solution)/shard_map/ppermute | solution.py:331
  29.8 12.3 %collective-permute-start.4 = (bf16[6,128,128]{2,1,0:T(8,128)(2,1)S(1)}, bf16[6,128,128]{2,1,0:T(8,128)(2,1)S(1)}, u32[]{:S(2)}, u32[]{:S(2)}) collective-permute-start(bf16[6,128,128]{2,1,0:T(8,128)(2,1)S(1)} %copy-done.8), channel_id=1, source_target_pairs={{0,20},{4,16},{8,28},{12,24},{16,4},{20,0},{24,12},{28,8},{1,21},{... | collective-permute-start | bytes 589832 | tf_op jit(solution)/shard_map/ppermute | solution.py:331
  29.8 12.2 %collective-permute-start.5 = (bf16[6,128,128]{2,1,0:T(8,128)(2,1)S(1)}, bf16[6,128,128]{2,1,0:T(8,128)(2,1)S(1)}, u32[]{:S(2)}, u32[]{:S(2)}) collective-permute-start(bf16[6,128,128]{2,1,0:T(8,128)(2,1)S(1)} %copy-done.7), channel_id=1, source_target_pairs={{0,12},{4,8},{8,4},{12,0},{16,28},{20,24},{24,20},{28,16},{1,13},{... | collective-permute-start | bytes 589832 | tf_op jit(solution)/shard_map/ppermute | solution.py:331
  33.3 8.7 %collective-permute-start.6 = (bf16[6,128,128]{2,1,0:T(8,128)(2,1)S(1)}, bf16[6,128,128]{2,1,0:T(8,128)(2,1)S(1)}, u32[]{:S(2)}, u32[]{:S(2)}) collective-permute-start(bf16[6,128,128]{2,1,0:T(8,128)(2,1)S(1)} %copy-done.6), channel_id=1, source_target_pairs={{0,4},{4,0},{8,12},{12,8},{16,20},{20,16},{24,28},{28,24},{1,5},{5... | collective-permute-start | bytes 589832 | tf_op jit(solution)/shard_map/ppermute | solution.py:331
  63.6 11.2 %collective-permute-start.11 = (bf16[1024,1024]{1,0:T(8,128)(2,1)S(1)}, bf16[1024,1024]{1,0:T(8,128)(2,1)S(1)}, u32[]{:S(2)}, u32[]{:S(2)}) collective-permute-start(bf16[1024,1024]{1,0:T(8,128)(2,1)S(1)} %collective-permute-done.9.refs_2_.refs_4_), channel_id=1, source_target_pairs={{0,4},{4,0},{8,12},{12,8},{16,20},{20,16},{24,28},{28,24},{1,5},{5... | collective-permute-start | bytes 6291464 | tf_op jit(solution)/shard_map/ppermute | solution.py:331
  63.6 11.2 %collective-permute-start.12 = (bf16[1024,1024]{1,0:T(8,128)(2,1)S(1)}, bf16[1024,1024]{1,0:T(8,128)(2,1)S(1)}, u32[]{:S(2)}, u32[]{:S(2)}) collective-permute-start(bf16[1024,1024]{1,0:T(8,128)(2,1)S(1)} %collective-permute-done.10.refs_4_.refs_6_), channel_id=1, source_target_pairs={{0,4},{4,0},{8,12},{12,8},{16,20},{20,16},{24,28},{28,24},{1,5},{5... | collective-permute-start | bytes 6291464 | tf_op jit(solution)/shard_map/ppermute | solution.py:331
  64.1 8.3 %collective-permute-start.14 = (bf16[128,1024]{1,0:T(8,128)(2,1)S(1)}, bf16[128,1024]{1,0:T(8,128)(2,1)S(1)}, u32[]{:S(2)}, u32[]{:S(2)}) collective-permute-start(bf16[128,1024]{1,0:T(8,128)(2,1)S(1)} %get-tuple-element.59.refs_0_), channel_id=1, source_target_pairs={{0,2},{1,3},{2,0},{3,1},{4,6},{5,7},{6,4},{7,5},{8,10},{9,11},{10,... | collective-permute-start | bytes 786440 | tf_op jit(solution)/shard_map/ppermute | solution.py:331
  65.7 9.1 %collective-permute-start.13 = (bf16[128,1024]{1,0:T(8,128)(2,1)S(1)}, bf16[128,1024]{1,0:T(8,128)(2,1)S(1)}, u32[]{:S(2)}, u32[]{:S(2)}) collective-permute-start(bf16[128,1024]{1,0:T(8,128)(2,1)S(1)} %get-tuple-element.59.refs_0_), channel_id=1, source_target_pairs={{0,1},{1,0},{2,3},{3,2},{4,5},{5,4},{6,7},{7,6},{8,9},{9,8},{10,11... | collective-permute-start | bytes 786440 | tf_op jit(solution)/shard_map/ppermute | solution.py:331
  70.2 8.9 %collective-permute-start.8 = (bf16[128,1024]{1,0:T(8,128)(2,1)S(1)}, bf16[128,1024]{1,0:T(8,128)(2,1)S(1)}, u32[]{:S(2)}, u32[]{:S(2)}) collective-permute-start(bf16[128,1024]{1,0:T(8,128)(2,1)S(1)} %get-tuple-element.60.refs_1_), channel_id=1, source_target_pairs={{0,2},{1,3},{2,0},{3,1},{4,6},{5,7},{6,4},{7,5},{8,10},{9,11},{10,... | collective-permute-start | bytes 786440 | tf_op jit(solution)/shard_map/ppermute | solution.py:331
  72.4 9.1 %collective-permute-start.7 = (bf16[128,1024]{1,0:T(8,128)(2,1)S(1)}, bf16[128,1024]{1,0:T(8,128)(2,1)S(1)}, u32[]{:S(2)}, u32[]{:S(2)}) collective-permute-start(bf16[128,1024]{1,0:T(8,128)(2,1)S(1)} %get-tuple-element.60.refs_1_), channel_id=1, source_target_pairs={{0,1},{1,0},{2,3},{3,2},{4,5},{5,4},{6,7},{7,6},{8,9},{9,8},{10,11... | collective-permute-start | bytes 786440 | tf_op jit(solution)/shard_map/ppermute | solution.py:331
  76.2 15.8 %collective-permute-start.15 = (bf16[128,1024]{1,0:T(8,128)(2,1)S(1)}, bf16[128,1024]{1,0:T(8,128)(2,1)S(1)}, u32[]{:S(2)}, u32[]{:S(2)}) collective-permute-start(bf16[128,1024]{1,0:T(8,128)(2,1)S(1)} %get-tuple-element.63), channel_id=1, source_target_pairs={{0,2},{1,3},{2,0},{3,1},{4,6},{5,7},{6,4},{7,5},{8,10},{9,11},{10,... | collective-permute-start | bytes 786440 | tf_op jit(solution)/shard_map/ppermute | solution.py:331
  77.8 14.2 %collective-permute-start.17 = (bf16[128,1024]{1,0:T(8,128)(2,1)S(1)}, bf16[128,1024]{1,0:T(8,128)(2,1)S(1)}, u32[]{:S(2)}, u32[]{:S(2)}) collective-permute-start(bf16[128,1024]{1,0:T(8,128)(2,1)S(1)} %get-tuple-element.64), channel_id=1, source_target_pairs={{0,1},{1,0},{2,3},{3,2},{4,5},{5,4},{6,7},{7,6},{8,9},{9,8},{10,11... | collective-permute-start | bytes 786440 | tf_op jit(solution)/shard_map/ppermute | solution.py:331
  82.9 9.1 %collective-permute-start.16 = (bf16[128,1024]{1,0:T(8,128)(2,1)S(1)}, bf16[128,1024]{1,0:T(8,128)(2,1)S(1)}, u32[]{:S(2)}, u32[]{:S(2)}) collective-permute-start(bf16[128,1024]{1,0:T(8,128)(2,1)S(1)} %get-tuple-element.57), channel_id=1, source_target_pairs={{0,2},{1,3},{2,0},{3,1},{4,6},{5,7},{6,4},{7,5},{8,10},{9,11},{10,... | collective-permute-start | bytes 786440 | tf_op jit(solution)/shard_map/ppermute | solution.py:331
  85.5 6.5 %collective-permute-start.18 = (bf16[128,1024]{1,0:T(8,128)(2,1)S(1)}, bf16[128,1024]{1,0:T(8,128)(2,1)S(1)}, u32[]{:S(2)}, u32[]{:S(2)}) collective-permute-start(bf16[128,1024]{1,0:T(8,128)(2,1)S(1)} %get-tuple-element.58), channel_id=1, source_target_pairs={{0,1},{1,0},{2,3},{3,2},{4,5},{5,4},{6,7},{7,6},{8,9},{9,8},{10,11... | collective-permute-start | bytes 786440 | tf_op jit(solution)/shard_map/ppermute | solution.py:331

commit v5 on v4

--- a/solution.py
+++ b/solution.py
@@ -344,12 +344,11 @@
     _, places = lax.optimization_barrier((packed, places))
     block_x, block_y = take_blocks(places, out_weight)
     late = [m for m in order if m % 2]
-    held, block_x, block_y = lax.optimization_barrier(([packed[m] for m in late], block_x, block_y))
     weight_x, weight_y = swap(block_x, "chan", 1), swap(block_y, "chan", 2)
-    for m, mine in zip(late, held):
-        packed[m] = mine
-    data = [swap(packed[m], "seq", m) if m else packed[m] for m in order]
-    (conv,) = convolve(here.reshape(1), data, order, 1)
+    data = {m: swap(packed[m], "seq", m) if m else packed[m] for m in order if m % 2 == 0}
+    held, data[order[0]] = lax.optimization_barrier(([packed[m] for m in late], data[order[0]]))
+    data.update({m: swap(mine, "seq", m) for m, mine in zip(late, held)})
+    (conv,) = convolve(here.reshape(1), [data[m] for m in order], order, 1)
     conv = lax.all_to_all(conv, "seq", split_axis=0, concat_axis=0, tiled=True)
     gated = gate(conv, gate_out, parts)
     weight_x, weight_y, _ = lax.optimization_barrier((weight_x, weight_y, gated))
@@ -360,17 +359,18 @@
     for p in range(parts):
         mine = gated[p]
         if p:
-            mine, _ = lax.optimization_barrier((mine, own))
+            mine, own, weights[1] = lax.optimization_barrier((mine, own, weights[1]))
         moved_x.append(swap(mine, "chan", 1))
         moved_y.append(swap(mine, "chan", 2))
     sums_a, sums_b = [], []
     for p in range(parts):
+        if p == parts - 1:
+            own_kept = own_part(me.reshape(1), gated, out_weight, ((0, 0), (0, 1)))
+            own, own_kept = lax.optimization_barrier((own, own_kept))
         sent = add_moved(core, own, moved_x[p:p + 1], moved_y[p:p + 1], weights, p, False, jnp.bfloat16)
         sums_a.append(swap(sent[0], "chan", 2))
         sums_b.append(swap(sent[1], "chan", 1))
-    gated, _ = lax.optimization_barrier((gated, sent))
-    own = own_part(me.reshape(1), gated, out_weight, ((0, 0), (0, 1)))
-    kept_a, kept_b = add_moved(core, own, moved_x, moved_y, weights, 0, True, jnp.float32)
+    kept_a, kept_b = add_moved(core, own_kept, moved_x, moved_y, weights, 0, True, jnp.float32)
     sums = jnp.concatenate([jnp.concatenate(sums_a, axis=0), jnp.concatenate(sums_b, axis=0)], axis=1)
     return (jnp.concatenate([kept_a, kept_b], axis=1) + sums.astype(jnp.float32)).astype(jnp.bfloat16)
 

time: 93.5 us -> 91.9 us (0.983)
  starting transfers between devices: 26.9 us -> 23.8 us
  waiting for transfers between devices: 26.2 us -> 27.8 us
    ppermute x19, starting transfers between devices: 26.9 us -> 23.8 us  [swap(): lax.ppermute(data, axis, [(i, i ^ flip) for i in range(lax.axis_size(axis...]
    ppermute x19, waiting for transfers between devices: 26.2 us -> 27.8 us  [swap(): lax.ppermute(data, axis, [(i, i ^ flip) for i in range(lax.axis_size(axis...]
  transfers between devices with their start and end apart: 19 -> 19, of which waited for: 5 -> 6; matrix products, arithmetic and copies ran while one was open for 0% -> 0% of each run, Pallas kernels for 18% -> 19%
where the time goes in v5:
time: 91.9 us; the launch traced here: 91.7 us
  waiting for transfers between devices  27.8 us (30%)
  starting transfers between devices  23.8 us (26%)
  Pallas kernels  20.2 us (22%)
  blocking collectives  18.3 us (20%)
  other arithmetic  1.34 us (1%)
    ppermute x19, waiting for transfers between devices, swap(): lax.ppermute(data, axis, [(i, i ^ flip) for i in range(lax.axis_size(axis...  27.8 us
    ppermute x19, starting transfers between devices, swap(): lax.ppermute(data, axis, [(i, i ^ flip) for i in range(lax.axis_size(axis...  23.8 us
    all_to_all x1, blocking collectives, by_channels(): conv = lax.all_to_all(conv, 'seq', split_axis=0, concat_axis=0, tiled=True)  18.3 us
    pallas_call x2, Pallas kernels, own_part(): pl.pallas_call(own_kernel, grid_spec=pltpu.PrefetchScalarGridSpec(num_sca...  6.1 us
    pallas_call x3, Pallas kernels, add_moved(): pl.pallas_call(functools.partial(add_kernel, parts, kept), grid=(1,), in_...  4.64 us
    pallas_call x1, Pallas kernels, take_blocks(): pl.pallas_call(take_kernel, in_specs=[pl.BlockSpec(memory_space=pltpu.SME...  3.19 us
    pallas_call x1, Pallas kernels, pack(): pl.pallas_call(functools.partial(pack_kernel, span), in_specs=[pl.BlockSp...  3.18 us
    pallas_call x1, Pallas kernels, convolve(): pl.pallas_call(functools.partial(conv_kernel, parts, order), in_specs=[pl...  2.7 us
  transfers between devices with their start and end apart: 19, of which 6 were waited for; matrix products, arithmetic and copies ran while one was open for 0% of the time, Pallas kernels for 19%

profile of v5, /device:TPU:0, one launch (start us, length us, event | category | flops | bytes accessed | tf_op | source)
XLA Modules:
  0.0 91.7 jit_solution(16807562596123195587)
XLA Ops:
  0.0 3.2 %pack.1 = (bf16[6,128,128]{2,1,0:T(8,128)(2,1)}, bf16[6,128,128]{2,1,0:T(8,128)(2,1)}, bf16[6,128,128]{2,1,0:T(8,128)(2,1)}, bf16[6,128,128]{2,1,0:T(8,128)(2,1)...) custom-call(s32[1]{0:T(128)} %bitcast.1.me_ref, ...), custom_call_target="tpu_custom_call" | custom-call | tf_op jit(solution)/shard_map/pack/pallas_call | solution.py:79
  3.2 5.1 %collective-permute-start = (bf16[6,128,128]{2,1,0:T(8,128)(2,1)}, bf16[6,128,128]{2,1,0:T(8,128)(2,1)S(1)}, u32[]{:S(2)}, u32[]{:S(2)}) collective-permute-start(bf16[6,128,128]{2,1,0:T(8,128)(2,1)} %get-tuple-element.40), channel_id=1, source_target_pairs={{0,24},{4,28},{8,16},{12,20},{16,8},{20,12},{24,0},{28,4},{1,25},{... | collective-permute-start | bytes 589832 | tf_op jit(solution)/shard_map/ppermute | solution.py:331
  8.3 0.1 pad_add_fusion.places_ref
  8.4 0.0 copy-start.7
  8.4 0.0 copy-start.6
  8.4 0.0 copy-start.1
  8.4 0.0 copy-start.2
  8.4 0.0 copy-start.3
  8.5 0.0 copy-start.4
  8.5 0.0 copy-start.5
  8.5 3.2 %take_blocks.1 = (bf16[1024,1024]{1,0:T(8,128)(2,1)S(1)}, bf16[1024,1024]{1,0:T(8,128)(2,1)S(1)}) custom-call(s32[2]{0:T(128)S(1)} %pad_add_fusion.places_ref, bf16[1024,8192]{1,0:T(8,128)(2,1)} %refs_3_.3), custom_call_target="tpu_custom_call" | custom-call | bytes 134217728 | tf_op jit(solution)/shard_map/take_blocks/pallas_call | solution.py:117
  11.7 1.6 %collective-permute-start.7 = (bf16[1024,1024]{1,0:T(8,128)(2,1)S(1)}, bf16[1024,1024]{1,0:T(8,128)(2,1)S(1)}, u32[]{:S(2)}, u32[]{:S(2)}) collective-permute-start(bf16[1024,1024]{1,0:T(8,128)(2,1)S(1)} %get-tuple-element.52), channel_id=1, source_target_pairs={{0,1},{1,0},{2,3},{3,2},{4,5},{5,4},{6,7},{7,6},{8,9},{9,8},{10,11... | collective-permute-start | bytes 6291464 | tf_op jit(solution)/shard_map/ppermute | solution.py:331
  13.2 1.5 %collective-permute-start.8 = (bf16[1024,1024]{1,0:T(8,128)(2,1)S(1)}, bf16[1024,1024]{1,0:T(8,128)(2,1)S(1)}, u32[]{:S(2)}, u32[]{:S(2)}) collective-permute-start(bf16[1024,1024]{1,0:T(8,128)(2,1)S(1)} %get-tuple-element.53), channel_id=1, source_target_pairs={{0,2},{1,3},{2,0},{3,1},{4,6},{5,7},{6,4},{7,5},{8,10},{9,11},{10,... | collective-permute-start | bytes 6291464 | tf_op jit(solution)/shard_map/ppermute | solution.py:331
  14.8 0.0 copy-done.11
  14.8 0.0 collective-permute-start.1
  14.8 0.0 copy-done.10
  14.8 0.8 collective-permute-start.2
  15.5 0.0 collective-permute-done.refs_0_
  15.5 0.0 copy-done.9
  15.5 1.6 %collective-permute-start.3 = (bf16[6,128,128]{2,1,0:T(8,128)(2,1)S(1)}, bf16[6,128,128]{2,1,0:T(8,128)(2,1)S(1)}, u32[]{:S(2)}, u32[]{:S(2)}) collective-permute-start(bf16[6,128,128]{2,1,0:T(8,128)(2,1)S(1)} %copy-done.9), channel_id=1, source_target_pairs={{0,28},{4,24},{8,20},{12,16},{16,12},{20,8},{24,4},{28,0},{1,29},{... | collective-permute-start | bytes 589832 | tf_op jit(solution)/shard_map/ppermute | solution.py:331
  17.2 12.6 %collective-permute-done.1.refs_1_ = bf16[6,128,128]{2,1,0:T(8,128)(2,1)S(1)} collective-permute-done((bf16[6,128,128]{2,1,0:T(8,128)(2,1)S(1)}, bf16[6,128,128]{2,1,0:T(8,128)(2,1)S(1)}, u32[]{:S(2)}, u32[]{:S(2)}) %collective-permute-start.1) | collective-permute-done | bytes 196640 | tf_op jit(solution)/shard_map/ppermute | solution.py:331
  29.8 0.0 copy-done.8
  29.8 0.0 collective-permute-start.4
  29.8 0.0 collective-permute-done.2.refs_2_
  29.8 0.0 copy-done.7
  29.8 3.5 %collective-permute-start.5 = (bf16[6,128,128]{2,1,0:T(8,128)(2,1)S(1)}, bf16[6,128,128]{2,1,0:T(8,128)(2,1)S(1)}, u32[]{:S(2)}, u32[]{:S(2)}) collective-permute-start(bf16[6,128,128]{2,1,0:T(8,128)(2,1)S(1)} %copy-done.7), channel_id=1, source_target_pairs={{0,12},{4,8},{8,4},{12,0},{16,28},{20,24},{24,20},{28,16},{1,13},{... | collective-permute-start | bytes 589832 | tf_op jit(solution)/shard_map/ppermute | solution.py:331
  33.3 0.0 collective-permute-done.3.refs_3_
  33.3 0.0 copy-done.6
  33.3 0.0 collective-permute-start.6
  33.3 8.7 %collective-permute-done.4.refs_4_ = bf16[6,128,128]{2,1,0:T(8,128)(2,1)S(1)} collective-permute-done((bf16[6,128,128]{2,1,0:T(8,128)(2,1)S(1)}, bf16[6,128,128]{2,1,0:T(8,128)(2,1)S(1)}, u32[]{:S(2)}, u32[]{:S(2)}) %collective-permute-start.4) | collective-permute-done | bytes 196640 | tf_op jit(solution)/shard_map/ppermute | solution.py:331
  42.1 0.0 collective-permute-done.5.refs_5_
  42.1 0.0 collective-permute-done.6.refs_6_
  42.1 0.0 copy-done.1
  42.1 2.7 %convolve.1 = bf16[8,2,128,128]{3,2,1,0:T(8,128)(2,1)S(1)} custom-call(s32[1]{0:T(128)} %bitcast.1.me_ref, bf16[6,128,128]{2,1,0:T(8,128)(2,1)S(1)} %collective-permute-done.refs_0_, bf16[6,128,128]{2,1,0:T(8,128)(2,1)S(1)} %collective-permute-done.1.refs_1_, bf16[6,128,128]{2,1,0:T(8,128)(2,1)S(1)} %collective-permute-done.2.refs_2_, ...), custom_call_target="tpu_custom_call" | custom-call | flops 6710886400 | bytes 8388608 | tf_op jit(solution)/shard_map/convolve/pallas_call | solution.py:181
  44.8 18.3 %all_to_all.5.conv_ref = bf16[8,2,128,128]{3,2,1,0:T(8,128)(2,1)S(1)} all-to-all(bf16[8,2,128,128]{3,2,1,0:T(8,128)(2,1)S(1)} %convolve.1), channel_id=1, replica_groups=mesh['seq'=8,'chan'=4] {'seq'}, dimensions={0} | all-to-all | bytes 1048576 | tf_op jit(solution)/shard_map/all_to_all | solution.py:352
  63.2 0.4 gate.1
  63.5 0.0 collective-permute-done.7.refs_4_.refs_2_
  63.5 0.0 collective-permute-done.8.refs_6_.refs_4_
  63.6 0.1 collective-permute-start.9
  63.6 0.5 collective-permute-start.14
  64.1 1.5 %collective-permute-start.10 = (bf16[128,1024]{1,0:T(8,128)(2,1)S(1)}, bf16[128,1024]{1,0:T(8,128)(2,1)S(1)}, u32[]{:S(2)}, u32[]{:S(2)}) collective-permute-start(bf16[128,1024]{1,0:T(8,128)(2,1)S(1)} %get-tuple-element.50.refs_0_), channel_id=1, source_target_pairs={{0,1},{1,0},{2,3},{3,2},{4,5},{5,4},{6,7},{7,6},{8,9},{9,8},{10,11... | collective-permute-start | bytes 786440 | tf_op jit(solution)/shard_map/ppermute | solution.py:331
  65.6 1.5 %collective-permute-start.12 = (bf16[128,1024]{1,0:T(8,128)(2,1)S(1)}, bf16[128,1024]{1,0:T(8,128)(2,1)S(1)}, u32[]{:S(2)}, u32[]{:S(2)}) collective-permute-start(bf16[128,1024]{1,0:T(8,128)(2,1)S(1)} %get-tuple-element.50.refs_0_), channel_id=1, source_target_pairs={{0,2},{1,3},{2,0},{3,1},{4,6},{5,7},{6,4},{7,5},{8,10},{9,11},{10,... | collective-permute-start | bytes 786440 | tf_op jit(solution)/shard_map/ppermute | solution.py:331
  67.1 3.1 %own_part.2.own_ref = f32[2,256,1024]{2,1,0:T(8,128)S(1)} custom-call(s32[1]{0:T(128)} %bitcast.2.me_ref, bf16[128,1024]{1,0:T(8,128)(2,1)S(1)} %get-tuple-element.50.refs_0_, bf16[128,1024]{1,0:T(8,128)(2,1)S(1)} %get-tuple-element.57.refs_1_, bf16[1024,8192]{1,0:T(8,128)(2,1)} %refs_3_.3, bf16[1024,8192]{1,0:T(8,128)(2,1)} %refs_3_.3), custom_call_target="tpu_custom_call" | custom-call | flops 1073741824 | bytes 4194304 | tf_op jit(solution)/shard_map/own_part/pallas_call | solution.py:244
  70.2 0.0 collective-permute-done.9.refs_5_.refs_3_
  70.2 0.6 collective-permute-start.11
  70.8 0.5 collective-permute-start.13
  71.3 3.0 %own_part.3.own_ref = f32[2,256,1024]{2,1,0:T(8,128)S(1)} custom-call(s32[1]{0:T(128)} %bitcast.2.me_ref, bf16[128,1024]{1,0:T(8,128)(2,1)S(1)} %get-tuple-element.50.refs_0_, bf16[128,1024]{1,0:T(8,128)(2,1)S(1)} %get-tuple-element.57.refs_1_, bf16[1024,8192]{1,0:T(8,128)(2,1)} %refs_3_.3, bf16[1024,8192]{1,0:T(8,128)(2,1)} %refs_3_.3), custom_call_target="tpu_custom_call" | custom-call | flops 1073741824 | bytes 4194304 | tf_op jit(solution)/shard_map/own_part/pallas_call | solution.py:244
  74.4 0.0 collective-permute-done.10.refs_0_
  74.4 0.1 collective-permute-done.12.refs_2_.refs_1_
  74.5 0.0 collective-permute-done.14.refs_7_.refs_5_
  74.5 1.4 %add_sent.2 = (bf16[128,1024]{1,0:T(8,128)(2,1)S(1)}, bf16[128,1024]{1,0:T(8,128)(2,1)S(1)}) custom-call(s32[1]{0:T(128)} %bitcast.core_ref, f32[2,256,1024]{2,1,0:T(8,128)S(1)} %own_part.2.own_ref, bf16[128,1024]{1,0:T(8,128)(2,1)S(1)} %collective-permute-done.10.refs_0_, bf16[128,1024]{1,0:T(8,128)(2,1)S(1)} %collective-permute-done.12.refs_2_.refs_1_, ...), custom_call_target="tpu_custom_call" | custom-call | flops 536870912 | bytes 4194304 | tf_op jit(solution)/shard_map/add_sent/pallas_call | solution.py:310
  75.9 1.9 %collective-permute-start.15 = (bf16[128,1024]{1,0:T(8,128)(2,1)S(1)}, bf16[128,1024]{1,0:T(8,128)(2,1)S(1)}, u32[]{:S(2)}, u32[]{:S(2)}) collective-permute-start(bf16[128,1024]{1,0:T(8,128)(2,1)S(1)} %get-tuple-element.62), channel_id=1, source_target_pairs={{0,2},{1,3},{2,0},{3,1},{4,6},{5,7},{6,4},{7,5},{8,10},{9,11},{10,... | collective-permute-start | bytes 786440 | tf_op jit(solution)/shard_map/ppermute | solution.py:331
  77.8 1.1 %collective-permute-start.17 = (bf16[128,1024]{1,0:T(8,128)(2,1)S(1)}, bf16[128,1024]{1,0:T(8,128)(2,1)S(1)}, u32[]{:S(2)}, u32[]{:S(2)}) collective-permute-start(bf16[128,1024]{1,0:T(8,128)(2,1)S(1)} %get-tuple-element.65), channel_id=1, source_target_pairs={{0,1},{1,0},{2,3},{3,2},{4,5},{5,4},{6,7},{7,6},{8,9},{9,8},{10,11... | collective-permute-start | bytes 786440 | tf_op jit(solution)/shard_map/ppermute | solution.py:331
  78.9 0.0 collective-permute-done.11.refs_1_.refs_0_
  78.9 1.3 %collective-permute-done.13.refs_3_.refs_1_ = bf16[128,1024]{1,0:T(8,128)(2,1)S(1)} collective-permute-done((bf16[128,1024]{1,0:T(8,128)(2,1)S(1)}, bf16[128,1024]{1,0:T(8,128)(2,1)S(1)}, u32[]{:S(2)}, u32[]{:S(2)}) %collective-permute-start.13) | collective-permute-done | bytes 262176 | tf_op jit(solution)/shard_map/ppermute | solution.py:331
  80.1 1.4 %add_sent.3 = (bf16[128,1024]{1,0:T(8,128)(2,1)S(1)}, bf16[128,1024]{1,0:T(8,128)(2,1)S(1)}) custom-call(s32[1]{0:T(128)} %bitcast.core_ref, f32[2,256,1024]{2,1,0:T(8,128)S(1)} %own_part.2.own_ref, bf16[128,1024]{1,0:T(8,128)(2,1)S(1)} %collective-permute-done.11.refs_1_.refs_0_, bf16[128,1024]{1,0:T(8,128)(2,1)S(1)} %collective-permute-done.13.refs_3_.refs_1_, ...), custom_call_target="tpu_custom_call" | custom-call | flops 536870912 | bytes 4194304 | tf_op jit(solution)/shard_map/add_sent/pallas_call | solution.py:310
  81.5 1.9 %collective-permute-start.16 = (bf16[128,1024]{1,0:T(8,128)(2,1)S(1)}, bf16[128,1024]{1,0:T(8,128)(2,1)S(1)}, u32[]{:S(2)}, u32[]{:S(2)}) collective-permute-start(bf16[128,1024]{1,0:T(8,128)(2,1)S(1)} %get-tuple-element.64), channel_id=1, source_target_pairs={{0,2},{1,3},{2,0},{3,1},{4,6},{5,7},{6,4},{7,5},{8,10},{9,11},{10,... | collective-permute-start | bytes 786440 | tf_op jit(solution)/shard_map/ppermute | solution.py:331
  83.4 0.1 collective-permute-start.18
  83.5 1.9 %add_kept.1 = (f32[256,1024]{1,0:T(8,128)S(1)}, f32[256,1024]{1,0:T(8,128)S(1)}) custom-call(s32[1]{0:T(128)} %bitcast.core_ref, f32[2,256,1024]{2,1,0:T(8,128)S(1)} %own_part.3.own_ref, bf16[128,1024]{1,0:T(8,128)(2,1)S(1)} %collective-permute-done.10.refs_0_, bf16[128,1024]{1,0:T(8,128)(2,1)S(1)} %collective-permute-done.11.refs_1_.refs_0_, ...), custom_call_target="tpu_custom_call" | custom-call | flops 1073741824 | bytes 4194304 | tf_op jit(solution)/shard_map/add_kept/pallas_call | solution.py:310
  85.4 0.3 collective-permute-done.15
  85.8 0.0 collective-permute-done.17
  85.8 4.7 %collective-permute-done.16 = bf16[128,1024]{1,0:T(8,128)(2,1)S(1)} collective-permute-done((bf16[128,1024]{1,0:T(8,128)(2,1)S(1)}, bf16[128,1024]{1,0:T(8,128)(2,1)S(1)}, u32[]{:S(2)}, u32[]{:S(2)}) %collective-permute-start.16) | collective-permute-done | bytes 262176 | tf_op jit(solution)/shard_map/ppermute | solution.py:331
  90.5 0.0 collective-permute-done.18
  90.5 1.3 %fusion = bf16[256,2048]{1,0:T(8,128)(2,1)} fusion(f32[256,1024]{1,0:T(8,128)S(1)} %get-tuple-element.61, f32[256,1024]{1,0:T(8,128)S(1)} %get-tuple-element.60, bf16[128,1024]{1,0:T(8,128)(2,1)S(1)} %collective-permute-done.18, bf16[128,1024]{1,0:T(8,128)(2,1)S(1)} %collective-permute-done.17, bf16[128,1024]{1,0:T(8,128)(2,1)S(1)} %collective-permute-done.16, ...), kind=kLoop, calls=%fused_computation.1 | loop fusion | flops 5767168 | bytes 4194304 | tf_op jit(solution)/shard_map/convert_element_type | solution.py:375
  (10 shorter events, 0.0 us)
Async XLA Ops:
  3.2 12.4 %collective-permute-start = (bf16[6,128,128]{2,1,0:T(8,128)(2,1)}, bf16[6,128,128]{2,1,0:T(8,128)(2,1)S(1)}, u32[]{:S(2)}, u32[]{:S(2)}) collective-permute-start(bf16[6,128,128]{2,1,0:T(8,128)(2,1)} %get-tuple-element.40), channel_id=1, source_target_pairs={{0,24},{4,28},{8,16},{12,20},{16,8},{20,12},{24,0},{28,4},{1,25},{... | collective-permute-start | bytes 589832 | tf_op jit(solution)/shard_map/ppermute | solution.py:331
  8.4 6.4 %copy-start.11 = (bf16[6,128,128]{2,1,0:T(8,128)(2,1)S(1)}, bf16[6,128,128]{2,1,0:T(8,128)(2,1)}, u32[]{:S(2)}) copy-start(bf16[6,128,128]{2,1,0:T(8,128)(2,1)} %get-tuple-element.42) | copy-start | bytes 589828
  8.4 6.4 %copy-start.10 = (bf16[6,128,128]{2,1,0:T(8,128)(2,1)S(1)}, bf16[6,128,128]{2,1,0:T(8,128)(2,1)}, u32[]{:S(2)}) copy-start(bf16[6,128,128]{2,1,0:T(8,128)(2,1)} %get-tuple-element.43) | copy-start | bytes 589828
  8.4 7.2 %copy-start.9 = (bf16[6,128,128]{2,1,0:T(8,128)(2,1)S(1)}, bf16[6,128,128]{2,1,0:T(8,128)(2,1)}, u32[]{:S(2)}) copy-start(bf16[6,128,128]{2,1,0:T(8,128)(2,1)} %get-tuple-element.44) | copy-start | bytes 589828
  8.4 21.4 %copy-start.8 = (bf16[6,128,128]{2,1,0:T(8,128)(2,1)S(1)}, bf16[6,128,128]{2,1,0:T(8,128)(2,1)}, u32[]{:S(2)}) copy-start(bf16[6,128,128]{2,1,0:T(8,128)(2,1)} %get-tuple-element.45) | copy-start | bytes 589828
  8.4 21.4 %copy-start.7 = (bf16[6,128,128]{2,1,0:T(8,128)(2,1)S(1)}, bf16[6,128,128]{2,1,0:T(8,128)(2,1)}, u32[]{:S(2)}) copy-start(bf16[6,128,128]{2,1,0:T(8,128)(2,1)} %get-tuple-element.46) | copy-start | bytes 589828
  8.4 24.9 %copy-start.6 = (bf16[6,128,128]{2,1,0:T(8,128)(2,1)S(1)}, bf16[6,128,128]{2,1,0:T(8,128)(2,1)}, u32[]{:S(2)}) copy-start(bf16[6,128,128]{2,1,0:T(8,128)(2,1)} %get-tuple-element.47) | copy-start | bytes 589828
  8.4 33.7 %copy-start.1 = (bf16[6,128,128]{2,1,0:T(8,128)(2,1)S(1)}, bf16[6,128,128]{2,1,0:T(8,128)(2,1)}, u32[]{:S(2)}) copy-start(bf16[6,128,128]{2,1,0:T(8,128)(2,1)} %get-tuple-element.48.refs_7_) | copy-start | bytes 589828
  8.4 33.7 %copy-start.2 = (bf16[1024,1024]{1,0:T(8,128)(2,1)S(1)}, bf16[1024,1024]{1,0:T(8,128)(2,1)}, u32[]{:S(2)}) copy-start(bf16[1024,1024]{1,0:T(8,128)(2,1)} %constant.31.clone.refs_8_) | copy-start | bytes 6291460
  8.4 33.6 %copy-start.3 = (bf16[1024,1024]{1,0:T(8,128)(2,1)S(1)}, bf16[1024,1024]{1,0:T(8,128)(2,1)}, u32[]{:S(2)}) copy-start(bf16[1024,1024]{1,0:T(8,128)(2,1)} %constant.32.clone.refs_9_) | copy-start | bytes 6291460
  8.5 33.6 %copy-start.4 = (f32[1024,128]{1,0:T(8,128)S(1)}, f32[1024,128]{1,0:T(8,128)}, u32[]{:S(2)}) copy-start(f32[1024,128]{1,0:T(8,128)} %constant.33.clone.refs_10_) | copy-start | bytes 1572868
  8.5 33.6 %copy-start.5 = (f32[1024,128]{1,0:T(8,128)S(1)}, f32[1024,128]{1,0:T(8,128)}, u32[]{:S(2)}) copy-start(f32[1024,128]{1,0:T(8,128)} %constant.34.clone.refs_11_) | copy-start | bytes 1572868
  11.7 51.9 %collective-permute-start.7 = (bf16[1024,1024]{1,0:T(8,128)(2,1)S(1)}, bf16[1024,1024]{1,0:T(8,128)(2,1)S(1)}, u32[]{:S(2)}, u32[]{:S(2)}) collective-permute-start(bf16[1024,1024]{1,0:T(8,128)(2,1)S(1)} %get-tuple-element.52), channel_id=1, source_target_pairs={{0,1},{1,0},{2,3},{3,2},{4,5},{5,4},{6,7},{7,6},{8,9},{9,8},{10,11... | collective-permute-start | bytes 6291464 | tf_op jit(solution)/shard_map/ppermute | solution.py:331
  13.2 49.9 %copy-start = (bf16[256,1024]{1,0:T(8,128)(2,1)S(1)}, bf16[256,1024]{1,0:T(8,128)(2,1)}, u32[]{:S(2)}) copy-start(bf16[256,1024]{1,0:T(8,128)(2,1)} %gate_ref.1) | copy-start | bytes 1572868
  13.2 50.3 %collective-permute-start.8 = (bf16[1024,1024]{1,0:T(8,128)(2,1)S(1)}, bf16[1024,1024]{1,0:T(8,128)(2,1)S(1)}, u32[]{:S(2)}, u32[]{:S(2)}) collective-permute-start(bf16[1024,1024]{1,0:T(8,128)(2,1)S(1)} %get-tuple-element.53), channel_id=1, source_target_pairs={{0,2},{1,3},{2,0},{3,1},{4,6},{5,7},{6,4},{7,5},{8,10},{9,11},{10,... | collective-permute-start | bytes 6291464 | tf_op jit(solution)/shard_map/ppermute | solution.py:331
  14.8 15.0 %collective-permute-start.1 = (bf16[6,128,128]{2,1,0:T(8,128)(2,1)S(1)}, bf16[6,128,128]{2,1,0:T(8,128)(2,1)S(1)}, u32[]{:S(2)}, u32[]{:S(2)}) collective-permute-start(bf16[6,128,128]{2,1,0:T(8,128)(2,1)S(1)} %copy-done.11), channel_id=1, source_target_pairs={{0,16},{4,20},{8,24},{12,28},{16,0},{20,4},{24,8},{28,12},{1,17},{... | collective-permute-start | bytes 589832 | tf_op jit(solution)/shard_map/ppermute | solution.py:331
  14.8 15.0 %collective-permute-start.2 = (bf16[6,128,128]{2,1,0:T(8,128)(2,1)S(1)}, bf16[6,128,128]{2,1,0:T(8,128)(2,1)S(1)}, u32[]{:S(2)}, u32[]{:S(2)}) collective-permute-start(bf16[6,128,128]{2,1,0:T(8,128)(2,1)S(1)} %copy-done.10), channel_id=1, source_target_pairs={{0,8},{4,12},{8,0},{12,4},{16,24},{20,28},{24,16},{28,20},{1,9},{5... | collective-permute-start | bytes 589832 | tf_op jit(solution)/shard_map/ppermute | solution.py:331
  15.5 17.8 %collective-permute-start.3 = (bf16[6,128,128]{2,1,0:T(8,128)(2,1)S(1)}, bf16[6,128,128]{2,1,0:T(8,128)(2,1)S(1)}, u32[]{:S(2)}, u32[]{:S(2)}) collective-permute-start(bf16[6,128,128]{2,1,0:T(8,128)(2,1)S(1)} %copy-done.9), channel_id=1, source_target_pairs={{0,28},{4,24},{8,20},{12,16},{16,12},{20,8},{24,4},{28,0},{1,29},{... | collective-permute-start | bytes 589832 | tf_op jit(solution)/shard_map/ppermute | solution.py:331
  29.8 12.3 %collective-permute-start.4 = (bf16[6,128,128]{2,1,0:T(8,128)(2,1)S(1)}, bf16[6,128,128]{2,1,0:T(8,128)(2,1)S(1)}, u32[]{:S(2)}, u32[]{:S(2)}) collective-permute-start(bf16[6,128,128]{2,1,0:T(8,128)(2,1)S(1)} %copy-done.8), channel_id=1, source_target_pairs={{0,20},{4,16},{8,28},{12,24},{16,4},{20,0},{24,12},{28,8},{1,21},{... | collective-permute-start | bytes 589832 | tf_op jit(solution)/shard_map/ppermute | solution.py:331
  29.8 12.2 %collective-permute-start.5 = (bf16[6,128,128]{2,1,0:T(8,128)(2,1)S(1)}, bf16[6,128,128]{2,1,0:T(8,128)(2,1)S(1)}, u32[]{:S(2)}, u32[]{:S(2)}) collective-permute-start(bf16[6,128,128]{2,1,0:T(8,128)(2,1)S(1)} %copy-done.7), channel_id=1, source_target_pairs={{0,12},{4,8},{8,4},{12,0},{16,28},{20,24},{24,20},{28,16},{1,13},{... | collective-permute-start | bytes 589832 | tf_op jit(solution)/shard_map/ppermute | solution.py:331
  33.3 8.7 %collective-permute-start.6 = (bf16[6,128,128]{2,1,0:T(8,128)(2,1)S(1)}, bf16[6,128,128]{2,1,0:T(8,128)(2,1)S(1)}, u32[]{:S(2)}, u32[]{:S(2)}) collective-permute-start(bf16[6,128,128]{2,1,0:T(8,128)(2,1)S(1)} %copy-done.6), channel_id=1, source_target_pairs={{0,4},{4,0},{8,12},{12,8},{16,20},{20,16},{24,28},{28,24},{1,5},{5... | collective-permute-start | bytes 589832 | tf_op jit(solution)/shard_map/ppermute | solution.py:331
  63.6 6.7 %collective-permute-start.9 = (bf16[1024,1024]{1,0:T(8,128)(2,1)S(1)}, bf16[1024,1024]{1,0:T(8,128)(2,1)S(1)}, u32[]{:S(2)}, u32[]{:S(2)}) collective-permute-start(bf16[1024,1024]{1,0:T(8,128)(2,1)S(1)} %collective-permute-done.7.refs_4_.refs_2_), channel_id=1, source_target_pairs={{0,4},{4,0},{8,12},{12,8},{16,20},{20,16},{24,28},{28,24},{1,5},{5... | collective-permute-start | bytes 6291464 | tf_op jit(solution)/shard_map/ppermute | solution.py:331
  63.6 10.9 %collective-permute-start.14 = (bf16[1024,1024]{1,0:T(8,128)(2,1)S(1)}, bf16[1024,1024]{1,0:T(8,128)(2,1)S(1)}, u32[]{:S(2)}, u32[]{:S(2)}) collective-permute-start(bf16[1024,1024]{1,0:T(8,128)(2,1)S(1)} %collective-permute-done.8.refs_6_.refs_4_), channel_id=1, source_target_pairs={{0,4},{4,0},{8,12},{12,8},{16,20},{20,16},{24,28},{28,24},{1,5},{5... | collective-permute-start | bytes 6291464 | tf_op jit(solution)/shard_map/ppermute | solution.py:331
  64.1 10.2 %collective-permute-start.10 = (bf16[128,1024]{1,0:T(8,128)(2,1)S(1)}, bf16[128,1024]{1,0:T(8,128)(2,1)S(1)}, u32[]{:S(2)}, u32[]{:S(2)}) collective-permute-start(bf16[128,1024]{1,0:T(8,128)(2,1)S(1)} %get-tuple-element.50.refs_0_), channel_id=1, source_target_pairs={{0,1},{1,0},{2,3},{3,2},{4,5},{5,4},{6,7},{7,6},{8,9},{9,8},{10,11... | collective-permute-start | bytes 786440 | tf_op jit(solution)/shard_map/ppermute | solution.py:331
  65.6 8.9 %collective-permute-start.12 = (bf16[128,1024]{1,0:T(8,128)(2,1)S(1)}, bf16[128,1024]{1,0:T(8,128)(2,1)S(1)}, u32[]{:S(2)}, u32[]{:S(2)}) collective-permute-start(bf16[128,1024]{1,0:T(8,128)(2,1)S(1)} %get-tuple-element.50.refs_0_), channel_id=1, source_target_pairs={{0,2},{1,3},{2,0},{3,1},{4,6},{5,7},{6,4},{7,5},{8,10},{9,11},{10,... | collective-permute-start | bytes 786440 | tf_op jit(solution)/shard_map/ppermute | solution.py:331
  70.2 8.7 %collective-permute-start.11 = (bf16[128,1024]{1,0:T(8,128)(2,1)S(1)}, bf16[128,1024]{1,0:T(8,128)(2,1)S(1)}, u32[]{:S(2)}, u32[]{:S(2)}) collective-permute-start(bf16[128,1024]{1,0:T(8,128)(2,1)S(1)} %get-tuple-element.57.refs_1_), channel_id=1, source_target_pairs={{0,1},{1,0},{2,3},{3,2},{4,5},{5,4},{6,7},{7,6},{8,9},{9,8},{10,11... | collective-permute-start | bytes 786440 | tf_op jit(solution)/shard_map/ppermute | solution.py:331
  70.8 9.3 %collective-permute-start.13 = (bf16[128,1024]{1,0:T(8,128)(2,1)S(1)}, bf16[128,1024]{1,0:T(8,128)(2,1)S(1)}, u32[]{:S(2)}, u32[]{:S(2)}) collective-permute-start(bf16[128,1024]{1,0:T(8,128)(2,1)S(1)} %get-tuple-element.57.refs_1_), channel_id=1, source_target_pairs={{0,2},{1,3},{2,0},{3,1},{4,6},{5,7},{6,4},{7,5},{8,10},{9,11},{10,... | collective-permute-start | bytes 786440 | tf_op jit(solution)/shard_map/ppermute | solution.py:331
  75.9 9.8 %collective-permute-start.15 = (bf16[128,1024]{1,0:T(8,128)(2,1)S(1)}, bf16[128,1024]{1,0:T(8,128)(2,1)S(1)}, u32[]{:S(2)}, u32[]{:S(2)}) collective-permute-start(bf16[128,1024]{1,0:T(8,128)(2,1)S(1)} %get-tuple-element.62), channel_id=1, source_target_pairs={{0,2},{1,3},{2,0},{3,1},{4,6},{5,7},{6,4},{7,5},{8,10},{9,11},{10,... | collective-permute-start | bytes 786440 | tf_op jit(solution)/shard_map/ppermute | solution.py:331
  77.8 8.0 %collective-permute-start.17 = (bf16[128,1024]{1,0:T(8,128)(2,1)S(1)}, bf16[128,1024]{1,0:T(8,128)(2,1)S(1)}, u32[]{:S(2)}, u32[]{:S(2)}) collective-permute-start(bf16[128,1024]{1,0:T(8,128)(2,1)S(1)} %get-tuple-element.65), channel_id=1, source_target_pairs={{0,1},{1,0},{2,3},{3,2},{4,5},{5,4},{6,7},{7,6},{8,9},{9,8},{10,11... | collective-permute-start | bytes 786440 | tf_op jit(solution)/shard_map/ppermute | solution.py:331
  81.5 9.0 %collective-permute-start.16 = (bf16[128,1024]{1,0:T(8,128)(2,1)S(1)}, bf16[128,1024]{1,0:T(8,128)(2,1)S(1)}, u32[]{:S(2)}, u32[]{:S(2)}) collective-permute-start(bf16[128,1024]{1,0:T(8,128)(2,1)S(1)} %get-tuple-element.64), channel_id=1, source_target_pairs={{0,2},{1,3},{2,0},{3,1},{4,6},{5,7},{6,4},{7,5},{8,10},{9,11},{10,... | collective-permute-start | bytes 786440 | tf_op jit(solution)/shard_map/ppermute | solution.py:331
  83.4 7.1 %collective-permute-start.18 = (bf16[128,1024]{1,0:T(8,128)(2,1)S(1)}, bf16[128,1024]{1,0:T(8,128)(2,1)S(1)}, u32[]{:S(2)}, u32[]{:S(2)}) collective-permute-start(bf16[128,1024]{1,0:T(8,128)(2,1)S(1)} %get-tuple-element.66), channel_id=1, source_target_pairs={{0,1},{1,0},{2,3},{3,2},{4,5},{5,4},{6,7},{7,6},{8,9},{9,8},{10,11... | collective-permute-start | bytes 786440 | tf_op jit(solution)/shard_map/ppermute | solution.py:331

commit v6 on v5

--- a/solution.py
+++ b/solution.py
@@ -126,11 +126,12 @@
     )(places, weight)
 
 
-def conv_kernel(parts, order, me_ref, *refs):
+def conv_kernel(order, me_ref, *refs):
     shares = len(order)
     data, (cos_ref, sin_ref, turn_cos_ref, turn_sin_ref) = refs[:shares], refs[shares:shares + 4]
-    outs, (cols_ref, filt_ref, re_ref, im_ref) = refs[shares + 4:shares + 4 + parts], refs[shares + 4 + parts:]
+    mine_ref, other_ref, cols_ref, filt_ref, re_ref, im_ref = refs[shares + 4:]
     me = me_ref[0]
+    chip, core = me // 2, me % 2
     rows = data[0].shape[1]
     for m, ref in zip(order, data):
         at = pl.ds(pl.multiple_of((me ^ m) * rows, rows), rows)
@@ -157,20 +158,19 @@
         re_ref[at, :] = jnp.concatenate([b0r, b1r], axis=1).astype(jnp.bfloat16)
         im_ref[at, :] = jnp.concatenate([b0i, b1i], axis=1).astype(jnp.bfloat16)
     scale = 1.0 / (shares * rows)
-    part_rows = rows // parts
     for i in range(shares * rows // step):
         at = slice(i * step, (i + 1) * step)
         conv = jnp.dot(cos_ref[at, :], re_ref[...], preferred_element_type=jnp.float32)
         conv = conv - jnp.dot(sin_ref[at, :], im_ref[...], preferred_element_type=jnp.float32)
         conv = (conv * scale).astype(jnp.bfloat16)
-        for s in range(2):
-            for p in range(parts):
-                begin = s * rows + p * part_rows
-                for b in range(2):
-                    outs[p][2 * i + s, b] = conv[begin:begin + part_rows, b * LANES:(b + 1) * LANES]
-
-
-def convolve(me, data, order, parts):
+        for b in range(2):
+            lanes = slice(b * LANES, (b + 1) * LANES)
+            low, high = conv[:rows, lanes], conv[rows:, lanes]
+            mine_ref[i ^ chip, b] = jnp.where(core == 0, low, high)
+            other_ref[i ^ chip, b] = jnp.where(core == 0, high, low)
+
+
+def convolve(me, data, order):
     shares = len(data)
     rows = data[0].shape[1]
     block = shares * rows
@@ -179,10 +179,10 @@
     vmem = pl.BlockSpec(memory_space=pltpu.VMEM)
     columns = pltpu.VMEM((block, 2 * LANES), jnp.bfloat16)
     return pl.pallas_call(
-        functools.partial(conv_kernel, parts, order),
+        functools.partial(conv_kernel, order),
         in_specs=[pl.BlockSpec(memory_space=pltpu.SMEM)] + [vmem] * (shares + 4),
-        out_specs=[vmem] * parts,
-        out_shape=[jax.ShapeDtypeStruct((shares, 2, rows // parts, LANES), jnp.bfloat16)] * parts,
+        out_specs=[vmem] * 2,
+        out_shape=[jax.ShapeDtypeStruct((shares // 2, 2, rows, LANES), jnp.bfloat16)] * 2,
         scratch_shapes=[columns, pltpu.VMEM((4, block, LANES), jnp.bfloat16), columns, columns],
         compiler_params=pltpu.CompilerParams(vmem_limit_bytes=24 << 20),
         cost_estimate=pl.CostEstimate(flops=50 * block * block * LANES, bytes_accessed=8 * block * block, transcendentals=0),
@@ -193,31 +193,33 @@
     )
 
 
-def gate_kernel(conv_ref, gate_ref, *refs):
-    outs, held_ref = refs[:-1], refs[-1]
-    shares, span, block_rows, _ = conv_ref.shape
+def gate_kernel(chips, me_ref, *refs):
+    held, gate_ref, outs, conv_ref = refs[:chips], refs[chips], refs[chips + 1:-1], refs[-1]
+    _, span, block_rows, _ = held[0].shape
     rows = span * block_rows
-    for s in range(shares):
-        held_ref[:, s * LANES:(s + 1) * LANES] = conv_ref[s].reshape(rows, LANES)
-    conv = jnp.dot(join_rows(rows, span), held_ref[...], preferred_element_type=jnp.float32)
+    for flip, ref in enumerate(held):
+        for core in range(2):
+            share = me_ref[0] ^ (2 * flip + core)
+            conv_ref[:, pl.ds(pl.multiple_of(share * LANES, LANES), LANES)] = ref[core].reshape(rows, LANES)
+    conv = jnp.dot(join_rows(rows, span), conv_ref[...], preferred_element_type=jnp.float32)
     gated = (conv * gate_ref[...].astype(jnp.float32)).astype(jnp.bfloat16)
     part = rows // len(outs)
     for p, out_ref in enumerate(outs):
         out_ref[...] = gated[p * part:(p + 1) * part]
 
 
-def gate(conv, gate_out, parts):
+def gate(me, held, gate_out, parts):
     rows, width = gate_out.shape
     vmem = pl.BlockSpec(memory_space=pltpu.VMEM)
     return pl.pallas_call(
-        gate_kernel,
-        in_specs=[vmem, vmem],
+        functools.partial(gate_kernel, len(held)),
+        in_specs=[pl.BlockSpec(memory_space=pltpu.SMEM)] + [vmem] * (len(held) + 1),
         out_specs=[vmem] * parts,
         out_shape=[jax.ShapeDtypeStruct((rows // parts, width), jnp.bfloat16)] * parts,
         scratch_shapes=[pltpu.VMEM((rows, width), jnp.bfloat16)],
         compiler_params=pltpu.CompilerParams(vmem_limit_bytes=16 << 20),
         name="gate",
-    )(conv, gate_out)
+    )(me, *held, gate_out)
 
 
 def own_kernel(me_ref, *refs):
@@ -348,9 +350,11 @@
     data = {m: swap(packed[m], "seq", m) if m else packed[m] for m in order if m % 2 == 0}
     held, data[order[0]] = lax.optimization_barrier(([packed[m] for m in late], data[order[0]]))
     data.update({m: swap(mine, "seq", m) for m, mine in zip(late, held)})
-    (conv,) = convolve(here.reshape(1), [data[m] for m in order], order, 1)
-    conv = lax.all_to_all(conv, "seq", split_axis=0, concat_axis=0, tiled=True)
-    gated = gate(conv, gate_out, parts)
+    mine, other = convolve(here.reshape(1), [data[m] for m in order], order)
+    other = swap(other, "seq", 1)
+    held = [jnp.stack([mine[flip], other[flip]]) for flip in range(seq_count // 2)]
+    held = [swap(both, "seq", 2 * flip) if flip else both for flip, both in enumerate(held)]
+    gated = gate(here.reshape(1), held, gate_out, parts)
     weight_x, weight_y, _ = lax.optimization_barrier((weight_x, weight_y, gated))
     weights = [weight_x, swap(weight_x, "seq", 1), weight_y, swap(weight_y, "seq", 1)]
     own = own_part(me.reshape(1), gated, out_weight, ((2, 0), (1, 1)))

time: 91.9 us -> 88.5 us (0.963)
  blocking collectives: 18.3 us -> 0 us
  waiting for transfers between devices: 27.8 us -> 38.1 us
  starting transfers between devices: 23.8 us -> 28.2 us
    all_to_all x1 -> x0, blocking collectives: 18.3 us -> none  [by_channels(): conv = lax.all_to_all(conv, 'seq', split_axis=0, concat_axis=0, tiled=True)]
    ppermute x19 -> x23, waiting for transfers between devices: 27.8 us -> 38.1 us  [swap(): lax.ppermute(data, axis, [(i, i ^ flip) for i in range(lax.axis_size(axis...]
    ppermute x19 -> x23, starting transfers between devices: 23.8 us -> 28.2 us  [swap(): lax.ppermute(data, axis, [(i, i ^ flip) for i in range(lax.axis_size(axis...]
  transfers between devices with their start and end apart: 19 -> 23, of which waited for: 6 -> 9; matrix products, arithmetic and copies ran while one was open for 0% -> 0% of each run, Pallas kernels for 19% -> 19%
where the time goes in v6:
time: 88.5 us; the launch traced here: 88.3 us
  waiting for transfers between devices  38.1 us (43%)
  starting transfers between devices  28.2 us (32%)
  Pallas kernels  20.3 us (23%)
  other arithmetic  1.4 us (2%)
    ppermute x23, waiting for transfers between devices, swap(): lax.ppermute(data, axis, [(i, i ^ flip) for i in range(lax.axis_size(axis...  38.1 us
    ppermute x23, starting transfers between devices, swap(): lax.ppermute(data, axis, [(i, i ^ flip) for i in range(lax.axis_size(axis...  28.2 us
    pallas_call x2, Pallas kernels, own_part(): pl.pallas_call(own_kernel, grid_spec=pltpu.PrefetchScalarGridSpec(num_sca...  6.1 us
    pallas_call x3, Pallas kernels, add_moved(): pl.pallas_call(functools.partial(add_kernel, parts, kept), grid=(1,), in_...  4.64 us
    pallas_call x1, Pallas kernels, pack(): pl.pallas_call(functools.partial(pack_kernel, span), in_specs=[pl.BlockSp...  3.19 us
    pallas_call x1, Pallas kernels, take_blocks(): pl.pallas_call(take_kernel, in_specs=[pl.BlockSpec(memory_space=pltpu.SME...  3.19 us
    pallas_call x1, Pallas kernels, convolve(): pl.pallas_call(functools.partial(conv_kernel, order), in_specs=[pl.BlockS...  2.7 us
  transfers between devices with their start and end apart: 23, of which 9 were waited for; matrix products, arithmetic and copies ran while one was open for 0% of the time, Pallas kernels for 19%

profile of v6, /device:TPU:0, one launch (start us, length us, event | category | flops | bytes accessed | tf_op | source)
XLA Modules:
  0.0 88.3 jit_solution(16885910654872664271)
XLA Ops:
  0.0 3.2 %pack.1 = (bf16[6,128,128]{2,1,0:T(8,128)(2,1)}, bf16[6,128,128]{2,1,0:T(8,128)(2,1)}, bf16[6,128,128]{2,1,0:T(8,128)(2,1)}, bf16[6,128,128]{2,1,0:T(8,128)(2,1)...) custom-call(s32[1]{0:T(128)} %bitcast.1.me_ref, ...), custom_call_target="tpu_custom_call" | custom-call | tf_op jit(solution)/shard_map/pack/pallas_call | solution.py:79
  3.2 5.1 %collective-permute-start = (bf16[6,128,128]{2,1,0:T(8,128)(2,1)}, bf16[6,128,128]{2,1,0:T(8,128)(2,1)S(1)}, u32[]{:S(2)}, u32[]{:S(2)}) collective-permute-start(bf16[6,128,128]{2,1,0:T(8,128)(2,1)} %get-tuple-element.42), channel_id=1, source_target_pairs={{0,24},{4,28},{8,16},{12,20},{16,8},{20,12},{24,0},{28,4},{1,25},{... | collective-permute-start | bytes 589832 | tf_op jit(solution)/shard_map/ppermute | solution.py:333
  8.3 0.1 pad_add_fusion.places_ref
  8.4 0.0 copy-start.1
  8.4 0.0 copy-start.2
  8.4 0.0 copy-start.3
  8.5 0.0 copy-start.4
  8.5 0.0 copy-start.5
  8.5 3.2 %take_blocks.1 = (bf16[1024,1024]{1,0:T(8,128)(2,1)S(1)}, bf16[1024,1024]{1,0:T(8,128)(2,1)S(1)}) custom-call(s32[2]{0:T(128)S(1)} %pad_add_fusion.places_ref, bf16[1024,8192]{1,0:T(8,128)(2,1)} %refs_3_.3), custom_call_target="tpu_custom_call" | custom-call | bytes 134217728 | tf_op jit(solution)/shard_map/take_blocks/pallas_call | solution.py:117
  11.7 1.6 %collective-permute-start.11 = (bf16[1024,1024]{1,0:T(8,128)(2,1)S(1)}, bf16[1024,1024]{1,0:T(8,128)(2,1)S(1)}, u32[]{:S(2)}, u32[]{:S(2)}) collective-permute-start(bf16[1024,1024]{1,0:T(8,128)(2,1)S(1)} %get-tuple-element.56), channel_id=1, source_target_pairs={{0,1},{1,0},{2,3},{3,2},{4,5},{5,4},{6,7},{7,6},{8,9},{9,8},{10,11... | collective-permute-start | bytes 6291464 | tf_op jit(solution)/shard_map/ppermute | solution.py:333
  13.2 1.5 %collective-permute-start.12 = (bf16[1024,1024]{1,0:T(8,128)(2,1)S(1)}, bf16[1024,1024]{1,0:T(8,128)(2,1)S(1)}, u32[]{:S(2)}, u32[]{:S(2)}) collective-permute-start(bf16[1024,1024]{1,0:T(8,128)(2,1)S(1)} %get-tuple-element.57), channel_id=1, source_target_pairs={{0,2},{1,3},{2,0},{3,1},{4,6},{5,7},{6,4},{7,5},{8,10},{9,11},{10,... | collective-permute-start | bytes 6291464 | tf_op jit(solution)/shard_map/ppermute | solution.py:333
  14.8 0.0 copy-done.11
  14.8 0.0 collective-permute-start.1
  14.8 0.8 collective-permute-start.2
  15.5 0.0 collective-permute-done.refs_0_
  15.6 1.6 %collective-permute-start.3 = (bf16[6,128,128]{2,1,0:T(8,128)(2,1)S(1)}, bf16[6,128,128]{2,1,0:T(8,128)(2,1)S(1)}, u32[]{:S(2)}, u32[]{:S(2)}) collective-permute-start(bf16[6,128,128]{2,1,0:T(8,128)(2,1)S(1)} %copy-done.9), channel_id=1, source_target_pairs={{0,28},{4,24},{8,20},{12,16},{16,12},{20,8},{24,4},{28,0},{1,29},{... | collective-permute-start | bytes 589832 | tf_op jit(solution)/shard_map/ppermute | solution.py:333
  17.2 12.6 %collective-permute-done.1.refs_1_ = bf16[6,128,128]{2,1,0:T(8,128)(2,1)S(1)} collective-permute-done((bf16[6,128,128]{2,1,0:T(8,128)(2,1)S(1)}, bf16[6,128,128]{2,1,0:T(8,128)(2,1)S(1)}, u32[]{:S(2)}, u32[]{:S(2)}) %collective-permute-start.1) | collective-permute-done | bytes 196640 | tf_op jit(solution)/shard_map/ppermute | solution.py:333
  29.8 0.0 collective-permute-start.4
  29.8 0.0 collective-permute-done.2.refs_2_
  29.8 3.5 %collective-permute-start.5 = (bf16[6,128,128]{2,1,0:T(8,128)(2,1)S(1)}, bf16[6,128,128]{2,1,0:T(8,128)(2,1)S(1)}, u32[]{:S(2)}, u32[]{:S(2)}) collective-permute-start(bf16[6,128,128]{2,1,0:T(8,128)(2,1)S(1)} %copy-done.7), channel_id=1, source_target_pairs={{0,12},{4,8},{8,4},{12,0},{16,28},{20,24},{24,20},{28,16},{1,13},{... | collective-permute-start | bytes 589832 | tf_op jit(solution)/shard_map/ppermute | solution.py:333
  33.3 0.0 collective-permute-done.3.refs_3_
  33.4 0.0 collective-permute-start.6
  33.4 8.7 %collective-permute-done.4.refs_4_ = bf16[6,128,128]{2,1,0:T(8,128)(2,1)S(1)} collective-permute-done((bf16[6,128,128]{2,1,0:T(8,128)(2,1)S(1)}, bf16[6,128,128]{2,1,0:T(8,128)(2,1)S(1)}, u32[]{:S(2)}, u32[]{:S(2)}) %collective-permute-start.4) | collective-permute-done | bytes 196640 | tf_op jit(solution)/shard_map/ppermute | solution.py:333
  42.1 0.0 collective-permute-done.5.refs_5_
  42.1 0.0 collective-permute-done.6.refs_6_
  42.1 2.7 %convolve.1 = (bf16[4,2,128,128]{3,2,1,0:T(8,128)(2,1)S(1)}, bf16[4,2,128,128]{3,2,1,0:T(8,128)(2,1)S(1)}) custom-call(s32[1]{0:T(128)} %bitcast.1.me_ref, bf16[6,128,128]{2,1,0:T(8,128)(2,1)S(1)} %collective-permute-done.refs_0_, bf16[6,128,128]{2,1,0:T(8,128)(2,1)S(1)} %collective-permute-done.1.refs_1_, ...), custom_call_target="tpu_custom_call" | custom-call | flops 6710886400 | bytes 8388608 | tf_op jit(solution)/shard_map/convolve/pallas_call | solution.py:181
  44.8 0.0 copy-start
  44.9 0.1 collective-permute-start.7
  45.0 1.5 %collective-permute-done.7 = bf16[4,2,128,128]{3,2,1,0:T(8,128)(2,1)S(1)} collective-permute-done((bf16[4,2,128,128]{3,2,1,0:T(8,128)(2,1)S(1)}, bf16[4,2,128,128]{3,2,1,0:T(8,128)(2,1)S(1)}, u32[]{:S(2)}, u32[]{:S(2)}) %collective-permute-start.7) | collective-permute-done | bytes 262176 | tf_op jit(solution)/shard_map/ppermute | solution.py:333
  46.5 2.0 %collective-permute-start.10 = (bf16[2,2,128,128]{3,2,1,0:T(8,128)(2,1)S(1)}, bf16[2,2,128,128]{3,2,1,0:T(8,128)(2,1)S(1)}, u32[]{:S(2)}, u32[]{:S(2)}) collective-permute-start(bf16[2,2,128,128]{3,2,1,0:T(8,128)(2,1)S(1)} %pad_maximum_fusion.3), channel_id=1, source_target_pairs={{0,24},{4,28},{8,16},{12,20},{16,8},{20,12},{24,0},{28,4},{1,25},{... | collective-permute-start | bytes 393224 | tf_op jit(solution)/shard_map/ppermute | solution.py:333
  48.5 0.1 collective-permute-start.9
  48.6 2.5 %collective-permute-start.8 = (bf16[2,2,128,128]{3,2,1,0:T(8,128)(2,1)S(1)}, bf16[2,2,128,128]{3,2,1,0:T(8,128)(2,1)S(1)}, u32[]{:S(2)}, u32[]{:S(2)}) collective-permute-start(bf16[2,2,128,128]{3,2,1,0:T(8,128)(2,1)S(1)} %pad_maximum_fusion.1), channel_id=1, source_target_pairs={{0,8},{4,12},{8,0},{12,4},{16,24},{20,28},{24,16},{28,20},{1,9},{5... | collective-permute-start | bytes 393224 | tf_op jit(solution)/shard_map/ppermute | solution.py:333
  51.1 3.7 %collective-permute-done.10.refs_3_ = bf16[2,2,128,128]{3,2,1,0:T(8,128)(2,1)S(1)} collective-permute-done((bf16[2,2,128,128]{3,2,1,0:T(8,128)(2,1)S(1)}, bf16[2,2,128,128]{3,2,1,0:T(8,128)(2,1)S(1)}, u32[]{:S(2)}, u32[]{:S(2)}) %collective-permute-start.10) | collective-permute-done | bytes 131104 | tf_op jit(solution)/shard_map/ppermute | solution.py:333
  54.8 4.8 %collective-permute-done.9.refs_2_ = bf16[2,2,128,128]{3,2,1,0:T(8,128)(2,1)S(1)} collective-permute-done((bf16[2,2,128,128]{3,2,1,0:T(8,128)(2,1)S(1)}, bf16[2,2,128,128]{3,2,1,0:T(8,128)(2,1)S(1)}, u32[]{:S(2)}, u32[]{:S(2)}) %collective-permute-start.9) | collective-permute-done | bytes 131104 | tf_op jit(solution)/shard_map/ppermute | solution.py:333
  59.6 0.0 collective-permute-done.8.refs_1_
  59.6 0.5 gate.1
  60.1 0.0 collective-permute-done.11.refs_4_.refs_2_
  60.1 0.0 collective-permute-done.12.refs_6_.refs_4_
  60.1 0.2 collective-permute-start.13
  60.3 0.4 collective-permute-start.18
  60.7 1.5 %collective-permute-start.14 = (bf16[128,1024]{1,0:T(8,128)(2,1)S(1)}, bf16[128,1024]{1,0:T(8,128)(2,1)S(1)}, u32[]{:S(2)}, u32[]{:S(2)}) collective-permute-start(bf16[128,1024]{1,0:T(8,128)(2,1)S(1)} %get-tuple-element.54.refs_0_), channel_id=1, source_target_pairs={{0,1},{1,0},{2,3},{3,2},{4,5},{5,4},{6,7},{7,6},{8,9},{9,8},{10,11... | collective-permute-start | bytes 786440 | tf_op jit(solution)/shard_map/ppermute | solution.py:333
  62.2 1.5 %collective-permute-start.16 = (bf16[128,1024]{1,0:T(8,128)(2,1)S(1)}, bf16[128,1024]{1,0:T(8,128)(2,1)S(1)}, u32[]{:S(2)}, u32[]{:S(2)}) collective-permute-start(bf16[128,1024]{1,0:T(8,128)(2,1)S(1)} %get-tuple-element.54.refs_0_), channel_id=1, source_target_pairs={{0,2},{1,3},{2,0},{3,1},{4,6},{5,7},{6,4},{7,5},{8,10},{9,11},{10,... | collective-permute-start | bytes 786440 | tf_op jit(solution)/shard_map/ppermute | solution.py:333
  63.7 3.1 %own_part.2.own_ref = f32[2,256,1024]{2,1,0:T(8,128)S(1)} custom-call(s32[1]{0:T(128)} %bitcast.2.me_ref, bf16[128,1024]{1,0:T(8,128)(2,1)S(1)} %get-tuple-element.54.refs_0_, bf16[128,1024]{1,0:T(8,128)(2,1)S(1)} %get-tuple-element.61.refs_1_, bf16[1024,8192]{1,0:T(8,128)(2,1)} %refs_3_.3, bf16[1024,8192]{1,0:T(8,128)(2,1)} %refs_3_.3), custom_call_target="tpu_custom_call" | custom-call | flops 1073741824 | bytes 4194304 | tf_op jit(solution)/shard_map/own_part/pallas_call | solution.py:246
  66.7 0.0 collective-permute-done.13.refs_5_.refs_3_
  66.7 0.6 collective-permute-start.15
  67.3 0.6 collective-permute-start.17
  67.9 3.1 %own_part.3.own_ref = f32[2,256,1024]{2,1,0:T(8,128)S(1)} custom-call(s32[1]{0:T(128)} %bitcast.2.me_ref, bf16[128,1024]{1,0:T(8,128)(2,1)S(1)} %get-tuple-element.54.refs_0_, bf16[128,1024]{1,0:T(8,128)(2,1)S(1)} %get-tuple-element.61.refs_1_, bf16[1024,8192]{1,0:T(8,128)(2,1)} %refs_3_.3, bf16[1024,8192]{1,0:T(8,128)(2,1)} %refs_3_.3), custom_call_target="tpu_custom_call" | custom-call | flops 1073741824 | bytes 4194304 | tf_op jit(solution)/shard_map/own_part/pallas_call | solution.py:246
  70.9 0.0 collective-permute-done.14.refs_0_
  71.0 0.2 collective-permute-done.16.refs_2_.refs_1_
  71.2 0.0 collective-permute-done.18.refs_7_.refs_5_
  71.2 1.4 %add_sent.2 = (bf16[128,1024]{1,0:T(8,128)(2,1)S(1)}, bf16[128,1024]{1,0:T(8,128)(2,1)S(1)}) custom-call(s32[1]{0:T(128)} %bitcast.core_ref, f32[2,256,1024]{2,1,0:T(8,128)S(1)} %own_part.2.own_ref, bf16[128,1024]{1,0:T(8,128)(2,1)S(1)} %collective-permute-done.14.refs_0_, bf16[128,1024]{1,0:T(8,128)(2,1)S(1)} %collective-permute-done.16.refs_2_.refs_1_, ...), custom_call_target="tpu_custom_call" | custom-call | flops 536870912 | bytes 4194304 | tf_op jit(solution)/shard_map/add_sent/pallas_call | solution.py:312
  72.6 1.7 %collective-permute-start.19 = (bf16[128,1024]{1,0:T(8,128)(2,1)S(1)}, bf16[128,1024]{1,0:T(8,128)(2,1)S(1)}, u32[]{:S(2)}, u32[]{:S(2)}) collective-permute-start(bf16[128,1024]{1,0:T(8,128)(2,1)S(1)} %get-tuple-element.66), channel_id=1, source_target_pairs={{0,2},{1,3},{2,0},{3,1},{4,6},{5,7},{6,4},{7,5},{8,10},{9,11},{10,... | collective-permute-start | bytes 786440 | tf_op jit(solution)/shard_map/ppermute | solution.py:333
  74.3 1.1 %collective-permute-start.21 = (bf16[128,1024]{1,0:T(8,128)(2,1)S(1)}, bf16[128,1024]{1,0:T(8,128)(2,1)S(1)}, u32[]{:S(2)}, u32[]{:S(2)}) collective-permute-start(bf16[128,1024]{1,0:T(8,128)(2,1)S(1)} %get-tuple-element.69), channel_id=1, source_target_pairs={{0,1},{1,0},{2,3},{3,2},{4,5},{5,4},{6,7},{7,6},{8,9},{9,8},{10,11... | collective-permute-start | bytes 786440 | tf_op jit(solution)/shard_map/ppermute | solution.py:333
  75.4 0.0 collective-permute-done.15.refs_1_.refs_0_
  75.4 1.4 %collective-permute-done.17.refs_3_.refs_1_ = bf16[128,1024]{1,0:T(8,128)(2,1)S(1)} collective-permute-done((bf16[128,1024]{1,0:T(8,128)(2,1)S(1)}, bf16[128,1024]{1,0:T(8,128)(2,1)S(1)}, u32[]{:S(2)}, u32[]{:S(2)}) %collective-permute-start.17) | collective-permute-done | bytes 262176 | tf_op jit(solution)/shard_map/ppermute | solution.py:333
  76.8 1.4 %add_sent.3 = (bf16[128,1024]{1,0:T(8,128)(2,1)S(1)}, bf16[128,1024]{1,0:T(8,128)(2,1)S(1)}) custom-call(s32[1]{0:T(128)} %bitcast.core_ref, f32[2,256,1024]{2,1,0:T(8,128)S(1)} %own_part.2.own_ref, bf16[128,1024]{1,0:T(8,128)(2,1)S(1)} %collective-permute-done.15.refs_1_.refs_0_, bf16[128,1024]{1,0:T(8,128)(2,1)S(1)} %collective-permute-done.17.refs_3_.refs_1_, ...), custom_call_target="tpu_custom_call" | custom-call | flops 536870912 | bytes 4194304 | tf_op jit(solution)/shard_map/add_sent/pallas_call | solution.py:312
  78.2 1.7 %collective-permute-start.20 = (bf16[128,1024]{1,0:T(8,128)(2,1)S(1)}, bf16[128,1024]{1,0:T(8,128)(2,1)S(1)}, u32[]{:S(2)}, u32[]{:S(2)}) collective-permute-start(bf16[128,1024]{1,0:T(8,128)(2,1)S(1)} %get-tuple-element.68), channel_id=1, source_target_pairs={{0,2},{1,3},{2,0},{3,1},{4,6},{5,7},{6,4},{7,5},{8,10},{9,11},{10,... | collective-permute-start | bytes 786440 | tf_op jit(solution)/shard_map/ppermute | solution.py:333
  79.9 0.2 collective-permute-start.22
  80.1 1.9 %add_kept.1 = (f32[256,1024]{1,0:T(8,128)S(1)}, f32[256,1024]{1,0:T(8,128)S(1)}) custom-call(s32[1]{0:T(128)} %bitcast.core_ref, f32[2,256,1024]{2,1,0:T(8,128)S(1)} %own_part.3.own_ref, bf16[128,1024]{1,0:T(8,128)(2,1)S(1)} %collective-permute-done.14.refs_0_, bf16[128,1024]{1,0:T(8,128)(2,1)S(1)} %collective-permute-done.15.refs_1_.refs_0_, ...), custom_call_target="tpu_custom_call" | custom-call | flops 1073741824 | bytes 4194304 | tf_op jit(solution)/shard_map/add_kept/pallas_call | solution.py:312
  82.0 0.4 collective-permute-done.19
  82.4 0.0 collective-permute-done.21
  82.4 4.7 %collective-permute-done.20 = bf16[128,1024]{1,0:T(8,128)(2,1)S(1)} collective-permute-done((bf16[128,1024]{1,0:T(8,128)(2,1)S(1)}, bf16[128,1024]{1,0:T(8,128)(2,1)S(1)}, u32[]{:S(2)}, u32[]{:S(2)}) %collective-permute-start.20) | collective-permute-done | bytes 262176 | tf_op jit(solution)/shard_map/ppermute | solution.py:333
  87.1 0.0 collective-permute-done.22
  87.1 1.3 %fusion = bf16[256,2048]{1,0:T(8,128)(2,1)} fusion(f32[256,1024]{1,0:T(8,128)S(1)} %get-tuple-element.65, f32[256,1024]{1,0:T(8,128)S(1)} %get-tuple-element.64, bf16[128,1024]{1,0:T(8,128)(2,1)S(1)} %collective-permute-done.22, bf16[128,1024]{1,0:T(8,128)(2,1)S(1)} %collective-permute-done.21, bf16[128,1024]{1,0:T(8,128)(2,1)S(1)} %collective-permute-done.20, ...), kind=kLoop, calls=%fused_computation.1 | loop fusion | flops 5767168 | bytes 4194304 | tf_op jit(solution)/shard_map/convert_element_type | solution.py:379
  (23 shorter events, 0.1 us)
Async XLA Ops:
  3.2 12.3 %collective-permute-start = (bf16[6,128,128]{2,1,0:T(8,128)(2,1)}, bf16[6,128,128]{2,1,0:T(8,128)(2,1)S(1)}, u32[]{:S(2)}, u32[]{:S(2)}) collective-permute-start(bf16[6,128,128]{2,1,0:T(8,128)(2,1)} %get-tuple-element.42), channel_id=1, source_target_pairs={{0,24},{4,28},{8,16},{12,20},{16,8},{20,12},{24,0},{28,4},{1,25},{... | collective-permute-start | bytes 589832 | tf_op jit(solution)/shard_map/ppermute | solution.py:333
  8.4 6.4 %copy-start.11 = (bf16[6,128,128]{2,1,0:T(8,128)(2,1)S(1)}, bf16[6,128,128]{2,1,0:T(8,128)(2,1)}, u32[]{:S(2)}) copy-start(bf16[6,128,128]{2,1,0:T(8,128)(2,1)} %get-tuple-element.44) | copy-start | bytes 589828
  8.4 6.4 %copy-start.10 = (bf16[6,128,128]{2,1,0:T(8,128)(2,1)S(1)}, bf16[6,128,128]{2,1,0:T(8,128)(2,1)}, u32[]{:S(2)}) copy-start(bf16[6,128,128]{2,1,0:T(8,128)(2,1)} %get-tuple-element.45) | copy-start | bytes 589828
  8.4 7.2 %copy-start.9 = (bf16[6,128,128]{2,1,0:T(8,128)(2,1)S(1)}, bf16[6,128,128]{2,1,0:T(8,128)(2,1)}, u32[]{:S(2)}) copy-start(bf16[6,128,128]{2,1,0:T(8,128)(2,1)} %get-tuple-element.46) | copy-start | bytes 589828
  8.4 21.4 %copy-start.8 = (bf16[6,128,128]{2,1,0:T(8,128)(2,1)S(1)}, bf16[6,128,128]{2,1,0:T(8,128)(2,1)}, u32[]{:S(2)}) copy-start(bf16[6,128,128]{2,1,0:T(8,128)(2,1)} %get-tuple-element.47) | copy-start | bytes 589828
  8.4 21.4 %copy-start.7 = (bf16[6,128,128]{2,1,0:T(8,128)(2,1)S(1)}, bf16[6,128,128]{2,1,0:T(8,128)(2,1)}, u32[]{:S(2)}) copy-start(bf16[6,128,128]{2,1,0:T(8,128)(2,1)} %get-tuple-element.48) | copy-start | bytes 589828
  8.4 24.9 %copy-start.6 = (bf16[6,128,128]{2,1,0:T(8,128)(2,1)S(1)}, bf16[6,128,128]{2,1,0:T(8,128)(2,1)}, u32[]{:S(2)}) copy-start(bf16[6,128,128]{2,1,0:T(8,128)(2,1)} %get-tuple-element.49) | copy-start | bytes 589828
  8.4 33.7 %copy-start.1 = (bf16[6,128,128]{2,1,0:T(8,128)(2,1)S(1)}, bf16[6,128,128]{2,1,0:T(8,128)(2,1)}, u32[]{:S(2)}) copy-start(bf16[6,128,128]{2,1,0:T(8,128)(2,1)} %get-tuple-element.50.refs_7_) | copy-start | bytes 589828
  8.4 33.7 %copy-start.2 = (bf16[1024,1024]{1,0:T(8,128)(2,1)S(1)}, bf16[1024,1024]{1,0:T(8,128)(2,1)}, u32[]{:S(2)}) copy-start(bf16[1024,1024]{1,0:T(8,128)(2,1)} %constant.31.clone.refs_8_) | copy-start | bytes 6291460
  8.4 33.6 %copy-start.3 = (bf16[1024,1024]{1,0:T(8,128)(2,1)S(1)}, bf16[1024,1024]{1,0:T(8,128)(2,1)}, u32[]{:S(2)}) copy-start(bf16[1024,1024]{1,0:T(8,128)(2,1)} %constant.32.clone.refs_9_) | copy-start | bytes 6291460
  8.5 33.6 %copy-start.4 = (f32[1024,128]{1,0:T(8,128)S(1)}, f32[1024,128]{1,0:T(8,128)}, u32[]{:S(2)}) copy-start(f32[1024,128]{1,0:T(8,128)} %constant.33.clone.refs_10_) | copy-start | bytes 1572868
  8.5 33.6 %copy-start.5 = (f32[1024,128]{1,0:T(8,128)S(1)}, f32[1024,128]{1,0:T(8,128)}, u32[]{:S(2)}) copy-start(f32[1024,128]{1,0:T(8,128)} %constant.34.clone.refs_11_) | copy-start | bytes 1572868
  11.7 48.4 %collective-permute-start.11 = (bf16[1024,1024]{1,0:T(8,128)(2,1)S(1)}, bf16[1024,1024]{1,0:T(8,128)(2,1)S(1)}, u32[]{:S(2)}, u32[]{:S(2)}) collective-permute-start(bf16[1024,1024]{1,0:T(8,128)(2,1)S(1)} %get-tuple-element.56), channel_id=1, source_target_pairs={{0,1},{1,0},{2,3},{3,2},{4,5},{5,4},{6,7},{7,6},{8,9},{9,8},{10,11... | collective-permute-start | bytes 6291464 | tf_op jit(solution)/shard_map/ppermute | solution.py:333
  13.2 46.9 %collective-permute-start.12 = (bf16[1024,1024]{1,0:T(8,128)(2,1)S(1)}, bf16[1024,1024]{1,0:T(8,128)(2,1)S(1)}, u32[]{:S(2)}, u32[]{:S(2)}) collective-permute-start(bf16[1024,1024]{1,0:T(8,128)(2,1)S(1)} %get-tuple-element.57), channel_id=1, source_target_pairs={{0,2},{1,3},{2,0},{3,1},{4,6},{5,7},{6,4},{7,5},{8,10},{9,11},{10,... | collective-permute-start | bytes 6291464 | tf_op jit(solution)/shard_map/ppermute | solution.py:333
  14.8 15.1 %collective-permute-start.1 = (bf16[6,128,128]{2,1,0:T(8,128)(2,1)S(1)}, bf16[6,128,128]{2,1,0:T(8,128)(2,1)S(1)}, u32[]{:S(2)}, u32[]{:S(2)}) collective-permute-start(bf16[6,128,128]{2,1,0:T(8,128)(2,1)S(1)} %copy-done.11), channel_id=1, source_target_pairs={{0,16},{4,20},{8,24},{12,28},{16,0},{20,4},{24,8},{28,12},{1,17},{... | collective-permute-start | bytes 589832 | tf_op jit(solution)/shard_map/ppermute | solution.py:333
  14.8 15.1 %collective-permute-start.2 = (bf16[6,128,128]{2,1,0:T(8,128)(2,1)S(1)}, bf16[6,128,128]{2,1,0:T(8,128)(2,1)S(1)}, u32[]{:S(2)}, u32[]{:S(2)}) collective-permute-start(bf16[6,128,128]{2,1,0:T(8,128)(2,1)S(1)} %copy-done.10), channel_id=1, source_target_pairs={{0,8},{4,12},{8,0},{12,4},{16,24},{20,28},{24,16},{28,20},{1,9},{5... | collective-permute-start | bytes 589832 | tf_op jit(solution)/shard_map/ppermute | solution.py:333
  15.6 17.8 %collective-permute-start.3 = (bf16[6,128,128]{2,1,0:T(8,128)(2,1)S(1)}, bf16[6,128,128]{2,1,0:T(8,128)(2,1)S(1)}, u32[]{:S(2)}, u32[]{:S(2)}) collective-permute-start(bf16[6,128,128]{2,1,0:T(8,128)(2,1)S(1)} %copy-done.9), channel_id=1, source_target_pairs={{0,28},{4,24},{8,20},{12,16},{16,12},{20,8},{24,4},{28,0},{1,29},{... | collective-permute-start | bytes 589832 | tf_op jit(solution)/shard_map/ppermute | solution.py:333
  29.8 12.3 %collective-permute-start.4 = (bf16[6,128,128]{2,1,0:T(8,128)(2,1)S(1)}, bf16[6,128,128]{2,1,0:T(8,128)(2,1)S(1)}, u32[]{:S(2)}, u32[]{:S(2)}) collective-permute-start(bf16[6,128,128]{2,1,0:T(8,128)(2,1)S(1)} %copy-done.8), channel_id=1, source_target_pairs={{0,20},{4,16},{8,28},{12,24},{16,4},{20,0},{24,12},{28,8},{1,21},{... | collective-permute-start | bytes 589832 | tf_op jit(solution)/shard_map/ppermute | solution.py:333
  29.8 12.2 %collective-permute-start.5 = (bf16[6,128,128]{2,1,0:T(8,128)(2,1)S(1)}, bf16[6,128,128]{2,1,0:T(8,128)(2,1)S(1)}, u32[]{:S(2)}, u32[]{:S(2)}) collective-permute-start(bf16[6,128,128]{2,1,0:T(8,128)(2,1)S(1)} %copy-done.7), channel_id=1, source_target_pairs={{0,12},{4,8},{8,4},{12,0},{16,28},{20,24},{24,20},{28,16},{1,13},{... | collective-permute-start | bytes 589832 | tf_op jit(solution)/shard_map/ppermute | solution.py:333
  33.4 8.7 %collective-permute-start.6 = (bf16[6,128,128]{2,1,0:T(8,128)(2,1)S(1)}, bf16[6,128,128]{2,1,0:T(8,128)(2,1)S(1)}, u32[]{:S(2)}, u32[]{:S(2)}) collective-permute-start(bf16[6,128,128]{2,1,0:T(8,128)(2,1)S(1)} %copy-done.6), channel_id=1, source_target_pairs={{0,4},{4,0},{8,12},{12,8},{16,20},{20,16},{24,28},{28,24},{1,5},{5... | collective-permute-start | bytes 589832 | tf_op jit(solution)/shard_map/ppermute | solution.py:333
  44.8 14.8 %copy-start = (bf16[256,1024]{1,0:T(8,128)(2,1)S(1)}, bf16[256,1024]{1,0:T(8,128)(2,1)}, u32[]{:S(2)}) copy-start(bf16[256,1024]{1,0:T(8,128)(2,1)} %refs_4_.1) | copy-start | bytes 1572868
  44.9 1.6 %collective-permute-start.7 = (bf16[4,2,128,128]{3,2,1,0:T(8,128)(2,1)S(1)}, bf16[4,2,128,128]{3,2,1,0:T(8,128)(2,1)S(1)}, u32[]{:S(2)}, u32[]{:S(2)}) collective-permute-start(bf16[4,2,128,128]{3,2,1,0:T(8,128)(2,1)S(1)} %get-tuple-element.52), channel_id=1, source_target_pairs={{0,4},{4,0},{8,12},{12,8},{16,20},{20,16},{24,28},{28,24},{1,5},{5... | collective-permute-start | bytes 786440 | tf_op jit(solution)/shard_map/ppermute | solution.py:333
  46.5 8.3 %collective-permute-start.10 = (bf16[2,2,128,128]{3,2,1,0:T(8,128)(2,1)S(1)}, bf16[2,2,128,128]{3,2,1,0:T(8,128)(2,1)S(1)}, u32[]{:S(2)}, u32[]{:S(2)}) collective-permute-start(bf16[2,2,128,128]{3,2,1,0:T(8,128)(2,1)S(1)} %pad_maximum_fusion.3), channel_id=1, source_target_pairs={{0,24},{4,28},{8,16},{12,20},{16,8},{20,12},{24,0},{28,4},{1,25},{... | collective-permute-start | bytes 393224 | tf_op jit(solution)/shard_map/ppermute | solution.py:333
  48.5 11.1 %collective-permute-start.9 = (bf16[2,2,128,128]{3,2,1,0:T(8,128)(2,1)S(1)}, bf16[2,2,128,128]{3,2,1,0:T(8,128)(2,1)S(1)}, u32[]{:S(2)}, u32[]{:S(2)}) collective-permute-start(bf16[2,2,128,128]{3,2,1,0:T(8,128)(2,1)S(1)} %pad_maximum_fusion.2), channel_id=1, source_target_pairs={{0,16},{4,20},{8,24},{12,28},{16,0},{20,4},{24,8},{28,12},{1,17},{... | collective-permute-start | bytes 393224 | tf_op jit(solution)/shard_map/ppermute | solution.py:333
  48.6 11.0 %collective-permute-start.8 = (bf16[2,2,128,128]{3,2,1,0:T(8,128)(2,1)S(1)}, bf16[2,2,128,128]{3,2,1,0:T(8,128)(2,1)S(1)}, u32[]{:S(2)}, u32[]{:S(2)}) collective-permute-start(bf16[2,2,128,128]{3,2,1,0:T(8,128)(2,1)S(1)} %pad_maximum_fusion.1), channel_id=1, source_target_pairs={{0,8},{4,12},{8,0},{12,4},{16,24},{20,28},{24,16},{28,20},{1,9},{5... | collective-permute-start | bytes 393224 | tf_op jit(solution)/shard_map/ppermute | solution.py:333
  60.1 6.6 %collective-permute-start.13 = (bf16[1024,1024]{1,0:T(8,128)(2,1)S(1)}, bf16[1024,1024]{1,0:T(8,128)(2,1)S(1)}, u32[]{:S(2)}, u32[]{:S(2)}) collective-permute-start(bf16[1024,1024]{1,0:T(8,128)(2,1)S(1)} %collective-permute-done.11.refs_4_.refs_2_), channel_id=1, source_target_pairs={{0,4},{4,0},{8,12},{12,8},{16,20},{20,16},{24,28},{28,24},{1,5},{5... | collective-permute-start | bytes 6291464 | tf_op jit(solution)/shard_map/ppermute | solution.py:333
  60.3 10.9 %collective-permute-start.18 = (bf16[1024,1024]{1,0:T(8,128)(2,1)S(1)}, bf16[1024,1024]{1,0:T(8,128)(2,1)S(1)}, u32[]{:S(2)}, u32[]{:S(2)}) collective-permute-start(bf16[1024,1024]{1,0:T(8,128)(2,1)S(1)} %collective-permute-done.12.refs_6_.refs_4_), channel_id=1, source_target_pairs={{0,4},{4,0},{8,12},{12,8},{16,20},{20,16},{24,28},{28,24},{1,5},{5... | collective-permute-start | bytes 6291464 | tf_op jit(solution)/shard_map/ppermute | solution.py:333
  60.7 10.2 %collective-permute-start.14 = (bf16[128,1024]{1,0:T(8,128)(2,1)S(1)}, bf16[128,1024]{1,0:T(8,128)(2,1)S(1)}, u32[]{:S(2)}, u32[]{:S(2)}) collective-permute-start(bf16[128,1024]{1,0:T(8,128)(2,1)S(1)} %get-tuple-element.54.refs_0_), channel_id=1, source_target_pairs={{0,1},{1,0},{2,3},{3,2},{4,5},{5,4},{6,7},{7,6},{8,9},{9,8},{10,11... | collective-permute-start | bytes 786440 | tf_op jit(solution)/shard_map/ppermute | solution.py:333
  62.2 9.0 %collective-permute-start.16 = (bf16[128,1024]{1,0:T(8,128)(2,1)S(1)}, bf16[128,1024]{1,0:T(8,128)(2,1)S(1)}, u32[]{:S(2)}, u32[]{:S(2)}) collective-permute-start(bf16[128,1024]{1,0:T(8,128)(2,1)S(1)} %get-tuple-element.54.refs_0_), channel_id=1, source_target_pairs={{0,2},{1,3},{2,0},{3,1},{4,6},{5,7},{6,4},{7,5},{8,10},{9,11},{10,... | collective-permute-start | bytes 786440 | tf_op jit(solution)/shard_map/ppermute | solution.py:333
  66.7 8.7 %collective-permute-start.15 = (bf16[128,1024]{1,0:T(8,128)(2,1)S(1)}, bf16[128,1024]{1,0:T(8,128)(2,1)S(1)}, u32[]{:S(2)}, u32[]{:S(2)}) collective-permute-start(bf16[128,1024]{1,0:T(8,128)(2,1)S(1)} %get-tuple-element.61.refs_1_), channel_id=1, source_target_pairs={{0,1},{1,0},{2,3},{3,2},{4,5},{5,4},{6,7},{7,6},{8,9},{9,8},{10,11... | collective-permute-start | bytes 786440 | tf_op jit(solution)/shard_map/ppermute | solution.py:333
  67.3 9.5 %collective-permute-start.17 = (bf16[128,1024]{1,0:T(8,128)(2,1)S(1)}, bf16[128,1024]{1,0:T(8,128)(2,1)S(1)}, u32[]{:S(2)}, u32[]{:S(2)}) collective-permute-start(bf16[128,1024]{1,0:T(8,128)(2,1)S(1)} %get-tuple-element.61.refs_1_), channel_id=1, source_target_pairs={{0,2},{1,3},{2,0},{3,1},{4,6},{5,7},{6,4},{7,5},{8,10},{9,11},{10,... | collective-permute-start | bytes 786440 | tf_op jit(solution)/shard_map/ppermute | solution.py:333
  72.6 9.9 %collective-permute-start.19 = (bf16[128,1024]{1,0:T(8,128)(2,1)S(1)}, bf16[128,1024]{1,0:T(8,128)(2,1)S(1)}, u32[]{:S(2)}, u32[]{:S(2)}) collective-permute-start(bf16[128,1024]{1,0:T(8,128)(2,1)S(1)} %get-tuple-element.66), channel_id=1, source_target_pairs={{0,2},{1,3},{2,0},{3,1},{4,6},{5,7},{6,4},{7,5},{8,10},{9,11},{10,... | collective-permute-start | bytes 786440 | tf_op jit(solution)/shard_map/ppermute | solution.py:333
  74.3 8.1 %collective-permute-start.21 = (bf16[128,1024]{1,0:T(8,128)(2,1)S(1)}, bf16[128,1024]{1,0:T(8,128)(2,1)S(1)}, u32[]{:S(2)}, u32[]{:S(2)}) collective-permute-start(bf16[128,1024]{1,0:T(8,128)(2,1)S(1)} %get-tuple-element.69), channel_id=1, source_target_pairs={{0,1},{1,0},{2,3},{3,2},{4,5},{5,4},{6,7},{7,6},{8,9},{9,8},{10,11... | collective-permute-start | bytes 786440 | tf_op jit(solution)/shard_map/ppermute | solution.py:333
  78.2 8.9 %collective-permute-start.20 = (bf16[128,1024]{1,0:T(8,128)(2,1)S(1)}, bf16[128,1024]{1,0:T(8,128)(2,1)S(1)}, u32[]{:S(2)}, u32[]{:S(2)}) collective-permute-start(bf16[128,1024]{1,0:T(8,128)(2,1)S(1)} %get-tuple-element.68), channel_id=1, source_target_pairs={{0,2},{1,3},{2,0},{3,1},{4,6},{5,7},{6,4},{7,5},{8,10},{9,11},{10,... | collective-permute-start | bytes 786440 | tf_op jit(solution)/shard_map/ppermute | solution.py:333
  79.9 7.2 %collective-permute-start.22 = (bf16[128,1024]{1,0:T(8,128)(2,1)S(1)}, bf16[128,1024]{1,0:T(8,128)(2,1)S(1)}, u32[]{:S(2)}, u32[]{:S(2)}) collective-permute-start(bf16[128,1024]{1,0:T(8,128)(2,1)S(1)} %get-tuple-element.70), channel_id=1, source_target_pairs={{0,1},{1,0},{2,3},{3,2},{4,5},{5,4},{6,7},{7,6},{8,9},{9,8},{10,11... | collective-permute-start | bytes 786440 | tf_op jit(solution)/shard_map/ppermute | solution.py:333

commit v7 on v6

--- a/solution.py
+++ b/solution.py
@@ -194,10 +194,10 @@
 
 
 def gate_kernel(chips, me_ref, *refs):
-    held, gate_ref, outs, conv_ref = refs[:chips], refs[chips], refs[chips + 1:-1], refs[-1]
+    held, (gate_ref, *outs, conv_ref) = refs[:len(chips)], refs[len(chips):]
     _, span, block_rows, _ = held[0].shape
     rows = span * block_rows
-    for flip, ref in enumerate(held):
+    for flip, ref in zip(chips, held):
         for core in range(2):
             share = me_ref[0] ^ (2 * flip + core)
             conv_ref[:, pl.ds(pl.multiple_of(share * LANES, LANES), LANES)] = ref[core].reshape(rows, LANES)
@@ -208,11 +208,11 @@
         out_ref[...] = gated[p * part:(p + 1) * part]
 
 
-def gate(me, held, gate_out, parts):
+def gate(me, held, chips, gate_out, parts):
     rows, width = gate_out.shape
     vmem = pl.BlockSpec(memory_space=pltpu.VMEM)
     return pl.pallas_call(
-        functools.partial(gate_kernel, len(held)),
+        functools.partial(gate_kernel, chips),
         in_specs=[pl.BlockSpec(memory_space=pltpu.SMEM)] + [vmem] * (len(held) + 1),
         out_specs=[vmem] * parts,
         out_shape=[jax.ShapeDtypeStruct((rows // parts, width), jnp.bfloat16)] * parts,
@@ -329,6 +329,31 @@
     )(core, own, *moved_x, *moved_y, *weights)
 
 
+def finish_kernel(kept_a_ref, kept_b_ref, sum_a_ref, sum_b_ref, *refs):
+    out_ref = refs[-1]
+    cols = kept_a_ref.shape[1]
+    out_ref[:, :cols] = (kept_a_ref[...] + sum_a_ref[...].astype(jnp.float32)).astype(out_ref.dtype)
+    out_ref[:, cols:] = (kept_b_ref[...] + sum_b_ref[...].astype(jnp.float32)).astype(out_ref.dtype)
+
+
+def finish(kept_a, kept_b, sum_a, sum_b, part, before):
+    rows, cols = sum_a.shape
+    total = kept_a.shape[0]
+    kept = pl.BlockSpec((rows, cols), lambda i: (part, 0))
+    sums = pl.BlockSpec((rows, cols), lambda i: (0, 0))
+    earlier = [] if before is None else [before]
+    return pl.pallas_call(
+        finish_kernel,
+        grid=(1,),
+        in_specs=[kept, kept, sums, sums] + [pl.BlockSpec(memory_space=pl.ANY)] * len(earlier),
+        out_specs=pl.BlockSpec((rows, 2 * cols), lambda i: (part, 0)),
+        out_shape=jax.ShapeDtypeStruct((total, 2 * cols), jnp.bfloat16),
+        input_output_aliases={4: 0} if earlier else {},
+        compiler_params=pltpu.CompilerParams(vmem_limit_bytes=16 << 20),
+        name="finish",
+    )(kept_a, kept_b, sum_a, sum_b, *earlier)
+
+
 def swap(data, axis, flip):
     return lax.ppermute(data, axis, [(i, i ^ flip) for i in range(lax.axis_size(axis))])
 
@@ -353,8 +378,9 @@
     mine, other = convolve(here.reshape(1), [data[m] for m in order], order)
     other = swap(other, "seq", 1)
     held = [jnp.stack([mine[flip], other[flip]]) for flip in range(seq_count // 2)]
-    held = [swap(both, "seq", 2 * flip) if flip else both for flip, both in enumerate(held)]
-    gated = gate(here.reshape(1), held, gate_out, parts)
+    chips = tuple(reversed(range(seq_count // 2)))
+    held = [swap(held[flip], "seq", 2 * flip) if flip else held[flip] for flip in chips]
+    gated = gate(here.reshape(1), held, chips, gate_out, parts)
     weight_x, weight_y, _ = lax.optimization_barrier((weight_x, weight_y, gated))
     weights = [weight_x, swap(weight_x, "seq", 1), weight_y, swap(weight_y, "seq", 1)]
     own = own_part(me.reshape(1), gated, out_weight, ((2, 0), (1, 1)))
@@ -375,8 +401,10 @@
         sums_a.append(swap(sent[0], "chan", 2))
         sums_b.append(swap(sent[1], "chan", 1))
     kept_a, kept_b = add_moved(core, own_kept, moved_x, moved_y, weights, 0, True, jnp.float32)
-    sums = jnp.concatenate([jnp.concatenate(sums_a, axis=0), jnp.concatenate(sums_b, axis=0)], axis=1)
-    return (jnp.concatenate([kept_a, kept_b], axis=1) + sums.astype(jnp.float32)).astype(jnp.bfloat16)
+    mixed = None
+    for p in range(parts):
+        mixed = finish(kept_a, kept_b, sums_a[p], sums_b[p], p, mixed)
+    return mixed
 
 
 def to_columns(data):

time: 88.5 us -> 88.1 us (level)
  Pallas kernels: 20.3 us -> 22.1 us
  other arithmetic: 1.4 us -> 0.13 us
  waiting for transfers between devices: 38.1 us -> 36.9 us
    pallas_call x1 -> x3, Pallas kernels: 0.45 us -> 2.32 us  [the longest x2 1.86 us: finish(): pl.pallas_call(finish_kernel, grid=(1,), in_specs=[kept, kept, sums, sums...]
    convert_element_type x1 -> x0, other arithmetic: 1.26 us -> none  [by_channels(): (jnp.concatenate([kept_a, kept_b], axis=1) + sums.astype(jnp.float32)).as...]
    ppermute x23, waiting for transfers between devices: 38.1 us -> 36.9 us  [swap(): lax.ppermute(data, axis, [(i, i ^ flip) for i in range(lax.axis_size(axis...]
  transfers between devices with their start and end apart: 23 -> 23, of which waited for: 9 -> 10; matrix products, arithmetic and copies ran while one was open for 0% -> 0% of each run, Pallas kernels for 19% -> 20%
where the time goes in v7:
time: 88.1 us; the launch traced here: 88 us
  waiting for transfers between devices  36.9 us (42%)
  starting transfers between devices  28.4 us (32%)
  Pallas kernels  22.1 us (25%)
    ppermute x23, waiting for transfers between devices, swap(): lax.ppermute(data, axis, [(i, i ^ flip) for i in range(lax.axis_size(axis...  36.9 us
    ppermute x23, starting transfers between devices, swap(): lax.ppermute(data, axis, [(i, i ^ flip) for i in range(lax.axis_size(axis...  28.4 us
    pallas_call x2, Pallas kernels, own_part(): pl.pallas_call(own_kernel, grid_spec=pltpu.PrefetchScalarGridSpec(num_sca...  6.1 us
    pallas_call x3, Pallas kernels, add_moved(): pl.pallas_call(functools.partial(add_kernel, parts, kept), grid=(1,), in_...  4.64 us
    pallas_call x1, Pallas kernels, pack(): pl.pallas_call(functools.partial(pack_kernel, span), in_specs=[pl.BlockSp...  3.19 us
    pallas_call x1, Pallas kernels, take_blocks(): pl.pallas_call(take_kernel, in_specs=[pl.BlockSpec(memory_space=pltpu.SME...  3.19 us
    pallas_call x1, Pallas kernels, convolve(): pl.pallas_call(functools.partial(conv_kernel, order), in_specs=[pl.BlockS...  2.71 us
    pallas_call x2, Pallas kernels, finish(): pl.pallas_call(finish_kernel, grid=(1,), in_specs=[kept, kept, sums, sums...  1.86 us
  transfers between devices with their start and end apart: 23, of which 10 were waited for; matrix products, arithmetic and copies ran while one was open for 0% of the time, Pallas kernels for 20%

profile of v7, /device:TPU:0, one launch (start us, length us, event | category | flops | bytes accessed | tf_op | source)
XLA Modules:
  0.0 88.0 jit_solution(4494438796403608238)
XLA Ops:
  0.0 3.2 %pack.1 = (bf16[6,128,128]{2,1,0:T(8,128)(2,1)}, bf16[6,128,128]{2,1,0:T(8,128)(2,1)}, bf16[6,128,128]{2,1,0:T(8,128)(2,1)}, bf16[6,128,128]{2,1,0:T(8,128)(2,1)...) custom-call(s32[1]{0:T(128)} %bitcast.1.me_ref, ...), custom_call_target="tpu_custom_call" | custom-call | tf_op jit(solution)/shard_map/pack/pallas_call | solution.py:79
  3.2 5.1 %collective-permute-start = (bf16[6,128,128]{2,1,0:T(8,128)(2,1)}, bf16[6,128,128]{2,1,0:T(8,128)(2,1)S(1)}, u32[]{:S(2)}, u32[]{:S(2)}) collective-permute-start(bf16[6,128,128]{2,1,0:T(8,128)(2,1)} %get-tuple-element.42), channel_id=1, source_target_pairs={{0,24},{4,28},{8,16},{12,20},{16,8},{20,12},{24,0},{28,4},{1,25},{... | collective-permute-start | bytes 589832 | tf_op jit(solution)/shard_map/ppermute | solution.py:358
  8.3 0.1 pad_add_fusion.places_ref
  8.4 0.0 copy-start.1
  8.4 0.0 copy-start.2
  8.4 0.0 copy-start.3
  8.5 0.0 copy-start.4
  8.5 0.0 copy-start.5
  8.5 3.2 %take_blocks.1 = (bf16[1024,1024]{1,0:T(8,128)(2,1)S(1)}, bf16[1024,1024]{1,0:T(8,128)(2,1)S(1)}) custom-call(s32[2]{0:T(128)S(1)} %pad_add_fusion.places_ref, bf16[1024,8192]{1,0:T(8,128)(2,1)} %refs_3_.3), custom_call_target="tpu_custom_call" | custom-call | bytes 134217728 | tf_op jit(solution)/shard_map/take_blocks/pallas_call | solution.py:117
  11.7 1.6 %collective-permute-start.11 = (bf16[1024,1024]{1,0:T(8,128)(2,1)S(1)}, bf16[1024,1024]{1,0:T(8,128)(2,1)S(1)}, u32[]{:S(2)}, u32[]{:S(2)}) collective-permute-start(bf16[1024,1024]{1,0:T(8,128)(2,1)S(1)} %get-tuple-element.56), channel_id=1, source_target_pairs={{0,1},{1,0},{2,3},{3,2},{4,5},{5,4},{6,7},{7,6},{8,9},{9,8},{10,11... | collective-permute-start | bytes 6291464 | tf_op jit(solution)/shard_map/ppermute | solution.py:358
  13.2 1.5 %collective-permute-start.12 = (bf16[1024,1024]{1,0:T(8,128)(2,1)S(1)}, bf16[1024,1024]{1,0:T(8,128)(2,1)S(1)}, u32[]{:S(2)}, u32[]{:S(2)}) collective-permute-start(bf16[1024,1024]{1,0:T(8,128)(2,1)S(1)} %get-tuple-element.57), channel_id=1, source_target_pairs={{0,2},{1,3},{2,0},{3,1},{4,6},{5,7},{6,4},{7,5},{8,10},{9,11},{10,... | collective-permute-start | bytes 6291464 | tf_op jit(solution)/shard_map/ppermute | solution.py:358
  14.8 0.0 collective-permute-start.1
  14.8 0.8 collective-permute-start.2
  15.5 0.0 collective-permute-done.refs_0_
  15.6 1.6 %collective-permute-start.3 = (bf16[6,128,128]{2,1,0:T(8,128)(2,1)S(1)}, bf16[6,128,128]{2,1,0:T(8,128)(2,1)S(1)}, u32[]{:S(2)}, u32[]{:S(2)}) collective-permute-start(bf16[6,128,128]{2,1,0:T(8,128)(2,1)S(1)} %copy-done.9), channel_id=1, source_target_pairs={{0,28},{4,24},{8,20},{12,16},{16,12},{20,8},{24,4},{28,0},{1,29},{... | collective-permute-start | bytes 589832 | tf_op jit(solution)/shard_map/ppermute | solution.py:358
  17.2 12.6 %collective-permute-done.1.refs_1_ = bf16[6,128,128]{2,1,0:T(8,128)(2,1)S(1)} collective-permute-done((bf16[6,128,128]{2,1,0:T(8,128)(2,1)S(1)}, bf16[6,128,128]{2,1,0:T(8,128)(2,1)S(1)}, u32[]{:S(2)}, u32[]{:S(2)}) %collective-permute-start.1) | collective-permute-done | bytes 196640 | tf_op jit(solution)/shard_map/ppermute | solution.py:358
  29.8 0.0 collective-permute-start.4
  29.8 0.0 collective-permute-done.2.refs_2_
  29.8 3.5 %collective-permute-start.5 = (bf16[6,128,128]{2,1,0:T(8,128)(2,1)S(1)}, bf16[6,128,128]{2,1,0:T(8,128)(2,1)S(1)}, u32[]{:S(2)}, u32[]{:S(2)}) collective-permute-start(bf16[6,128,128]{2,1,0:T(8,128)(2,1)S(1)} %copy-done.7), channel_id=1, source_target_pairs={{0,12},{4,8},{8,4},{12,0},{16,28},{20,24},{24,20},{28,16},{1,13},{... | collective-permute-start | bytes 589832 | tf_op jit(solution)/shard_map/ppermute | solution.py:358
  33.3 0.0 collective-permute-done.3.refs_3_
  33.4 0.0 collective-permute-start.6
  33.4 8.7 %collective-permute-done.4.refs_4_ = bf16[6,128,128]{2,1,0:T(8,128)(2,1)S(1)} collective-permute-done((bf16[6,128,128]{2,1,0:T(8,128)(2,1)S(1)}, bf16[6,128,128]{2,1,0:T(8,128)(2,1)S(1)}, u32[]{:S(2)}, u32[]{:S(2)}) %collective-permute-start.4) | collective-permute-done | bytes 196640 | tf_op jit(solution)/shard_map/ppermute | solution.py:358
  42.1 0.0 collective-permute-done.5.refs_5_
  42.1 0.0 collective-permute-done.6.refs_6_
  42.1 2.7 %convolve.1 = (bf16[4,2,128,128]{3,2,1,0:T(8,128)(2,1)S(1)}, bf16[4,2,128,128]{3,2,1,0:T(8,128)(2,1)S(1)}) custom-call(s32[1]{0:T(128)} %bitcast.1.me_ref, bf16[6,128,128]{2,1,0:T(8,128)(2,1)S(1)} %collective-permute-done.refs_0_, bf16[6,128,128]{2,1,0:T(8,128)(2,1)S(1)} %collective-permute-done.1.refs_1_, ...), custom_call_target="tpu_custom_call" | custom-call | flops 6710886400 | bytes 8388608 | tf_op jit(solution)/shard_map/convolve/pallas_call | solution.py:181
  44.8 0.0 copy-start
  44.9 0.1 collective-permute-start.7
  45.0 1.5 %collective-permute-done.7 = bf16[4,2,128,128]{3,2,1,0:T(8,128)(2,1)S(1)} collective-permute-done((bf16[4,2,128,128]{3,2,1,0:T(8,128)(2,1)S(1)}, bf16[4,2,128,128]{3,2,1,0:T(8,128)(2,1)S(1)}, u32[]{:S(2)}, u32[]{:S(2)}) %collective-permute-start.7) | collective-permute-done | bytes 262176 | tf_op jit(solution)/shard_map/ppermute | solution.py:358
  46.5 2.0 %collective-permute-start.8 = (bf16[2,2,128,128]{3,2,1,0:T(8,128)(2,1)S(1)}, bf16[2,2,128,128]{3,2,1,0:T(8,128)(2,1)S(1)}, u32[]{:S(2)}, u32[]{:S(2)}) collective-permute-start(bf16[2,2,128,128]{3,2,1,0:T(8,128)(2,1)S(1)} %pad_maximum_fusion), channel_id=1, source_target_pairs={{0,24},{4,28},{8,16},{12,20},{16,8},{20,12},{24,0},{28,4},{1,25},{... | collective-permute-start | bytes 393224 | tf_op jit(solution)/shard_map/ppermute | solution.py:358
  48.5 0.1 collective-permute-start.9
  48.6 2.5 %collective-permute-start.10 = (bf16[2,2,128,128]{3,2,1,0:T(8,128)(2,1)S(1)}, bf16[2,2,128,128]{3,2,1,0:T(8,128)(2,1)S(1)}, u32[]{:S(2)}, u32[]{:S(2)}) collective-permute-start(bf16[2,2,128,128]{3,2,1,0:T(8,128)(2,1)S(1)} %pad_maximum_fusion.2), channel_id=1, source_target_pairs={{0,8},{4,12},{8,0},{12,4},{16,24},{20,28},{24,16},{28,20},{1,9},{5... | collective-permute-start | bytes 393224 | tf_op jit(solution)/shard_map/ppermute | solution.py:358
  51.1 3.7 %collective-permute-done.8.refs_0_ = bf16[2,2,128,128]{3,2,1,0:T(8,128)(2,1)S(1)} collective-permute-done((bf16[2,2,128,128]{3,2,1,0:T(8,128)(2,1)S(1)}, bf16[2,2,128,128]{3,2,1,0:T(8,128)(2,1)S(1)}, u32[]{:S(2)}, u32[]{:S(2)}) %collective-permute-start.8) | collective-permute-done | bytes 131104 | tf_op jit(solution)/shard_map/ppermute | solution.py:358
  54.8 4.8 %collective-permute-done.9.refs_1_ = bf16[2,2,128,128]{3,2,1,0:T(8,128)(2,1)S(1)} collective-permute-done((bf16[2,2,128,128]{3,2,1,0:T(8,128)(2,1)S(1)}, bf16[2,2,128,128]{3,2,1,0:T(8,128)(2,1)S(1)}, u32[]{:S(2)}, u32[]{:S(2)}) %collective-permute-start.9) | collective-permute-done | bytes 131104 | tf_op jit(solution)/shard_map/ppermute | solution.py:358
  59.6 0.0 collective-permute-done.10.refs_2_
  59.6 0.5 gate.1
  60.1 0.0 collective-permute-done.11.refs_4_.refs_2_
  60.1 0.0 collective-permute-done.12.refs_6_.refs_4_
  60.1 0.2 collective-permute-start.13
  60.3 0.4 collective-permute-start.18
  60.7 1.5 %collective-permute-start.16 = (bf16[128,1024]{1,0:T(8,128)(2,1)S(1)}, bf16[128,1024]{1,0:T(8,128)(2,1)S(1)}, u32[]{:S(2)}, u32[]{:S(2)}) collective-permute-start(bf16[128,1024]{1,0:T(8,128)(2,1)S(1)} %get-tuple-element.54.refs_0_), channel_id=1, source_target_pairs={{0,2},{1,3},{2,0},{3,1},{4,6},{5,7},{6,4},{7,5},{8,10},{9,11},{10,... | collective-permute-start | bytes 786440 | tf_op jit(solution)/shard_map/ppermute | solution.py:358
  62.2 1.5 %collective-permute-start.14 = (bf16[128,1024]{1,0:T(8,128)(2,1)S(1)}, bf16[128,1024]{1,0:T(8,128)(2,1)S(1)}, u32[]{:S(2)}, u32[]{:S(2)}) collective-permute-start(bf16[128,1024]{1,0:T(8,128)(2,1)S(1)} %get-tuple-element.54.refs_0_), channel_id=1, source_target_pairs={{0,1},{1,0},{2,3},{3,2},{4,5},{5,4},{6,7},{7,6},{8,9},{9,8},{10,11... | collective-permute-start | bytes 786440 | tf_op jit(solution)/shard_map/ppermute | solution.py:358
  63.7 3.1 %own_part.2.own_ref = f32[2,256,1024]{2,1,0:T(8,128)S(1)} custom-call(s32[1]{0:T(128)} %bitcast.2.me_ref, bf16[128,1024]{1,0:T(8,128)(2,1)S(1)} %get-tuple-element.54.refs_0_, bf16[128,1024]{1,0:T(8,128)(2,1)S(1)} %get-tuple-element.61.refs_1_, bf16[1024,8192]{1,0:T(8,128)(2,1)} %refs_3_.3, bf16[1024,8192]{1,0:T(8,128)(2,1)} %refs_3_.3), custom_call_target="tpu_custom_call" | custom-call | flops 1073741824 | bytes 4194304 | tf_op jit(solution)/shard_map/own_part/pallas_call | solution.py:246
  66.7 0.0 collective-permute-done.13.refs_5_.refs_3_
  66.7 0.6 collective-permute-start.17
  67.3 0.5 collective-permute-start.15
  67.8 3.0 %own_part.3.own_ref = f32[2,256,1024]{2,1,0:T(8,128)S(1)} custom-call(s32[1]{0:T(128)} %bitcast.2.me_ref, bf16[128,1024]{1,0:T(8,128)(2,1)S(1)} %get-tuple-element.54.refs_0_, bf16[128,1024]{1,0:T(8,128)(2,1)S(1)} %get-tuple-element.61.refs_1_, bf16[1024,8192]{1,0:T(8,128)(2,1)} %refs_3_.3, bf16[1024,8192]{1,0:T(8,128)(2,1)} %refs_3_.3), custom_call_target="tpu_custom_call" | custom-call | flops 1073741824 | bytes 4194304 | tf_op jit(solution)/shard_map/own_part/pallas_call | solution.py:246
  70.9 0.0 collective-permute-done.16.refs_2_.refs_1_
  70.9 0.2 collective-permute-done.14.refs_0_
  71.2 0.0 collective-permute-done.18.refs_7_.refs_5_
  71.2 1.4 %add_sent.3 = (bf16[128,1024]{1,0:T(8,128)(2,1)S(1)}, bf16[128,1024]{1,0:T(8,128)(2,1)S(1)}) custom-call(s32[1]{0:T(128)} %bitcast.core_ref, f32[2,256,1024]{2,1,0:T(8,128)S(1)} %own_part.2.own_ref, bf16[128,1024]{1,0:T(8,128)(2,1)S(1)} %collective-permute-done.14.refs_0_, bf16[128,1024]{1,0:T(8,128)(2,1)S(1)} %collective-permute-done.16.refs_2_.refs_1_, ...), custom_call_target="tpu_custom_call" | custom-call | flops 536870912 | bytes 4194304 | tf_op jit(solution)/shard_map/add_sent/pallas_call | solution.py:312
  72.6 1.3 %collective-permute-start.21 = (bf16[128,1024]{1,0:T(8,128)(2,1)S(1)}, bf16[128,1024]{1,0:T(8,128)(2,1)S(1)}, u32[]{:S(2)}, u32[]{:S(2)}) collective-permute-start(bf16[128,1024]{1,0:T(8,128)(2,1)S(1)} %get-tuple-element.69), channel_id=1, source_target_pairs={{0,2},{1,3},{2,0},{3,1},{4,6},{5,7},{6,4},{7,5},{8,10},{9,11},{10,... | collective-permute-start | bytes 786440 | tf_op jit(solution)/shard_map/ppermute | solution.py:358
  73.9 1.5 %collective-permute-start.22 = (bf16[128,1024]{1,0:T(8,128)(2,1)S(1)}, bf16[128,1024]{1,0:T(8,128)(2,1)S(1)}, u32[]{:S(2)}, u32[]{:S(2)}) collective-permute-start(bf16[128,1024]{1,0:T(8,128)(2,1)S(1)} %get-tuple-element.70), channel_id=1, source_target_pairs={{0,1},{1,0},{2,3},{3,2},{4,5},{5,4},{6,7},{7,6},{8,9},{9,8},{10,11... | collective-permute-start | bytes 786440 | tf_op jit(solution)/shard_map/ppermute | solution.py:358
  75.4 0.0 collective-permute-done.17.refs_3_.refs_1_
  75.4 1.0 %collective-permute-done.15.refs_1_.refs_0_ = bf16[128,1024]{1,0:T(8,128)(2,1)S(1)} collective-permute-done((bf16[128,1024]{1,0:T(8,128)(2,1)S(1)}, bf16[128,1024]{1,0:T(8,128)(2,1)S(1)}, u32[]{:S(2)}, u32[]{:S(2)}) %collective-permute-start.15) | collective-permute-done | bytes 262176 | tf_op jit(solution)/shard_map/ppermute | solution.py:358
  76.4 1.4 %add_sent.2 = (bf16[128,1024]{1,0:T(8,128)(2,1)S(1)}, bf16[128,1024]{1,0:T(8,128)(2,1)S(1)}) custom-call(s32[1]{0:T(128)} %bitcast.core_ref, f32[2,256,1024]{2,1,0:T(8,128)S(1)} %own_part.2.own_ref, bf16[128,1024]{1,0:T(8,128)(2,1)S(1)} %collective-permute-done.15.refs_1_.refs_0_, bf16[128,1024]{1,0:T(8,128)(2,1)S(1)} %collective-permute-done.17.refs_3_.refs_1_, ...), custom_call_target="tpu_custom_call" | custom-call | flops 536870912 | bytes 4194304 | tf_op jit(solution)/shard_map/add_sent/pallas_call | solution.py:312
  77.7 0.5 collective-permute-start.19
  78.3 1.5 %collective-permute-start.20 = (bf16[128,1024]{1,0:T(8,128)(2,1)S(1)}, bf16[128,1024]{1,0:T(8,128)(2,1)S(1)}, u32[]{:S(2)}, u32[]{:S(2)}) collective-permute-start(bf16[128,1024]{1,0:T(8,128)(2,1)S(1)} %get-tuple-element.68), channel_id=1, source_target_pairs={{0,1},{1,0},{2,3},{3,2},{4,5},{5,4},{6,7},{7,6},{8,9},{9,8},{10,11... | collective-permute-start | bytes 786440 | tf_op jit(solution)/shard_map/ppermute | solution.py:358
  79.8 1.9 %add_kept.1 = (f32[256,1024]{1,0:T(8,128)S(1)}, f32[256,1024]{1,0:T(8,128)S(1)}) custom-call(s32[1]{0:T(128)} %bitcast.core_ref, f32[2,256,1024]{2,1,0:T(8,128)S(1)} %own_part.3.own_ref, bf16[128,1024]{1,0:T(8,128)(2,1)S(1)} %collective-permute-done.14.refs_0_, bf16[128,1024]{1,0:T(8,128)(2,1)S(1)} %collective-permute-done.15.refs_1_.refs_0_, ...), custom_call_target="tpu_custom_call" | custom-call | flops 1073741824 | bytes 4194304 | tf_op jit(solution)/shard_map/add_kept/pallas_call | solution.py:312
  81.7 0.0 collective-permute-done.21.sum_a_ref
  81.7 1.4 %collective-permute-done.22.sum_b_ref = bf16[128,1024]{1,0:T(8,128)(2,1)S(1)} collective-permute-done((bf16[128,1024]{1,0:T(8,128)(2,1)S(1)}, bf16[128,1024]{1,0:T(8,128)(2,1)S(1)}, u32[]{:S(2)}, u32[]{:S(2)}) %collective-permute-start.22) | collective-permute-done | bytes 262176 | tf_op jit(solution)/shard_map/ppermute | solution.py:358
  83.1 0.9 %finish.2.refs_0_ = bf16[256,2048]{1,0:T(8,128)(2,1)} custom-call(f32[256,1024]{1,0:T(8,128)S(1)} %get-tuple-element.64.kept_a_ref, f32[256,1024]{1,0:T(8,128)S(1)} %get-tuple-element.65.kept_b_ref, bf16[128,1024]{1,0:T(8,128)(2,1)S(1)} %collective-permute-done.21.sum_a_ref, bf16[128,1024]{1,0:T(8,128)(2,1)S(1)} %collective-permute-done.22.sum_b_ref), custom_call_target="tpu_custom_call" | custom-call | tf_op jit(solution)/shard_map/finish/pallas_call | solution.py:345
  84.1 1.8 %collective-permute-done.19.sum_a_ref = bf16[128,1024]{1,0:T(8,128)(2,1)S(1)} collective-permute-done((bf16[128,1024]{1,0:T(8,128)(2,1)S(1)}, bf16[128,1024]{1,0:T(8,128)(2,1)S(1)}, u32[]{:S(2)}, u32[]{:S(2)}) %collective-permute-start.19) | collective-permute-done | bytes 262176 | tf_op jit(solution)/shard_map/ppermute | solution.py:358
  85.8 1.2 %collective-permute-done.20.sum_b_ref = bf16[128,1024]{1,0:T(8,128)(2,1)S(1)} collective-permute-done((bf16[128,1024]{1,0:T(8,128)(2,1)S(1)}, bf16[128,1024]{1,0:T(8,128)(2,1)S(1)}, u32[]{:S(2)}, u32[]{:S(2)}) %collective-permute-start.20) | collective-permute-done | bytes 262176 | tf_op jit(solution)/shard_map/ppermute | solution.py:358
  87.1 0.9 %finish.3 = bf16[256,2048]{1,0:T(8,128)(2,1)} custom-call(f32[256,1024]{1,0:T(8,128)S(1)} %get-tuple-element.64.kept_a_ref, f32[256,1024]{1,0:T(8,128)S(1)} %get-tuple-element.65.kept_b_ref, bf16[128,1024]{1,0:T(8,128)(2,1)S(1)} %collective-permute-done.19.sum_a_ref, ...), custom_call_target="tpu_custom_call", output_to_operand_aliasing={{}: (4, {})} | custom-call | tf_op jit(solution)/shard_map/finish/pallas_call | solution.py:345
  (24 shorter events, 0.1 us)
Async XLA Ops:
  3.2 12.3 %collective-permute-start = (bf16[6,128,128]{2,1,0:T(8,128)(2,1)}, bf16[6,128,128]{2,1,0:T(8,128)(2,1)S(1)}, u32[]{:S(2)}, u32[]{:S(2)}) collective-permute-start(bf16[6,128,128]{2,1,0:T(8,128)(2,1)} %get-tuple-element.42), channel_id=1, source_target_pairs={{0,24},{4,28},{8,16},{12,20},{16,8},{20,12},{24,0},{28,4},{1,25},{... | collective-permute-start | bytes 589832 | tf_op jit(solution)/shard_map/ppermute | solution.py:358
  8.4 6.4 %copy-start.11 = (bf16[6,128,128]{2,1,0:T(8,128)(2,1)S(1)}, bf16[6,128,128]{2,1,0:T(8,128)(2,1)}, u32[]{:S(2)}) copy-start(bf16[6,128,128]{2,1,0:T(8,128)(2,1)} %get-tuple-element.44) | copy-start | bytes 589828
  8.4 6.4 %copy-start.10 = (bf16[6,128,128]{2,1,0:T(8,128)(2,1)S(1)}, bf16[6,128,128]{2,1,0:T(8,128)(2,1)}, u32[]{:S(2)}) copy-start(bf16[6,128,128]{2,1,0:T(8,128)(2,1)} %get-tuple-element.45) | copy-start | bytes 589828
  8.4 7.2 %copy-start.9 = (bf16[6,128,128]{2,1,0:T(8,128)(2,1)S(1)}, bf16[6,128,128]{2,1,0:T(8,128)(2,1)}, u32[]{:S(2)}) copy-start(bf16[6,128,128]{2,1,0:T(8,128)(2,1)} %get-tuple-element.46) | copy-start | bytes 589828
  8.4 21.4 %copy-start.8 = (bf16[6,128,128]{2,1,0:T(8,128)(2,1)S(1)}, bf16[6,128,128]{2,1,0:T(8,128)(2,1)}, u32[]{:S(2)}) copy-start(bf16[6,128,128]{2,1,0:T(8,128)(2,1)} %get-tuple-element.47) | copy-start | bytes 589828
  8.4 21.4 %copy-start.7 = (bf16[6,128,128]{2,1,0:T(8,128)(2,1)S(1)}, bf16[6,128,128]{2,1,0:T(8,128)(2,1)}, u32[]{:S(2)}) copy-start(bf16[6,128,128]{2,1,0:T(8,128)(2,1)} %get-tuple-element.48) | copy-start | bytes 589828
  8.4 24.9 %copy-start.6 = (bf16[6,128,128]{2,1,0:T(8,128)(2,1)S(1)}, bf16[6,128,128]{2,1,0:T(8,128)(2,1)}, u32[]{:S(2)}) copy-start(bf16[6,128,128]{2,1,0:T(8,128)(2,1)} %get-tuple-element.49) | copy-start | bytes 589828
  8.4 33.7 %copy-start.1 = (bf16[6,128,128]{2,1,0:T(8,128)(2,1)S(1)}, bf16[6,128,128]{2,1,0:T(8,128)(2,1)}, u32[]{:S(2)}) copy-start(bf16[6,128,128]{2,1,0:T(8,128)(2,1)} %get-tuple-element.50.refs_7_) | copy-start | bytes 589828
  8.4 33.7 %copy-start.2 = (bf16[1024,1024]{1,0:T(8,128)(2,1)S(1)}, bf16[1024,1024]{1,0:T(8,128)(2,1)}, u32[]{:S(2)}) copy-start(bf16[1024,1024]{1,0:T(8,128)(2,1)} %constant.32.clone.refs_9_) | copy-start | bytes 6291460
  8.4 33.6 %copy-start.3 = (bf16[1024,1024]{1,0:T(8,128)(2,1)S(1)}, bf16[1024,1024]{1,0:T(8,128)(2,1)}, u32[]{:S(2)}) copy-start(bf16[1024,1024]{1,0:T(8,128)(2,1)} %constant.31.clone.refs_8_) | copy-start | bytes 6291460
  8.5 33.6 %copy-start.4 = (f32[1024,128]{1,0:T(8,128)S(1)}, f32[1024,128]{1,0:T(8,128)}, u32[]{:S(2)}) copy-start(f32[1024,128]{1,0:T(8,128)} %constant.34.clone.refs_11_) | copy-start | bytes 1572868
  8.5 33.6 %copy-start.5 = (f32[1024,128]{1,0:T(8,128)S(1)}, f32[1024,128]{1,0:T(8,128)}, u32[]{:S(2)}) copy-start(f32[1024,128]{1,0:T(8,128)} %constant.33.clone.refs_10_) | copy-start | bytes 1572868
  11.7 48.4 %collective-permute-start.11 = (bf16[1024,1024]{1,0:T(8,128)(2,1)S(1)}, bf16[1024,1024]{1,0:T(8,128)(2,1)S(1)}, u32[]{:S(2)}, u32[]{:S(2)}) collective-permute-start(bf16[1024,1024]{1,0:T(8,128)(2,1)S(1)} %get-tuple-element.56), channel_id=1, source_target_pairs={{0,1},{1,0},{2,3},{3,2},{4,5},{5,4},{6,7},{7,6},{8,9},{9,8},{10,11... | collective-permute-start | bytes 6291464 | tf_op jit(solution)/shard_map/ppermute | solution.py:358
  13.2 46.8 %collective-permute-start.12 = (bf16[1024,1024]{1,0:T(8,128)(2,1)S(1)}, bf16[1024,1024]{1,0:T(8,128)(2,1)S(1)}, u32[]{:S(2)}, u32[]{:S(2)}) collective-permute-start(bf16[1024,1024]{1,0:T(8,128)(2,1)S(1)} %get-tuple-element.57), channel_id=1, source_target_pairs={{0,2},{1,3},{2,0},{3,1},{4,6},{5,7},{6,4},{7,5},{8,10},{9,11},{10,... | collective-permute-start | bytes 6291464 | tf_op jit(solution)/shard_map/ppermute | solution.py:358
  14.8 15.1 %collective-permute-start.1 = (bf16[6,128,128]{2,1,0:T(8,128)(2,1)S(1)}, bf16[6,128,128]{2,1,0:T(8,128)(2,1)S(1)}, u32[]{:S(2)}, u32[]{:S(2)}) collective-permute-start(bf16[6,128,128]{2,1,0:T(8,128)(2,1)S(1)} %copy-done.11), channel_id=1, source_target_pairs={{0,16},{4,20},{8,24},{12,28},{16,0},{20,4},{24,8},{28,12},{1,17},{... | collective-permute-start | bytes 589832 | tf_op jit(solution)/shard_map/ppermute | solution.py:358
  14.8 15.1 %collective-permute-start.2 = (bf16[6,128,128]{2,1,0:T(8,128)(2,1)S(1)}, bf16[6,128,128]{2,1,0:T(8,128)(2,1)S(1)}, u32[]{:S(2)}, u32[]{:S(2)}) collective-permute-start(bf16[6,128,128]{2,1,0:T(8,128)(2,1)S(1)} %copy-done.10), channel_id=1, source_target_pairs={{0,8},{4,12},{8,0},{12,4},{16,24},{20,28},{24,16},{28,20},{1,9},{5... | collective-permute-start | bytes 589832 | tf_op jit(solution)/shard_map/ppermute | solution.py:358
  15.6 17.8 %collective-permute-start.3 = (bf16[6,128,128]{2,1,0:T(8,128)(2,1)S(1)}, bf16[6,128,128]{2,1,0:T(8,128)(2,1)S(1)}, u32[]{:S(2)}, u32[]{:S(2)}) collective-permute-start(bf16[6,128,128]{2,1,0:T(8,128)(2,1)S(1)} %copy-done.9), channel_id=1, source_target_pairs={{0,28},{4,24},{8,20},{12,16},{16,12},{20,8},{24,4},{28,0},{1,29},{... | collective-permute-start | bytes 589832 | tf_op jit(solution)/shard_map/ppermute | solution.py:358
  29.8 12.3 %collective-permute-start.4 = (bf16[6,128,128]{2,1,0:T(8,128)(2,1)S(1)}, bf16[6,128,128]{2,1,0:T(8,128)(2,1)S(1)}, u32[]{:S(2)}, u32[]{:S(2)}) collective-permute-start(bf16[6,128,128]{2,1,0:T(8,128)(2,1)S(1)} %copy-done.8), channel_id=1, source_target_pairs={{0,20},{4,16},{8,28},{12,24},{16,4},{20,0},{24,12},{28,8},{1,21},{... | collective-permute-start | bytes 589832 | tf_op jit(solution)/shard_map/ppermute | solution.py:358
  29.8 12.2 %collective-permute-start.5 = (bf16[6,128,128]{2,1,0:T(8,128)(2,1)S(1)}, bf16[6,128,128]{2,1,0:T(8,128)(2,1)S(1)}, u32[]{:S(2)}, u32[]{:S(2)}) collective-permute-start(bf16[6,128,128]{2,1,0:T(8,128)(2,1)S(1)} %copy-done.7), channel_id=1, source_target_pairs={{0,12},{4,8},{8,4},{12,0},{16,28},{20,24},{24,20},{28,16},{1,13},{... | collective-permute-start | bytes 589832 | tf_op jit(solution)/shard_map/ppermute | solution.py:358
  33.4 8.7 %collective-permute-start.6 = (bf16[6,128,128]{2,1,0:T(8,128)(2,1)S(1)}, bf16[6,128,128]{2,1,0:T(8,128)(2,1)S(1)}, u32[]{:S(2)}, u32[]{:S(2)}) collective-permute-start(bf16[6,128,128]{2,1,0:T(8,128)(2,1)S(1)} %copy-done.6), channel_id=1, source_target_pairs={{0,4},{4,0},{8,12},{12,8},{16,20},{20,16},{24,28},{28,24},{1,5},{5... | collective-permute-start | bytes 589832 | tf_op jit(solution)/shard_map/ppermute | solution.py:358
  44.8 14.8 %copy-start = (bf16[256,1024]{1,0:T(8,128)(2,1)S(1)}, bf16[256,1024]{1,0:T(8,128)(2,1)}, u32[]{:S(2)}) copy-start(bf16[256,1024]{1,0:T(8,128)(2,1)} %refs_4_.1) | copy-start | bytes 1572868
  44.9 1.6 %collective-permute-start.7 = (bf16[4,2,128,128]{3,2,1,0:T(8,128)(2,1)S(1)}, bf16[4,2,128,128]{3,2,1,0:T(8,128)(2,1)S(1)}, u32[]{:S(2)}, u32[]{:S(2)}) collective-permute-start(bf16[4,2,128,128]{3,2,1,0:T(8,128)(2,1)S(1)} %get-tuple-element.52), channel_id=1, source_target_pairs={{0,4},{4,0},{8,12},{12,8},{16,20},{20,16},{24,28},{28,24},{1,5},{5... | collective-permute-start | bytes 786440 | tf_op jit(solution)/shard_map/ppermute | solution.py:358
  46.5 8.3 %collective-permute-start.8 = (bf16[2,2,128,128]{3,2,1,0:T(8,128)(2,1)S(1)}, bf16[2,2,128,128]{3,2,1,0:T(8,128)(2,1)S(1)}, u32[]{:S(2)}, u32[]{:S(2)}) collective-permute-start(bf16[2,2,128,128]{3,2,1,0:T(8,128)(2,1)S(1)} %pad_maximum_fusion), channel_id=1, source_target_pairs={{0,24},{4,28},{8,16},{12,20},{16,8},{20,12},{24,0},{28,4},{1,25},{... | collective-permute-start | bytes 393224 | tf_op jit(solution)/shard_map/ppermute | solution.py:358
  48.5 11.1 %collective-permute-start.9 = (bf16[2,2,128,128]{3,2,1,0:T(8,128)(2,1)S(1)}, bf16[2,2,128,128]{3,2,1,0:T(8,128)(2,1)S(1)}, u32[]{:S(2)}, u32[]{:S(2)}) collective-permute-start(bf16[2,2,128,128]{3,2,1,0:T(8,128)(2,1)S(1)} %pad_maximum_fusion.1), channel_id=1, source_target_pairs={{0,16},{4,20},{8,24},{12,28},{16,0},{20,4},{24,8},{28,12},{1,17},{... | collective-permute-start | bytes 393224 | tf_op jit(solution)/shard_map/ppermute | solution.py:358
  48.6 11.0 %collective-permute-start.10 = (bf16[2,2,128,128]{3,2,1,0:T(8,128)(2,1)S(1)}, bf16[2,2,128,128]{3,2,1,0:T(8,128)(2,1)S(1)}, u32[]{:S(2)}, u32[]{:S(2)}) collective-permute-start(bf16[2,2,128,128]{3,2,1,0:T(8,128)(2,1)S(1)} %pad_maximum_fusion.2), channel_id=1, source_target_pairs={{0,8},{4,12},{8,0},{12,4},{16,24},{20,28},{24,16},{28,20},{1,9},{5... | collective-permute-start | bytes 393224 | tf_op jit(solution)/shard_map/ppermute | solution.py:358
  60.1 6.6 %collective-permute-start.13 = (bf16[1024,1024]{1,0:T(8,128)(2,1)S(1)}, bf16[1024,1024]{1,0:T(8,128)(2,1)S(1)}, u32[]{:S(2)}, u32[]{:S(2)}) collective-permute-start(bf16[1024,1024]{1,0:T(8,128)(2,1)S(1)} %collective-permute-done.11.refs_4_.refs_2_), channel_id=1, source_target_pairs={{0,4},{4,0},{8,12},{12,8},{16,20},{20,16},{24,28},{28,24},{1,5},{5... | collective-permute-start | bytes 6291464 | tf_op jit(solution)/shard_map/ppermute | solution.py:358
  60.3 10.9 %collective-permute-start.18 = (bf16[1024,1024]{1,0:T(8,128)(2,1)S(1)}, bf16[1024,1024]{1,0:T(8,128)(2,1)S(1)}, u32[]{:S(2)}, u32[]{:S(2)}) collective-permute-start(bf16[1024,1024]{1,0:T(8,128)(2,1)S(1)} %collective-permute-done.12.refs_6_.refs_4_), channel_id=1, source_target_pairs={{0,4},{4,0},{8,12},{12,8},{16,20},{20,16},{24,28},{28,24},{1,5},{5... | collective-permute-start | bytes 6291464 | tf_op jit(solution)/shard_map/ppermute | solution.py:358
  60.7 10.2 %collective-permute-start.16 = (bf16[128,1024]{1,0:T(8,128)(2,1)S(1)}, bf16[128,1024]{1,0:T(8,128)(2,1)S(1)}, u32[]{:S(2)}, u32[]{:S(2)}) collective-permute-start(bf16[128,1024]{1,0:T(8,128)(2,1)S(1)} %get-tuple-element.54.refs_0_), channel_id=1, source_target_pairs={{0,2},{1,3},{2,0},{3,1},{4,6},{5,7},{6,4},{7,5},{8,10},{9,11},{10,... | collective-permute-start | bytes 786440 | tf_op jit(solution)/shard_map/ppermute | solution.py:358
  62.2 9.0 %collective-permute-start.14 = (bf16[128,1024]{1,0:T(8,128)(2,1)S(1)}, bf16[128,1024]{1,0:T(8,128)(2,1)S(1)}, u32[]{:S(2)}, u32[]{:S(2)}) collective-permute-start(bf16[128,1024]{1,0:T(8,128)(2,1)S(1)} %get-tuple-element.54.refs_0_), channel_id=1, source_target_pairs={{0,1},{1,0},{2,3},{3,2},{4,5},{5,4},{6,7},{7,6},{8,9},{9,8},{10,11... | collective-permute-start | bytes 786440 | tf_op jit(solution)/shard_map/ppermute | solution.py:358
  66.7 8.7 %collective-permute-start.17 = (bf16[128,1024]{1,0:T(8,128)(2,1)S(1)}, bf16[128,1024]{1,0:T(8,128)(2,1)S(1)}, u32[]{:S(2)}, u32[]{:S(2)}) collective-permute-start(bf16[128,1024]{1,0:T(8,128)(2,1)S(1)} %get-tuple-element.61.refs_1_), channel_id=1, source_target_pairs={{0,2},{1,3},{2,0},{3,1},{4,6},{5,7},{6,4},{7,5},{8,10},{9,11},{10,... | collective-permute-start | bytes 786440 | tf_op jit(solution)/shard_map/ppermute | solution.py:358
  67.3 9.0 %collective-permute-start.15 = (bf16[128,1024]{1,0:T(8,128)(2,1)S(1)}, bf16[128,1024]{1,0:T(8,128)(2,1)S(1)}, u32[]{:S(2)}, u32[]{:S(2)}) collective-permute-start(bf16[128,1024]{1,0:T(8,128)(2,1)S(1)} %get-tuple-element.61.refs_1_), channel_id=1, source_target_pairs={{0,1},{1,0},{2,3},{3,2},{4,5},{5,4},{6,7},{7,6},{8,9},{9,8},{10,11... | collective-permute-start | bytes 786440 | tf_op jit(solution)/shard_map/ppermute | solution.py:358
  72.6 9.2 %collective-permute-start.21 = (bf16[128,1024]{1,0:T(8,128)(2,1)S(1)}, bf16[128,1024]{1,0:T(8,128)(2,1)S(1)}, u32[]{:S(2)}, u32[]{:S(2)}) collective-permute-start(bf16[128,1024]{1,0:T(8,128)(2,1)S(1)} %get-tuple-element.69), channel_id=1, source_target_pairs={{0,2},{1,3},{2,0},{3,1},{4,6},{5,7},{6,4},{7,5},{8,10},{9,11},{10,... | collective-permute-start | bytes 786440 | tf_op jit(solution)/shard_map/ppermute | solution.py:358
  73.9 9.2 %collective-permute-start.22 = (bf16[128,1024]{1,0:T(8,128)(2,1)S(1)}, bf16[128,1024]{1,0:T(8,128)(2,1)S(1)}, u32[]{:S(2)}, u32[]{:S(2)}) collective-permute-start(bf16[128,1024]{1,0:T(8,128)(2,1)S(1)} %get-tuple-element.70), channel_id=1, source_target_pairs={{0,1},{1,0},{2,3},{3,2},{4,5},{5,4},{6,7},{7,6},{8,9},{9,8},{10,11... | collective-permute-start | bytes 786440 | tf_op jit(solution)/shard_map/ppermute | solution.py:358
  77.7 8.1 %collective-permute-start.19 = (bf16[128,1024]{1,0:T(8,128)(2,1)S(1)}, bf16[128,1024]{1,0:T(8,128)(2,1)S(1)}, u32[]{:S(2)}, u32[]{:S(2)}) collective-permute-start(bf16[128,1024]{1,0:T(8,128)(2,1)S(1)} %get-tuple-element.67), channel_id=1, source_target_pairs={{0,2},{1,3},{2,0},{3,1},{4,6},{5,7},{6,4},{7,5},{8,10},{9,11},{10,... | collective-permute-start | bytes 786440 | tf_op jit(solution)/shard_map/ppermute | solution.py:358
  78.3 8.8 %collective-permute-start.20 = (bf16[128,1024]{1,0:T(8,128)(2,1)S(1)}, bf16[128,1024]{1,0:T(8,128)(2,1)S(1)}, u32[]{:S(2)}, u32[]{:S(2)}) collective-permute-start(bf16[128,1024]{1,0:T(8,128)(2,1)S(1)} %get-tuple-element.68), channel_id=1, source_target_pairs={{0,1},{1,0},{2,3},{3,2},{4,5},{5,4},{6,7},{7,6},{8,9},{9,8},{10,11... | collective-permute-start | bytes 786440 | tf_op jit(solution)/shard_map/ppermute | solution.py:358

commit v8 on v7

--- a/solution.py
+++ b/solution.py
@@ -129,9 +129,8 @@
 def conv_kernel(order, me_ref, *refs):
     shares = len(order)
     data, (cos_ref, sin_ref, turn_cos_ref, turn_sin_ref) = refs[:shares], refs[shares:shares + 4]
-    mine_ref, other_ref, cols_ref, filt_ref, re_ref, im_ref = refs[shares + 4:]
+    other_ref, re_ref, im_ref, cols_ref, filt_ref = refs[shares + 4:]
     me = me_ref[0]
-    chip, core = me // 2, me % 2
     rows = data[0].shape[1]
     for m, ref in zip(order, data):
         at = pl.ds(pl.multiple_of((me ^ m) * rows, rows), rows)
@@ -157,17 +156,23 @@
         b1r, b1i = b1r * tc - b1i * ts, b1i * tc + b1r * ts
         re_ref[at, :] = jnp.concatenate([b0r, b1r], axis=1).astype(jnp.bfloat16)
         im_ref[at, :] = jnp.concatenate([b0i, b1i], axis=1).astype(jnp.bfloat16)
-    scale = 1.0 / (shares * rows)
-    for i in range(shares * rows // step):
-        at = slice(i * step, (i + 1) * step)
+    invert(me, 1, cos_ref, sin_ref, re_ref, im_ref, other_ref)
+
+
+def invert(me, flip, cos_ref, sin_ref, re_ref, im_ref, out_ref):
+    chips, _, rows, _ = out_ref.shape
+    scale = 1.0 / (2 * chips * rows)
+    for i in range(chips):
+        at = pl.ds(pl.multiple_of((me ^ (2 * i + flip)) * rows, rows), rows)
         conv = jnp.dot(cos_ref[at, :], re_ref[...], preferred_element_type=jnp.float32)
         conv = conv - jnp.dot(sin_ref[at, :], im_ref[...], preferred_element_type=jnp.float32)
         conv = (conv * scale).astype(jnp.bfloat16)
         for b in range(2):
-            lanes = slice(b * LANES, (b + 1) * LANES)
-            low, high = conv[:rows, lanes], conv[rows:, lanes]
-            mine_ref[i ^ chip, b] = jnp.where(core == 0, low, high)
-            other_ref[i ^ chip, b] = jnp.where(core == 0, high, low)
+            out_ref[i, b] = conv[:, b * LANES:(b + 1) * LANES]
+
+
+def rest_kernel(me_ref, re_ref, im_ref, cos_ref, sin_ref, out_ref):
+    invert(me_ref[0], 0, cos_ref, sin_ref, re_ref, im_ref, out_ref)
 
 
 def convolve(me, data, order):
@@ -176,21 +181,37 @@
     block = shares * rows
     angle = angles(block, block, block)
     turn = np.broadcast_to(angles(block, 2, 2 * block)[:, 1:], (block, LANES))
-    vmem = pl.BlockSpec(memory_space=pltpu.VMEM)
-    columns = pltpu.VMEM((block, 2 * LANES), jnp.bfloat16)
-    return pl.pallas_call(
+    vmem, smem = pl.BlockSpec(memory_space=pltpu.VMEM), pl.BlockSpec(memory_space=pltpu.SMEM)
+    share = jax.ShapeDtypeStruct((shares // 2, 2, rows, LANES), jnp.bfloat16)
+    columns = jax.ShapeDtypeStruct((block, 2 * LANES), jnp.bfloat16)
+    block_cos, block_sin = rounded(np.cos(angle)), rounded(np.sin(angle))
+    other, rotated_re, rotated_im = pl.pallas_call(
         functools.partial(conv_kernel, order),
-        in_specs=[pl.BlockSpec(memory_space=pltpu.SMEM)] + [vmem] * (shares + 4),
-        out_specs=[vmem] * 2,
-        out_shape=[jax.ShapeDtypeStruct((shares // 2, 2, rows, LANES), jnp.bfloat16)] * 2,
-        scratch_shapes=[columns, pltpu.VMEM((4, block, LANES), jnp.bfloat16), columns, columns],
+        in_specs=[smem] + [vmem] * (shares + 4),
+        out_specs=[vmem] * 3,
+        out_shape=[share, columns, columns],
+        scratch_shapes=[
+            pltpu.VMEM((block, 2 * LANES), jnp.bfloat16),
+            pltpu.VMEM((4, block, LANES), jnp.bfloat16),
+        ],
         compiler_params=pltpu.CompilerParams(vmem_limit_bytes=24 << 20),
         cost_estimate=pl.CostEstimate(flops=50 * block * block * LANES, bytes_accessed=8 * block * block, transcendentals=0),
         name="convolve",
     )(
-        me, *data, rounded(np.cos(angle)), rounded(np.sin(angle)),
+        me, *data, block_cos, block_sin,
         jnp.asarray(np.cos(turn).astype(np.float32)), jnp.asarray(np.sin(turn).astype(np.float32)),
     )
+    other = swap(other, "seq", 1)
+    mine = pl.pallas_call(
+        rest_kernel,
+        in_specs=[smem] + [vmem] * 4,
+        out_specs=vmem,
+        out_shape=share,
+        compiler_params=pltpu.CompilerParams(vmem_limit_bytes=24 << 20),
+        cost_estimate=pl.CostEstimate(flops=4 * block * block * LANES, bytes_accessed=4 * block * block, transcendentals=0),
+        name="convolve_rest",
+    )(me, rotated_re, rotated_im, block_cos, block_sin)
+    return mine, other
 
 
 def gate_kernel(chips, me_ref, *refs):
@@ -376,7 +397,6 @@
     held, data[order[0]] = lax.optimization_barrier(([packed[m] for m in late], data[order[0]]))
     data.update({m: swap(mine, "seq", m) for m, mine in zip(late, held)})
     mine, other = convolve(here.reshape(1), [data[m] for m in order], order)
-    other = swap(other, "seq", 1)
     held = [jnp.stack([mine[flip], other[flip]]) for flip in range(seq_count // 2)]
     chips = tuple(reversed(range(seq_count // 2)))
     held = [swap(held[flip], "seq", 2 * flip) if flip else held[flip] for flip in chips]

time: 88.1 us -> 87.9 us (level)
    pallas_call x1 -> x2, Pallas kernels: 2.71 us -> 3.25 us  [the longest x1 2.53 us: convolve(): pl.pallas_call(functools.partial(conv_kernel, order), in_specs=[smem] + [...]
  transfers between devices with their start and end apart: 23 -> 23, of which waited for: 10 -> 11; matrix products, arithmetic and copies ran while one was open for 0% -> 0% of each run, Pallas kernels for 20% -> 21%
where the time goes in v8:
time: 87.9 us; the launch traced here: 87.8 us
  waiting for transfers between devices  36.2 us (41%)
  starting transfers between devices  28.4 us (32%)
  Pallas kernels  22.7 us (26%)
    ppermute x23, waiting for transfers between devices, swap(): lax.ppermute(data, axis, [(i, i ^ flip) for i in range(lax.axis_size(axis...  36.2 us
    ppermute x23, starting transfers between devices, swap(): lax.ppermute(data, axis, [(i, i ^ flip) for i in range(lax.axis_size(axis...  28.4 us
    pallas_call x2, Pallas kernels, own_part(): pl.pallas_call(own_kernel, grid_spec=pltpu.PrefetchScalarGridSpec(num_sca...  6.1 us
    pallas_call x3, Pallas kernels, add_moved(): pl.pallas_call(functools.partial(add_kernel, parts, kept), grid=(1,), in_...  4.64 us
    pallas_call x1, Pallas kernels, pack(): pl.pallas_call(functools.partial(pack_kernel, span), in_specs=[pl.BlockSp...  3.19 us
    pallas_call x1, Pallas kernels, take_blocks(): pl.pallas_call(take_kernel, in_specs=[pl.BlockSpec(memory_space=pltpu.SME...  3.19 us
    pallas_call x1, Pallas kernels, convolve(): pl.pallas_call(functools.partial(conv_kernel, order), in_specs=[smem] + [...  2.53 us
    pallas_call x2, Pallas kernels, finish(): pl.pallas_call(finish_kernel, grid=(1,), in_specs=[kept, kept, sums, sums...  1.86 us
  transfers between devices with their start and end apart: 23, of which 11 were waited for; matrix products, arithmetic and copies ran while one was open for 0% of the time, Pallas kernels for 21%

profile of v8, /device:TPU:0, one launch (start us, length us, event | category | flops | bytes accessed | tf_op | source)
XLA Modules:
  0.0 87.8 jit_solution(1699844297467526036)
XLA Ops:
  0.0 3.2 %pack.1 = (bf16[6,128,128]{2,1,0:T(8,128)(2,1)}, bf16[6,128,128]{2,1,0:T(8,128)(2,1)}, bf16[6,128,128]{2,1,0:T(8,128)(2,1)}, bf16[6,128,128]{2,1,0:T(8,128)(2,1)...) custom-call(s32[1]{0:T(128)} %bitcast.1.me_ref, ...), custom_call_target="tpu_custom_call" | custom-call | tf_op jit(solution)/shard_map/pack/pallas_call | solution.py:79
  3.2 5.1 %collective-permute-start = (bf16[6,128,128]{2,1,0:T(8,128)(2,1)}, bf16[6,128,128]{2,1,0:T(8,128)(2,1)S(1)}, u32[]{:S(2)}, u32[]{:S(2)}) collective-permute-start(bf16[6,128,128]{2,1,0:T(8,128)(2,1)} %get-tuple-element.43), channel_id=1, source_target_pairs={{0,24},{4,28},{8,16},{12,20},{16,8},{20,12},{24,0},{28,4},{1,25},{... | collective-permute-start | bytes 589832 | tf_op jit(solution)/shard_map/ppermute | solution.py:379
  8.3 0.1 pad_add_fusion.places_ref
  8.4 0.0 copy-start
  8.4 0.0 copy-start.1
  8.4 0.0 copy-start.3
  8.5 0.0 copy-start.4
  8.5 0.0 copy-start.5
  8.5 3.2 %take_blocks.1 = (bf16[1024,1024]{1,0:T(8,128)(2,1)S(1)}, bf16[1024,1024]{1,0:T(8,128)(2,1)S(1)}) custom-call(s32[2]{0:T(128)S(1)} %pad_add_fusion.places_ref, bf16[1024,8192]{1,0:T(8,128)(2,1)} %refs_3_.3), custom_call_target="tpu_custom_call" | custom-call | bytes 134217728 | tf_op jit(solution)/shard_map/take_blocks/pallas_call | solution.py:117
  11.7 1.6 %collective-permute-start.11 = (bf16[1024,1024]{1,0:T(8,128)(2,1)S(1)}, bf16[1024,1024]{1,0:T(8,128)(2,1)S(1)}, u32[]{:S(2)}, u32[]{:S(2)}) collective-permute-start(bf16[1024,1024]{1,0:T(8,128)(2,1)S(1)} %get-tuple-element.58), channel_id=1, source_target_pairs={{0,1},{1,0},{2,3},{3,2},{4,5},{5,4},{6,7},{7,6},{8,9},{9,8},{10,11... | collective-permute-start | bytes 6291464 | tf_op jit(solution)/shard_map/ppermute | solution.py:379
  13.2 1.5 %collective-permute-start.12 = (bf16[1024,1024]{1,0:T(8,128)(2,1)S(1)}, bf16[1024,1024]{1,0:T(8,128)(2,1)S(1)}, u32[]{:S(2)}, u32[]{:S(2)}) collective-permute-start(bf16[1024,1024]{1,0:T(8,128)(2,1)S(1)} %get-tuple-element.59), channel_id=1, source_target_pairs={{0,2},{1,3},{2,0},{3,1},{4,6},{5,7},{6,4},{7,5},{8,10},{9,11},{10,... | collective-permute-start | bytes 6291464 | tf_op jit(solution)/shard_map/ppermute | solution.py:379
  14.8 0.0 collective-permute-start.1
  14.8 0.8 collective-permute-start.2
  15.5 0.0 collective-permute-done.refs_0_
  15.6 1.6 %collective-permute-start.3 = (bf16[6,128,128]{2,1,0:T(8,128)(2,1)S(1)}, bf16[6,128,128]{2,1,0:T(8,128)(2,1)S(1)}, u32[]{:S(2)}, u32[]{:S(2)}) collective-permute-start(bf16[6,128,128]{2,1,0:T(8,128)(2,1)S(1)} %copy-done.9), channel_id=1, source_target_pairs={{0,28},{4,24},{8,20},{12,16},{16,12},{20,8},{24,4},{28,0},{1,29},{... | collective-permute-start | bytes 589832 | tf_op jit(solution)/shard_map/ppermute | solution.py:379
  17.2 12.6 %collective-permute-done.1.refs_1_ = bf16[6,128,128]{2,1,0:T(8,128)(2,1)S(1)} collective-permute-done((bf16[6,128,128]{2,1,0:T(8,128)(2,1)S(1)}, bf16[6,128,128]{2,1,0:T(8,128)(2,1)S(1)}, u32[]{:S(2)}, u32[]{:S(2)}) %collective-permute-start.1) | collective-permute-done | bytes 196640 | tf_op jit(solution)/shard_map/ppermute | solution.py:379
  29.8 0.0 collective-permute-start.4
  29.8 0.0 collective-permute-done.2.refs_2_
  29.8 3.5 %collective-permute-start.5 = (bf16[6,128,128]{2,1,0:T(8,128)(2,1)S(1)}, bf16[6,128,128]{2,1,0:T(8,128)(2,1)S(1)}, u32[]{:S(2)}, u32[]{:S(2)}) collective-permute-start(bf16[6,128,128]{2,1,0:T(8,128)(2,1)S(1)} %copy-done.7), channel_id=1, source_target_pairs={{0,12},{4,8},{8,4},{12,0},{16,28},{20,24},{24,20},{28,16},{1,13},{... | collective-permute-start | bytes 589832 | tf_op jit(solution)/shard_map/ppermute | solution.py:379
  33.3 0.0 collective-permute-done.3.refs_3_
  33.4 0.0 collective-permute-start.6
  33.4 8.7 %collective-permute-done.4.refs_4_ = bf16[6,128,128]{2,1,0:T(8,128)(2,1)S(1)} collective-permute-done((bf16[6,128,128]{2,1,0:T(8,128)(2,1)S(1)}, bf16[6,128,128]{2,1,0:T(8,128)(2,1)S(1)}, u32[]{:S(2)}, u32[]{:S(2)}) %collective-permute-start.4) | collective-permute-done | bytes 196640 | tf_op jit(solution)/shard_map/ppermute | solution.py:379
  42.1 0.0 collective-permute-done.5.refs_5_
  42.1 0.0 collective-permute-done.6.refs_6_
  42.1 2.5 %convolve.1 = (bf16[4,2,128,128]{3,2,1,0:T(8,128)(2,1)S(1)}, bf16[1024,256]{1,0:T(8,128)(2,1)S(1)}, bf16[1024,256]{1,0:T(8,128)(2,1)S(1)}) custom-call(s32[1]{0:T(128)} %bitcast.1.me_ref, bf16[6,128,128]{2,1,0:T(8,128)(2,1)S(1)} %collective-permute-done.refs_0_, bf16[6,128,128]{2,1,0:T(8,128)(2,1)S(1)} %collective-permute-done.1.refs_1_, ...), custom_call_target="tpu_custom_call" | custom-call | flops 6710886400 | bytes 8388608 | tf_op jit(solution)/shard_map/convolve/pallas_call | solution.py:188
  44.7 0.1 collective-permute-start.7
  44.8 0.7 convolve_rest.1
  45.5 0.0 copy-start.2
  45.5 0.7 collective-permute-done.7
  46.3 2.0 %collective-permute-start.8 = (bf16[2,2,128,128]{3,2,1,0:T(8,128)(2,1)S(1)}, bf16[2,2,128,128]{3,2,1,0:T(8,128)(2,1)S(1)}, u32[]{:S(2)}, u32[]{:S(2)}) collective-permute-start(bf16[2,2,128,128]{3,2,1,0:T(8,128)(2,1)S(1)} %pad_maximum_fusion), channel_id=1, source_target_pairs={{0,24},{4,28},{8,16},{12,20},{16,8},{20,12},{24,0},{28,4},{1,25},{... | collective-permute-start | bytes 393224 | tf_op jit(solution)/shard_map/ppermute | solution.py:379
  48.3 0.1 collective-permute-start.9
  48.4 2.5 %collective-permute-start.10 = (bf16[2,2,128,128]{3,2,1,0:T(8,128)(2,1)S(1)}, bf16[2,2,128,128]{3,2,1,0:T(8,128)(2,1)S(1)}, u32[]{:S(2)}, u32[]{:S(2)}) collective-permute-start(bf16[2,2,128,128]{3,2,1,0:T(8,128)(2,1)S(1)} %pad_maximum_fusion.2), channel_id=1, source_target_pairs={{0,8},{4,12},{8,0},{12,4},{16,24},{20,28},{24,16},{28,20},{1,9},{5... | collective-permute-start | bytes 393224 | tf_op jit(solution)/shard_map/ppermute | solution.py:379
  51.0 3.7 %collective-permute-done.8.refs_0_ = bf16[2,2,128,128]{3,2,1,0:T(8,128)(2,1)S(1)} collective-permute-done((bf16[2,2,128,128]{3,2,1,0:T(8,128)(2,1)S(1)}, bf16[2,2,128,128]{3,2,1,0:T(8,128)(2,1)S(1)}, u32[]{:S(2)}, u32[]{:S(2)}) %collective-permute-start.8) | collective-permute-done | bytes 131104 | tf_op jit(solution)/shard_map/ppermute | solution.py:379
  54.6 4.8 %collective-permute-done.9.refs_1_ = bf16[2,2,128,128]{3,2,1,0:T(8,128)(2,1)S(1)} collective-permute-done((bf16[2,2,128,128]{3,2,1,0:T(8,128)(2,1)S(1)}, bf16[2,2,128,128]{3,2,1,0:T(8,128)(2,1)S(1)}, u32[]{:S(2)}, u32[]{:S(2)}) %collective-permute-start.9) | collective-permute-done | bytes 131104 | tf_op jit(solution)/shard_map/ppermute | solution.py:379
  59.4 0.0 collective-permute-done.10.refs_2_
  59.4 0.5 gate.1
  59.9 0.0 collective-permute-done.11.refs_4_.refs_2_
  59.9 0.2 collective-permute-done.12.refs_6_.refs_4_
  60.1 0.0 collective-permute-start.13
  60.1 0.5 collective-permute-start.18
  60.6 1.5 %collective-permute-start.16 = (bf16[128,1024]{1,0:T(8,128)(2,1)S(1)}, bf16[128,1024]{1,0:T(8,128)(2,1)S(1)}, u32[]{:S(2)}, u32[]{:S(2)}) collective-permute-start(bf16[128,1024]{1,0:T(8,128)(2,1)S(1)} %get-tuple-element.56.refs_0_), channel_id=1, source_target_pairs={{0,2},{1,3},{2,0},{3,1},{4,6},{5,7},{6,4},{7,5},{8,10},{9,11},{10,... | collective-permute-start | bytes 786440 | tf_op jit(solution)/shard_map/ppermute | solution.py:379
  62.1 1.4 %collective-permute-start.14 = (bf16[128,1024]{1,0:T(8,128)(2,1)S(1)}, bf16[128,1024]{1,0:T(8,128)(2,1)S(1)}, u32[]{:S(2)}, u32[]{:S(2)}) collective-permute-start(bf16[128,1024]{1,0:T(8,128)(2,1)S(1)} %get-tuple-element.56.refs_0_), channel_id=1, source_target_pairs={{0,1},{1,0},{2,3},{3,2},{4,5},{5,4},{6,7},{7,6},{8,9},{9,8},{10,11... | collective-permute-start | bytes 786440 | tf_op jit(solution)/shard_map/ppermute | solution.py:379
  63.5 3.1 %own_part.2.own_ref = f32[2,256,1024]{2,1,0:T(8,128)S(1)} custom-call(s32[1]{0:T(128)} %bitcast.2.me_ref, bf16[128,1024]{1,0:T(8,128)(2,1)S(1)} %get-tuple-element.56.refs_0_, bf16[128,1024]{1,0:T(8,128)(2,1)S(1)} %get-tuple-element.63.refs_1_, bf16[1024,8192]{1,0:T(8,128)(2,1)} %refs_3_.3, bf16[1024,8192]{1,0:T(8,128)(2,1)} %refs_3_.3), custom_call_target="tpu_custom_call" | custom-call | flops 1073741824 | bytes 4194304 | tf_op jit(solution)/shard_map/own_part/pallas_call | solution.py:267
  66.5 0.0 collective-permute-done.13.refs_5_.refs_3_
  66.5 0.6 collective-permute-start.17
  67.2 0.6 collective-permute-start.15
  67.7 3.0 %own_part.3.own_ref = f32[2,256,1024]{2,1,0:T(8,128)S(1)} custom-call(s32[1]{0:T(128)} %bitcast.2.me_ref, bf16[128,1024]{1,0:T(8,128)(2,1)S(1)} %get-tuple-element.56.refs_0_, bf16[128,1024]{1,0:T(8,128)(2,1)S(1)} %get-tuple-element.63.refs_1_, bf16[1024,8192]{1,0:T(8,128)(2,1)} %refs_3_.3, bf16[1024,8192]{1,0:T(8,128)(2,1)} %refs_3_.3), custom_call_target="tpu_custom_call" | custom-call | flops 1073741824 | bytes 4194304 | tf_op jit(solution)/shard_map/own_part/pallas_call | solution.py:267
  70.8 0.0 collective-permute-done.16.refs_2_.refs_1_
  70.8 0.1 collective-permute-done.14.refs_0_
  70.9 1.4 %add_sent.3 = (bf16[128,1024]{1,0:T(8,128)(2,1)S(1)}, bf16[128,1024]{1,0:T(8,128)(2,1)S(1)}) custom-call(s32[1]{0:T(128)} %bitcast.core_ref, f32[2,256,1024]{2,1,0:T(8,128)S(1)} %own_part.2.own_ref, bf16[128,1024]{1,0:T(8,128)(2,1)S(1)} %collective-permute-done.14.refs_0_, bf16[128,1024]{1,0:T(8,128)(2,1)S(1)} %collective-permute-done.16.refs_2_.refs_1_, ...), custom_call_target="tpu_custom_call" | custom-call | flops 536870912 | bytes 4194304 | tf_op jit(solution)/shard_map/add_sent/pallas_call | solution.py:333
  72.3 1.5 %collective-permute-start.21 = (bf16[128,1024]{1,0:T(8,128)(2,1)S(1)}, bf16[128,1024]{1,0:T(8,128)(2,1)S(1)}, u32[]{:S(2)}, u32[]{:S(2)}) collective-permute-start(bf16[128,1024]{1,0:T(8,128)(2,1)S(1)} %get-tuple-element.71), channel_id=1, source_target_pairs={{0,2},{1,3},{2,0},{3,1},{4,6},{5,7},{6,4},{7,5},{8,10},{9,11},{10,... | collective-permute-start | bytes 786440 | tf_op jit(solution)/shard_map/ppermute | solution.py:379
  73.8 1.4 %collective-permute-start.22 = (bf16[128,1024]{1,0:T(8,128)(2,1)S(1)}, bf16[128,1024]{1,0:T(8,128)(2,1)S(1)}, u32[]{:S(2)}, u32[]{:S(2)}) collective-permute-start(bf16[128,1024]{1,0:T(8,128)(2,1)S(1)} %get-tuple-element.72), channel_id=1, source_target_pairs={{0,1},{1,0},{2,3},{3,2},{4,5},{5,4},{6,7},{7,6},{8,9},{9,8},{10,11... | collective-permute-start | bytes 786440 | tf_op jit(solution)/shard_map/ppermute | solution.py:379
  75.2 0.0 collective-permute-done.17.refs_3_.refs_1_
  75.2 1.0 %collective-permute-done.15.refs_1_.refs_0_ = bf16[128,1024]{1,0:T(8,128)(2,1)S(1)} collective-permute-done((bf16[128,1024]{1,0:T(8,128)(2,1)S(1)}, bf16[128,1024]{1,0:T(8,128)(2,1)S(1)}, u32[]{:S(2)}, u32[]{:S(2)}) %collective-permute-start.15) | collective-permute-done | bytes 262176 | tf_op jit(solution)/shard_map/ppermute | solution.py:379
  76.2 1.4 %add_sent.2 = (bf16[128,1024]{1,0:T(8,128)(2,1)S(1)}, bf16[128,1024]{1,0:T(8,128)(2,1)S(1)}) custom-call(s32[1]{0:T(128)} %bitcast.core_ref, f32[2,256,1024]{2,1,0:T(8,128)S(1)} %own_part.2.own_ref, bf16[128,1024]{1,0:T(8,128)(2,1)S(1)} %collective-permute-done.15.refs_1_.refs_0_, bf16[128,1024]{1,0:T(8,128)(2,1)S(1)} %collective-permute-done.17.refs_3_.refs_1_, ...), custom_call_target="tpu_custom_call" | custom-call | flops 536870912 | bytes 4194304 | tf_op jit(solution)/shard_map/add_sent/pallas_call | solution.py:333
  77.6 0.5 collective-permute-start.19
  78.1 1.6 %collective-permute-start.20 = (bf16[128,1024]{1,0:T(8,128)(2,1)S(1)}, bf16[128,1024]{1,0:T(8,128)(2,1)S(1)}, u32[]{:S(2)}, u32[]{:S(2)}) collective-permute-start(bf16[128,1024]{1,0:T(8,128)(2,1)S(1)} %get-tuple-element.70), channel_id=1, source_target_pairs={{0,1},{1,0},{2,3},{3,2},{4,5},{5,4},{6,7},{7,6},{8,9},{9,8},{10,11... | collective-permute-start | bytes 786440 | tf_op jit(solution)/shard_map/ppermute | solution.py:379
  79.7 1.9 %add_kept.1 = (f32[256,1024]{1,0:T(8,128)S(1)}, f32[256,1024]{1,0:T(8,128)S(1)}) custom-call(s32[1]{0:T(128)} %bitcast.core_ref, f32[2,256,1024]{2,1,0:T(8,128)S(1)} %own_part.3.own_ref, bf16[128,1024]{1,0:T(8,128)(2,1)S(1)} %collective-permute-done.14.refs_0_, bf16[128,1024]{1,0:T(8,128)(2,1)S(1)} %collective-permute-done.15.refs_1_.refs_0_, ...), custom_call_target="tpu_custom_call" | custom-call | flops 1073741824 | bytes 4194304 | tf_op jit(solution)/shard_map/add_kept/pallas_call | solution.py:333
  81.6 0.0 collective-permute-done.21.sum_a_ref
  81.6 1.5 %collective-permute-done.22.sum_b_ref = bf16[128,1024]{1,0:T(8,128)(2,1)S(1)} collective-permute-done((bf16[128,1024]{1,0:T(8,128)(2,1)S(1)}, bf16[128,1024]{1,0:T(8,128)(2,1)S(1)}, u32[]{:S(2)}, u32[]{:S(2)}) %collective-permute-start.22) | collective-permute-done | bytes 262176 | tf_op jit(solution)/shard_map/ppermute | solution.py:379
  83.1 0.9 %finish.2.refs_0_ = bf16[256,2048]{1,0:T(8,128)(2,1)} custom-call(f32[256,1024]{1,0:T(8,128)S(1)} %get-tuple-element.66.kept_a_ref, f32[256,1024]{1,0:T(8,128)S(1)} %get-tuple-element.67.kept_b_ref, bf16[128,1024]{1,0:T(8,128)(2,1)S(1)} %collective-permute-done.21.sum_a_ref, bf16[128,1024]{1,0:T(8,128)(2,1)S(1)} %collective-permute-done.22.sum_b_ref), custom_call_target="tpu_custom_call" | custom-call | tf_op jit(solution)/shard_map/finish/pallas_call | solution.py:366
  84.0 1.6 %collective-permute-done.19.sum_a_ref = bf16[128,1024]{1,0:T(8,128)(2,1)S(1)} collective-permute-done((bf16[128,1024]{1,0:T(8,128)(2,1)S(1)}, bf16[128,1024]{1,0:T(8,128)(2,1)S(1)}, u32[]{:S(2)}, u32[]{:S(2)}) %collective-permute-start.19) | collective-permute-done | bytes 262176 | tf_op jit(solution)/shard_map/ppermute | solution.py:379
  85.6 1.2 %collective-permute-done.20.sum_b_ref = bf16[128,1024]{1,0:T(8,128)(2,1)S(1)} collective-permute-done((bf16[128,1024]{1,0:T(8,128)(2,1)S(1)}, bf16[128,1024]{1,0:T(8,128)(2,1)S(1)}, u32[]{:S(2)}, u32[]{:S(2)}) %collective-permute-start.20) | collective-permute-done | bytes 262176 | tf_op jit(solution)/shard_map/ppermute | solution.py:379
  86.9 0.9 %finish.3 = bf16[256,2048]{1,0:T(8,128)(2,1)} custom-call(f32[256,1024]{1,0:T(8,128)S(1)} %get-tuple-element.66.kept_a_ref, f32[256,1024]{1,0:T(8,128)S(1)} %get-tuple-element.67.kept_b_ref, bf16[128,1024]{1,0:T(8,128)(2,1)S(1)} %collective-permute-done.19.sum_a_ref, ...), custom_call_target="tpu_custom_call", output_to_operand_aliasing={{}: (4, {})} | custom-call | tf_op jit(solution)/shard_map/finish/pallas_call | solution.py:366
  (25 shorter events, 0.1 us)
Async XLA Ops:
  3.2 12.3 %collective-permute-start = (bf16[6,128,128]{2,1,0:T(8,128)(2,1)}, bf16[6,128,128]{2,1,0:T(8,128)(2,1)S(1)}, u32[]{:S(2)}, u32[]{:S(2)}) collective-permute-start(bf16[6,128,128]{2,1,0:T(8,128)(2,1)} %get-tuple-element.43), channel_id=1, source_target_pairs={{0,24},{4,28},{8,16},{12,20},{16,8},{20,12},{24,0},{28,4},{1,25},{... | collective-permute-start | bytes 589832 | tf_op jit(solution)/shard_map/ppermute | solution.py:379
  8.4 6.4 %copy-start.11 = (bf16[6,128,128]{2,1,0:T(8,128)(2,1)S(1)}, bf16[6,128,128]{2,1,0:T(8,128)(2,1)}, u32[]{:S(2)}) copy-start(bf16[6,128,128]{2,1,0:T(8,128)(2,1)} %get-tuple-element.45) | copy-start | bytes 589828
  8.4 6.4 %copy-start.10 = (bf16[6,128,128]{2,1,0:T(8,128)(2,1)S(1)}, bf16[6,128,128]{2,1,0:T(8,128)(2,1)}, u32[]{:S(2)}) copy-start(bf16[6,128,128]{2,1,0:T(8,128)(2,1)} %get-tuple-element.46) | copy-start | bytes 589828
  8.4 7.2 %copy-start.9 = (bf16[6,128,128]{2,1,0:T(8,128)(2,1)S(1)}, bf16[6,128,128]{2,1,0:T(8,128)(2,1)}, u32[]{:S(2)}) copy-start(bf16[6,128,128]{2,1,0:T(8,128)(2,1)} %get-tuple-element.47) | copy-start | bytes 589828
  8.4 21.4 %copy-start.8 = (bf16[6,128,128]{2,1,0:T(8,128)(2,1)S(1)}, bf16[6,128,128]{2,1,0:T(8,128)(2,1)}, u32[]{:S(2)}) copy-start(bf16[6,128,128]{2,1,0:T(8,128)(2,1)} %get-tuple-element.48) | copy-start | bytes 589828
  8.4 21.4 %copy-start.7 = (bf16[6,128,128]{2,1,0:T(8,128)(2,1)S(1)}, bf16[6,128,128]{2,1,0:T(8,128)(2,1)}, u32[]{:S(2)}) copy-start(bf16[6,128,128]{2,1,0:T(8,128)(2,1)} %get-tuple-element.49) | copy-start | bytes 589828
  8.4 24.9 %copy-start.6 = (bf16[6,128,128]{2,1,0:T(8,128)(2,1)S(1)}, bf16[6,128,128]{2,1,0:T(8,128)(2,1)}, u32[]{:S(2)}) copy-start(bf16[6,128,128]{2,1,0:T(8,128)(2,1)} %get-tuple-element.50) | copy-start | bytes 589828
  8.4 33.7 %copy-start = (bf16[1024,1024]{1,0:T(8,128)(2,1)S(1)}, bf16[1024,1024]{1,0:T(8,128)(2,1)}, u32[]{:S(2)}) copy-start(bf16[1024,1024]{1,0:T(8,128)(2,1)} %constant.32.clone.refs_9_.sin_ref) | copy-start | bytes 6291460
  8.4 33.7 %copy-start.1 = (bf16[1024,1024]{1,0:T(8,128)(2,1)S(1)}, bf16[1024,1024]{1,0:T(8,128)(2,1)}, u32[]{:S(2)}) copy-start(bf16[1024,1024]{1,0:T(8,128)(2,1)} %constant.31.clone.refs_8_.cos_ref) | copy-start | bytes 6291460
  8.4 33.6 %copy-start.3 = (bf16[6,128,128]{2,1,0:T(8,128)(2,1)S(1)}, bf16[6,128,128]{2,1,0:T(8,128)(2,1)}, u32[]{:S(2)}) copy-start(bf16[6,128,128]{2,1,0:T(8,128)(2,1)} %get-tuple-element.51.refs_7_) | copy-start | bytes 589828
  8.5 33.6 %copy-start.4 = (f32[1024,128]{1,0:T(8,128)S(1)}, f32[1024,128]{1,0:T(8,128)}, u32[]{:S(2)}) copy-start(f32[1024,128]{1,0:T(8,128)} %constant.34.clone.refs_11_) | copy-start | bytes 1572868
  8.5 33.6 %copy-start.5 = (f32[1024,128]{1,0:T(8,128)S(1)}, f32[1024,128]{1,0:T(8,128)}, u32[]{:S(2)}) copy-start(f32[1024,128]{1,0:T(8,128)} %constant.33.clone.refs_10_) | copy-start | bytes 1572868
  11.7 48.2 %collective-permute-start.11 = (bf16[1024,1024]{1,0:T(8,128)(2,1)S(1)}, bf16[1024,1024]{1,0:T(8,128)(2,1)S(1)}, u32[]{:S(2)}, u32[]{:S(2)}) collective-permute-start(bf16[1024,1024]{1,0:T(8,128)(2,1)S(1)} %get-tuple-element.58), channel_id=1, source_target_pairs={{0,1},{1,0},{2,3},{3,2},{4,5},{5,4},{6,7},{7,6},{8,9},{9,8},{10,11... | collective-permute-start | bytes 6291464 | tf_op jit(solution)/shard_map/ppermute | solution.py:379
  13.2 46.8 %collective-permute-start.12 = (bf16[1024,1024]{1,0:T(8,128)(2,1)S(1)}, bf16[1024,1024]{1,0:T(8,128)(2,1)S(1)}, u32[]{:S(2)}, u32[]{:S(2)}) collective-permute-start(bf16[1024,1024]{1,0:T(8,128)(2,1)S(1)} %get-tuple-element.59), channel_id=1, source_target_pairs={{0,2},{1,3},{2,0},{3,1},{4,6},{5,7},{6,4},{7,5},{8,10},{9,11},{10,... | collective-permute-start | bytes 6291464 | tf_op jit(solution)/shard_map/ppermute | solution.py:379
  14.8 15.1 %collective-permute-start.1 = (bf16[6,128,128]{2,1,0:T(8,128)(2,1)S(1)}, bf16[6,128,128]{2,1,0:T(8,128)(2,1)S(1)}, u32[]{:S(2)}, u32[]{:S(2)}) collective-permute-start(bf16[6,128,128]{2,1,0:T(8,128)(2,1)S(1)} %copy-done.11), channel_id=1, source_target_pairs={{0,16},{4,20},{8,24},{12,28},{16,0},{20,4},{24,8},{28,12},{1,17},{... | collective-permute-start | bytes 589832 | tf_op jit(solution)/shard_map/ppermute | solution.py:379
  14.8 15.1 %collective-permute-start.2 = (bf16[6,128,128]{2,1,0:T(8,128)(2,1)S(1)}, bf16[6,128,128]{2,1,0:T(8,128)(2,1)S(1)}, u32[]{:S(2)}, u32[]{:S(2)}) collective-permute-start(bf16[6,128,128]{2,1,0:T(8,128)(2,1)S(1)} %copy-done.10), channel_id=1, source_target_pairs={{0,8},{4,12},{8,0},{12,4},{16,24},{20,28},{24,16},{28,20},{1,9},{5... | collective-permute-start | bytes 589832 | tf_op jit(solution)/shard_map/ppermute | solution.py:379
  15.6 17.8 %collective-permute-start.3 = (bf16[6,128,128]{2,1,0:T(8,128)(2,1)S(1)}, bf16[6,128,128]{2,1,0:T(8,128)(2,1)S(1)}, u32[]{:S(2)}, u32[]{:S(2)}) collective-permute-start(bf16[6,128,128]{2,1,0:T(8,128)(2,1)S(1)} %copy-done.9), channel_id=1, source_target_pairs={{0,28},{4,24},{8,20},{12,16},{16,12},{20,8},{24,4},{28,0},{1,29},{... | collective-permute-start | bytes 589832 | tf_op jit(solution)/shard_map/ppermute | solution.py:379
  29.8 12.3 %collective-permute-start.4 = (bf16[6,128,128]{2,1,0:T(8,128)(2,1)S(1)}, bf16[6,128,128]{2,1,0:T(8,128)(2,1)S(1)}, u32[]{:S(2)}, u32[]{:S(2)}) collective-permute-start(bf16[6,128,128]{2,1,0:T(8,128)(2,1)S(1)} %copy-done.8), channel_id=1, source_target_pairs={{0,20},{4,16},{8,28},{12,24},{16,4},{20,0},{24,12},{28,8},{1,21},{... | collective-permute-start | bytes 589832 | tf_op jit(solution)/shard_map/ppermute | solution.py:379
  29.8 12.2 %collective-permute-start.5 = (bf16[6,128,128]{2,1,0:T(8,128)(2,1)S(1)}, bf16[6,128,128]{2,1,0:T(8,128)(2,1)S(1)}, u32[]{:S(2)}, u32[]{:S(2)}) collective-permute-start(bf16[6,128,128]{2,1,0:T(8,128)(2,1)S(1)} %copy-done.7), channel_id=1, source_target_pairs={{0,12},{4,8},{8,4},{12,0},{16,28},{20,24},{24,20},{28,16},{1,13},{... | collective-permute-start | bytes 589832 | tf_op jit(solution)/shard_map/ppermute | solution.py:379
  33.4 8.7 %collective-permute-start.6 = (bf16[6,128,128]{2,1,0:T(8,128)(2,1)S(1)}, bf16[6,128,128]{2,1,0:T(8,128)(2,1)S(1)}, u32[]{:S(2)}, u32[]{:S(2)}) collective-permute-start(bf16[6,128,128]{2,1,0:T(8,128)(2,1)S(1)} %copy-done.6), channel_id=1, source_target_pairs={{0,4},{4,0},{8,12},{12,8},{16,20},{20,16},{24,28},{28,24},{1,5},{5... | collective-permute-start | bytes 589832 | tf_op jit(solution)/shard_map/ppermute | solution.py:379
  44.7 1.6 %collective-permute-start.7 = (bf16[4,2,128,128]{3,2,1,0:T(8,128)(2,1)S(1)}, bf16[4,2,128,128]{3,2,1,0:T(8,128)(2,1)S(1)}, u32[]{:S(2)}, u32[]{:S(2)}) collective-permute-start(bf16[4,2,128,128]{3,2,1,0:T(8,128)(2,1)S(1)} %get-tuple-element.54), channel_id=1, source_target_pairs={{0,4},{4,0},{8,12},{12,8},{16,20},{20,16},{24,28},{28,24},{1,5},{5... | collective-permute-start | bytes 786440 | tf_op jit(solution)/shard_map/ppermute | solution.py:379
  45.5 13.9 %copy-start.2 = (bf16[256,1024]{1,0:T(8,128)(2,1)S(1)}, bf16[256,1024]{1,0:T(8,128)(2,1)}, u32[]{:S(2)}) copy-start(bf16[256,1024]{1,0:T(8,128)(2,1)} %refs_4_.1) | copy-start | bytes 1572868
  46.3 8.3 %collective-permute-start.8 = (bf16[2,2,128,128]{3,2,1,0:T(8,128)(2,1)S(1)}, bf16[2,2,128,128]{3,2,1,0:T(8,128)(2,1)S(1)}, u32[]{:S(2)}, u32[]{:S(2)}) collective-permute-start(bf16[2,2,128,128]{3,2,1,0:T(8,128)(2,1)S(1)} %pad_maximum_fusion), channel_id=1, source_target_pairs={{0,24},{4,28},{8,16},{12,20},{16,8},{20,12},{24,0},{28,4},{1,25},{... | collective-permute-start | bytes 393224 | tf_op jit(solution)/shard_map/ppermute | solution.py:379
  48.3 11.1 %collective-permute-start.9 = (bf16[2,2,128,128]{3,2,1,0:T(8,128)(2,1)S(1)}, bf16[2,2,128,128]{3,2,1,0:T(8,128)(2,1)S(1)}, u32[]{:S(2)}, u32[]{:S(2)}) collective-permute-start(bf16[2,2,128,128]{3,2,1,0:T(8,128)(2,1)S(1)} %pad_maximum_fusion.1), channel_id=1, source_target_pairs={{0,16},{4,20},{8,24},{12,28},{16,0},{20,4},{24,8},{28,12},{1,17},{... | collective-permute-start | bytes 393224 | tf_op jit(solution)/shard_map/ppermute | solution.py:379
  48.4 11.0 %collective-permute-start.10 = (bf16[2,2,128,128]{3,2,1,0:T(8,128)(2,1)S(1)}, bf16[2,2,128,128]{3,2,1,0:T(8,128)(2,1)S(1)}, u32[]{:S(2)}, u32[]{:S(2)}) collective-permute-start(bf16[2,2,128,128]{3,2,1,0:T(8,128)(2,1)S(1)} %pad_maximum_fusion.2), channel_id=1, source_target_pairs={{0,8},{4,12},{8,0},{12,4},{16,24},{20,28},{24,16},{28,20},{1,9},{5... | collective-permute-start | bytes 393224 | tf_op jit(solution)/shard_map/ppermute | solution.py:379
  60.1 6.5 %collective-permute-start.13 = (bf16[1024,1024]{1,0:T(8,128)(2,1)S(1)}, bf16[1024,1024]{1,0:T(8,128)(2,1)S(1)}, u32[]{:S(2)}, u32[]{:S(2)}) collective-permute-start(bf16[1024,1024]{1,0:T(8,128)(2,1)S(1)} %collective-permute-done.11.refs_4_.refs_2_), channel_id=1, source_target_pairs={{0,4},{4,0},{8,12},{12,8},{16,20},{20,16},{24,28},{28,24},{1,5},{5... | collective-permute-start | bytes 6291464 | tf_op jit(solution)/shard_map/ppermute | solution.py:379
  60.1 10.9 %collective-permute-start.18 = (bf16[1024,1024]{1,0:T(8,128)(2,1)S(1)}, bf16[1024,1024]{1,0:T(8,128)(2,1)S(1)}, u32[]{:S(2)}, u32[]{:S(2)}) collective-permute-start(bf16[1024,1024]{1,0:T(8,128)(2,1)S(1)} %collective-permute-done.12.refs_6_.refs_4_), channel_id=1, source_target_pairs={{0,4},{4,0},{8,12},{12,8},{16,20},{20,16},{24,28},{28,24},{1,5},{5... | collective-permute-start | bytes 6291464 | tf_op jit(solution)/shard_map/ppermute | solution.py:379
  60.6 10.2 %collective-permute-start.16 = (bf16[128,1024]{1,0:T(8,128)(2,1)S(1)}, bf16[128,1024]{1,0:T(8,128)(2,1)S(1)}, u32[]{:S(2)}, u32[]{:S(2)}) collective-permute-start(bf16[128,1024]{1,0:T(8,128)(2,1)S(1)} %get-tuple-element.56.refs_0_), channel_id=1, source_target_pairs={{0,2},{1,3},{2,0},{3,1},{4,6},{5,7},{6,4},{7,5},{8,10},{9,11},{10,... | collective-permute-start | bytes 786440 | tf_op jit(solution)/shard_map/ppermute | solution.py:379
  62.1 8.8 %collective-permute-start.14 = (bf16[128,1024]{1,0:T(8,128)(2,1)S(1)}, bf16[128,1024]{1,0:T(8,128)(2,1)S(1)}, u32[]{:S(2)}, u32[]{:S(2)}) collective-permute-start(bf16[128,1024]{1,0:T(8,128)(2,1)S(1)} %get-tuple-element.56.refs_0_), channel_id=1, source_target_pairs={{0,1},{1,0},{2,3},{3,2},{4,5},{5,4},{6,7},{7,6},{8,9},{9,8},{10,11... | collective-permute-start | bytes 786440 | tf_op jit(solution)/shard_map/ppermute | solution.py:379
  66.5 8.7 %collective-permute-start.17 = (bf16[128,1024]{1,0:T(8,128)(2,1)S(1)}, bf16[128,1024]{1,0:T(8,128)(2,1)S(1)}, u32[]{:S(2)}, u32[]{:S(2)}) collective-permute-start(bf16[128,1024]{1,0:T(8,128)(2,1)S(1)} %get-tuple-element.63.refs_1_), channel_id=1, source_target_pairs={{0,2},{1,3},{2,0},{3,1},{4,6},{5,7},{6,4},{7,5},{8,10},{9,11},{10,... | collective-permute-start | bytes 786440 | tf_op jit(solution)/shard_map/ppermute | solution.py:379
  67.2 9.0 %collective-permute-start.15 = (bf16[128,1024]{1,0:T(8,128)(2,1)S(1)}, bf16[128,1024]{1,0:T(8,128)(2,1)S(1)}, u32[]{:S(2)}, u32[]{:S(2)}) collective-permute-start(bf16[128,1024]{1,0:T(8,128)(2,1)S(1)} %get-tuple-element.63.refs_1_), channel_id=1, source_target_pairs={{0,1},{1,0},{2,3},{3,2},{4,5},{5,4},{6,7},{7,6},{8,9},{9,8},{10,11... | collective-permute-start | bytes 786440 | tf_op jit(solution)/shard_map/ppermute | solution.py:379
  72.3 9.3 %collective-permute-start.21 = (bf16[128,1024]{1,0:T(8,128)(2,1)S(1)}, bf16[128,1024]{1,0:T(8,128)(2,1)S(1)}, u32[]{:S(2)}, u32[]{:S(2)}) collective-permute-start(bf16[128,1024]{1,0:T(8,128)(2,1)S(1)} %get-tuple-element.71), channel_id=1, source_target_pairs={{0,2},{1,3},{2,0},{3,1},{4,6},{5,7},{6,4},{7,5},{8,10},{9,11},{10,... | collective-permute-start | bytes 786440 | tf_op jit(solution)/shard_map/ppermute | solution.py:379
  73.8 9.2 %collective-permute-start.22 = (bf16[128,1024]{1,0:T(8,128)(2,1)S(1)}, bf16[128,1024]{1,0:T(8,128)(2,1)S(1)}, u32[]{:S(2)}, u32[]{:S(2)}) collective-permute-start(bf16[128,1024]{1,0:T(8,128)(2,1)S(1)} %get-tuple-element.72), channel_id=1, source_target_pairs={{0,1},{1,0},{2,3},{3,2},{4,5},{5,4},{6,7},{7,6},{8,9},{9,8},{10,11... | collective-permute-start | bytes 786440 | tf_op jit(solution)/shard_map/ppermute | solution.py:379
  77.6 8.1 %collective-permute-start.19 = (bf16[128,1024]{1,0:T(8,128)(2,1)S(1)}, bf16[128,1024]{1,0:T(8,128)(2,1)S(1)}, u32[]{:S(2)}, u32[]{:S(2)}) collective-permute-start(bf16[128,1024]{1,0:T(8,128)(2,1)S(1)} %get-tuple-element.69), channel_id=1, source_target_pairs={{0,2},{1,3},{2,0},{3,1},{4,6},{5,7},{6,4},{7,5},{8,10},{9,11},{10,... | collective-permute-start | bytes 786440 | tf_op jit(solution)/shard_map/ppermute | solution.py:379
  78.1 8.8 %collective-permute-start.20 = (bf16[128,1024]{1,0:T(8,128)(2,1)S(1)}, bf16[128,1024]{1,0:T(8,128)(2,1)S(1)}, u32[]{:S(2)}, u32[]{:S(2)}) collective-permute-start(bf16[128,1024]{1,0:T(8,128)(2,1)S(1)} %get-tuple-element.70), channel_id=1, source_target_pairs={{0,1},{1,0},{2,3},{3,2},{4,5},{5,4},{6,7},{7,6},{8,9},{9,8},{10,11... | collective-permute-start | bytes 786440 | tf_op jit(solution)/shard_map/ppermute | solution.py:379

commit v9 on v8

--- a/solution.py
+++ b/solution.py
@@ -144,15 +144,15 @@
         first_re = jnp.dot(cos_ref[at, :], cols_ref[...], preferred_element_type=jnp.float32)
         first_sin = jnp.dot(sin_ref[at, :], cols_ref[...], preferred_element_type=jnp.float32)
         tc, ts = turn_cos_ref[at, :], turn_sin_ref[at, :]
-        re0, im0 = first_re[:, :LANES], -first_sin[:, :LANES]
-        re1, im1 = first_re[:, LANES:], -first_sin[:, LANES:]
-        re1, im1 = re1 * tc + im1 * ts, im1 * tc - re1 * ts
-        f0r, f0i, f1r, f1i = re0 + re1, im0 + im1, re0 - re1, im0 - im1
+        re0, sin0 = first_re[:, :LANES], first_sin[:, :LANES]
+        re1, sin1 = first_re[:, LANES:], first_sin[:, LANES:]
+        re1, sin1 = re1 * tc - sin1 * ts, sin1 * tc + re1 * ts
+        f0r, f0s, f1r, f1s = re0 + re1, sin0 + sin1, re0 - re1, sin0 - sin1
         s0r, s1r, s0i, s1i = (filt_ref[part, at, :].astype(jnp.float32) for part in range(4))
-        p0r, p0i = f0r * s0r - f0i * s0i, f0r * s0i + f0i * s0r
-        p1r, p1i = f1r * s1r - f1i * s1i, f1r * s1i + f1i * s1r
-        b0r, b0i = 0.5 * (p0r + p1r), 0.5 * (p0i + p1i)
-        b1r, b1i = 0.5 * (p0r - p1r), 0.5 * (p0i - p1i)
+        p0r, p0i = f0r * s0r + f0s * s0i, f0r * s0i - f0s * s0r
+        p1r, p1i = f1r * s1r + f1s * s1i, f1r * s1i - f1s * s1r
+        b0r, b0i = p0r + p1r, p0i + p1i
+        b1r, b1i = p0r - p1r, p0i - p1i
         b1r, b1i = b1r * tc - b1i * ts, b1i * tc + b1r * ts
         re_ref[at, :] = jnp.concatenate([b0r, b1r], axis=1).astype(jnp.bfloat16)
         im_ref[at, :] = jnp.concatenate([b0i, b1i], axis=1).astype(jnp.bfloat16)
@@ -161,7 +161,7 @@
 
 def invert(me, flip, cos_ref, sin_ref, re_ref, im_ref, out_ref):
     chips, _, rows, _ = out_ref.shape
-    scale = 1.0 / (2 * chips * rows)
+    scale = 1.0 / (2 * 2 * chips * rows)
     for i in range(chips):
         at = pl.ds(pl.multiple_of((me ^ (2 * i + flip)) * rows, rows), rows)
         conv = jnp.dot(cos_ref[at, :], re_ref[...], preferred_element_type=jnp.float32)

time: 87.9 us -> 87.9 us (level)
  no operation moved by 1% of the time
where the time goes in v9:
time: 87.9 us; the launch traced here: 87.8 us
  waiting for transfers between devices  36.5 us (42%)
  starting transfers between devices  28.2 us (32%)
  Pallas kernels  22.6 us (26%)
    ppermute x23, waiting for transfers between devices, swap(): lax.ppermute(data, axis, [(i, i ^ flip) for i in range(lax.axis_size(axis...  36.5 us
    ppermute x23, starting transfers between devices, swap(): lax.ppermute(data, axis, [(i, i ^ flip) for i in range(lax.axis_size(axis...  28.2 us
    pallas_call x2, Pallas kernels, own_part(): pl.pallas_call(own_kernel, grid_spec=pltpu.PrefetchScalarGridSpec(num_sca...  6.09 us
    pallas_call x3, Pallas kernels, add_moved(): pl.pallas_call(functools.partial(add_kernel, parts, kept), grid=(1,), in_...  4.64 us
    pallas_call x1, Pallas kernels, pack(): pl.pallas_call(functools.partial(pack_kernel, span), in_specs=[pl.BlockSp...  3.19 us
    pallas_call x1, Pallas kernels, take_blocks(): pl.pallas_call(take_kernel, in_specs=[pl.BlockSpec(memory_space=pltpu.SME...  3.19 us
    pallas_call x1, Pallas kernels, convolve(): pl.pallas_call(functools.partial(conv_kernel, order), in_specs=[smem] + [...  2.45 us
    pallas_call x2, Pallas kernels, finish(): pl.pallas_call(finish_kernel, grid=(1,), in_specs=[kept, kept, sums, sums...  1.86 us
  transfers between devices with their start and end apart: 23, of which 11 were waited for; matrix products, arithmetic and copies ran while one was open for 0% of the time, Pallas kernels for 21%

profile of v9, /device:TPU:0, one launch (start us, length us, event | category | flops | bytes accessed | tf_op | source)
XLA Modules:
  0.0 87.8 jit_solution(14715406812746138455)
XLA Ops:
  0.0 3.2 %pack.1 = (bf16[6,128,128]{2,1,0:T(8,128)(2,1)}, bf16[6,128,128]{2,1,0:T(8,128)(2,1)}, bf16[6,128,128]{2,1,0:T(8,128)(2,1)}, bf16[6,128,128]{2,1,0:T(8,128)(2,1)...) custom-call(s32[1]{0:T(128)} %bitcast.1.me_ref, ...), custom_call_target="tpu_custom_call" | custom-call | tf_op jit(solution)/shard_map/pack/pallas_call | solution.py:79
  3.2 5.1 %collective-permute-start = (bf16[6,128,128]{2,1,0:T(8,128)(2,1)}, bf16[6,128,128]{2,1,0:T(8,128)(2,1)S(1)}, u32[]{:S(2)}, u32[]{:S(2)}) collective-permute-start(bf16[6,128,128]{2,1,0:T(8,128)(2,1)} %get-tuple-element.43), channel_id=1, source_target_pairs={{0,24},{4,28},{8,16},{12,20},{16,8},{20,12},{24,0},{28,4},{1,25},{... | collective-permute-start | bytes 589832 | tf_op jit(solution)/shard_map/ppermute | solution.py:379
  8.3 0.1 pad_add_fusion.places_ref
  8.4 0.0 copy-start
  8.4 0.0 copy-start.1
  8.4 0.0 copy-start.3
  8.5 0.0 copy-start.4
  8.5 0.0 copy-start.5
  8.5 3.2 %take_blocks.1 = (bf16[1024,1024]{1,0:T(8,128)(2,1)S(1)}, bf16[1024,1024]{1,0:T(8,128)(2,1)S(1)}) custom-call(s32[2]{0:T(128)S(1)} %pad_add_fusion.places_ref, bf16[1024,8192]{1,0:T(8,128)(2,1)} %refs_3_.3), custom_call_target="tpu_custom_call" | custom-call | bytes 134217728 | tf_op jit(solution)/shard_map/take_blocks/pallas_call | solution.py:117
  11.7 1.6 %collective-permute-start.11 = (bf16[1024,1024]{1,0:T(8,128)(2,1)S(1)}, bf16[1024,1024]{1,0:T(8,128)(2,1)S(1)}, u32[]{:S(2)}, u32[]{:S(2)}) collective-permute-start(bf16[1024,1024]{1,0:T(8,128)(2,1)S(1)} %get-tuple-element.58), channel_id=1, source_target_pairs={{0,1},{1,0},{2,3},{3,2},{4,5},{5,4},{6,7},{7,6},{8,9},{9,8},{10,11... | collective-permute-start | bytes 6291464 | tf_op jit(solution)/shard_map/ppermute | solution.py:379
  13.2 1.5 %collective-permute-start.12 = (bf16[1024,1024]{1,0:T(8,128)(2,1)S(1)}, bf16[1024,1024]{1,0:T(8,128)(2,1)S(1)}, u32[]{:S(2)}, u32[]{:S(2)}) collective-permute-start(bf16[1024,1024]{1,0:T(8,128)(2,1)S(1)} %get-tuple-element.59), channel_id=1, source_target_pairs={{0,2},{1,3},{2,0},{3,1},{4,6},{5,7},{6,4},{7,5},{8,10},{9,11},{10,... | collective-permute-start | bytes 6291464 | tf_op jit(solution)/shard_map/ppermute | solution.py:379
  14.8 0.0 collective-permute-start.1
  14.8 0.8 collective-permute-start.2
  15.5 0.0 collective-permute-done.refs_0_
  15.6 1.6 %collective-permute-start.3 = (bf16[6,128,128]{2,1,0:T(8,128)(2,1)S(1)}, bf16[6,128,128]{2,1,0:T(8,128)(2,1)S(1)}, u32[]{:S(2)}, u32[]{:S(2)}) collective-permute-start(bf16[6,128,128]{2,1,0:T(8,128)(2,1)S(1)} %copy-done.9), channel_id=1, source_target_pairs={{0,28},{4,24},{8,20},{12,16},{16,12},{20,8},{24,4},{28,0},{1,29},{... | collective-permute-start | bytes 589832 | tf_op jit(solution)/shard_map/ppermute | solution.py:379
  17.2 12.6 %collective-permute-done.1.refs_1_ = bf16[6,128,128]{2,1,0:T(8,128)(2,1)S(1)} collective-permute-done((bf16[6,128,128]{2,1,0:T(8,128)(2,1)S(1)}, bf16[6,128,128]{2,1,0:T(8,128)(2,1)S(1)}, u32[]{:S(2)}, u32[]{:S(2)}) %collective-permute-start.1) | collective-permute-done | bytes 196640 | tf_op jit(solution)/shard_map/ppermute | solution.py:379
  29.8 0.0 collective-permute-start.4
  29.8 0.0 collective-permute-done.2.refs_2_
  29.8 3.5 %collective-permute-start.5 = (bf16[6,128,128]{2,1,0:T(8,128)(2,1)S(1)}, bf16[6,128,128]{2,1,0:T(8,128)(2,1)S(1)}, u32[]{:S(2)}, u32[]{:S(2)}) collective-permute-start(bf16[6,128,128]{2,1,0:T(8,128)(2,1)S(1)} %copy-done.7), channel_id=1, source_target_pairs={{0,12},{4,8},{8,4},{12,0},{16,28},{20,24},{24,20},{28,16},{1,13},{... | collective-permute-start | bytes 589832 | tf_op jit(solution)/shard_map/ppermute | solution.py:379
  33.3 0.0 collective-permute-done.3.refs_3_
  33.4 0.0 collective-permute-start.6
  33.4 8.7 %collective-permute-done.4.refs_4_ = bf16[6,128,128]{2,1,0:T(8,128)(2,1)S(1)} collective-permute-done((bf16[6,128,128]{2,1,0:T(8,128)(2,1)S(1)}, bf16[6,128,128]{2,1,0:T(8,128)(2,1)S(1)}, u32[]{:S(2)}, u32[]{:S(2)}) %collective-permute-start.4) | collective-permute-done | bytes 196640 | tf_op jit(solution)/shard_map/ppermute | solution.py:379
  42.1 0.0 collective-permute-done.5.refs_5_
  42.1 0.0 collective-permute-done.6.refs_6_
  42.1 2.5 %convolve.1 = (bf16[4,2,128,128]{3,2,1,0:T(8,128)(2,1)S(1)}, bf16[1024,256]{1,0:T(8,128)(2,1)S(1)}, bf16[1024,256]{1,0:T(8,128)(2,1)S(1)}) custom-call(s32[1]{0:T(128)} %bitcast.1.me_ref, bf16[6,128,128]{2,1,0:T(8,128)(2,1)S(1)} %collective-permute-done.refs_0_, bf16[6,128,128]{2,1,0:T(8,128)(2,1)S(1)} %collective-permute-done.1.refs_1_, ...), custom_call_target="tpu_custom_call" | custom-call | flops 6710886400 | bytes 8388608 | tf_op jit(solution)/shard_map/convolve/pallas_call | solution.py:188
  44.6 0.1 collective-permute-start.7
  44.7 0.7 convolve_rest.1
  45.4 0.0 copy-start.2
  45.5 0.7 collective-permute-done.7
  46.2 2.0 %collective-permute-start.8 = (bf16[2,2,128,128]{3,2,1,0:T(8,128)(2,1)S(1)}, bf16[2,2,128,128]{3,2,1,0:T(8,128)(2,1)S(1)}, u32[]{:S(2)}, u32[]{:S(2)}) collective-permute-start(bf16[2,2,128,128]{3,2,1,0:T(8,128)(2,1)S(1)} %pad_maximum_fusion), channel_id=1, source_target_pairs={{0,24},{4,28},{8,16},{12,20},{16,8},{20,12},{24,0},{28,4},{1,25},{... | collective-permute-start | bytes 393224 | tf_op jit(solution)/shard_map/ppermute | solution.py:379
  48.2 0.1 collective-permute-start.9
  48.3 2.5 %collective-permute-start.10 = (bf16[2,2,128,128]{3,2,1,0:T(8,128)(2,1)S(1)}, bf16[2,2,128,128]{3,2,1,0:T(8,128)(2,1)S(1)}, u32[]{:S(2)}, u32[]{:S(2)}) collective-permute-start(bf16[2,2,128,128]{3,2,1,0:T(8,128)(2,1)S(1)} %pad_maximum_fusion.2), channel_id=1, source_target_pairs={{0,8},{4,12},{8,0},{12,4},{16,24},{20,28},{24,16},{28,20},{1,9},{5... | collective-permute-start | bytes 393224 | tf_op jit(solution)/shard_map/ppermute | solution.py:379
  50.9 3.7 %collective-permute-done.8.refs_0_ = bf16[2,2,128,128]{3,2,1,0:T(8,128)(2,1)S(1)} collective-permute-done((bf16[2,2,128,128]{3,2,1,0:T(8,128)(2,1)S(1)}, bf16[2,2,128,128]{3,2,1,0:T(8,128)(2,1)S(1)}, u32[]{:S(2)}, u32[]{:S(2)}) %collective-permute-start.8) | collective-permute-done | bytes 131104 | tf_op jit(solution)/shard_map/ppermute | solution.py:379
  54.6 4.8 %collective-permute-done.9.refs_1_ = bf16[2,2,128,128]{3,2,1,0:T(8,128)(2,1)S(1)} collective-permute-done((bf16[2,2,128,128]{3,2,1,0:T(8,128)(2,1)S(1)}, bf16[2,2,128,128]{3,2,1,0:T(8,128)(2,1)S(1)}, u32[]{:S(2)}, u32[]{:S(2)}) %collective-permute-start.9) | collective-permute-done | bytes 131104 | tf_op jit(solution)/shard_map/ppermute | solution.py:379
  59.4 0.0 collective-permute-done.10.refs_2_
  59.4 0.5 gate.1
  59.8 0.0 collective-permute-done.11.refs_4_.refs_2_
  59.8 0.2 collective-permute-done.12.refs_6_.refs_4_
  60.1 0.0 collective-permute-start.13
  60.1 0.5 collective-permute-start.18
  60.6 1.5 %collective-permute-start.16 = (bf16[128,1024]{1,0:T(8,128)(2,1)S(1)}, bf16[128,1024]{1,0:T(8,128)(2,1)S(1)}, u32[]{:S(2)}, u32[]{:S(2)}) collective-permute-start(bf16[128,1024]{1,0:T(8,128)(2,1)S(1)} %get-tuple-element.56.refs_0_), channel_id=1, source_target_pairs={{0,2},{1,3},{2,0},{3,1},{4,6},{5,7},{6,4},{7,5},{8,10},{9,11},{10,... | collective-permute-start | bytes 786440 | tf_op jit(solution)/shard_map/ppermute | solution.py:379
  62.1 1.3 %collective-permute-start.14 = (bf16[128,1024]{1,0:T(8,128)(2,1)S(1)}, bf16[128,1024]{1,0:T(8,128)(2,1)S(1)}, u32[]{:S(2)}, u32[]{:S(2)}) collective-permute-start(bf16[128,1024]{1,0:T(8,128)(2,1)S(1)} %get-tuple-element.56.refs_0_), channel_id=1, source_target_pairs={{0,1},{1,0},{2,3},{3,2},{4,5},{5,4},{6,7},{7,6},{8,9},{9,8},{10,11... | collective-permute-start | bytes 786440 | tf_op jit(solution)/shard_map/ppermute | solution.py:379
  63.4 3.0 %own_part.2.own_ref = f32[2,256,1024]{2,1,0:T(8,128)S(1)} custom-call(s32[1]{0:T(128)} %bitcast.2.me_ref, bf16[128,1024]{1,0:T(8,128)(2,1)S(1)} %get-tuple-element.56.refs_0_, bf16[128,1024]{1,0:T(8,128)(2,1)S(1)} %get-tuple-element.63.refs_1_, bf16[1024,8192]{1,0:T(8,128)(2,1)} %refs_3_.3, bf16[1024,8192]{1,0:T(8,128)(2,1)} %refs_3_.3), custom_call_target="tpu_custom_call" | custom-call | flops 1073741824 | bytes 4194304 | tf_op jit(solution)/shard_map/own_part/pallas_call | solution.py:267
  66.4 0.0 collective-permute-done.13.refs_5_.refs_3_
  66.5 0.6 collective-permute-start.17
  67.1 0.7 collective-permute-start.15
  67.7 3.0 %own_part.3.own_ref = f32[2,256,1024]{2,1,0:T(8,128)S(1)} custom-call(s32[1]{0:T(128)} %bitcast.2.me_ref, bf16[128,1024]{1,0:T(8,128)(2,1)S(1)} %get-tuple-element.56.refs_0_, bf16[128,1024]{1,0:T(8,128)(2,1)S(1)} %get-tuple-element.63.refs_1_, bf16[1024,8192]{1,0:T(8,128)(2,1)} %refs_3_.3, bf16[1024,8192]{1,0:T(8,128)(2,1)} %refs_3_.3), custom_call_target="tpu_custom_call" | custom-call | flops 1073741824 | bytes 4194304 | tf_op jit(solution)/shard_map/own_part/pallas_call | solution.py:267
  70.8 0.2 collective-permute-done.14.refs_0_
  71.0 0.0 collective-permute-done.18.refs_7_.refs_5_
  71.0 1.4 %add_sent.3 = (bf16[128,1024]{1,0:T(8,128)(2,1)S(1)}, bf16[128,1024]{1,0:T(8,128)(2,1)S(1)}) custom-call(s32[1]{0:T(128)} %bitcast.core_ref, f32[2,256,1024]{2,1,0:T(8,128)S(1)} %own_part.2.own_ref, bf16[128,1024]{1,0:T(8,128)(2,1)S(1)} %collective-permute-done.14.refs_0_, bf16[128,1024]{1,0:T(8,128)(2,1)S(1)} %collective-permute-done.16.refs_2_.refs_1_, ...), custom_call_target="tpu_custom_call" | custom-call | flops 536870912 | bytes 4194304 | tf_op jit(solution)/shard_map/add_sent/pallas_call | solution.py:333
  72.4 1.4 %collective-permute-start.21 = (bf16[128,1024]{1,0:T(8,128)(2,1)S(1)}, bf16[128,1024]{1,0:T(8,128)(2,1)S(1)}, u32[]{:S(2)}, u32[]{:S(2)}) collective-permute-start(bf16[128,1024]{1,0:T(8,128)(2,1)S(1)} %get-tuple-element.71), channel_id=1, source_target_pairs={{0,2},{1,3},{2,0},{3,1},{4,6},{5,7},{6,4},{7,5},{8,10},{9,11},{10,... | collective-permute-start | bytes 786440 | tf_op jit(solution)/shard_map/ppermute | solution.py:379
  73.8 1.3 %collective-permute-start.22 = (bf16[128,1024]{1,0:T(8,128)(2,1)S(1)}, bf16[128,1024]{1,0:T(8,128)(2,1)S(1)}, u32[]{:S(2)}, u32[]{:S(2)}) collective-permute-start(bf16[128,1024]{1,0:T(8,128)(2,1)S(1)} %get-tuple-element.72), channel_id=1, source_target_pairs={{0,1},{1,0},{2,3},{3,2},{4,5},{5,4},{6,7},{7,6},{8,9},{9,8},{10,11... | collective-permute-start | bytes 786440 | tf_op jit(solution)/shard_map/ppermute | solution.py:379
  75.1 0.0 collective-permute-done.17.refs_3_.refs_1_
  75.1 1.1 %collective-permute-done.15.refs_1_.refs_0_ = bf16[128,1024]{1,0:T(8,128)(2,1)S(1)} collective-permute-done((bf16[128,1024]{1,0:T(8,128)(2,1)S(1)}, bf16[128,1024]{1,0:T(8,128)(2,1)S(1)}, u32[]{:S(2)}, u32[]{:S(2)}) %collective-permute-start.15) | collective-permute-done | bytes 262176 | tf_op jit(solution)/shard_map/ppermute | solution.py:379
  76.2 1.4 %add_sent.2 = (bf16[128,1024]{1,0:T(8,128)(2,1)S(1)}, bf16[128,1024]{1,0:T(8,128)(2,1)S(1)}) custom-call(s32[1]{0:T(128)} %bitcast.core_ref, f32[2,256,1024]{2,1,0:T(8,128)S(1)} %own_part.2.own_ref, bf16[128,1024]{1,0:T(8,128)(2,1)S(1)} %collective-permute-done.15.refs_1_.refs_0_, bf16[128,1024]{1,0:T(8,128)(2,1)S(1)} %collective-permute-done.17.refs_3_.refs_1_, ...), custom_call_target="tpu_custom_call" | custom-call | flops 536870912 | bytes 4194304 | tf_op jit(solution)/shard_map/add_sent/pallas_call | solution.py:333
  77.6 0.6 collective-permute-start.19
  78.1 1.4 %collective-permute-start.20 = (bf16[128,1024]{1,0:T(8,128)(2,1)S(1)}, bf16[128,1024]{1,0:T(8,128)(2,1)S(1)}, u32[]{:S(2)}, u32[]{:S(2)}) collective-permute-start(bf16[128,1024]{1,0:T(8,128)(2,1)S(1)} %get-tuple-element.70), channel_id=1, source_target_pairs={{0,1},{1,0},{2,3},{3,2},{4,5},{5,4},{6,7},{7,6},{8,9},{9,8},{10,11... | collective-permute-start | bytes 786440 | tf_op jit(solution)/shard_map/ppermute | solution.py:379
  79.6 1.9 %add_kept.1 = (f32[256,1024]{1,0:T(8,128)S(1)}, f32[256,1024]{1,0:T(8,128)S(1)}) custom-call(s32[1]{0:T(128)} %bitcast.core_ref, f32[2,256,1024]{2,1,0:T(8,128)S(1)} %own_part.3.own_ref, bf16[128,1024]{1,0:T(8,128)(2,1)S(1)} %collective-permute-done.14.refs_0_, bf16[128,1024]{1,0:T(8,128)(2,1)S(1)} %collective-permute-done.15.refs_1_.refs_0_, ...), custom_call_target="tpu_custom_call" | custom-call | flops 1073741824 | bytes 4194304 | tf_op jit(solution)/shard_map/add_kept/pallas_call | solution.py:333
  81.5 0.0 collective-permute-done.21.sum_a_ref
  81.5 1.6 %collective-permute-done.22.sum_b_ref = bf16[128,1024]{1,0:T(8,128)(2,1)S(1)} collective-permute-done((bf16[128,1024]{1,0:T(8,128)(2,1)S(1)}, bf16[128,1024]{1,0:T(8,128)(2,1)S(1)}, u32[]{:S(2)}, u32[]{:S(2)}) %collective-permute-start.22) | collective-permute-done | bytes 262176 | tf_op jit(solution)/shard_map/ppermute | solution.py:379
  83.1 0.9 %finish.2.refs_0_ = bf16[256,2048]{1,0:T(8,128)(2,1)} custom-call(f32[256,1024]{1,0:T(8,128)S(1)} %get-tuple-element.66.kept_a_ref, f32[256,1024]{1,0:T(8,128)S(1)} %get-tuple-element.67.kept_b_ref, bf16[128,1024]{1,0:T(8,128)(2,1)S(1)} %collective-permute-done.21.sum_a_ref, bf16[128,1024]{1,0:T(8,128)(2,1)S(1)} %collective-permute-done.22.sum_b_ref), custom_call_target="tpu_custom_call" | custom-call | tf_op jit(solution)/shard_map/finish/pallas_call | solution.py:366
  84.0 1.6 %collective-permute-done.19.sum_a_ref = bf16[128,1024]{1,0:T(8,128)(2,1)S(1)} collective-permute-done((bf16[128,1024]{1,0:T(8,128)(2,1)S(1)}, bf16[128,1024]{1,0:T(8,128)(2,1)S(1)}, u32[]{:S(2)}, u32[]{:S(2)}) %collective-permute-start.19) | collective-permute-done | bytes 262176 | tf_op jit(solution)/shard_map/ppermute | solution.py:379
  85.6 1.2 %collective-permute-done.20.sum_b_ref = bf16[128,1024]{1,0:T(8,128)(2,1)S(1)} collective-permute-done((bf16[128,1024]{1,0:T(8,128)(2,1)S(1)}, bf16[128,1024]{1,0:T(8,128)(2,1)S(1)}, u32[]{:S(2)}, u32[]{:S(2)}) %collective-permute-start.20) | collective-permute-done | bytes 262176 | tf_op jit(solution)/shard_map/ppermute | solution.py:379
  86.9 0.9 %finish.3 = bf16[256,2048]{1,0:T(8,128)(2,1)} custom-call(f32[256,1024]{1,0:T(8,128)S(1)} %get-tuple-element.66.kept_a_ref, f32[256,1024]{1,0:T(8,128)S(1)} %get-tuple-element.67.kept_b_ref, bf16[128,1024]{1,0:T(8,128)(2,1)S(1)} %collective-permute-done.19.sum_a_ref, ...), custom_call_target="tpu_custom_call", output_to_operand_aliasing={{}: (4, {})} | custom-call | tf_op jit(solution)/shard_map/finish/pallas_call | solution.py:366
  (25 shorter events, 0.1 us)
Async XLA Ops:
  3.2 12.3 %collective-permute-start = (bf16[6,128,128]{2,1,0:T(8,128)(2,1)}, bf16[6,128,128]{2,1,0:T(8,128)(2,1)S(1)}, u32[]{:S(2)}, u32[]{:S(2)}) collective-permute-start(bf16[6,128,128]{2,1,0:T(8,128)(2,1)} %get-tuple-element.43), channel_id=1, source_target_pairs={{0,24},{4,28},{8,16},{12,20},{16,8},{20,12},{24,0},{28,4},{1,25},{... | collective-permute-start | bytes 589832 | tf_op jit(solution)/shard_map/ppermute | solution.py:379
  8.4 6.4 %copy-start.11 = (bf16[6,128,128]{2,1,0:T(8,128)(2,1)S(1)}, bf16[6,128,128]{2,1,0:T(8,128)(2,1)}, u32[]{:S(2)}) copy-start(bf16[6,128,128]{2,1,0:T(8,128)(2,1)} %get-tuple-element.45) | copy-start | bytes 589828
  8.4 6.4 %copy-start.10 = (bf16[6,128,128]{2,1,0:T(8,128)(2,1)S(1)}, bf16[6,128,128]{2,1,0:T(8,128)(2,1)}, u32[]{:S(2)}) copy-start(bf16[6,128,128]{2,1,0:T(8,128)(2,1)} %get-tuple-element.46) | copy-start | bytes 589828
  8.4 7.2 %copy-start.9 = (bf16[6,128,128]{2,1,0:T(8,128)(2,1)S(1)}, bf16[6,128,128]{2,1,0:T(8,128)(2,1)}, u32[]{:S(2)}) copy-start(bf16[6,128,128]{2,1,0:T(8,128)(2,1)} %get-tuple-element.47) | copy-start | bytes 589828
  8.4 21.4 %copy-start.8 = (bf16[6,128,128]{2,1,0:T(8,128)(2,1)S(1)}, bf16[6,128,128]{2,1,0:T(8,128)(2,1)}, u32[]{:S(2)}) copy-start(bf16[6,128,128]{2,1,0:T(8,128)(2,1)} %get-tuple-element.48) | copy-start | bytes 589828
  8.4 21.4 %copy-start.7 = (bf16[6,128,128]{2,1,0:T(8,128)(2,1)S(1)}, bf16[6,128,128]{2,1,0:T(8,128)(2,1)}, u32[]{:S(2)}) copy-start(bf16[6,128,128]{2,1,0:T(8,128)(2,1)} %get-tuple-element.49) | copy-start | bytes 589828
  8.4 24.9 %copy-start.6 = (bf16[6,128,128]{2,1,0:T(8,128)(2,1)S(1)}, bf16[6,128,128]{2,1,0:T(8,128)(2,1)}, u32[]{:S(2)}) copy-start(bf16[6,128,128]{2,1,0:T(8,128)(2,1)} %get-tuple-element.50) | copy-start | bytes 589828
  8.4 33.7 %copy-start = (bf16[1024,1024]{1,0:T(8,128)(2,1)S(1)}, bf16[1024,1024]{1,0:T(8,128)(2,1)}, u32[]{:S(2)}) copy-start(bf16[1024,1024]{1,0:T(8,128)(2,1)} %constant.32.clone.refs_9_.sin_ref) | copy-start | bytes 6291460
  8.4 33.7 %copy-start.1 = (bf16[1024,1024]{1,0:T(8,128)(2,1)S(1)}, bf16[1024,1024]{1,0:T(8,128)(2,1)}, u32[]{:S(2)}) copy-start(bf16[1024,1024]{1,0:T(8,128)(2,1)} %constant.31.clone.refs_8_.cos_ref) | copy-start | bytes 6291460
  8.4 33.6 %copy-start.3 = (bf16[6,128,128]{2,1,0:T(8,128)(2,1)S(1)}, bf16[6,128,128]{2,1,0:T(8,128)(2,1)}, u32[]{:S(2)}) copy-start(bf16[6,128,128]{2,1,0:T(8,128)(2,1)} %get-tuple-element.51.refs_7_) | copy-start | bytes 589828
  8.5 33.6 %copy-start.4 = (f32[1024,128]{1,0:T(8,128)S(1)}, f32[1024,128]{1,0:T(8,128)}, u32[]{:S(2)}) copy-start(f32[1024,128]{1,0:T(8,128)} %constant.34.clone.refs_11_) | copy-start | bytes 1572868
  8.5 33.6 %copy-start.5 = (f32[1024,128]{1,0:T(8,128)S(1)}, f32[1024,128]{1,0:T(8,128)}, u32[]{:S(2)}) copy-start(f32[1024,128]{1,0:T(8,128)} %constant.33.clone.refs_10_) | copy-start | bytes 1572868
  11.7 48.2 %collective-permute-start.11 = (bf16[1024,1024]{1,0:T(8,128)(2,1)S(1)}, bf16[1024,1024]{1,0:T(8,128)(2,1)S(1)}, u32[]{:S(2)}, u32[]{:S(2)}) collective-permute-start(bf16[1024,1024]{1,0:T(8,128)(2,1)S(1)} %get-tuple-element.58), channel_id=1, source_target_pairs={{0,1},{1,0},{2,3},{3,2},{4,5},{5,4},{6,7},{7,6},{8,9},{9,8},{10,11... | collective-permute-start | bytes 6291464 | tf_op jit(solution)/shard_map/ppermute | solution.py:379
  13.2 46.8 %collective-permute-start.12 = (bf16[1024,1024]{1,0:T(8,128)(2,1)S(1)}, bf16[1024,1024]{1,0:T(8,128)(2,1)S(1)}, u32[]{:S(2)}, u32[]{:S(2)}) collective-permute-start(bf16[1024,1024]{1,0:T(8,128)(2,1)S(1)} %get-tuple-element.59), channel_id=1, source_target_pairs={{0,2},{1,3},{2,0},{3,1},{4,6},{5,7},{6,4},{7,5},{8,10},{9,11},{10,... | collective-permute-start | bytes 6291464 | tf_op jit(solution)/shard_map/ppermute | solution.py:379
  14.8 15.1 %collective-permute-start.1 = (bf16[6,128,128]{2,1,0:T(8,128)(2,1)S(1)}, bf16[6,128,128]{2,1,0:T(8,128)(2,1)S(1)}, u32[]{:S(2)}, u32[]{:S(2)}) collective-permute-start(bf16[6,128,128]{2,1,0:T(8,128)(2,1)S(1)} %copy-done.11), channel_id=1, source_target_pairs={{0,16},{4,20},{8,24},{12,28},{16,0},{20,4},{24,8},{28,12},{1,17},{... | collective-permute-start | bytes 589832 | tf_op jit(solution)/shard_map/ppermute | solution.py:379
  14.8 15.1 %collective-permute-start.2 = (bf16[6,128,128]{2,1,0:T(8,128)(2,1)S(1)}, bf16[6,128,128]{2,1,0:T(8,128)(2,1)S(1)}, u32[]{:S(2)}, u32[]{:S(2)}) collective-permute-start(bf16[6,128,128]{2,1,0:T(8,128)(2,1)S(1)} %copy-done.10), channel_id=1, source_target_pairs={{0,8},{4,12},{8,0},{12,4},{16,24},{20,28},{24,16},{28,20},{1,9},{5... | collective-permute-start | bytes 589832 | tf_op jit(solution)/shard_map/ppermute | solution.py:379
  15.6 17.8 %collective-permute-start.3 = (bf16[6,128,128]{2,1,0:T(8,128)(2,1)S(1)}, bf16[6,128,128]{2,1,0:T(8,128)(2,1)S(1)}, u32[]{:S(2)}, u32[]{:S(2)}) collective-permute-start(bf16[6,128,128]{2,1,0:T(8,128)(2,1)S(1)} %copy-done.9), channel_id=1, source_target_pairs={{0,28},{4,24},{8,20},{12,16},{16,12},{20,8},{24,4},{28,0},{1,29},{... | collective-permute-start | bytes 589832 | tf_op jit(solution)/shard_map/ppermute | solution.py:379
  29.8 12.3 %collective-permute-start.4 = (bf16[6,128,128]{2,1,0:T(8,128)(2,1)S(1)}, bf16[6,128,128]{2,1,0:T(8,128)(2,1)S(1)}, u32[]{:S(2)}, u32[]{:S(2)}) collective-permute-start(bf16[6,128,128]{2,1,0:T(8,128)(2,1)S(1)} %copy-done.8), channel_id=1, source_target_pairs={{0,20},{4,16},{8,28},{12,24},{16,4},{20,0},{24,12},{28,8},{1,21},{... | collective-permute-start | bytes 589832 | tf_op jit(solution)/shard_map/ppermute | solution.py:379
  29.8 12.2 %collective-permute-start.5 = (bf16[6,128,128]{2,1,0:T(8,128)(2,1)S(1)}, bf16[6,128,128]{2,1,0:T(8,128)(2,1)S(1)}, u32[]{:S(2)}, u32[]{:S(2)}) collective-permute-start(bf16[6,128,128]{2,1,0:T(8,128)(2,1)S(1)} %copy-done.7), channel_id=1, source_target_pairs={{0,12},{4,8},{8,4},{12,0},{16,28},{20,24},{24,20},{28,16},{1,13},{... | collective-permute-start | bytes 589832 | tf_op jit(solution)/shard_map/ppermute | solution.py:379
  33.4 8.7 %collective-permute-start.6 = (bf16[6,128,128]{2,1,0:T(8,128)(2,1)S(1)}, bf16[6,128,128]{2,1,0:T(8,128)(2,1)S(1)}, u32[]{:S(2)}, u32[]{:S(2)}) collective-permute-start(bf16[6,128,128]{2,1,0:T(8,128)(2,1)S(1)} %copy-done.6), channel_id=1, source_target_pairs={{0,4},{4,0},{8,12},{12,8},{16,20},{20,16},{24,28},{28,24},{1,5},{5... | collective-permute-start | bytes 589832 | tf_op jit(solution)/shard_map/ppermute | solution.py:379
  44.6 1.6 %collective-permute-start.7 = (bf16[4,2,128,128]{3,2,1,0:T(8,128)(2,1)S(1)}, bf16[4,2,128,128]{3,2,1,0:T(8,128)(2,1)S(1)}, u32[]{:S(2)}, u32[]{:S(2)}) collective-permute-start(bf16[4,2,128,128]{3,2,1,0:T(8,128)(2,1)S(1)} %get-tuple-element.54), channel_id=1, source_target_pairs={{0,4},{4,0},{8,12},{12,8},{16,20},{20,16},{24,28},{28,24},{1,5},{5... | collective-permute-start | bytes 786440 | tf_op jit(solution)/shard_map/ppermute | solution.py:379
  45.4 14.0 %copy-start.2 = (bf16[256,1024]{1,0:T(8,128)(2,1)S(1)}, bf16[256,1024]{1,0:T(8,128)(2,1)}, u32[]{:S(2)}) copy-start(bf16[256,1024]{1,0:T(8,128)(2,1)} %refs_4_.1) | copy-start | bytes 1572868
  46.2 8.3 %collective-permute-start.8 = (bf16[2,2,128,128]{3,2,1,0:T(8,128)(2,1)S(1)}, bf16[2,2,128,128]{3,2,1,0:T(8,128)(2,1)S(1)}, u32[]{:S(2)}, u32[]{:S(2)}) collective-permute-start(bf16[2,2,128,128]{3,2,1,0:T(8,128)(2,1)S(1)} %pad_maximum_fusion), channel_id=1, source_target_pairs={{0,24},{4,28},{8,16},{12,20},{16,8},{20,12},{24,0},{28,4},{1,25},{... | collective-permute-start | bytes 393224 | tf_op jit(solution)/shard_map/ppermute | solution.py:379
  48.2 11.1 %collective-permute-start.9 = (bf16[2,2,128,128]{3,2,1,0:T(8,128)(2,1)S(1)}, bf16[2,2,128,128]{3,2,1,0:T(8,128)(2,1)S(1)}, u32[]{:S(2)}, u32[]{:S(2)}) collective-permute-start(bf16[2,2,128,128]{3,2,1,0:T(8,128)(2,1)S(1)} %pad_maximum_fusion.1), channel_id=1, source_target_pairs={{0,16},{4,20},{8,24},{12,28},{16,0},{20,4},{24,8},{28,12},{1,17},{... | collective-permute-start | bytes 393224 | tf_op jit(solution)/shard_map/ppermute | solution.py:379
  48.3 11.0 %collective-permute-start.10 = (bf16[2,2,128,128]{3,2,1,0:T(8,128)(2,1)S(1)}, bf16[2,2,128,128]{3,2,1,0:T(8,128)(2,1)S(1)}, u32[]{:S(2)}, u32[]{:S(2)}) collective-permute-start(bf16[2,2,128,128]{3,2,1,0:T(8,128)(2,1)S(1)} %pad_maximum_fusion.2), channel_id=1, source_target_pairs={{0,8},{4,12},{8,0},{12,4},{16,24},{20,28},{24,16},{28,20},{1,9},{5... | collective-permute-start | bytes 393224 | tf_op jit(solution)/shard_map/ppermute | solution.py:379
  60.1 6.4 %collective-permute-start.13 = (bf16[1024,1024]{1,0:T(8,128)(2,1)S(1)}, bf16[1024,1024]{1,0:T(8,128)(2,1)S(1)}, u32[]{:S(2)}, u32[]{:S(2)}) collective-permute-start(bf16[1024,1024]{1,0:T(8,128)(2,1)S(1)} %collective-permute-done.11.refs_4_.refs_2_), channel_id=1, source_target_pairs={{0,4},{4,0},{8,12},{12,8},{16,20},{20,16},{24,28},{28,24},{1,5},{5... | collective-permute-start | bytes 6291464 | tf_op jit(solution)/shard_map/ppermute | solution.py:379
  60.1 11.0 %collective-permute-start.18 = (bf16[1024,1024]{1,0:T(8,128)(2,1)S(1)}, bf16[1024,1024]{1,0:T(8,128)(2,1)S(1)}, u32[]{:S(2)}, u32[]{:S(2)}) collective-permute-start(bf16[1024,1024]{1,0:T(8,128)(2,1)S(1)} %collective-permute-done.12.refs_6_.refs_4_), channel_id=1, source_target_pairs={{0,4},{4,0},{8,12},{12,8},{16,20},{20,16},{24,28},{28,24},{1,5},{5... | collective-permute-start | bytes 6291464 | tf_op jit(solution)/shard_map/ppermute | solution.py:379
  60.6 10.2 %collective-permute-start.16 = (bf16[128,1024]{1,0:T(8,128)(2,1)S(1)}, bf16[128,1024]{1,0:T(8,128)(2,1)S(1)}, u32[]{:S(2)}, u32[]{:S(2)}) collective-permute-start(bf16[128,1024]{1,0:T(8,128)(2,1)S(1)} %get-tuple-element.56.refs_0_), channel_id=1, source_target_pairs={{0,2},{1,3},{2,0},{3,1},{4,6},{5,7},{6,4},{7,5},{8,10},{9,11},{10,... | collective-permute-start | bytes 786440 | tf_op jit(solution)/shard_map/ppermute | solution.py:379
  62.1 8.9 %collective-permute-start.14 = (bf16[128,1024]{1,0:T(8,128)(2,1)S(1)}, bf16[128,1024]{1,0:T(8,128)(2,1)S(1)}, u32[]{:S(2)}, u32[]{:S(2)}) collective-permute-start(bf16[128,1024]{1,0:T(8,128)(2,1)S(1)} %get-tuple-element.56.refs_0_), channel_id=1, source_target_pairs={{0,1},{1,0},{2,3},{3,2},{4,5},{5,4},{6,7},{7,6},{8,9},{9,8},{10,11... | collective-permute-start | bytes 786440 | tf_op jit(solution)/shard_map/ppermute | solution.py:379
  66.5 8.7 %collective-permute-start.17 = (bf16[128,1024]{1,0:T(8,128)(2,1)S(1)}, bf16[128,1024]{1,0:T(8,128)(2,1)S(1)}, u32[]{:S(2)}, u32[]{:S(2)}) collective-permute-start(bf16[128,1024]{1,0:T(8,128)(2,1)S(1)} %get-tuple-element.63.refs_1_), channel_id=1, source_target_pairs={{0,2},{1,3},{2,0},{3,1},{4,6},{5,7},{6,4},{7,5},{8,10},{9,11},{10,... | collective-permute-start | bytes 786440 | tf_op jit(solution)/shard_map/ppermute | solution.py:379
  67.1 9.1 %collective-permute-start.15 = (bf16[128,1024]{1,0:T(8,128)(2,1)S(1)}, bf16[128,1024]{1,0:T(8,128)(2,1)S(1)}, u32[]{:S(2)}, u32[]{:S(2)}) collective-permute-start(bf16[128,1024]{1,0:T(8,128)(2,1)S(1)} %get-tuple-element.63.refs_1_), channel_id=1, source_target_pairs={{0,1},{1,0},{2,3},{3,2},{4,5},{5,4},{6,7},{7,6},{8,9},{9,8},{10,11... | collective-permute-start | bytes 786440 | tf_op jit(solution)/shard_map/ppermute | solution.py:379
  72.4 9.1 %collective-permute-start.21 = (bf16[128,1024]{1,0:T(8,128)(2,1)S(1)}, bf16[128,1024]{1,0:T(8,128)(2,1)S(1)}, u32[]{:S(2)}, u32[]{:S(2)}) collective-permute-start(bf16[128,1024]{1,0:T(8,128)(2,1)S(1)} %get-tuple-element.71), channel_id=1, source_target_pairs={{0,2},{1,3},{2,0},{3,1},{4,6},{5,7},{6,4},{7,5},{8,10},{9,11},{10,... | collective-permute-start | bytes 786440 | tf_op jit(solution)/shard_map/ppermute | solution.py:379
  73.8 9.2 %collective-permute-start.22 = (bf16[128,1024]{1,0:T(8,128)(2,1)S(1)}, bf16[128,1024]{1,0:T(8,128)(2,1)S(1)}, u32[]{:S(2)}, u32[]{:S(2)}) collective-permute-start(bf16[128,1024]{1,0:T(8,128)(2,1)S(1)} %get-tuple-element.72), channel_id=1, source_target_pairs={{0,1},{1,0},{2,3},{3,2},{4,5},{5,4},{6,7},{7,6},{8,9},{9,8},{10,11... | collective-permute-start | bytes 786440 | tf_op jit(solution)/shard_map/ppermute | solution.py:379
  77.6 8.1 %collective-permute-start.19 = (bf16[128,1024]{1,0:T(8,128)(2,1)S(1)}, bf16[128,1024]{1,0:T(8,128)(2,1)S(1)}, u32[]{:S(2)}, u32[]{:S(2)}) collective-permute-start(bf16[128,1024]{1,0:T(8,128)(2,1)S(1)} %get-tuple-element.69), channel_id=1, source_target_pairs={{0,2},{1,3},{2,0},{3,1},{4,6},{5,7},{6,4},{7,5},{8,10},{9,11},{10,... | collective-permute-start | bytes 786440 | tf_op jit(solution)/shard_map/ppermute | solution.py:379
  78.1 8.7 %collective-permute-start.20 = (bf16[128,1024]{1,0:T(8,128)(2,1)S(1)}, bf16[128,1024]{1,0:T(8,128)(2,1)S(1)}, u32[]{:S(2)}, u32[]{:S(2)}) collective-permute-start(bf16[128,1024]{1,0:T(8,128)(2,1)S(1)} %get-tuple-element.70), channel_id=1, source_target_pairs={{0,1},{1,0},{2,3},{3,2},{4,5},{5,4},{6,7},{7,6},{8,9},{9,8},{10,11... | collective-permute-start | bytes 786440 | tf_op jit(solution)/shard_map/ppermute | solution.py:379

commit v10 on v8

--- a/solution.py
+++ b/solution.py
@@ -350,29 +350,25 @@
     )(core, own, *moved_x, *moved_y, *weights)
 
 
-def finish_kernel(kept_a_ref, kept_b_ref, sum_a_ref, sum_b_ref, *refs):
+def finish_kernel(kept_ref, sum_ref, *refs):
     out_ref = refs[-1]
-    cols = kept_a_ref.shape[1]
-    out_ref[:, :cols] = (kept_a_ref[...] + sum_a_ref[...].astype(jnp.float32)).astype(out_ref.dtype)
-    out_ref[:, cols:] = (kept_b_ref[...] + sum_b_ref[...].astype(jnp.float32)).astype(out_ref.dtype)
-
-
-def finish(kept_a, kept_b, sum_a, sum_b, part, before):
-    rows, cols = sum_a.shape
-    total = kept_a.shape[0]
-    kept = pl.BlockSpec((rows, cols), lambda i: (part, 0))
-    sums = pl.BlockSpec((rows, cols), lambda i: (0, 0))
+    out_ref[...] = (kept_ref[...] + sum_ref[...].astype(jnp.float32)).astype(out_ref.dtype)
+
+
+def finish(kept, summed, part, side, before):
+    rows, cols = summed.shape
     earlier = [] if before is None else [before]
     return pl.pallas_call(
         finish_kernel,
         grid=(1,),
-        in_specs=[kept, kept, sums, sums] + [pl.BlockSpec(memory_space=pl.ANY)] * len(earlier),
-        out_specs=pl.BlockSpec((rows, 2 * cols), lambda i: (part, 0)),
-        out_shape=jax.ShapeDtypeStruct((total, 2 * cols), jnp.bfloat16),
-        input_output_aliases={4: 0} if earlier else {},
+        in_specs=[pl.BlockSpec((rows, cols), lambda i: (part, 0)), pl.BlockSpec((rows, cols), lambda i: (0, 0))]
+        + [pl.BlockSpec(memory_space=pl.ANY)] * len(earlier),
+        out_specs=pl.BlockSpec((rows, cols), lambda i: (part, side)),
+        out_shape=jax.ShapeDtypeStruct((kept.shape[0], 2 * cols), jnp.bfloat16),
+        input_output_aliases={2: 0} if earlier else {},
         compiler_params=pltpu.CompilerParams(vmem_limit_bytes=16 << 20),
         name="finish",
-    )(kept_a, kept_b, sum_a, sum_b, *earlier)
+    )(kept, summed, *earlier)
 
 
 def swap(data, axis, flip):
@@ -423,7 +419,8 @@
     kept_a, kept_b = add_moved(core, own_kept, moved_x, moved_y, weights, 0, True, jnp.float32)
     mixed = None
     for p in range(parts):
-        mixed = finish(kept_a, kept_b, sums_a[p], sums_b[p], p, mixed)
+        mixed = finish(kept_a, sums_a[p], p, 0, mixed)
+        mixed = finish(kept_b, sums_b[p], p, 1, mixed)
     return mixed
 
 

time: 87.9 us -> 87.9 us (level)
  Pallas kernels: 22.7 us -> 23.9 us
  waiting for transfers between devices: 36.2 us -> 35.1 us
    pallas_call x2 -> x4, Pallas kernels: 1.86 us -> 3.03 us  [finish(): pl.pallas_call(finish_kernel, grid=(1,), in_specs=[pl.BlockSpec((rows, co...]
    ppermute x23, waiting for transfers between devices: 36.2 us -> 35.1 us  [swap(): lax.ppermute(data, axis, [(i, i ^ flip) for i in range(lax.axis_size(axis...]
  transfers between devices with their start and end apart: 23 -> 23, of which waited for: 11 -> 10; matrix products, arithmetic and copies ran while one was open for 0% -> 0% of each run, Pallas kernels for 21% -> 23%
where the time goes in v10:
time: 87.9 us; the launch traced here: 87.8 us
  waiting for transfers between devices  35.1 us (40%)
  starting transfers between devices  28.3 us (32%)
  Pallas kernels  23.9 us (27%)
    ppermute x23, waiting for transfers between devices, swap(): lax.ppermute(data, axis, [(i, i ^ flip) for i in range(lax.axis_size(axis...  35.1 us
    ppermute x23, starting transfers between devices, swap(): lax.ppermute(data, axis, [(i, i ^ flip) for i in range(lax.axis_size(axis...  28.3 us
    pallas_call x2, Pallas kernels, own_part(): pl.pallas_call(own_kernel, grid_spec=pltpu.PrefetchScalarGridSpec(num_sca...  6.1 us
    pallas_call x3, Pallas kernels, add_moved(): pl.pallas_call(functools.partial(add_kernel, parts, kept), grid=(1,), in_...  4.65 us
    pallas_call x1, Pallas kernels, pack(): pl.pallas_call(functools.partial(pack_kernel, span), in_specs=[pl.BlockSp...  3.19 us
    pallas_call x1, Pallas kernels, take_blocks(): pl.pallas_call(take_kernel, in_specs=[pl.BlockSpec(memory_space=pltpu.SME...  3.19 us
    pallas_call x4, Pallas kernels, finish(): pl.pallas_call(finish_kernel, grid=(1,), in_specs=[pl.BlockSpec((rows, co...  3.03 us
    pallas_call x1, Pallas kernels, convolve(): pl.pallas_call(functools.partial(conv_kernel, order), in_specs=[smem] + [...  2.53 us
  transfers between devices with their start and end apart: 23, of which 10 were waited for; matrix products, arithmetic and copies ran while one was open for 0% of the time, Pallas kernels for 23%

profile of v10, /device:TPU:0, one launch (start us, length us, event | category | flops | bytes accessed | tf_op | source)
XLA Modules:
  0.0 87.8 jit_solution(10959252453052420606)
XLA Ops:
  0.0 3.2 %pack.1 = (bf16[6,128,128]{2,1,0:T(8,128)(2,1)}, bf16[6,128,128]{2,1,0:T(8,128)(2,1)}, bf16[6,128,128]{2,1,0:T(8,128)(2,1)}, bf16[6,128,128]{2,1,0:T(8,128)(2,1)...) custom-call(s32[1]{0:T(128)} %bitcast.1.me_ref, ...), custom_call_target="tpu_custom_call" | custom-call | tf_op jit(solution)/shard_map/pack/pallas_call | solution.py:79
  3.2 5.1 %collective-permute-start = (bf16[6,128,128]{2,1,0:T(8,128)(2,1)}, bf16[6,128,128]{2,1,0:T(8,128)(2,1)S(1)}, u32[]{:S(2)}, u32[]{:S(2)}) collective-permute-start(bf16[6,128,128]{2,1,0:T(8,128)(2,1)} %get-tuple-element.43), channel_id=1, source_target_pairs={{0,24},{4,28},{8,16},{12,20},{16,8},{20,12},{24,0},{28,4},{1,25},{... | collective-permute-start | bytes 589832 | tf_op jit(solution)/shard_map/ppermute | solution.py:375
  8.3 0.1 pad_add_fusion.places_ref
  8.4 0.0 copy-start
  8.4 0.0 copy-start.1
  8.4 0.0 copy-start.3
  8.5 0.0 copy-start.4
  8.5 0.0 copy-start.5
  8.5 3.2 %take_blocks.1 = (bf16[1024,1024]{1,0:T(8,128)(2,1)S(1)}, bf16[1024,1024]{1,0:T(8,128)(2,1)S(1)}) custom-call(s32[2]{0:T(128)S(1)} %pad_add_fusion.places_ref, bf16[1024,8192]{1,0:T(8,128)(2,1)} %refs_3_.3), custom_call_target="tpu_custom_call" | custom-call | bytes 134217728 | tf_op jit(solution)/shard_map/take_blocks/pallas_call | solution.py:117
  11.7 1.6 %collective-permute-start.11 = (bf16[1024,1024]{1,0:T(8,128)(2,1)S(1)}, bf16[1024,1024]{1,0:T(8,128)(2,1)S(1)}, u32[]{:S(2)}, u32[]{:S(2)}) collective-permute-start(bf16[1024,1024]{1,0:T(8,128)(2,1)S(1)} %get-tuple-element.58), channel_id=1, source_target_pairs={{0,1},{1,0},{2,3},{3,2},{4,5},{5,4},{6,7},{7,6},{8,9},{9,8},{10,11... | collective-permute-start | bytes 6291464 | tf_op jit(solution)/shard_map/ppermute | solution.py:375
  13.2 1.5 %collective-permute-start.12 = (bf16[1024,1024]{1,0:T(8,128)(2,1)S(1)}, bf16[1024,1024]{1,0:T(8,128)(2,1)S(1)}, u32[]{:S(2)}, u32[]{:S(2)}) collective-permute-start(bf16[1024,1024]{1,0:T(8,128)(2,1)S(1)} %get-tuple-element.59), channel_id=1, source_target_pairs={{0,2},{1,3},{2,0},{3,1},{4,6},{5,7},{6,4},{7,5},{8,10},{9,11},{10,... | collective-permute-start | bytes 6291464 | tf_op jit(solution)/shard_map/ppermute | solution.py:375
  14.8 0.0 collective-permute-start.1
  14.8 0.8 collective-permute-start.2
  15.5 0.0 collective-permute-done.refs_0_
  15.6 1.6 %collective-permute-start.3 = (bf16[6,128,128]{2,1,0:T(8,128)(2,1)S(1)}, bf16[6,128,128]{2,1,0:T(8,128)(2,1)S(1)}, u32[]{:S(2)}, u32[]{:S(2)}) collective-permute-start(bf16[6,128,128]{2,1,0:T(8,128)(2,1)S(1)} %copy-done.9), channel_id=1, source_target_pairs={{0,28},{4,24},{8,20},{12,16},{16,12},{20,8},{24,4},{28,0},{1,29},{... | collective-permute-start | bytes 589832 | tf_op jit(solution)/shard_map/ppermute | solution.py:375
  17.2 12.6 %collective-permute-done.1.refs_1_ = bf16[6,128,128]{2,1,0:T(8,128)(2,1)S(1)} collective-permute-done((bf16[6,128,128]{2,1,0:T(8,128)(2,1)S(1)}, bf16[6,128,128]{2,1,0:T(8,128)(2,1)S(1)}, u32[]{:S(2)}, u32[]{:S(2)}) %collective-permute-start.1) | collective-permute-done | bytes 196640 | tf_op jit(solution)/shard_map/ppermute | solution.py:375
  29.8 0.0 collective-permute-start.4
  29.8 0.0 collective-permute-done.2.refs_2_
  29.8 3.5 %collective-permute-start.5 = (bf16[6,128,128]{2,1,0:T(8,128)(2,1)S(1)}, bf16[6,128,128]{2,1,0:T(8,128)(2,1)S(1)}, u32[]{:S(2)}, u32[]{:S(2)}) collective-permute-start(bf16[6,128,128]{2,1,0:T(8,128)(2,1)S(1)} %copy-done.7), channel_id=1, source_target_pairs={{0,12},{4,8},{8,4},{12,0},{16,28},{20,24},{24,20},{28,16},{1,13},{... | collective-permute-start | bytes 589832 | tf_op jit(solution)/shard_map/ppermute | solution.py:375
  33.3 0.0 collective-permute-done.3.refs_3_
  33.4 0.0 collective-permute-start.6
  33.4 8.7 %collective-permute-done.4.refs_4_ = bf16[6,128,128]{2,1,0:T(8,128)(2,1)S(1)} collective-permute-done((bf16[6,128,128]{2,1,0:T(8,128)(2,1)S(1)}, bf16[6,128,128]{2,1,0:T(8,128)(2,1)S(1)}, u32[]{:S(2)}, u32[]{:S(2)}) %collective-permute-start.4) | collective-permute-done | bytes 196640 | tf_op jit(solution)/shard_map/ppermute | solution.py:375
  42.1 0.0 collective-permute-done.5.refs_5_
  42.1 0.0 collective-permute-done.6.refs_6_
  42.1 2.5 %convolve.1 = (bf16[4,2,128,128]{3,2,1,0:T(8,128)(2,1)S(1)}, bf16[1024,256]{1,0:T(8,128)(2,1)S(1)}, bf16[1024,256]{1,0:T(8,128)(2,1)S(1)}) custom-call(s32[1]{0:T(128)} %bitcast.1.me_ref, bf16[6,128,128]{2,1,0:T(8,128)(2,1)S(1)} %collective-permute-done.refs_0_, bf16[6,128,128]{2,1,0:T(8,128)(2,1)S(1)} %collective-permute-done.1.refs_1_, ...), custom_call_target="tpu_custom_call" | custom-call | flops 6710886400 | bytes 8388608 | tf_op jit(solution)/shard_map/convolve/pallas_call | solution.py:188
  44.7 0.1 collective-permute-start.7
  44.8 0.7 convolve_rest.1
  45.5 0.0 copy-start.2
  45.5 0.7 collective-permute-done.7
  46.3 2.0 %collective-permute-start.8 = (bf16[2,2,128,128]{3,2,1,0:T(8,128)(2,1)S(1)}, bf16[2,2,128,128]{3,2,1,0:T(8,128)(2,1)S(1)}, u32[]{:S(2)}, u32[]{:S(2)}) collective-permute-start(bf16[2,2,128,128]{3,2,1,0:T(8,128)(2,1)S(1)} %pad_maximum_fusion), channel_id=1, source_target_pairs={{0,24},{4,28},{8,16},{12,20},{16,8},{20,12},{24,0},{28,4},{1,25},{... | collective-permute-start | bytes 393224 | tf_op jit(solution)/shard_map/ppermute | solution.py:375
  48.3 0.1 collective-permute-start.9
  48.4 2.5 %collective-permute-start.10 = (bf16[2,2,128,128]{3,2,1,0:T(8,128)(2,1)S(1)}, bf16[2,2,128,128]{3,2,1,0:T(8,128)(2,1)S(1)}, u32[]{:S(2)}, u32[]{:S(2)}) collective-permute-start(bf16[2,2,128,128]{3,2,1,0:T(8,128)(2,1)S(1)} %pad_maximum_fusion.2), channel_id=1, source_target_pairs={{0,8},{4,12},{8,0},{12,4},{16,24},{20,28},{24,16},{28,20},{1,9},{5... | collective-permute-start | bytes 393224 | tf_op jit(solution)/shard_map/ppermute | solution.py:375
  51.0 3.7 %collective-permute-done.8.refs_0_ = bf16[2,2,128,128]{3,2,1,0:T(8,128)(2,1)S(1)} collective-permute-done((bf16[2,2,128,128]{3,2,1,0:T(8,128)(2,1)S(1)}, bf16[2,2,128,128]{3,2,1,0:T(8,128)(2,1)S(1)}, u32[]{:S(2)}, u32[]{:S(2)}) %collective-permute-start.8) | collective-permute-done | bytes 131104 | tf_op jit(solution)/shard_map/ppermute | solution.py:375
  54.6 4.8 %collective-permute-done.9.refs_1_ = bf16[2,2,128,128]{3,2,1,0:T(8,128)(2,1)S(1)} collective-permute-done((bf16[2,2,128,128]{3,2,1,0:T(8,128)(2,1)S(1)}, bf16[2,2,128,128]{3,2,1,0:T(8,128)(2,1)S(1)}, u32[]{:S(2)}, u32[]{:S(2)}) %collective-permute-start.9) | collective-permute-done | bytes 131104 | tf_op jit(solution)/shard_map/ppermute | solution.py:375
  59.4 0.0 collective-permute-done.10.refs_2_
  59.4 0.5 gate.1
  59.9 0.0 collective-permute-done.11.refs_4_.refs_2_
  59.9 0.2 collective-permute-done.12.refs_6_.refs_4_
  60.1 0.0 collective-permute-start.13
  60.1 0.5 collective-permute-start.18
  60.6 1.5 %collective-permute-start.16 = (bf16[128,1024]{1,0:T(8,128)(2,1)S(1)}, bf16[128,1024]{1,0:T(8,128)(2,1)S(1)}, u32[]{:S(2)}, u32[]{:S(2)}) collective-permute-start(bf16[128,1024]{1,0:T(8,128)(2,1)S(1)} %get-tuple-element.56.refs_0_), channel_id=1, source_target_pairs={{0,2},{1,3},{2,0},{3,1},{4,6},{5,7},{6,4},{7,5},{8,10},{9,11},{10,... | collective-permute-start | bytes 786440 | tf_op jit(solution)/shard_map/ppermute | solution.py:375
  62.1 1.4 %collective-permute-start.14 = (bf16[128,1024]{1,0:T(8,128)(2,1)S(1)}, bf16[128,1024]{1,0:T(8,128)(2,1)S(1)}, u32[]{:S(2)}, u32[]{:S(2)}) collective-permute-start(bf16[128,1024]{1,0:T(8,128)(2,1)S(1)} %get-tuple-element.56.refs_0_), channel_id=1, source_target_pairs={{0,1},{1,0},{2,3},{3,2},{4,5},{5,4},{6,7},{7,6},{8,9},{9,8},{10,11... | collective-permute-start | bytes 786440 | tf_op jit(solution)/shard_map/ppermute | solution.py:375
  63.5 3.1 %own_part.2.own_ref = f32[2,256,1024]{2,1,0:T(8,128)S(1)} custom-call(s32[1]{0:T(128)} %bitcast.2.me_ref, bf16[128,1024]{1,0:T(8,128)(2,1)S(1)} %get-tuple-element.56.refs_0_, bf16[128,1024]{1,0:T(8,128)(2,1)S(1)} %get-tuple-element.63.refs_1_, bf16[1024,8192]{1,0:T(8,128)(2,1)} %refs_3_.3, bf16[1024,8192]{1,0:T(8,128)(2,1)} %refs_3_.3), custom_call_target="tpu_custom_call" | custom-call | flops 1073741824 | bytes 4194304 | tf_op jit(solution)/shard_map/own_part/pallas_call | solution.py:267
  66.5 0.0 collective-permute-done.13.refs_5_.refs_3_
  66.5 0.6 collective-permute-start.17
  67.2 0.6 collective-permute-start.15
  67.7 3.0 %own_part.3.own_ref = f32[2,256,1024]{2,1,0:T(8,128)S(1)} custom-call(s32[1]{0:T(128)} %bitcast.2.me_ref, bf16[128,1024]{1,0:T(8,128)(2,1)S(1)} %get-tuple-element.56.refs_0_, bf16[128,1024]{1,0:T(8,128)(2,1)S(1)} %get-tuple-element.63.refs_1_, bf16[1024,8192]{1,0:T(8,128)(2,1)} %refs_3_.3, bf16[1024,8192]{1,0:T(8,128)(2,1)} %refs_3_.3), custom_call_target="tpu_custom_call" | custom-call | flops 1073741824 | bytes 4194304 | tf_op jit(solution)/shard_map/own_part/pallas_call | solution.py:267
  70.8 0.1 collective-permute-done.14.refs_0_
  70.9 1.4 %add_sent.3 = (bf16[128,1024]{1,0:T(8,128)(2,1)S(1)}, bf16[128,1024]{1,0:T(8,128)(2,1)S(1)}) custom-call(s32[1]{0:T(128)} %bitcast.core_ref, f32[2,256,1024]{2,1,0:T(8,128)S(1)} %own_part.2.own_ref, bf16[128,1024]{1,0:T(8,128)(2,1)S(1)} %collective-permute-done.14.refs_0_, bf16[128,1024]{1,0:T(8,128)(2,1)S(1)} %collective-permute-done.16.refs_2_.refs_1_, ...), custom_call_target="tpu_custom_call" | custom-call | flops 536870912 | bytes 4194304 | tf_op jit(solution)/shard_map/add_sent/pallas_call | solution.py:333
  72.3 1.8 %collective-permute-start.21 = (bf16[128,1024]{1,0:T(8,128)(2,1)S(1)}, bf16[128,1024]{1,0:T(8,128)(2,1)S(1)}, u32[]{:S(2)}, u32[]{:S(2)}) collective-permute-start(bf16[128,1024]{1,0:T(8,128)(2,1)S(1)} %get-tuple-element.71), channel_id=1, source_target_pairs={{0,1},{1,0},{2,3},{3,2},{4,5},{5,4},{6,7},{7,6},{8,9},{9,8},{10,11... | collective-permute-start | bytes 786440 | tf_op jit(solution)/shard_map/ppermute | solution.py:375
  74.1 1.1 %collective-permute-start.22 = (bf16[128,1024]{1,0:T(8,128)(2,1)S(1)}, bf16[128,1024]{1,0:T(8,128)(2,1)S(1)}, u32[]{:S(2)}, u32[]{:S(2)}) collective-permute-start(bf16[128,1024]{1,0:T(8,128)(2,1)S(1)} %get-tuple-element.72), channel_id=1, source_target_pairs={{0,2},{1,3},{2,0},{3,1},{4,6},{5,7},{6,4},{7,5},{8,10},{9,11},{10,... | collective-permute-start | bytes 786440 | tf_op jit(solution)/shard_map/ppermute | solution.py:375
  75.2 1.3 %collective-permute-done.15.refs_1_.refs_0_ = bf16[128,1024]{1,0:T(8,128)(2,1)S(1)} collective-permute-done((bf16[128,1024]{1,0:T(8,128)(2,1)S(1)}, bf16[128,1024]{1,0:T(8,128)(2,1)S(1)}, u32[]{:S(2)}, u32[]{:S(2)}) %collective-permute-start.15) | collective-permute-done | bytes 262176 | tf_op jit(solution)/shard_map/ppermute | solution.py:375
  76.5 1.4 %add_sent.2 = (bf16[128,1024]{1,0:T(8,128)(2,1)S(1)}, bf16[128,1024]{1,0:T(8,128)(2,1)S(1)}) custom-call(s32[1]{0:T(128)} %bitcast.core_ref, f32[2,256,1024]{2,1,0:T(8,128)S(1)} %own_part.2.own_ref, bf16[128,1024]{1,0:T(8,128)(2,1)S(1)} %collective-permute-done.15.refs_1_.refs_0_, bf16[128,1024]{1,0:T(8,128)(2,1)S(1)} %collective-permute-done.17.refs_3_.refs_1_, ...), custom_call_target="tpu_custom_call" | custom-call | flops 536870912 | bytes 4194304 | tf_op jit(solution)/shard_map/add_sent/pallas_call | solution.py:333
  77.9 0.5 collective-permute-start.20
  78.4 1.6 %collective-permute-start.19 = (bf16[128,1024]{1,0:T(8,128)(2,1)S(1)}, bf16[128,1024]{1,0:T(8,128)(2,1)S(1)}, u32[]{:S(2)}, u32[]{:S(2)}) collective-permute-start(bf16[128,1024]{1,0:T(8,128)(2,1)S(1)} %get-tuple-element.68), channel_id=1, source_target_pairs={{0,1},{1,0},{2,3},{3,2},{4,5},{5,4},{6,7},{7,6},{8,9},{9,8},{10,11... | collective-permute-start | bytes 786440 | tf_op jit(solution)/shard_map/ppermute | solution.py:375
  80.0 1.9 %add_kept.1 = (f32[256,1024]{1,0:T(8,128)S(1)}, f32[256,1024]{1,0:T(8,128)S(1)}) custom-call(s32[1]{0:T(128)} %bitcast.core_ref, f32[2,256,1024]{2,1,0:T(8,128)S(1)} %own_part.3.own_ref, bf16[128,1024]{1,0:T(8,128)(2,1)S(1)} %collective-permute-done.14.refs_0_, bf16[128,1024]{1,0:T(8,128)(2,1)S(1)} %collective-permute-done.15.refs_1_.refs_0_, ...), custom_call_target="tpu_custom_call" | custom-call | flops 1073741824 | bytes 4194304 | tf_op jit(solution)/shard_map/add_kept/pallas_call | solution.py:333
  81.9 0.5 collective-permute-done.22.sum_ref
  82.4 0.8 finish.4.refs_0_
  83.2 0.0 collective-permute-done.21.sum_ref
  83.2 0.8 finish.5.refs_0_
  84.0 2.3 %collective-permute-done.20.sum_ref = bf16[128,1024]{1,0:T(8,128)(2,1)S(1)} collective-permute-done((bf16[128,1024]{1,0:T(8,128)(2,1)S(1)}, bf16[128,1024]{1,0:T(8,128)(2,1)S(1)}, u32[]{:S(2)}, u32[]{:S(2)}) %collective-permute-start.20) | collective-permute-done | bytes 262176 | tf_op jit(solution)/shard_map/ppermute | solution.py:375
  86.3 0.7 finish.6.refs_0_
  87.0 0.0 collective-permute-done.19.sum_ref
  87.0 0.8 finish.7
  (27 shorter events, 0.1 us)
Async XLA Ops:
  3.2 12.3 %collective-permute-start = (bf16[6,128,128]{2,1,0:T(8,128)(2,1)}, bf16[6,128,128]{2,1,0:T(8,128)(2,1)S(1)}, u32[]{:S(2)}, u32[]{:S(2)}) collective-permute-start(bf16[6,128,128]{2,1,0:T(8,128)(2,1)} %get-tuple-element.43), channel_id=1, source_target_pairs={{0,24},{4,28},{8,16},{12,20},{16,8},{20,12},{24,0},{28,4},{1,25},{... | collective-permute-start | bytes 589832 | tf_op jit(solution)/shard_map/ppermute | solution.py:375
  8.4 6.4 %copy-start.11 = (bf16[6,128,128]{2,1,0:T(8,128)(2,1)S(1)}, bf16[6,128,128]{2,1,0:T(8,128)(2,1)}, u32[]{:S(2)}) copy-start(bf16[6,128,128]{2,1,0:T(8,128)(2,1)} %get-tuple-element.45) | copy-start | bytes 589828
  8.4 6.4 %copy-start.10 = (bf16[6,128,128]{2,1,0:T(8,128)(2,1)S(1)}, bf16[6,128,128]{2,1,0:T(8,128)(2,1)}, u32[]{:S(2)}) copy-start(bf16[6,128,128]{2,1,0:T(8,128)(2,1)} %get-tuple-element.46) | copy-start | bytes 589828
  8.4 7.2 %copy-start.9 = (bf16[6,128,128]{2,1,0:T(8,128)(2,1)S(1)}, bf16[6,128,128]{2,1,0:T(8,128)(2,1)}, u32[]{:S(2)}) copy-start(bf16[6,128,128]{2,1,0:T(8,128)(2,1)} %get-tuple-element.47) | copy-start | bytes 589828
  8.4 21.4 %copy-start.8 = (bf16[6,128,128]{2,1,0:T(8,128)(2,1)S(1)}, bf16[6,128,128]{2,1,0:T(8,128)(2,1)}, u32[]{:S(2)}) copy-start(bf16[6,128,128]{2,1,0:T(8,128)(2,1)} %get-tuple-element.48) | copy-start | bytes 589828
  8.4 21.4 %copy-start.7 = (bf16[6,128,128]{2,1,0:T(8,128)(2,1)S(1)}, bf16[6,128,128]{2,1,0:T(8,128)(2,1)}, u32[]{:S(2)}) copy-start(bf16[6,128,128]{2,1,0:T(8,128)(2,1)} %get-tuple-element.49) | copy-start | bytes 589828
  8.4 24.9 %copy-start.6 = (bf16[6,128,128]{2,1,0:T(8,128)(2,1)S(1)}, bf16[6,128,128]{2,1,0:T(8,128)(2,1)}, u32[]{:S(2)}) copy-start(bf16[6,128,128]{2,1,0:T(8,128)(2,1)} %get-tuple-element.50) | copy-start | bytes 589828
  8.4 33.7 %copy-start = (bf16[1024,1024]{1,0:T(8,128)(2,1)S(1)}, bf16[1024,1024]{1,0:T(8,128)(2,1)}, u32[]{:S(2)}) copy-start(bf16[1024,1024]{1,0:T(8,128)(2,1)} %constant.32.clone.refs_9_.sin_ref) | copy-start | bytes 6291460
  8.4 33.7 %copy-start.1 = (bf16[1024,1024]{1,0:T(8,128)(2,1)S(1)}, bf16[1024,1024]{1,0:T(8,128)(2,1)}, u32[]{:S(2)}) copy-start(bf16[1024,1024]{1,0:T(8,128)(2,1)} %constant.31.clone.refs_8_.cos_ref) | copy-start | bytes 6291460
  8.4 33.6 %copy-start.3 = (bf16[6,128,128]{2,1,0:T(8,128)(2,1)S(1)}, bf16[6,128,128]{2,1,0:T(8,128)(2,1)}, u32[]{:S(2)}) copy-start(bf16[6,128,128]{2,1,0:T(8,128)(2,1)} %get-tuple-element.51.refs_7_) | copy-start | bytes 589828
  8.5 33.6 %copy-start.4 = (f32[1024,128]{1,0:T(8,128)S(1)}, f32[1024,128]{1,0:T(8,128)}, u32[]{:S(2)}) copy-start(f32[1024,128]{1,0:T(8,128)} %constant.34.clone.refs_11_) | copy-start | bytes 1572868
  8.5 33.6 %copy-start.5 = (f32[1024,128]{1,0:T(8,128)S(1)}, f32[1024,128]{1,0:T(8,128)}, u32[]{:S(2)}) copy-start(f32[1024,128]{1,0:T(8,128)} %constant.33.clone.refs_10_) | copy-start | bytes 1572868
  11.7 48.2 %collective-permute-start.11 = (bf16[1024,1024]{1,0:T(8,128)(2,1)S(1)}, bf16[1024,1024]{1,0:T(8,128)(2,1)S(1)}, u32[]{:S(2)}, u32[]{:S(2)}) collective-permute-start(bf16[1024,1024]{1,0:T(8,128)(2,1)S(1)} %get-tuple-element.58), channel_id=1, source_target_pairs={{0,1},{1,0},{2,3},{3,2},{4,5},{5,4},{6,7},{7,6},{8,9},{9,8},{10,11... | collective-permute-start | bytes 6291464 | tf_op jit(solution)/shard_map/ppermute | solution.py:375
  13.2 46.8 %collective-permute-start.12 = (bf16[1024,1024]{1,0:T(8,128)(2,1)S(1)}, bf16[1024,1024]{1,0:T(8,128)(2,1)S(1)}, u32[]{:S(2)}, u32[]{:S(2)}) collective-permute-start(bf16[1024,1024]{1,0:T(8,128)(2,1)S(1)} %get-tuple-element.59), channel_id=1, source_target_pairs={{0,2},{1,3},{2,0},{3,1},{4,6},{5,7},{6,4},{7,5},{8,10},{9,11},{10,... | collective-permute-start | bytes 6291464 | tf_op jit(solution)/shard_map/ppermute | solution.py:375
  14.8 15.1 %collective-permute-start.1 = (bf16[6,128,128]{2,1,0:T(8,128)(2,1)S(1)}, bf16[6,128,128]{2,1,0:T(8,128)(2,1)S(1)}, u32[]{:S(2)}, u32[]{:S(2)}) collective-permute-start(bf16[6,128,128]{2,1,0:T(8,128)(2,1)S(1)} %copy-done.11), channel_id=1, source_target_pairs={{0,16},{4,20},{8,24},{12,28},{16,0},{20,4},{24,8},{28,12},{1,17},{... | collective-permute-start | bytes 589832 | tf_op jit(solution)/shard_map/ppermute | solution.py:375
  14.8 15.1 %collective-permute-start.2 = (bf16[6,128,128]{2,1,0:T(8,128)(2,1)S(1)}, bf16[6,128,128]{2,1,0:T(8,128)(2,1)S(1)}, u32[]{:S(2)}, u32[]{:S(2)}) collective-permute-start(bf16[6,128,128]{2,1,0:T(8,128)(2,1)S(1)} %copy-done.10), channel_id=1, source_target_pairs={{0,8},{4,12},{8,0},{12,4},{16,24},{20,28},{24,16},{28,20},{1,9},{5... | collective-permute-start | bytes 589832 | tf_op jit(solution)/shard_map/ppermute | solution.py:375
  15.6 17.8 %collective-permute-start.3 = (bf16[6,128,128]{2,1,0:T(8,128)(2,1)S(1)}, bf16[6,128,128]{2,1,0:T(8,128)(2,1)S(1)}, u32[]{:S(2)}, u32[]{:S(2)}) collective-permute-start(bf16[6,128,128]{2,1,0:T(8,128)(2,1)S(1)} %copy-done.9), channel_id=1, source_target_pairs={{0,28},{4,24},{8,20},{12,16},{16,12},{20,8},{24,4},{28,0},{1,29},{... | collective-permute-start | bytes 589832 | tf_op jit(solution)/shard_map/ppermute | solution.py:375
  29.8 12.3 %collective-permute-start.4 = (bf16[6,128,128]{2,1,0:T(8,128)(2,1)S(1)}, bf16[6,128,128]{2,1,0:T(8,128)(2,1)S(1)}, u32[]{:S(2)}, u32[]{:S(2)}) collective-permute-start(bf16[6,128,128]{2,1,0:T(8,128)(2,1)S(1)} %copy-done.8), channel_id=1, source_target_pairs={{0,20},{4,16},{8,28},{12,24},{16,4},{20,0},{24,12},{28,8},{1,21},{... | collective-permute-start | bytes 589832 | tf_op jit(solution)/shard_map/ppermute | solution.py:375
  29.8 12.2 %collective-permute-start.5 = (bf16[6,128,128]{2,1,0:T(8,128)(2,1)S(1)}, bf16[6,128,128]{2,1,0:T(8,128)(2,1)S(1)}, u32[]{:S(2)}, u32[]{:S(2)}) collective-permute-start(bf16[6,128,128]{2,1,0:T(8,128)(2,1)S(1)} %copy-done.7), channel_id=1, source_target_pairs={{0,12},{4,8},{8,4},{12,0},{16,28},{20,24},{24,20},{28,16},{1,13},{... | collective-permute-start | bytes 589832 | tf_op jit(solution)/shard_map/ppermute | solution.py:375
  33.4 8.7 %collective-permute-start.6 = (bf16[6,128,128]{2,1,0:T(8,128)(2,1)S(1)}, bf16[6,128,128]{2,1,0:T(8,128)(2,1)S(1)}, u32[]{:S(2)}, u32[]{:S(2)}) collective-permute-start(bf16[6,128,128]{2,1,0:T(8,128)(2,1)S(1)} %copy-done.6), channel_id=1, source_target_pairs={{0,4},{4,0},{8,12},{12,8},{16,20},{20,16},{24,28},{28,24},{1,5},{5... | collective-permute-start | bytes 589832 | tf_op jit(solution)/shard_map/ppermute | solution.py:375
  44.7 1.6 %collective-permute-start.7 = (bf16[4,2,128,128]{3,2,1,0:T(8,128)(2,1)S(1)}, bf16[4,2,128,128]{3,2,1,0:T(8,128)(2,1)S(1)}, u32[]{:S(2)}, u32[]{:S(2)}) collective-permute-start(bf16[4,2,128,128]{3,2,1,0:T(8,128)(2,1)S(1)} %get-tuple-element.54), channel_id=1, source_target_pairs={{0,4},{4,0},{8,12},{12,8},{16,20},{20,16},{24,28},{28,24},{1,5},{5... | collective-permute-start | bytes 786440 | tf_op jit(solution)/shard_map/ppermute | solution.py:375
  45.5 13.9 %copy-start.2 = (bf16[256,1024]{1,0:T(8,128)(2,1)S(1)}, bf16[256,1024]{1,0:T(8,128)(2,1)}, u32[]{:S(2)}) copy-start(bf16[256,1024]{1,0:T(8,128)(2,1)} %refs_4_.1) | copy-start | bytes 1572868
  46.3 8.3 %collective-permute-start.8 = (bf16[2,2,128,128]{3,2,1,0:T(8,128)(2,1)S(1)}, bf16[2,2,128,128]{3,2,1,0:T(8,128)(2,1)S(1)}, u32[]{:S(2)}, u32[]{:S(2)}) collective-permute-start(bf16[2,2,128,128]{3,2,1,0:T(8,128)(2,1)S(1)} %pad_maximum_fusion), channel_id=1, source_target_pairs={{0,24},{4,28},{8,16},{12,20},{16,8},{20,12},{24,0},{28,4},{1,25},{... | collective-permute-start | bytes 393224 | tf_op jit(solution)/shard_map/ppermute | solution.py:375
  48.3 11.1 %collective-permute-start.9 = (bf16[2,2,128,128]{3,2,1,0:T(8,128)(2,1)S(1)}, bf16[2,2,128,128]{3,2,1,0:T(8,128)(2,1)S(1)}, u32[]{:S(2)}, u32[]{:S(2)}) collective-permute-start(bf16[2,2,128,128]{3,2,1,0:T(8,128)(2,1)S(1)} %pad_maximum_fusion.1), channel_id=1, source_target_pairs={{0,16},{4,20},{8,24},{12,28},{16,0},{20,4},{24,8},{28,12},{1,17},{... | collective-permute-start | bytes 393224 | tf_op jit(solution)/shard_map/ppermute | solution.py:375
  48.4 11.0 %collective-permute-start.10 = (bf16[2,2,128,128]{3,2,1,0:T(8,128)(2,1)S(1)}, bf16[2,2,128,128]{3,2,1,0:T(8,128)(2,1)S(1)}, u32[]{:S(2)}, u32[]{:S(2)}) collective-permute-start(bf16[2,2,128,128]{3,2,1,0:T(8,128)(2,1)S(1)} %pad_maximum_fusion.2), channel_id=1, source_target_pairs={{0,8},{4,12},{8,0},{12,4},{16,24},{20,28},{24,16},{28,20},{1,9},{5... | collective-permute-start | bytes 393224 | tf_op jit(solution)/shard_map/ppermute | solution.py:375
  60.1 6.5 %collective-permute-start.13 = (bf16[1024,1024]{1,0:T(8,128)(2,1)S(1)}, bf16[1024,1024]{1,0:T(8,128)(2,1)S(1)}, u32[]{:S(2)}, u32[]{:S(2)}) collective-permute-start(bf16[1024,1024]{1,0:T(8,128)(2,1)S(1)} %collective-permute-done.11.refs_4_.refs_2_), channel_id=1, source_target_pairs={{0,4},{4,0},{8,12},{12,8},{16,20},{20,16},{24,28},{28,24},{1,5},{5... | collective-permute-start | bytes 6291464 | tf_op jit(solution)/shard_map/ppermute | solution.py:375
  60.1 10.9 %collective-permute-start.18 = (bf16[1024,1024]{1,0:T(8,128)(2,1)S(1)}, bf16[1024,1024]{1,0:T(8,128)(2,1)S(1)}, u32[]{:S(2)}, u32[]{:S(2)}) collective-permute-start(bf16[1024,1024]{1,0:T(8,128)(2,1)S(1)} %collective-permute-done.12.refs_6_.refs_4_), channel_id=1, source_target_pairs={{0,4},{4,0},{8,12},{12,8},{16,20},{20,16},{24,28},{28,24},{1,5},{5... | collective-permute-start | bytes 6291464 | tf_op jit(solution)/shard_map/ppermute | solution.py:375
  60.6 10.2 %collective-permute-start.16 = (bf16[128,1024]{1,0:T(8,128)(2,1)S(1)}, bf16[128,1024]{1,0:T(8,128)(2,1)S(1)}, u32[]{:S(2)}, u32[]{:S(2)}) collective-permute-start(bf16[128,1024]{1,0:T(8,128)(2,1)S(1)} %get-tuple-element.56.refs_0_), channel_id=1, source_target_pairs={{0,2},{1,3},{2,0},{3,1},{4,6},{5,7},{6,4},{7,5},{8,10},{9,11},{10,... | collective-permute-start | bytes 786440 | tf_op jit(solution)/shard_map/ppermute | solution.py:375
  62.1 8.8 %collective-permute-start.14 = (bf16[128,1024]{1,0:T(8,128)(2,1)S(1)}, bf16[128,1024]{1,0:T(8,128)(2,1)S(1)}, u32[]{:S(2)}, u32[]{:S(2)}) collective-permute-start(bf16[128,1024]{1,0:T(8,128)(2,1)S(1)} %get-tuple-element.56.refs_0_), channel_id=1, source_target_pairs={{0,1},{1,0},{2,3},{3,2},{4,5},{5,4},{6,7},{7,6},{8,9},{9,8},{10,11... | collective-permute-start | bytes 786440 | tf_op jit(solution)/shard_map/ppermute | solution.py:375
  66.5 8.7 %collective-permute-start.17 = (bf16[128,1024]{1,0:T(8,128)(2,1)S(1)}, bf16[128,1024]{1,0:T(8,128)(2,1)S(1)}, u32[]{:S(2)}, u32[]{:S(2)}) collective-permute-start(bf16[128,1024]{1,0:T(8,128)(2,1)S(1)} %get-tuple-element.63.refs_1_), channel_id=1, source_target_pairs={{0,2},{1,3},{2,0},{3,1},{4,6},{5,7},{6,4},{7,5},{8,10},{9,11},{10,... | collective-permute-start | bytes 786440 | tf_op jit(solution)/shard_map/ppermute | solution.py:375
  67.2 9.4 %collective-permute-start.15 = (bf16[128,1024]{1,0:T(8,128)(2,1)S(1)}, bf16[128,1024]{1,0:T(8,128)(2,1)S(1)}, u32[]{:S(2)}, u32[]{:S(2)}) collective-permute-start(bf16[128,1024]{1,0:T(8,128)(2,1)S(1)} %get-tuple-element.63.refs_1_), channel_id=1, source_target_pairs={{0,1},{1,0},{2,3},{3,2},{4,5},{5,4},{6,7},{7,6},{8,9},{9,8},{10,11... | collective-permute-start | bytes 786440 | tf_op jit(solution)/shard_map/ppermute | solution.py:375
  72.3 10.9 %collective-permute-start.21 = (bf16[128,1024]{1,0:T(8,128)(2,1)S(1)}, bf16[128,1024]{1,0:T(8,128)(2,1)S(1)}, u32[]{:S(2)}, u32[]{:S(2)}) collective-permute-start(bf16[128,1024]{1,0:T(8,128)(2,1)S(1)} %get-tuple-element.71), channel_id=1, source_target_pairs={{0,1},{1,0},{2,3},{3,2},{4,5},{5,4},{6,7},{7,6},{8,9},{9,8},{10,11... | collective-permute-start | bytes 786440 | tf_op jit(solution)/shard_map/ppermute | solution.py:375
  74.1 8.3 %collective-permute-start.22 = (bf16[128,1024]{1,0:T(8,128)(2,1)S(1)}, bf16[128,1024]{1,0:T(8,128)(2,1)S(1)}, u32[]{:S(2)}, u32[]{:S(2)}) collective-permute-start(bf16[128,1024]{1,0:T(8,128)(2,1)S(1)} %get-tuple-element.72), channel_id=1, source_target_pairs={{0,2},{1,3},{2,0},{3,1},{4,6},{5,7},{6,4},{7,5},{8,10},{9,11},{10,... | collective-permute-start | bytes 786440 | tf_op jit(solution)/shard_map/ppermute | solution.py:375
  77.9 8.4 %collective-permute-start.20 = (bf16[128,1024]{1,0:T(8,128)(2,1)S(1)}, bf16[128,1024]{1,0:T(8,128)(2,1)S(1)}, u32[]{:S(2)}, u32[]{:S(2)}) collective-permute-start(bf16[128,1024]{1,0:T(8,128)(2,1)S(1)} %get-tuple-element.70), channel_id=1, source_target_pairs={{0,2},{1,3},{2,0},{3,1},{4,6},{5,7},{6,4},{7,5},{8,10},{9,11},{10,... | collective-permute-start | bytes 786440 | tf_op jit(solution)/shard_map/ppermute | solution.py:375
  78.4 8.6 %collective-permute-start.19 = (bf16[128,1024]{1,0:T(8,128)(2,1)S(1)}, bf16[128,1024]{1,0:T(8,128)(2,1)S(1)}, u32[]{:S(2)}, u32[]{:S(2)}) collective-permute-start(bf16[128,1024]{1,0:T(8,128)(2,1)S(1)} %get-tuple-element.68), channel_id=1, source_target_pairs={{0,1},{1,0},{2,3},{3,2},{4,5},{5,4},{6,7},{7,6},{8,9},{9,8},{10,11... | collective-permute-start | bytes 786440 | tf_op jit(solution)/shard_map/ppermute | solution.py:375

commit v11 on v8

--- a/solution.py
+++ b/solution.py
@@ -243,8 +243,7 @@
     )(me, *held, gate_out)
 
 
-def own_kernel(me_ref, *refs):
-    parts = (len(refs) - 1) // 2
+def own_kernel(parts, me_ref, *refs):
     gated, slabs, out_ref = refs[:parts], refs[parts:-1], refs[-1]
     rows, depth = gated[0].shape[0], slabs[0].shape[0]
     for p, gated_ref in enumerate(gated):
@@ -255,7 +254,7 @@
 
 
 def own_part(me, gated, weight, blocks):
-    parts = len(gated)
+    parts, slabs = len(gated), 4
     part_rows, depth = gated[0].shape
     cols = weight.shape[1] // 8
 
@@ -265,12 +264,12 @@
         return slab, (me_ref[0] ^ flip) * 2 + half
 
     return pl.pallas_call(
-        own_kernel,
+        functools.partial(own_kernel, parts),
         grid_spec=pltpu.PrefetchScalarGridSpec(
             num_scalar_prefetch=1,
             grid=(len(blocks),),
             in_specs=[pl.BlockSpec((part_rows, depth), lambda i, m: (0, 0))] * parts
-            + [pl.BlockSpec((depth // parts, cols), functools.partial(column, slab)) for slab in range(parts)],
+            + [pl.BlockSpec((depth // slabs, cols), functools.partial(column, slab)) for slab in range(slabs)],
             out_specs=pl.BlockSpec((1, parts * part_rows, cols), lambda i, m: (i, 0, 0)),
         ),
         out_shape=jax.ShapeDtypeStruct((len(blocks), parts * part_rows, cols), jnp.float32),
@@ -280,7 +279,7 @@
             bytes_accessed=2 * depth * cols * len(blocks), transcendentals=0,
         ),
         name="own_part",
-    )(me, *gated, *[weight] * parts)
+    )(me, *gated, *[weight] * slabs)
 
 
 def add_kernel(parts, kept, core_ref, own_ref, *refs):

time: 87.9 us -> 87.9 us (level)
  no operation moved by 1% of the time
where the time goes in v11:
time: 87.9 us; the launch traced here: 87.8 us
  waiting for transfers between devices  36.1 us (41%)
  starting transfers between devices  28.5 us (32%)
  Pallas kernels  22.7 us (26%)
    ppermute x23, waiting for transfers between devices, swap(): lax.ppermute(data, axis, [(i, i ^ flip) for i in range(lax.axis_size(axis...  36.1 us
    ppermute x23, starting transfers between devices, swap(): lax.ppermute(data, axis, [(i, i ^ flip) for i in range(lax.axis_size(axis...  28.5 us
    pallas_call x2, Pallas kernels, own_part(): pl.pallas_call(functools.partial(own_kernel, parts), grid_spec=pltpu.Pref...  6.12 us
    pallas_call x3, Pallas kernels, add_moved(): pl.pallas_call(functools.partial(add_kernel, parts, kept), grid=(1,), in_...  4.64 us
    pallas_call x1, Pallas kernels, pack(): pl.pallas_call(functools.partial(pack_kernel, span), in_specs=[pl.BlockSp...  3.19 us
    pallas_call x1, Pallas kernels, take_blocks(): pl.pallas_call(take_kernel, in_specs=[pl.BlockSpec(memory_space=pltpu.SME...  3.19 us
    pallas_call x1, Pallas kernels, convolve(): pl.pallas_call(functools.partial(conv_kernel, order), in_specs=[smem] + [...  2.53 us
    pallas_call x2, Pallas kernels, finish(): pl.pallas_call(finish_kernel, grid=(1,), in_specs=[kept, kept, sums, sums...  1.86 us
  transfers between devices with their start and end apart: 23, of which 11 were waited for; matrix products, arithmetic and copies ran while one was open for 0% of the time, Pallas kernels for 21%

profile of v11, /device:TPU:0, one launch (start us, length us, event | category | flops | bytes accessed | tf_op | source)
XLA Modules:
  0.0 87.8 jit_solution(11004398947392263354)
XLA Ops:
  0.0 3.2 %pack.1 = (bf16[6,128,128]{2,1,0:T(8,128)(2,1)}, bf16[6,128,128]{2,1,0:T(8,128)(2,1)}, bf16[6,128,128]{2,1,0:T(8,128)(2,1)}, bf16[6,128,128]{2,1,0:T(8,128)(2,1)...) custom-call(s32[1]{0:T(128)} %bitcast.1.me_ref, ...), custom_call_target="tpu_custom_call" | custom-call | tf_op jit(solution)/shard_map/pack/pallas_call | solution.py:79
  3.2 5.1 %collective-permute-start = (bf16[6,128,128]{2,1,0:T(8,128)(2,1)}, bf16[6,128,128]{2,1,0:T(8,128)(2,1)S(1)}, u32[]{:S(2)}, u32[]{:S(2)}) collective-permute-start(bf16[6,128,128]{2,1,0:T(8,128)(2,1)} %get-tuple-element.43), channel_id=1, source_target_pairs={{0,24},{4,28},{8,16},{12,20},{16,8},{20,12},{24,0},{28,4},{1,25},{... | collective-permute-start | bytes 589832 | tf_op jit(solution)/shard_map/ppermute | solution.py:378
  8.3 0.1 pad_add_fusion.places_ref
  8.4 0.0 copy-start
  8.4 0.0 copy-start.1
  8.4 0.0 copy-start.3
  8.5 0.0 copy-start.4
  8.5 0.0 copy-start.5
  8.5 3.2 %take_blocks.1 = (bf16[1024,1024]{1,0:T(8,128)(2,1)S(1)}, bf16[1024,1024]{1,0:T(8,128)(2,1)S(1)}) custom-call(s32[2]{0:T(128)S(1)} %pad_add_fusion.places_ref, bf16[1024,8192]{1,0:T(8,128)(2,1)} %refs_5_.3), custom_call_target="tpu_custom_call" | custom-call | bytes 134217728 | tf_op jit(solution)/shard_map/take_blocks/pallas_call | solution.py:117
  11.7 1.6 %collective-permute-start.11 = (bf16[1024,1024]{1,0:T(8,128)(2,1)S(1)}, bf16[1024,1024]{1,0:T(8,128)(2,1)S(1)}, u32[]{:S(2)}, u32[]{:S(2)}) collective-permute-start(bf16[1024,1024]{1,0:T(8,128)(2,1)S(1)} %get-tuple-element.58), channel_id=1, source_target_pairs={{0,1},{1,0},{2,3},{3,2},{4,5},{5,4},{6,7},{7,6},{8,9},{9,8},{10,11... | collective-permute-start | bytes 6291464 | tf_op jit(solution)/shard_map/ppermute | solution.py:378
  13.2 1.5 %collective-permute-start.12 = (bf16[1024,1024]{1,0:T(8,128)(2,1)S(1)}, bf16[1024,1024]{1,0:T(8,128)(2,1)S(1)}, u32[]{:S(2)}, u32[]{:S(2)}) collective-permute-start(bf16[1024,1024]{1,0:T(8,128)(2,1)S(1)} %get-tuple-element.59), channel_id=1, source_target_pairs={{0,2},{1,3},{2,0},{3,1},{4,6},{5,7},{6,4},{7,5},{8,10},{9,11},{10,... | collective-permute-start | bytes 6291464 | tf_op jit(solution)/shard_map/ppermute | solution.py:378
  14.8 0.0 collective-permute-start.1
  14.8 0.8 collective-permute-start.2
  15.5 0.0 collective-permute-done.refs_0_
  15.6 1.6 %collective-permute-start.3 = (bf16[6,128,128]{2,1,0:T(8,128)(2,1)S(1)}, bf16[6,128,128]{2,1,0:T(8,128)(2,1)S(1)}, u32[]{:S(2)}, u32[]{:S(2)}) collective-permute-start(bf16[6,128,128]{2,1,0:T(8,128)(2,1)S(1)} %copy-done.9), channel_id=1, source_target_pairs={{0,28},{4,24},{8,20},{12,16},{16,12},{20,8},{24,4},{28,0},{1,29},{... | collective-permute-start | bytes 589832 | tf_op jit(solution)/shard_map/ppermute | solution.py:378
  17.2 12.6 %collective-permute-done.1.refs_1_ = bf16[6,128,128]{2,1,0:T(8,128)(2,1)S(1)} collective-permute-done((bf16[6,128,128]{2,1,0:T(8,128)(2,1)S(1)}, bf16[6,128,128]{2,1,0:T(8,128)(2,1)S(1)}, u32[]{:S(2)}, u32[]{:S(2)}) %collective-permute-start.1) | collective-permute-done | bytes 196640 | tf_op jit(solution)/shard_map/ppermute | solution.py:378
  29.8 0.0 collective-permute-start.4
  29.8 0.0 collective-permute-done.2.refs_2_
  29.8 3.5 %collective-permute-start.5 = (bf16[6,128,128]{2,1,0:T(8,128)(2,1)S(1)}, bf16[6,128,128]{2,1,0:T(8,128)(2,1)S(1)}, u32[]{:S(2)}, u32[]{:S(2)}) collective-permute-start(bf16[6,128,128]{2,1,0:T(8,128)(2,1)S(1)} %copy-done.7), channel_id=1, source_target_pairs={{0,12},{4,8},{8,4},{12,0},{16,28},{20,24},{24,20},{28,16},{1,13},{... | collective-permute-start | bytes 589832 | tf_op jit(solution)/shard_map/ppermute | solution.py:378
  33.3 0.0 collective-permute-done.3.refs_3_
  33.4 0.0 collective-permute-start.6
  33.4 8.7 %collective-permute-done.4.refs_4_ = bf16[6,128,128]{2,1,0:T(8,128)(2,1)S(1)} collective-permute-done((bf16[6,128,128]{2,1,0:T(8,128)(2,1)S(1)}, bf16[6,128,128]{2,1,0:T(8,128)(2,1)S(1)}, u32[]{:S(2)}, u32[]{:S(2)}) %collective-permute-start.4) | collective-permute-done | bytes 196640 | tf_op jit(solution)/shard_map/ppermute | solution.py:378
  42.1 0.0 collective-permute-done.5.refs_5_
  42.1 0.0 collective-permute-done.6.refs_6_
  42.1 2.5 %convolve.1 = (bf16[4,2,128,128]{3,2,1,0:T(8,128)(2,1)S(1)}, bf16[1024,256]{1,0:T(8,128)(2,1)S(1)}, bf16[1024,256]{1,0:T(8,128)(2,1)S(1)}) custom-call(s32[1]{0:T(128)} %bitcast.1.me_ref, bf16[6,128,128]{2,1,0:T(8,128)(2,1)S(1)} %collective-permute-done.refs_0_, bf16[6,128,128]{2,1,0:T(8,128)(2,1)S(1)} %collective-permute-done.1.refs_1_, ...), custom_call_target="tpu_custom_call" | custom-call | flops 6710886400 | bytes 8388608 | tf_op jit(solution)/shard_map/convolve/pallas_call | solution.py:188
  44.7 0.1 collective-permute-start.7
  44.8 0.7 convolve_rest.1
  45.5 0.0 copy-start.2
  45.5 0.7 collective-permute-done.7
  46.3 2.0 %collective-permute-start.8 = (bf16[2,2,128,128]{3,2,1,0:T(8,128)(2,1)S(1)}, bf16[2,2,128,128]{3,2,1,0:T(8,128)(2,1)S(1)}, u32[]{:S(2)}, u32[]{:S(2)}) collective-permute-start(bf16[2,2,128,128]{3,2,1,0:T(8,128)(2,1)S(1)} %pad_maximum_fusion), channel_id=1, source_target_pairs={{0,24},{4,28},{8,16},{12,20},{16,8},{20,12},{24,0},{28,4},{1,25},{... | collective-permute-start | bytes 393224 | tf_op jit(solution)/shard_map/ppermute | solution.py:378
  48.3 0.1 collective-permute-start.9
  48.4 2.5 %collective-permute-start.10 = (bf16[2,2,128,128]{3,2,1,0:T(8,128)(2,1)S(1)}, bf16[2,2,128,128]{3,2,1,0:T(8,128)(2,1)S(1)}, u32[]{:S(2)}, u32[]{:S(2)}) collective-permute-start(bf16[2,2,128,128]{3,2,1,0:T(8,128)(2,1)S(1)} %pad_maximum_fusion.2), channel_id=1, source_target_pairs={{0,8},{4,12},{8,0},{12,4},{16,24},{20,28},{24,16},{28,20},{1,9},{5... | collective-permute-start | bytes 393224 | tf_op jit(solution)/shard_map/ppermute | solution.py:378
  51.0 3.7 %collective-permute-done.8.refs_0_ = bf16[2,2,128,128]{3,2,1,0:T(8,128)(2,1)S(1)} collective-permute-done((bf16[2,2,128,128]{3,2,1,0:T(8,128)(2,1)S(1)}, bf16[2,2,128,128]{3,2,1,0:T(8,128)(2,1)S(1)}, u32[]{:S(2)}, u32[]{:S(2)}) %collective-permute-start.8) | collective-permute-done | bytes 131104 | tf_op jit(solution)/shard_map/ppermute | solution.py:378
  54.6 4.8 %collective-permute-done.9.refs_1_ = bf16[2,2,128,128]{3,2,1,0:T(8,128)(2,1)S(1)} collective-permute-done((bf16[2,2,128,128]{3,2,1,0:T(8,128)(2,1)S(1)}, bf16[2,2,128,128]{3,2,1,0:T(8,128)(2,1)S(1)}, u32[]{:S(2)}, u32[]{:S(2)}) %collective-permute-start.9) | collective-permute-done | bytes 131104 | tf_op jit(solution)/shard_map/ppermute | solution.py:378
  59.4 0.0 collective-permute-done.10.refs_2_
  59.4 0.5 gate.1
  59.9 0.0 collective-permute-done.11.refs_4_.refs_2_
  59.9 0.2 collective-permute-done.12.refs_6_.refs_4_
  60.1 0.0 collective-permute-start.13
  60.1 0.5 collective-permute-start.18
  60.6 1.5 %collective-permute-start.16 = (bf16[128,1024]{1,0:T(8,128)(2,1)S(1)}, bf16[128,1024]{1,0:T(8,128)(2,1)S(1)}, u32[]{:S(2)}, u32[]{:S(2)}) collective-permute-start(bf16[128,1024]{1,0:T(8,128)(2,1)S(1)} %get-tuple-element.56.refs_0_), channel_id=1, source_target_pairs={{0,2},{1,3},{2,0},{3,1},{4,6},{5,7},{6,4},{7,5},{8,10},{9,11},{10,... | collective-permute-start | bytes 786440 | tf_op jit(solution)/shard_map/ppermute | solution.py:378
  62.1 1.4 %collective-permute-start.14 = (bf16[128,1024]{1,0:T(8,128)(2,1)S(1)}, bf16[128,1024]{1,0:T(8,128)(2,1)S(1)}, u32[]{:S(2)}, u32[]{:S(2)}) collective-permute-start(bf16[128,1024]{1,0:T(8,128)(2,1)S(1)} %get-tuple-element.56.refs_0_), channel_id=1, source_target_pairs={{0,1},{1,0},{2,3},{3,2},{4,5},{5,4},{6,7},{7,6},{8,9},{9,8},{10,11... | collective-permute-start | bytes 786440 | tf_op jit(solution)/shard_map/ppermute | solution.py:378
  63.5 3.1 %own_part.2.own_ref = f32[2,256,1024]{2,1,0:T(8,128)S(1)} custom-call(s32[1]{0:T(128)} %bitcast.2.me_ref, bf16[128,1024]{1,0:T(8,128)(2,1)S(1)} %get-tuple-element.56.refs_0_, bf16[128,1024]{1,0:T(8,128)(2,1)S(1)} %get-tuple-element.63.refs_1_, bf16[1024,8192]{1,0:T(8,128)(2,1)} %refs_5_.3, bf16[1024,8192]{1,0:T(8,128)(2,1)} %refs_5_.3, ...), custom_call_target="tpu_custom_call" | custom-call | flops 1073741824 | bytes 4194304 | tf_op jit(solution)/shard_map/own_part/pallas_call | solution.py:266
  66.5 0.0 collective-permute-done.13.refs_5_.refs_3_
  66.5 0.6 collective-permute-start.17
  67.2 0.6 collective-permute-start.15
  67.8 3.1 %own_part.3.own_ref = f32[2,256,1024]{2,1,0:T(8,128)S(1)} custom-call(s32[1]{0:T(128)} %bitcast.2.me_ref, bf16[128,1024]{1,0:T(8,128)(2,1)S(1)} %get-tuple-element.56.refs_0_, bf16[128,1024]{1,0:T(8,128)(2,1)S(1)} %get-tuple-element.63.refs_1_, bf16[1024,8192]{1,0:T(8,128)(2,1)} %refs_5_.3, bf16[1024,8192]{1,0:T(8,128)(2,1)} %refs_5_.3, ...), custom_call_target="tpu_custom_call" | custom-call | flops 1073741824 | bytes 4194304 | tf_op jit(solution)/shard_map/own_part/pallas_call | solution.py:266
  70.8 0.0 collective-permute-done.16.refs_2_.refs_1_
  70.8 0.1 collective-permute-done.14.refs_0_
  70.9 1.4 %add_sent.3 = (bf16[128,1024]{1,0:T(8,128)(2,1)S(1)}, bf16[128,1024]{1,0:T(8,128)(2,1)S(1)}) custom-call(s32[1]{0:T(128)} %bitcast.core_ref, f32[2,256,1024]{2,1,0:T(8,128)S(1)} %own_part.2.own_ref, bf16[128,1024]{1,0:T(8,128)(2,1)S(1)} %collective-permute-done.14.refs_0_, bf16[128,1024]{1,0:T(8,128)(2,1)S(1)} %collective-permute-done.16.refs_2_.refs_1_, ...), custom_call_target="tpu_custom_call" | custom-call | flops 536870912 | bytes 4194304 | tf_op jit(solution)/shard_map/add_sent/pallas_call | solution.py:332
  72.3 1.5 %collective-permute-start.21 = (bf16[128,1024]{1,0:T(8,128)(2,1)S(1)}, bf16[128,1024]{1,0:T(8,128)(2,1)S(1)}, u32[]{:S(2)}, u32[]{:S(2)}) collective-permute-start(bf16[128,1024]{1,0:T(8,128)(2,1)S(1)} %get-tuple-element.71), channel_id=1, source_target_pairs={{0,2},{1,3},{2,0},{3,1},{4,6},{5,7},{6,4},{7,5},{8,10},{9,11},{10,... | collective-permute-start | bytes 786440 | tf_op jit(solution)/shard_map/ppermute | solution.py:378
  73.8 1.4 %collective-permute-start.22 = (bf16[128,1024]{1,0:T(8,128)(2,1)S(1)}, bf16[128,1024]{1,0:T(8,128)(2,1)S(1)}, u32[]{:S(2)}, u32[]{:S(2)}) collective-permute-start(bf16[128,1024]{1,0:T(8,128)(2,1)S(1)} %get-tuple-element.72), channel_id=1, source_target_pairs={{0,1},{1,0},{2,3},{3,2},{4,5},{5,4},{6,7},{7,6},{8,9},{9,8},{10,11... | collective-permute-start | bytes 786440 | tf_op jit(solution)/shard_map/ppermute | solution.py:378
  75.2 0.0 collective-permute-done.17.refs_3_.refs_1_
  75.2 0.9 %collective-permute-done.15.refs_1_.refs_0_ = bf16[128,1024]{1,0:T(8,128)(2,1)S(1)} collective-permute-done((bf16[128,1024]{1,0:T(8,128)(2,1)S(1)}, bf16[128,1024]{1,0:T(8,128)(2,1)S(1)}, u32[]{:S(2)}, u32[]{:S(2)}) %collective-permute-start.15) | collective-permute-done | bytes 262176 | tf_op jit(solution)/shard_map/ppermute | solution.py:378
  76.2 1.4 %add_sent.2 = (bf16[128,1024]{1,0:T(8,128)(2,1)S(1)}, bf16[128,1024]{1,0:T(8,128)(2,1)S(1)}) custom-call(s32[1]{0:T(128)} %bitcast.core_ref, f32[2,256,1024]{2,1,0:T(8,128)S(1)} %own_part.2.own_ref, bf16[128,1024]{1,0:T(8,128)(2,1)S(1)} %collective-permute-done.15.refs_1_.refs_0_, bf16[128,1024]{1,0:T(8,128)(2,1)S(1)} %collective-permute-done.17.refs_3_.refs_1_, ...), custom_call_target="tpu_custom_call" | custom-call | flops 536870912 | bytes 4194304 | tf_op jit(solution)/shard_map/add_sent/pallas_call | solution.py:332
  77.5 0.5 collective-permute-start.19
  78.1 1.6 %collective-permute-start.20 = (bf16[128,1024]{1,0:T(8,128)(2,1)S(1)}, bf16[128,1024]{1,0:T(8,128)(2,1)S(1)}, u32[]{:S(2)}, u32[]{:S(2)}) collective-permute-start(bf16[128,1024]{1,0:T(8,128)(2,1)S(1)} %get-tuple-element.70), channel_id=1, source_target_pairs={{0,1},{1,0},{2,3},{3,2},{4,5},{5,4},{6,7},{7,6},{8,9},{9,8},{10,11... | collective-permute-start | bytes 786440 | tf_op jit(solution)/shard_map/ppermute | solution.py:378
  79.7 1.9 %add_kept.1 = (f32[256,1024]{1,0:T(8,128)S(1)}, f32[256,1024]{1,0:T(8,128)S(1)}) custom-call(s32[1]{0:T(128)} %bitcast.core_ref, f32[2,256,1024]{2,1,0:T(8,128)S(1)} %own_part.3.own_ref, bf16[128,1024]{1,0:T(8,128)(2,1)S(1)} %collective-permute-done.14.refs_0_, bf16[128,1024]{1,0:T(8,128)(2,1)S(1)} %collective-permute-done.15.refs_1_.refs_0_, ...), custom_call_target="tpu_custom_call" | custom-call | flops 1073741824 | bytes 4194304 | tf_op jit(solution)/shard_map/add_kept/pallas_call | solution.py:332
  81.6 0.0 collective-permute-done.21.sum_a_ref
  81.6 1.5 %collective-permute-done.22.sum_b_ref = bf16[128,1024]{1,0:T(8,128)(2,1)S(1)} collective-permute-done((bf16[128,1024]{1,0:T(8,128)(2,1)S(1)}, bf16[128,1024]{1,0:T(8,128)(2,1)S(1)}, u32[]{:S(2)}, u32[]{:S(2)}) %collective-permute-start.22) | collective-permute-done | bytes 262176 | tf_op jit(solution)/shard_map/ppermute | solution.py:378
  83.1 0.9 %finish.2.refs_0_ = bf16[256,2048]{1,0:T(8,128)(2,1)} custom-call(f32[256,1024]{1,0:T(8,128)S(1)} %get-tuple-element.66.kept_a_ref, f32[256,1024]{1,0:T(8,128)S(1)} %get-tuple-element.67.kept_b_ref, bf16[128,1024]{1,0:T(8,128)(2,1)S(1)} %collective-permute-done.21.sum_a_ref, bf16[128,1024]{1,0:T(8,128)(2,1)S(1)} %collective-permute-done.22.sum_b_ref), custom_call_target="tpu_custom_call" | custom-call | tf_op jit(solution)/shard_map/finish/pallas_call | solution.py:365
  84.0 1.6 %collective-permute-done.19.sum_a_ref = bf16[128,1024]{1,0:T(8,128)(2,1)S(1)} collective-permute-done((bf16[128,1024]{1,0:T(8,128)(2,1)S(1)}, bf16[128,1024]{1,0:T(8,128)(2,1)S(1)}, u32[]{:S(2)}, u32[]{:S(2)}) %collective-permute-start.19) | collective-permute-done | bytes 262176 | tf_op jit(solution)/shard_map/ppermute | solution.py:378
  85.6 1.2 %collective-permute-done.20.sum_b_ref = bf16[128,1024]{1,0:T(8,128)(2,1)S(1)} collective-permute-done((bf16[128,1024]{1,0:T(8,128)(2,1)S(1)}, bf16[128,1024]{1,0:T(8,128)(2,1)S(1)}, u32[]{:S(2)}, u32[]{:S(2)}) %collective-permute-start.20) | collective-permute-done | bytes 262176 | tf_op jit(solution)/shard_map/ppermute | solution.py:378
  86.9 0.9 %finish.3 = bf16[256,2048]{1,0:T(8,128)(2,1)} custom-call(f32[256,1024]{1,0:T(8,128)S(1)} %get-tuple-element.66.kept_a_ref, f32[256,1024]{1,0:T(8,128)S(1)} %get-tuple-element.67.kept_b_ref, bf16[128,1024]{1,0:T(8,128)(2,1)S(1)} %collective-permute-done.19.sum_a_ref, ...), custom_call_target="tpu_custom_call", output_to_operand_aliasing={{}: (4, {})} | custom-call | tf_op jit(solution)/shard_map/finish/pallas_call | solution.py:365
  (25 shorter events, 0.1 us)
Async XLA Ops:
  3.2 12.3 %collective-permute-start = (bf16[6,128,128]{2,1,0:T(8,128)(2,1)}, bf16[6,128,128]{2,1,0:T(8,128)(2,1)S(1)}, u32[]{:S(2)}, u32[]{:S(2)}) collective-permute-start(bf16[6,128,128]{2,1,0:T(8,128)(2,1)} %get-tuple-element.43), channel_id=1, source_target_pairs={{0,24},{4,28},{8,16},{12,20},{16,8},{20,12},{24,0},{28,4},{1,25},{... | collective-permute-start | bytes 589832 | tf_op jit(solution)/shard_map/ppermute | solution.py:378
  8.4 6.4 %copy-start.11 = (bf16[6,128,128]{2,1,0:T(8,128)(2,1)S(1)}, bf16[6,128,128]{2,1,0:T(8,128)(2,1)}, u32[]{:S(2)}) copy-start(bf16[6,128,128]{2,1,0:T(8,128)(2,1)} %get-tuple-element.45) | copy-start | bytes 589828
  8.4 6.4 %copy-start.10 = (bf16[6,128,128]{2,1,0:T(8,128)(2,1)S(1)}, bf16[6,128,128]{2,1,0:T(8,128)(2,1)}, u32[]{:S(2)}) copy-start(bf16[6,128,128]{2,1,0:T(8,128)(2,1)} %get-tuple-element.46) | copy-start | bytes 589828
  8.4 7.2 %copy-start.9 = (bf16[6,128,128]{2,1,0:T(8,128)(2,1)S(1)}, bf16[6,128,128]{2,1,0:T(8,128)(2,1)}, u32[]{:S(2)}) copy-start(bf16[6,128,128]{2,1,0:T(8,128)(2,1)} %get-tuple-element.47) | copy-start | bytes 589828
  8.4 21.4 %copy-start.8 = (bf16[6,128,128]{2,1,0:T(8,128)(2,1)S(1)}, bf16[6,128,128]{2,1,0:T(8,128)(2,1)}, u32[]{:S(2)}) copy-start(bf16[6,128,128]{2,1,0:T(8,128)(2,1)} %get-tuple-element.48) | copy-start | bytes 589828
  8.4 21.4 %copy-start.7 = (bf16[6,128,128]{2,1,0:T(8,128)(2,1)S(1)}, bf16[6,128,128]{2,1,0:T(8,128)(2,1)}, u32[]{:S(2)}) copy-start(bf16[6,128,128]{2,1,0:T(8,128)(2,1)} %get-tuple-element.49) | copy-start | bytes 589828
  8.4 24.9 %copy-start.6 = (bf16[6,128,128]{2,1,0:T(8,128)(2,1)S(1)}, bf16[6,128,128]{2,1,0:T(8,128)(2,1)}, u32[]{:S(2)}) copy-start(bf16[6,128,128]{2,1,0:T(8,128)(2,1)} %get-tuple-element.50) | copy-start | bytes 589828
  8.4 33.7 %copy-start = (bf16[1024,1024]{1,0:T(8,128)(2,1)S(1)}, bf16[1024,1024]{1,0:T(8,128)(2,1)}, u32[]{:S(2)}) copy-start(bf16[1024,1024]{1,0:T(8,128)(2,1)} %constant.32.clone.refs_9_.sin_ref) | copy-start | bytes 6291460
  8.4 33.7 %copy-start.1 = (bf16[1024,1024]{1,0:T(8,128)(2,1)S(1)}, bf16[1024,1024]{1,0:T(8,128)(2,1)}, u32[]{:S(2)}) copy-start(bf16[1024,1024]{1,0:T(8,128)(2,1)} %constant.31.clone.refs_8_.cos_ref) | copy-start | bytes 6291460
  8.4 33.6 %copy-start.3 = (bf16[6,128,128]{2,1,0:T(8,128)(2,1)S(1)}, bf16[6,128,128]{2,1,0:T(8,128)(2,1)}, u32[]{:S(2)}) copy-start(bf16[6,128,128]{2,1,0:T(8,128)(2,1)} %get-tuple-element.51.refs_7_) | copy-start | bytes 589828
  8.5 33.6 %copy-start.4 = (f32[1024,128]{1,0:T(8,128)S(1)}, f32[1024,128]{1,0:T(8,128)}, u32[]{:S(2)}) copy-start(f32[1024,128]{1,0:T(8,128)} %constant.34.clone.refs_11_) | copy-start | bytes 1572868
  8.5 33.6 %copy-start.5 = (f32[1024,128]{1,0:T(8,128)S(1)}, f32[1024,128]{1,0:T(8,128)}, u32[]{:S(2)}) copy-start(f32[1024,128]{1,0:T(8,128)} %constant.33.clone.refs_10_) | copy-start | bytes 1572868
  11.7 48.2 %collective-permute-start.11 = (bf16[1024,1024]{1,0:T(8,128)(2,1)S(1)}, bf16[1024,1024]{1,0:T(8,128)(2,1)S(1)}, u32[]{:S(2)}, u32[]{:S(2)}) collective-permute-start(bf16[1024,1024]{1,0:T(8,128)(2,1)S(1)} %get-tuple-element.58), channel_id=1, source_target_pairs={{0,1},{1,0},{2,3},{3,2},{4,5},{5,4},{6,7},{7,6},{8,9},{9,8},{10,11... | collective-permute-start | bytes 6291464 | tf_op jit(solution)/shard_map/ppermute | solution.py:378
  13.2 46.8 %collective-permute-start.12 = (bf16[1024,1024]{1,0:T(8,128)(2,1)S(1)}, bf16[1024,1024]{1,0:T(8,128)(2,1)S(1)}, u32[]{:S(2)}, u32[]{:S(2)}) collective-permute-start(bf16[1024,1024]{1,0:T(8,128)(2,1)S(1)} %get-tuple-element.59), channel_id=1, source_target_pairs={{0,2},{1,3},{2,0},{3,1},{4,6},{5,7},{6,4},{7,5},{8,10},{9,11},{10,... | collective-permute-start | bytes 6291464 | tf_op jit(solution)/shard_map/ppermute | solution.py:378
  14.8 15.1 %collective-permute-start.1 = (bf16[6,128,128]{2,1,0:T(8,128)(2,1)S(1)}, bf16[6,128,128]{2,1,0:T(8,128)(2,1)S(1)}, u32[]{:S(2)}, u32[]{:S(2)}) collective-permute-start(bf16[6,128,128]{2,1,0:T(8,128)(2,1)S(1)} %copy-done.11), channel_id=1, source_target_pairs={{0,16},{4,20},{8,24},{12,28},{16,0},{20,4},{24,8},{28,12},{1,17},{... | collective-permute-start | bytes 589832 | tf_op jit(solution)/shard_map/ppermute | solution.py:378
  14.8 15.1 %collective-permute-start.2 = (bf16[6,128,128]{2,1,0:T(8,128)(2,1)S(1)}, bf16[6,128,128]{2,1,0:T(8,128)(2,1)S(1)}, u32[]{:S(2)}, u32[]{:S(2)}) collective-permute-start(bf16[6,128,128]{2,1,0:T(8,128)(2,1)S(1)} %copy-done.10), channel_id=1, source_target_pairs={{0,8},{4,12},{8,0},{12,4},{16,24},{20,28},{24,16},{28,20},{1,9},{5... | collective-permute-start | bytes 589832 | tf_op jit(solution)/shard_map/ppermute | solution.py:378
  15.6 17.8 %collective-permute-start.3 = (bf16[6,128,128]{2,1,0:T(8,128)(2,1)S(1)}, bf16[6,128,128]{2,1,0:T(8,128)(2,1)S(1)}, u32[]{:S(2)}, u32[]{:S(2)}) collective-permute-start(bf16[6,128,128]{2,1,0:T(8,128)(2,1)S(1)} %copy-done.9), channel_id=1, source_target_pairs={{0,28},{4,24},{8,20},{12,16},{16,12},{20,8},{24,4},{28,0},{1,29},{... | collective-permute-start | bytes 589832 | tf_op jit(solution)/shard_map/ppermute | solution.py:378
  29.8 12.3 %collective-permute-start.4 = (bf16[6,128,128]{2,1,0:T(8,128)(2,1)S(1)}, bf16[6,128,128]{2,1,0:T(8,128)(2,1)S(1)}, u32[]{:S(2)}, u32[]{:S(2)}) collective-permute-start(bf16[6,128,128]{2,1,0:T(8,128)(2,1)S(1)} %copy-done.8), channel_id=1, source_target_pairs={{0,20},{4,16},{8,28},{12,24},{16,4},{20,0},{24,12},{28,8},{1,21},{... | collective-permute-start | bytes 589832 | tf_op jit(solution)/shard_map/ppermute | solution.py:378
  29.8 12.2 %collective-permute-start.5 = (bf16[6,128,128]{2,1,0:T(8,128)(2,1)S(1)}, bf16[6,128,128]{2,1,0:T(8,128)(2,1)S(1)}, u32[]{:S(2)}, u32[]{:S(2)}) collective-permute-start(bf16[6,128,128]{2,1,0:T(8,128)(2,1)S(1)} %copy-done.7), channel_id=1, source_target_pairs={{0,12},{4,8},{8,4},{12,0},{16,28},{20,24},{24,20},{28,16},{1,13},{... | collective-permute-start | bytes 589832 | tf_op jit(solution)/shard_map/ppermute | solution.py:378
  33.4 8.7 %collective-permute-start.6 = (bf16[6,128,128]{2,1,0:T(8,128)(2,1)S(1)}, bf16[6,128,128]{2,1,0:T(8,128)(2,1)S(1)}, u32[]{:S(2)}, u32[]{:S(2)}) collective-permute-start(bf16[6,128,128]{2,1,0:T(8,128)(2,1)S(1)} %copy-done.6), channel_id=1, source_target_pairs={{0,4},{4,0},{8,12},{12,8},{16,20},{20,16},{24,28},{28,24},{1,5},{5... | collective-permute-start | bytes 589832 | tf_op jit(solution)/shard_map/ppermute | solution.py:378
  44.7 1.6 %collective-permute-start.7 = (bf16[4,2,128,128]{3,2,1,0:T(8,128)(2,1)S(1)}, bf16[4,2,128,128]{3,2,1,0:T(8,128)(2,1)S(1)}, u32[]{:S(2)}, u32[]{:S(2)}) collective-permute-start(bf16[4,2,128,128]{3,2,1,0:T(8,128)(2,1)S(1)} %get-tuple-element.54), channel_id=1, source_target_pairs={{0,4},{4,0},{8,12},{12,8},{16,20},{20,16},{24,28},{28,24},{1,5},{5... | collective-permute-start | bytes 786440 | tf_op jit(solution)/shard_map/ppermute | solution.py:378
  45.5 13.9 %copy-start.2 = (bf16[256,1024]{1,0:T(8,128)(2,1)S(1)}, bf16[256,1024]{1,0:T(8,128)(2,1)}, u32[]{:S(2)}) copy-start(bf16[256,1024]{1,0:T(8,128)(2,1)} %refs_4_.3) | copy-start | bytes 1572868
  46.3 8.3 %collective-permute-start.8 = (bf16[2,2,128,128]{3,2,1,0:T(8,128)(2,1)S(1)}, bf16[2,2,128,128]{3,2,1,0:T(8,128)(2,1)S(1)}, u32[]{:S(2)}, u32[]{:S(2)}) collective-permute-start(bf16[2,2,128,128]{3,2,1,0:T(8,128)(2,1)S(1)} %pad_maximum_fusion), channel_id=1, source_target_pairs={{0,24},{4,28},{8,16},{12,20},{16,8},{20,12},{24,0},{28,4},{1,25},{... | collective-permute-start | bytes 393224 | tf_op jit(solution)/shard_map/ppermute | solution.py:378
  48.3 11.1 %collective-permute-start.9 = (bf16[2,2,128,128]{3,2,1,0:T(8,128)(2,1)S(1)}, bf16[2,2,128,128]{3,2,1,0:T(8,128)(2,1)S(1)}, u32[]{:S(2)}, u32[]{:S(2)}) collective-permute-start(bf16[2,2,128,128]{3,2,1,0:T(8,128)(2,1)S(1)} %pad_maximum_fusion.1), channel_id=1, source_target_pairs={{0,16},{4,20},{8,24},{12,28},{16,0},{20,4},{24,8},{28,12},{1,17},{... | collective-permute-start | bytes 393224 | tf_op jit(solution)/shard_map/ppermute | solution.py:378
  48.4 11.0 %collective-permute-start.10 = (bf16[2,2,128,128]{3,2,1,0:T(8,128)(2,1)S(1)}, bf16[2,2,128,128]{3,2,1,0:T(8,128)(2,1)S(1)}, u32[]{:S(2)}, u32[]{:S(2)}) collective-permute-start(bf16[2,2,128,128]{3,2,1,0:T(8,128)(2,1)S(1)} %pad_maximum_fusion.2), channel_id=1, source_target_pairs={{0,8},{4,12},{8,0},{12,4},{16,24},{20,28},{24,16},{28,20},{1,9},{5... | collective-permute-start | bytes 393224 | tf_op jit(solution)/shard_map/ppermute | solution.py:378
  60.1 6.5 %collective-permute-start.13 = (bf16[1024,1024]{1,0:T(8,128)(2,1)S(1)}, bf16[1024,1024]{1,0:T(8,128)(2,1)S(1)}, u32[]{:S(2)}, u32[]{:S(2)}) collective-permute-start(bf16[1024,1024]{1,0:T(8,128)(2,1)S(1)} %collective-permute-done.11.refs_4_.refs_2_), channel_id=1, source_target_pairs={{0,4},{4,0},{8,12},{12,8},{16,20},{20,16},{24,28},{28,24},{1,5},{5... | collective-permute-start | bytes 6291464 | tf_op jit(solution)/shard_map/ppermute | solution.py:378
  60.1 10.9 %collective-permute-start.18 = (bf16[1024,1024]{1,0:T(8,128)(2,1)S(1)}, bf16[1024,1024]{1,0:T(8,128)(2,1)S(1)}, u32[]{:S(2)}, u32[]{:S(2)}) collective-permute-start(bf16[1024,1024]{1,0:T(8,128)(2,1)S(1)} %collective-permute-done.12.refs_6_.refs_4_), channel_id=1, source_target_pairs={{0,4},{4,0},{8,12},{12,8},{16,20},{20,16},{24,28},{28,24},{1,5},{5... | collective-permute-start | bytes 6291464 | tf_op jit(solution)/shard_map/ppermute | solution.py:378
  60.6 10.3 %collective-permute-start.16 = (bf16[128,1024]{1,0:T(8,128)(2,1)S(1)}, bf16[128,1024]{1,0:T(8,128)(2,1)S(1)}, u32[]{:S(2)}, u32[]{:S(2)}) collective-permute-start(bf16[128,1024]{1,0:T(8,128)(2,1)S(1)} %get-tuple-element.56.refs_0_), channel_id=1, source_target_pairs={{0,2},{1,3},{2,0},{3,1},{4,6},{5,7},{6,4},{7,5},{8,10},{9,11},{10,... | collective-permute-start | bytes 786440 | tf_op jit(solution)/shard_map/ppermute | solution.py:378
  62.1 8.8 %collective-permute-start.14 = (bf16[128,1024]{1,0:T(8,128)(2,1)S(1)}, bf16[128,1024]{1,0:T(8,128)(2,1)S(1)}, u32[]{:S(2)}, u32[]{:S(2)}) collective-permute-start(bf16[128,1024]{1,0:T(8,128)(2,1)S(1)} %get-tuple-element.56.refs_0_), channel_id=1, source_target_pairs={{0,1},{1,0},{2,3},{3,2},{4,5},{5,4},{6,7},{7,6},{8,9},{9,8},{10,11... | collective-permute-start | bytes 786440 | tf_op jit(solution)/shard_map/ppermute | solution.py:378
  66.5 8.7 %collective-permute-start.17 = (bf16[128,1024]{1,0:T(8,128)(2,1)S(1)}, bf16[128,1024]{1,0:T(8,128)(2,1)S(1)}, u32[]{:S(2)}, u32[]{:S(2)}) collective-permute-start(bf16[128,1024]{1,0:T(8,128)(2,1)S(1)} %get-tuple-element.63.refs_1_), channel_id=1, source_target_pairs={{0,2},{1,3},{2,0},{3,1},{4,6},{5,7},{6,4},{7,5},{8,10},{9,11},{10,... | collective-permute-start | bytes 786440 | tf_op jit(solution)/shard_map/ppermute | solution.py:378
  67.2 9.0 %collective-permute-start.15 = (bf16[128,1024]{1,0:T(8,128)(2,1)S(1)}, bf16[128,1024]{1,0:T(8,128)(2,1)S(1)}, u32[]{:S(2)}, u32[]{:S(2)}) collective-permute-start(bf16[128,1024]{1,0:T(8,128)(2,1)S(1)} %get-tuple-element.63.refs_1_), channel_id=1, source_target_pairs={{0,1},{1,0},{2,3},{3,2},{4,5},{5,4},{6,7},{7,6},{8,9},{9,8},{10,11... | collective-permute-start | bytes 786440 | tf_op jit(solution)/shard_map/ppermute | solution.py:378
  72.3 9.3 %collective-permute-start.21 = (bf16[128,1024]{1,0:T(8,128)(2,1)S(1)}, bf16[128,1024]{1,0:T(8,128)(2,1)S(1)}, u32[]{:S(2)}, u32[]{:S(2)}) collective-permute-start(bf16[128,1024]{1,0:T(8,128)(2,1)S(1)} %get-tuple-element.71), channel_id=1, source_target_pairs={{0,2},{1,3},{2,0},{3,1},{4,6},{5,7},{6,4},{7,5},{8,10},{9,11},{10,... | collective-permute-start | bytes 786440 | tf_op jit(solution)/shard_map/ppermute | solution.py:378
  73.8 9.2 %collective-permute-start.22 = (bf16[128,1024]{1,0:T(8,128)(2,1)S(1)}, bf16[128,1024]{1,0:T(8,128)(2,1)S(1)}, u32[]{:S(2)}, u32[]{:S(2)}) collective-permute-start(bf16[128,1024]{1,0:T(8,128)(2,1)S(1)} %get-tuple-element.72), channel_id=1, source_target_pairs={{0,1},{1,0},{2,3},{3,2},{4,5},{5,4},{6,7},{7,6},{8,9},{9,8},{10,11... | collective-permute-start | bytes 786440 | tf_op jit(solution)/shard_map/ppermute | solution.py:378
  77.5 8.1 %collective-permute-start.19 = (bf16[128,1024]{1,0:T(8,128)(2,1)S(1)}, bf16[128,1024]{1,0:T(8,128)(2,1)S(1)}, u32[]{:S(2)}, u32[]{:S(2)}) collective-permute-start(bf16[128,1024]{1,0:T(8,128)(2,1)S(1)} %get-tuple-element.69), channel_id=1, source_target_pairs={{0,2},{1,3},{2,0},{3,1},{4,6},{5,7},{6,4},{7,5},{8,10},{9,11},{10,... | collective-permute-start | bytes 786440 | tf_op jit(solution)/shard_map/ppermute | solution.py:378
  78.1 8.8 %collective-permute-start.20 = (bf16[128,1024]{1,0:T(8,128)(2,1)S(1)}, bf16[128,1024]{1,0:T(8,128)(2,1)S(1)}, u32[]{:S(2)}, u32[]{:S(2)}) collective-permute-start(bf16[128,1024]{1,0:T(8,128)(2,1)S(1)} %get-tuple-element.70), channel_id=1, source_target_pairs={{0,1},{1,0},{2,3},{3,2},{4,5},{5,4},{6,7},{7,6},{8,9},{9,8},{10,11... | collective-permute-start | bytes 786440 | tf_op jit(solution)/shard_map/ppermute | solution.py:378
